TPU v7x, 32 devices: a whole 2x2x4 slice. The times are simulated.
32 devices in a mesh: prow: 4 (over y, x), pcol: 8 (over z, core).
Axes of the slice: x: 2, y: 2, z: 4, core: 2. Of those that a mesh axis runs over, the one named last changes fastest.
Arguments:
- matrix: float32 [4096, 2048], P('prow', 'pcol'), may hold values from -6 to 6
- l_panels: float32 [2, 4096, 256], P(None, ('prow', 'pcol')), may hold values from -0.375 to 0.375
- l_inverse: float32 [2, 256, 256], replicated, as said below
- pivots: int32 [2, 256], replicated, may hold values from 0 to 4095, as said below
Outputs:
- updated: float32 [4096, 2048], P('prow', 'pcol')
Inputs may be any that keep to these rules, and one draw needn't show every extreme that they name: `pivots`: for each step s, entry k is either s * 256 + k or a row at or after (s + 1) * 256; the entries of one step are distinct. `l_inverse`: each block is unit lower triangular.
All inputs are finite; a program needn't handle non-finite values.
Results may differ from a plain program's by a relative error of at most 0.0001.
Values sent between devices are 32-bit elements; how exact they have to be, the bound alone decides.
No kernel may reach another device: no remote copies, remote signals or barrier semaphores. Data moves between devices by JAX's collectives and lax.ppermute only.
A program may use at most 64 MiB of HBM per device.

v0:
```python
import jax
import jax.numpy as jnp
from jax import lax
from jax.sharding import PartitionSpec as P


def from_root(block, axis, source):
    block = jnp.where(lax.axis_index(axis) == source, block, jnp.zeros_like(block))
    return lax.psum(block, axis)


def per_device(matrix, l_panels, l_inverse, pivots):
    rows_dev = matrix.shape[0]
    first_row = lax.axis_index("prow") * rows_dev
    is_root = lax.axis_index("prow") == 0
    current = matrix
    for step in range(pivots.shape[0]):
        chosen = pivots[step]
        width = chosen.shape[0]
        begin = step * width
        offset = chosen - first_row
        owned = (offset >= 0) & (offset < rows_dev)
        clipped = jnp.clip(offset, 0, rows_dev - 1)
        own_rows = jnp.where(owned[:, None], current[clipped], jnp.float32(0.0))
        picked = lax.psum(own_rows, "prow")
        old_top = from_root(current[begin : begin + width], "prow", 0)
        target = jnp.where(owned, offset, rows_dev)
        current = current.at[target].set(old_top, mode="drop")
        upper = jnp.dot(
            l_inverse[step],
            picked,
            precision=lax.Precision.HIGHEST,
            preferred_element_type=jnp.float32,
        )
        kept_rows = current[begin : begin + width]
        current = current.at[begin : begin + width].set(jnp.where(is_root, upper, kept_rows))

        def apply_panel(piece, start, upper=upper, limit=begin + width):
            global_rows = first_row + jnp.arange(piece.shape[0], dtype=jnp.int32)
            factor = jnp.where((global_rows >= limit)[:, None], piece, jnp.float32(0.0))
            return jnp.dot(
                factor, upper, precision=lax.Precision.HIGHEST, preferred_element_type=jnp.float32
            )

        update = apply_panel(
            lax.all_gather(l_panels[step], "pcol", axis=0, tiled=True), jnp.int32(0)
        )
        current = current - update
    return current


def solution(mesh):
    placed = (P("prow", "pcol"), P(None, ("prow", "pcol"), None), P(), P())
    return jax.shard_map(
        per_device, mesh=mesh, in_specs=placed, out_specs=P("prow", "pcol"), check_vma=False
    )
```

profile of v0, /device:TPU:0, one launch (start us, length us, event | category | flops | bytes accessed | tf_op | source)
XLA Modules:
  0.0 130.7 jit_solution(606331782686596711)
XLA Ops:
  7.4 1.2 copy.39
  8.6 0.7 copy-done.5
  9.4 1.0 gather_fusion
  10.6 0.8 broadcast_select_fusion.1
  11.5 0.9 copy-done.4
  12.4 0.8 fusion.15
  13.3 46.6 %all-reduce.7.cloned.1.call-done = (f32[256,256]{0,1:T(8,128)}, f32[256,256]{0,1:T(8,128)}) async-done(((f32[256,256]{0,1:T(8,128)}, f32[256,256]{0,1:T(8,128)}), (f32[256,256]{0,1:T(8,128)}, f32[256,256]{0,1:T(8,128)})) %all-reduce.7.cloned.1.call-update) | async-done | bytes 524304 | tf_op jit(solution)/shard_map/psum | solution.py:9
  59.8 1.1 copy.16
  60.9 1.8 %scatter_fusion = f32[1024,256]{1,0:T(8,128)S(1)} fusion(f32[1024,256]{1,0:T(8,128)S(1)} %copy.39, s32[256]{0:T(256)S(1)} %bitcast.39, f32[256,256]{1,0:T(8,128)S(1)} %copy.16), kind=kCustom, calls=%fused_computation.2 | custom fusion | bytes 787456 | tf_op jit(solution)/shard_map/scatter | solution.py:28
  62.8 0.3 copy.19
  63.1 0.7 copy-done
  63.8 0.5 fusion.4
  64.4 2.4 %convolution_subtract_fusion.1 = f32[1024,256]{0,1:T(8,128)S(1)} fusion(f32[1024,256]{0,1:T(8,128)S(1)} %get-tuple-element.41, f32[256,256]{1,0:T(8,128)S(1)} %get-tuple-element.42, f32[1,1024,256]{2,1,0:T(8,128)} %all-gather.5.cloned.1.call-done, pred[1024]{0:T(1024)(128)(4,1)S(1)} %fusion.12), kind=kOutput, calls=%fused_computation.5 | convolution fusion | flops 805830656 | bytes 3408896 | tf_op jit(solution)/shard_map/dot_general | solution.py:41
  66.8 0.3 copy.21
  67.2 0.7 slice_select_fusion
  67.9 1.0 gather_fusion.1
  69.0 0.7 broadcast_select_fusion
  69.8 0.5 all-gather.7.cloned.1.call-update
  70.4 45.0 %all-reduce.5.cloned.1.call-done = (f32[256,256]{0,1:T(8,128)}, f32[256,256]{0,1:T(8,128)}) async-done(((f32[256,256]{0,1:T(8,128)}, f32[256,256]{0,1:T(8,128)}), (f32[256,256]{0,1:T(8,128)}, f32[256,256]{0,1:T(8,128)})) %all-reduce.5.cloned.1.call-update) | async-done | bytes 524304 | tf_op jit(solution)/shard_map/psum | solution.py:9
  115.4 1.1 copy.22
  116.5 1.8 %scatter_fusion.1 = f32[1024,256]{1,0:T(8,128)S(1)} fusion(f32[1024,256]{1,0:T(8,128)S(1)} %copy.21, s32[256]{0:T(256)S(1)} %bitcast.38, f32[256,256]{1,0:T(8,128)S(1)} %copy.22), kind=kCustom, calls=%fused_computation.3 | custom fusion | bytes 787456 | tf_op jit(solution)/shard_map/scatter | solution.py:28
  118.5 0.9 copy-done.1
  119.4 0.4 bitcast_select_fusion.4
  120.1 3.2 %convolution_subtract_fusion = f32[1024,256]{1,0:T(8,128)} fusion(f32[1024,256]{1,0:T(8,128)S(1)} %constant_dynamic-update-slice_fusion, f32[256,256]{1,0:T(8,128)S(1)} %get-tuple-element.44, f32[1,1024,256]{2,1,0:T(8,128)} %all-gather.7.cloned.1.call-done, pred[1024]{0:T(1024)(128)(4,1)S(1)} %fusion.11), kind=kOutput, calls=%fused_computation.4 | convolution fusion | flops 805830656 | bytes 3408896 | tf_op jit(solution)/shard_map/dot_general | solution.py:41
  (31 shorter events, 1.1 us)
Async XLA Ops:
  7.4 52.4 %all-reduce.7.cloned.1.call-start = ((), (), s32[]{:S(2)}) async-start(), calls=%async_computation.3 | async-start | bytes 1048576 | tf_op jit(solution)/shard_map/psum | solution.py:9
  8.6 0.7 copy-start.5
  11.4 0.9 copy-start.4
  11.5 52.9 %all-gather.5.cloned.1.call-start = ((), (), s32[]{:S(2)}) async-start(), calls=%async_computation | async-start | bytes 1179648 | tf_op jit(solution)/shard_map/all_gather | solution.py:46
  13.2 102.2 %all-reduce.5.cloned.1.call-start = ((), (), s32[]{:S(2)}) async-start(), calls=%async_computation.2 | async-start | bytes 1048576 | tf_op jit(solution)/shard_map/psum | solution.py:9
  62.7 1.0 copy-start
  62.7 1.1 copy-start.2
  69.8 50.3 %all-gather.7.cloned.1.call-start = ((), (), s32[]{:S(2)}) async-start(), calls=%async_computation.1 | async-start | bytes 1179648 | tf_op jit(solution)/shard_map/all_gather | solution.py:46
  118.3 1.0 copy-start.1
  118.4 1.1 copy-start.3
Sparse Core Ops, SparseCore 0:
  11.6 48.1 all-reduce.6
  69.9 45.4 all-reduce.4
Sparse Core Ops, SparseCore 1:
  13.5 24.6 all-gather.4
  71.9 21.9 all-gather.6
where the time goes:
time: 131 us
  waiting for transfers between devices  92.2 us (70%)
  between operations  15.1 us (12%)
  local copies, waits for them, and re-layouts  14.3 us (11%)
  matrix products  6.59 us (5%)
  other arithmetic  2.36 us (2%)
    psum x2, waiting for transfers between devices, from_root(): return lax.psum(block, axis)  91.6 us
    dot_general x2, matrix products, apply_panel(): jnp.dot(factor, upper, precision=lax.Precision.HIGHEST, preferred_element...  5.65 us
    unnamed x15, local copies, waits for them, and re-layouts  4.73 us
    scatter x3, local copies, waits for them, and re-layouts, per_device(): current = current.at[target].set(old_top, mode='drop')  3.99 us
  transfers between devices with their start and end apart: 4, of which 2 were waited for; matrix products, arithmetic and copies ran while one was open for 6% of the time, Pallas kernels for 0%

commit v1 on v0

v1 whole, which is shorter than its diff:
```python
import functools

import jax
import jax.numpy as jnp
from jax import lax
from jax.experimental import pallas as pl
from jax.experimental.pallas import tpu as pltpu
from jax.sharding import PartitionSpec as P

VMEM = pl.BlockSpec(memory_space=pltpu.VMEM)
SMEM = pl.BlockSpec(memory_space=pltpu.SMEM)
GRANT = pltpu.CompilerParams(vmem_limit_bytes=40 * 1024 * 1024)
F32 = jnp.float32


def split(values):
    high = values.astype(jnp.bfloat16)
    low = (values - high.astype(F32)).astype(jnp.bfloat16)
    return high, low


def dot(left, right):
    product = functools.partial(jnp.dot, preferred_element_type=F32)
    return product(left[0], right[0]) + (product(left[0], right[1]) + product(left[1], right[0]))


def slot_rows(source, pivots, step, width, rows_dev, out):
    row = lax.axis_index("prow")
    first = row * rows_dev
    begin = step * width

    def body(k, carry):
        offset = pivots[step, k] - first
        owned = (offset >= 0) & (offset < rows_dev)
        place = jnp.where(owned, offset, jnp.where(row == 0, begin + k, 0))
        out[pl.ds(k, 1), :] = source[pl.ds(place, 1), :]
        return carry

    lax.fori_loop(0, width, body, 0, unroll=8)


def first_slots(rows_dev, width, matrix, pivots, out):
    slot_rows(matrix, pivots, 0, width, rows_dev, out)


def merge(schedule, stage, sent, received, owner, outs):
    row = lax.axis_index("prow")
    start = 0
    for half, bits in enumerate(schedule):
        bit = bits[stage]
        known = sum(bits[:stage])
        partner = row ^ bit
        rows = sent[half].shape[0]
        who = owner[start : start + rows, :]
        keep = ~known
        theirs = ((who ^ partner) & keep) == 0
        neither = ((who ^ row) & ~(known | bit)) != 0
        take = theirs | (neither & ((partner & keep) == 0))
        outs[half][...] = jnp.where(take, received[half][...], sent[half][...])
        start += rows


def merge_kernel(schedule, stage, *refs):
    merge(schedule, stage, refs[0:2], refs[2:4], refs[4], refs[5:7])


def swap_and_solve(schedule, step, width, rows_dev, inverse, pivots, sent, received, owner, picked, displaced, current):
    row = lax.axis_index("prow")
    first = row * rows_dev
    begin = step * width
    stages = len(schedule[0])
    start = 0
    for half, bits in enumerate(schedule):
        rows = sent[half].shape[0]
        part = slice(start, start + rows)
        bit = bits[-1]
        mine = ((owner[part, :] ^ row) & bit) == 0
        picked[part, :] = jnp.where(mine, sent[half][...], received[stages - 1][half][...])
        value = received[stages - 1][half][...]
        for stage in reversed(range(stages - 1)):
            reached = (row & ~sum(bits[: stage + 1])) == 0
            value = jnp.where(reached, received[stage][half][...], value)
        displaced[part, :] = value
        start += rows

    @pl.when(row != 0)
    def _():
        def body(k, carry):
            offset = pivots[step, k] - first

            @pl.when((offset >= 0) & (offset < rows_dev))
            def _():
                current[pl.ds(offset, 1), :] = displaced[pl.ds(k, 1), :]

            return carry

        lax.fori_loop(0, width, body, 0, unroll=8)

    upper = dot(split(inverse[step]), split(picked[...]))

    @pl.when(row == 0)
    def _():
        displaced[...] = current[begin : begin + width, :]

        def body(k, carry):
            offset = pivots[step, k]

            @pl.when(offset < rows_dev)
            def _():
                current[pl.ds(offset, 1), :] = displaced[pl.ds(k, 1), :]

            return carry

        lax.fori_loop(0, width, body, 0, unroll=8)
        current[begin : begin + width, :] = upper

    return upper


def update_kernel(schedule, step, steps, width, matrix, pivots, inverse, owner, *refs):
    rows_dev = matrix.shape[0]
    stages = len(schedule[0])
    refs = list(refs)
    sent = [refs.pop(0) for _ in schedule]
    received = [[refs.pop(0) for _ in schedule] for _ in range(stages)]
    last = step == steps - 1
    picked, displaced = refs[-2:]
    outs = refs[-3:-2] if last else refs[-4:-2]
    blocks = refs[: -3 if last else -4]
    current = outs[0]
    current[...] = matrix[...]
    upper = swap_and_solve(
        schedule, step, width, rows_dev, inverse, pivots, sent, received, owner, picked, displaced, current
    )
    upper = split(upper)
    row = lax.axis_index("prow")
    col = lax.axis_index("pcol")
    pairs = len(blocks) // 2
    limit = (step + 1) * width
    for distance in range(pairs):
        chip = lax.rem(col // 2 - distance + pairs, pairs)
        for side in range(2):
            core = (col % 2) if side == 0 else 1 - (col % 2)
            block = blocks[side * pairs + distance]
            rows = block.shape[0]
            start = pl.multiple_of((chip * 2 + core) * rows, rows)
            index = row * rows_dev + start + lax.broadcasted_iota(jnp.int32, block.shape, 0)
            factor = jnp.where(index >= limit, block[...], F32(0))
            current[pl.ds(start, rows), :] -= dot(split(factor), upper)
    if not last:
        slot_rows(current, pivots, step + 1, width, rows_dev, outs[1])


def gather_panel(block, count):
    onward = [(i, (i + 2) % count) for i in range(count)]
    across = [(i, i ^ 1) for i in range(count)]
    own = [block]
    for _ in range(count // 2 - 1):
        own.append(lax.ppermute(own[-1], "pcol", onward))
    return own + [lax.ppermute(piece, "pcol", across) for piece in own]


def per_device(mesh, matrix, l_panels, l_inverse, pivots):
    rows_dev, columns = matrix.shape
    steps, width = pivots.shape
    process_rows, process_columns = mesh.shape["prow"], mesh.shape["pcol"]
    bits = [1 << b for b in range(process_rows.bit_length() - 1)]
    schedule = (tuple(bits), tuple(reversed(bits)))
    half = width // 2
    shape = jax.ShapeDtypeStruct
    owner = jnp.broadcast_to((pivots // rows_dev)[:, :, None], (steps, width, columns))

    slots = pl.pallas_call(
        functools.partial(first_slots, rows_dev, width),
        out_shape=shape((width, columns), F32),
        in_specs=[VMEM, SMEM],
        out_specs=VMEM,
        compiler_params=GRANT,
        name="first_slots",
    )(matrix, pivots)
    panels = [gather_panel(l_panels[step], process_columns) for step in range(steps)]
    current = matrix
    for step in range(steps):
        sent = [slots[:half], slots[half:]]
        received = []
        for stage in range(len(bits)):
            if stage:
                sent = pl.pallas_call(
                    functools.partial(merge_kernel, schedule, stage - 1),
                    out_shape=[shape((half, columns), F32)] * 2,
                    in_specs=[VMEM] * 5,
                    out_specs=[VMEM] * 2,
                    compiler_params=GRANT,
                    name="merge",
                )(*sent, *received[-1], owner[step])
            received.append(
                [
                    lax.ppermute(sent[h], "prow", [(i, i ^ schedule[h][stage]) for i in range(process_rows)])
                    for h in range(2)
                ]
            )
        last = step == steps - 1
        outs = [shape((rows_dev, columns), F32)] + ([] if last else [shape((width, columns), F32)])
        operands = [matrix if step == 0 else current, pivots, l_inverse, owner[step], *sent]
        operands += [piece for pair in received for piece in pair] + panels[step]
        result = pl.pallas_call(
            functools.partial(update_kernel, schedule, step, steps, width),
            out_shape=outs,
            in_specs=[VMEM, SMEM] + [VMEM] * (len(operands) - 2),
            out_specs=[VMEM] * len(outs),
            scratch_shapes=[pltpu.VMEM((width, columns), F32), pltpu.VMEM((width, columns), F32)],
            compiler_params=GRANT,
            name="update",
        )(*operands)
        current = result[0]
        slots = None if last else result[1]
    return current


def solution(mesh):
    placed = (P("prow", "pcol"), P(None, ("prow", "pcol"), None), P(), P())
    return jax.shard_map(
        functools.partial(per_device, mesh), mesh=mesh, in_specs=placed, out_specs=P("prow", "pcol"), check_vma=False
    )
```

time: 131 us -> 54.1 us (0.41)
  waiting for transfers between devices: 92.2 us -> 19.7 us
  starting transfers between devices: 0.13 us -> 17.3 us
  between operations: 15.1 us -> 0.13 us
  Pallas kernels: 0 us -> 14.4 us
  local copies, waits for them, and re-layouts: 14.3 us -> 2.47 us
  matrix products: 6.59 us -> 0 us
  other arithmetic: 2.36 us -> 0.01 us
    psum x2 -> x0, waiting for transfers between devices: 91.6 us -> none  [from_root(): return lax.psum(block, axis)]
    ppermute x0 -> x22, waiting for transfers between devices: none -> 19.7 us  [the longest x6 10.7 us: gather_panel(): own.append(lax.ppermute(own[-1], 'pcol', onward))]
    ppermute x0 -> x22, starting transfers between devices: none -> 17.3 us  [the longest x8 8.61 us: per_device(): lax.ppermute(sent[h], 'prow', [(i, i ^ schedule[h][stage]) for i in range...]
    pallas_call x0 -> x5, Pallas kernels: none -> 14.4 us  [the longest x2 12 us: per_device(): pl.pallas_call(functools.partial(update_kernel, schedule, step, steps, wi...]
    dot_general x4 -> x0, matrix products: 6.59 us -> none  [the longest x2 5.65 us: apply_panel(): jnp.dot(factor, upper, precision=lax.Precision.HIGHEST, preferred_element...]
    scatter x4 -> x0, local copies, waits for them, and re-layouts: 4.01 us -> none  [the longest x3 3.99 us: per_device(): current = current.at[target].set(old_top, mode='drop')]
    unnamed x15 -> x8, local copies, waits for them, and re-layouts: 4.73 us -> 1.24 us
    select_n x4 -> x1, other arithmetic: 2.31 us -> 0.01 us  [per_device(): pivots // rows_dev]
  transfers between devices with their start and end apart: 4 -> 22, of which waited for: 2 -> 8; matrix products, arithmetic and copies ran while one was open for 6% -> 0% of each run, Pallas kernels for 0% -> 16%
where the time goes in v1:
time: 54.1 us; the launch traced here: 53.9 us
  waiting for transfers between devices  19.7 us (36%)
  starting transfers between devices  17.3 us (32%)
  Pallas kernels  14.4 us (27%)
  local copies, waits for them, and re-layouts  2.47 us (5%)
    pallas_call x2, Pallas kernels, per_device(): pl.pallas_call(functools.partial(update_kernel, schedule, step, steps, wi...  12 us
    ppermute x6, waiting for transfers between devices, gather_panel(): own.append(lax.ppermute(own[-1], 'pcol', onward))  10.7 us
    ppermute x8, waiting for transfers between devices, per_device(): lax.ppermute(sent[h], 'prow', [(i, i ^ schedule[h][stage]) for i in range...  8.89 us
    ppermute x8, starting transfers between devices, per_device(): lax.ppermute(sent[h], 'prow', [(i, i ^ schedule[h][stage]) for i in range...  8.61 us
    ppermute x6, starting transfers between devices, gather_panel(): own.append(lax.ppermute(own[-1], 'pcol', onward))  7.65 us
    pallas_call x1, Pallas kernels, per_device(): pl.pallas_call(functools.partial(first_slots, rows_dev, width), out_shape...  2.23 us
    unnamed x8, local copies, waits for them, and re-layouts  1.24 us
  transfers between devices with their start and end apart: 22, of which 8 were waited for; matrix products, arithmetic and copies ran while one was open for 0% of the time, Pallas kernels for 16%

profile of v1, /device:TPU:0, one launch (start us, length us, event | category | flops | bytes accessed | tf_op | source)
XLA Modules:
  0.0 53.9 jit_solution(17862037964614549636)
XLA Ops:
  0.0 1.0 %slice_bitcast_fusion = (f32[128,256]{1,0:T(8,128)S(1)}, f32[128,256]{1,0:T(8,128)S(1)}) fusion(f32[2,128,256]{2,1,0:T(8,128)} %param.5), kind=kLoop, calls=%fused_computation | loop fusion | bytes 524288 | tf_op jit(solution)/shard_map/squeeze | solution.py:181
  1.0 3.1 %collective-permute-start.4 = (f32[128,256]{1,0:T(8,128)S(1)}, f32[128,256]{1,0:T(8,128)S(1)}, u32[]{:S(2)}, u32[]{:S(2)}) collective-permute-start(f32[128,256]{1,0:T(8,128)S(1)} %get-tuple-element.18.refs_6_), channel_id=1, source_target_pairs={{0,2},{1,3},{2,4},{3,5},{4,6},{5,7},{6,0},{7,1},{8,10},{9,11},{10,... | collective-permute-start | bytes 393224 | tf_op jit(solution)/shard_map/ppermute | solution.py:159
  4.1 1.2 %copy-done = f32[1024,256]{1,0:T(8,128)S(1)} copy-done((f32[1024,256]{1,0:T(8,128)S(1)}, f32[1024,256]{1,0:T(8,128)}, u32[]{:S(2)}) %copy-start) | copy-done | bytes 1048600
  5.3 2.2 %first_slots.1 = f32[256,256]{1,0:T(8,128)S(1)} custom-call(f32[1024,256]{1,0:T(8,128)S(1)} %copy-done, s32[2,256]{1,0:T(2,128)S(1)} %copy-done.3), custom_call_target="tpu_custom_call" | custom-call | tf_op jit(solution)/shard_map/first_slots/pallas_call | solution.py:173
  7.6 1.6 %collective-permute-start = (f32[128,256]{1,0:T(8,128)S(1)}, f32[128,256]{1,0:T(8,128)S(1)}, u32[]{:S(2)}, u32[]{:S(2)}) collective-permute-start(f32[128,256]{1,0:T(8,128)S(1)} %get-tuple-element.22.refs_0_), channel_id=1, source_target_pairs={{0,8},{8,0},{16,24},{24,16},{1,9},{9,1},{17,25},{25,17},{2,10},{10... | collective-permute-start | bytes 393224 | tf_op jit(solution)/shard_map/ppermute | solution.py:198
  9.1 1.5 %collective-permute-start.1 = (f32[128,256]{1,0:T(8,128)S(1)}, f32[128,256]{1,0:T(8,128)S(1)}, u32[]{:S(2)}, u32[]{:S(2)}) collective-permute-start(f32[128,256]{1,0:T(8,128)S(1)} %get-tuple-element.21.refs_1_), channel_id=1, source_target_pairs={{0,16},{8,24},{16,0},{24,8},{1,17},{9,25},{17,1},{25,9},{2,18},{10... | collective-permute-start | bytes 393224 | tf_op jit(solution)/shard_map/ppermute | solution.py:198
  10.7 1.6 %collective-permute-start.15 = (f32[128,256]{1,0:T(8,128)S(1)}, f32[128,256]{1,0:T(8,128)S(1)}, u32[]{:S(2)}, u32[]{:S(2)}) collective-permute-start(f32[128,256]{1,0:T(8,128)S(1)} %get-tuple-element.17.refs_6_), channel_id=1, source_target_pairs={{0,2},{1,3},{2,4},{3,5},{4,6},{5,7},{6,0},{7,1},{8,10},{9,11},{10,... | collective-permute-start | bytes 393224 | tf_op jit(solution)/shard_map/ppermute | solution.py:159
  12.3 1.6 %collective-permute-start.5 = (f32[128,256]{1,0:T(8,128)S(1)}, f32[128,256]{1,0:T(8,128)S(1)}, u32[]{:S(2)}, u32[]{:S(2)}) collective-permute-start(f32[128,256]{1,0:T(8,128)S(1)} %collective-permute-done.4.refs_7_), channel_id=1, source_target_pairs={{0,2},{1,3},{2,4},{3,5},{4,6},{5,7},{6,0},{7,1},{8,10},{9,11},{10,... | collective-permute-start | bytes 393224 | tf_op jit(solution)/shard_map/ppermute | solution.py:159
  13.9 0.9 %collective-permute-done.1.refs_3_ = f32[128,256]{1,0:T(8,128)S(1)} collective-permute-done((f32[128,256]{1,0:T(8,128)S(1)}, f32[128,256]{1,0:T(8,128)S(1)}, u32[]{:S(2)}, u32[]{:S(2)}) %collective-permute-start.1) | collective-permute-done | bytes 131104 | tf_op jit(solution)/shard_map/ppermute | solution.py:198
  15.0 1.6 %collective-permute-start.2 = (f32[128,256]{1,0:T(8,128)S(1)}, f32[128,256]{1,0:T(8,128)S(1)}, u32[]{:S(2)}, u32[]{:S(2)}) collective-permute-start(f32[128,256]{1,0:T(8,128)S(1)} %get-tuple-element.11.refs_0_), channel_id=1, source_target_pairs={{0,16},{8,24},{16,0},{24,8},{1,17},{9,25},{17,1},{25,9},{2,18},{10... | collective-permute-start | bytes 393224 | tf_op jit(solution)/shard_map/ppermute | solution.py:198
  16.6 4.1 %collective-permute-done.5.refs_8_ = f32[128,256]{1,0:T(8,128)S(1)} collective-permute-done((f32[128,256]{1,0:T(8,128)S(1)}, f32[128,256]{1,0:T(8,128)S(1)}, u32[]{:S(2)}, u32[]{:S(2)}) %collective-permute-start.5) | collective-permute-done | bytes 131104 | tf_op jit(solution)/shard_map/ppermute | solution.py:159
  20.6 0.5 collective-permute-start.3
  21.2 1.4 %collective-permute-start.16 = (f32[128,256]{1,0:T(8,128)S(1)}, f32[128,256]{1,0:T(8,128)S(1)}, u32[]{:S(2)}, u32[]{:S(2)}) collective-permute-start(f32[128,256]{1,0:T(8,128)S(1)} %collective-permute-done.15.refs_7_), channel_id=1, source_target_pairs={{0,2},{1,3},{2,4},{3,5},{4,6},{5,7},{6,0},{7,1},{8,10},{9,11},{10,... | collective-permute-start | bytes 393224 | tf_op jit(solution)/shard_map/ppermute | solution.py:159
  23.0 5.3 %collective-permute-done.6.refs_9_ = f32[128,256]{1,0:T(8,128)S(1)} collective-permute-done((f32[128,256]{1,0:T(8,128)S(1)}, f32[128,256]{1,0:T(8,128)S(1)}, u32[]{:S(2)}, u32[]{:S(2)}) %collective-permute-start.6) | collective-permute-done | bytes 131104 | tf_op jit(solution)/shard_map/ppermute | solution.py:159
  28.3 1.4 %collective-permute-done.16.refs_8_ = f32[128,256]{1,0:T(8,128)S(1)} collective-permute-done((f32[128,256]{1,0:T(8,128)S(1)}, f32[128,256]{1,0:T(8,128)S(1)}, u32[]{:S(2)}, u32[]{:S(2)}) %collective-permute-start.16) | collective-permute-done | bytes 131104 | tf_op jit(solution)/shard_map/ppermute | solution.py:159
  29.8 6.4 %update.2 = (f32[1024,256]{1,0:T(8,128)S(1)}, f32[256,256]{1,0:T(8,128)S(1)}) custom-call(f32[1024,256]{1,0:T(8,128)S(1)} %copy-done.1, s32[2,256]{1,0:T(2,128)S(1)} %copy-done.3, f32[2,256,256]{2,1,0:T(8,128)S(1)} %copy-done.2, s32[256,256]{1,0:T(8,128)S(1)} %broadcast_in_dim.13.refs_4_.owner, f32[128,256]{1,0:T(8,128)S(1)} %get-tuple-element.11.refs_0_, ...), custom_call_target="tpu_custom_call" | custom-call | tf_op jit(solution)/shard_map/update/pallas_call | solution.py:206
  36.2 0.8 %collective-permute-start.11 = (f32[128,256]{1,0:T(8,128)S(1)}, f32[128,256]{1,0:T(8,128)S(1)}, u32[]{:S(2)}, u32[]{:S(2)}) collective-permute-start(f32[128,256]{1,0:T(8,128)S(1)} %get-tuple-element.20.refs_0_), channel_id=1, source_target_pairs={{0,8},{8,0},{16,24},{24,16},{1,9},{9,1},{17,25},{25,17},{2,10},{10... | collective-permute-start | bytes 393224 | tf_op jit(solution)/shard_map/ppermute | solution.py:198
  37.0 0.5 collective-permute-start.12
  37.5 0.5 collective-permute-start.19
  38.1 3.6 %collective-permute-done.11.refs_2_ = f32[128,256]{1,0:T(8,128)S(1)} collective-permute-done((f32[128,256]{1,0:T(8,128)S(1)}, f32[128,256]{1,0:T(8,128)S(1)}, u32[]{:S(2)}, u32[]{:S(2)}) %collective-permute-start.11) | collective-permute-done | bytes 131104 | tf_op jit(solution)/shard_map/ppermute | solution.py:198
  42.4 0.6 %collective-permute-start.13 = (f32[128,256]{1,0:T(8,128)S(1)}, f32[128,256]{1,0:T(8,128)S(1)}, u32[]{:S(2)}, u32[]{:S(2)}) collective-permute-start(f32[128,256]{1,0:T(8,128)S(1)} %get-tuple-element.15.refs_0_), channel_id=1, source_target_pairs={{0,16},{8,24},{16,0},{24,8},{1,17},{9,25},{17,1},{25,9},{2,18},{10... | collective-permute-start | bytes 393224 | tf_op jit(solution)/shard_map/ppermute | solution.py:198
  43.0 1.5 %collective-permute-start.14 = (f32[128,256]{1,0:T(8,128)S(1)}, f32[128,256]{1,0:T(8,128)S(1)}, u32[]{:S(2)}, u32[]{:S(2)}) collective-permute-start(f32[128,256]{1,0:T(8,128)S(1)} %get-tuple-element.16.refs_1_), channel_id=1, source_target_pairs={{0,8},{8,0},{16,24},{24,16},{1,9},{9,1},{17,25},{25,17},{2,10},{10... | collective-permute-start | bytes 393224 | tf_op jit(solution)/shard_map/ppermute | solution.py:198
  44.5 3.4 %collective-permute-done.13.refs_4_ = f32[128,256]{1,0:T(8,128)S(1)} collective-permute-done((f32[128,256]{1,0:T(8,128)S(1)}, f32[128,256]{1,0:T(8,128)S(1)}, u32[]{:S(2)}, u32[]{:S(2)}) %collective-permute-start.13) | collective-permute-done | bytes 131104 | tf_op jit(solution)/shard_map/ppermute | solution.py:198
  48.3 5.6 %update.3 = f32[1024,256]{1,0:T(8,128)} custom-call(f32[1024,256]{1,0:T(8,128)S(1)} %get-tuple-element.13.matrix, s32[2,256]{1,0:T(2,128)S(1)} %copy-done.3, f32[2,256,256]{2,1,0:T(8,128)S(1)} %copy-done.2, s32[256,256]{1,0:T(8,128)S(1)} %broadcast_in_dim.15.refs_4_.owner, f32[128,256]{1,0:T(8,128)S(1)} %get-tuple-element.15.refs_0_, ...), custom_call_target="tpu_custom_call" | custom-call | tf_op jit(solution)/shard_map/update/pallas_call | solution.py:206
  (40 shorter events, 2.0 us)
Async XLA Ops:
  1.0 11.2 %collective-permute-start.4 = (f32[128,256]{1,0:T(8,128)S(1)}, f32[128,256]{1,0:T(8,128)S(1)}, u32[]{:S(2)}, u32[]{:S(2)}) collective-permute-start(f32[128,256]{1,0:T(8,128)S(1)} %get-tuple-element.18.refs_6_), channel_id=1, source_target_pairs={{0,2},{1,3},{2,4},{3,5},{4,6},{5,7},{6,0},{7,1},{8,10},{9,11},{10,... | collective-permute-start | bytes 393224 | tf_op jit(solution)/shard_map/ppermute | solution.py:159
  4.1 18.4 %collective-permute-start.7 = (f32[128,256]{1,0:T(8,128)S(1)}, f32[128,256]{1,0:T(8,128)S(1)}, u32[]{:S(2)}, u32[]{:S(2)}) collective-permute-start(f32[128,256]{1,0:T(8,128)S(1)} %get-tuple-element.18.refs_6_), channel_id=1, source_target_pairs={{0,1},{1,0},{2,3},{3,2},{4,5},{5,4},{6,7},{7,6},{8,9},{9,8},{10,11... | collective-permute-start | bytes 393224 | tf_op jit(solution)/shard_map/ppermute | solution.py:160
  7.5 22.2 %copy-start.1 = (f32[1024,256]{1,0:T(8,128)S(1)}, f32[1024,256]{1,0:T(8,128)}, u32[]{:S(2)}) copy-start(f32[1024,256]{1,0:T(8,128)} %matrix.3) | copy-start | bytes 3145732
  7.6 6.3 %collective-permute-start = (f32[128,256]{1,0:T(8,128)S(1)}, f32[128,256]{1,0:T(8,128)S(1)}, u32[]{:S(2)}, u32[]{:S(2)}) collective-permute-start(f32[128,256]{1,0:T(8,128)S(1)} %get-tuple-element.22.refs_0_), channel_id=1, source_target_pairs={{0,8},{8,0},{16,24},{24,16},{1,9},{9,1},{17,25},{25,17},{2,10},{10... | collective-permute-start | bytes 393224 | tf_op jit(solution)/shard_map/ppermute | solution.py:198
  9.1 5.6 %collective-permute-start.1 = (f32[128,256]{1,0:T(8,128)S(1)}, f32[128,256]{1,0:T(8,128)S(1)}, u32[]{:S(2)}, u32[]{:S(2)}) collective-permute-start(f32[128,256]{1,0:T(8,128)S(1)} %get-tuple-element.21.refs_1_), channel_id=1, source_target_pairs={{0,16},{8,24},{16,0},{24,8},{1,17},{9,25},{17,1},{25,9},{2,18},{10... | collective-permute-start | bytes 393224 | tf_op jit(solution)/shard_map/ppermute | solution.py:198
  10.7 10.5 %collective-permute-start.15 = (f32[128,256]{1,0:T(8,128)S(1)}, f32[128,256]{1,0:T(8,128)S(1)}, u32[]{:S(2)}, u32[]{:S(2)}) collective-permute-start(f32[128,256]{1,0:T(8,128)S(1)} %get-tuple-element.17.refs_6_), channel_id=1, source_target_pairs={{0,2},{1,3},{2,4},{3,5},{4,6},{5,7},{6,0},{7,1},{8,10},{9,11},{10,... | collective-permute-start | bytes 393224 | tf_op jit(solution)/shard_map/ppermute | solution.py:159
  12.3 8.4 %collective-permute-start.5 = (f32[128,256]{1,0:T(8,128)S(1)}, f32[128,256]{1,0:T(8,128)S(1)}, u32[]{:S(2)}, u32[]{:S(2)}) collective-permute-start(f32[128,256]{1,0:T(8,128)S(1)} %collective-permute-done.4.refs_7_), channel_id=1, source_target_pairs={{0,2},{1,3},{2,4},{3,5},{4,6},{5,7},{6,0},{7,1},{8,10},{9,11},{10,... | collective-permute-start | bytes 393224 | tf_op jit(solution)/shard_map/ppermute | solution.py:159
  14.8 15.0 %copy-start.2 = (f32[2,256,256]{2,1,0:T(8,128)S(1)}, f32[2,256,256]{2,1,0:T(8,128)}, u32[]{:S(2)}) copy-start(f32[2,256,256]{2,1,0:T(8,128)} %inverse.3) | copy-start | bytes 1572868
  15.0 7.6 %collective-permute-start.2 = (f32[128,256]{1,0:T(8,128)S(1)}, f32[128,256]{1,0:T(8,128)S(1)}, u32[]{:S(2)}, u32[]{:S(2)}) collective-permute-start(f32[128,256]{1,0:T(8,128)S(1)} %get-tuple-element.11.refs_0_), channel_id=1, source_target_pairs={{0,16},{8,24},{16,0},{24,8},{1,17},{9,25},{17,1},{25,9},{2,18},{10... | collective-permute-start | bytes 393224 | tf_op jit(solution)/shard_map/ppermute | solution.py:198
  20.6 7.7 %collective-permute-start.6 = (f32[128,256]{1,0:T(8,128)S(1)}, f32[128,256]{1,0:T(8,128)S(1)}, u32[]{:S(2)}, u32[]{:S(2)}) collective-permute-start(f32[128,256]{1,0:T(8,128)S(1)} %collective-permute-done.5.refs_8_), channel_id=1, source_target_pairs={{0,2},{1,3},{2,4},{3,5},{4,6},{5,7},{6,0},{7,1},{8,10},{9,11},{10,... | collective-permute-start | bytes 393224 | tf_op jit(solution)/shard_map/ppermute | solution.py:159
  20.6 9.1 %collective-permute-start.3 = (f32[128,256]{1,0:T(8,128)S(1)}, f32[128,256]{1,0:T(8,128)S(1)}, u32[]{:S(2)}, u32[]{:S(2)}) collective-permute-start(f32[128,256]{1,0:T(8,128)S(1)} %get-tuple-element.12.refs_1_), channel_id=1, source_target_pairs={{0,8},{8,0},{16,24},{24,16},{1,9},{9,1},{17,25},{25,17},{2,10},{10... | collective-permute-start | bytes 393224 | tf_op jit(solution)/shard_map/ppermute | solution.py:198
  21.2 8.6 %collective-permute-start.16 = (f32[128,256]{1,0:T(8,128)S(1)}, f32[128,256]{1,0:T(8,128)S(1)}, u32[]{:S(2)}, u32[]{:S(2)}) collective-permute-start(f32[128,256]{1,0:T(8,128)S(1)} %collective-permute-done.15.refs_7_), channel_id=1, source_target_pairs={{0,2},{1,3},{2,4},{3,5},{4,6},{5,7},{6,0},{7,1},{8,10},{9,11},{10,... | collective-permute-start | bytes 393224 | tf_op jit(solution)/shard_map/ppermute | solution.py:159
  22.5 7.2 %collective-permute-start.8 = (f32[128,256]{1,0:T(8,128)S(1)}, f32[128,256]{1,0:T(8,128)S(1)}, u32[]{:S(2)}, u32[]{:S(2)}) collective-permute-start(f32[128,256]{1,0:T(8,128)S(1)} %collective-permute-done.4.refs_7_), channel_id=1, source_target_pairs={{0,1},{1,0},{2,3},{3,2},{4,5},{5,4},{6,7},{7,6},{8,9},{9,8},{10,11... | collective-permute-start | bytes 393224 | tf_op jit(solution)/shard_map/ppermute | solution.py:160
  22.5 7.2 %collective-permute-start.9 = (f32[128,256]{1,0:T(8,128)S(1)}, f32[128,256]{1,0:T(8,128)S(1)}, u32[]{:S(2)}, u32[]{:S(2)}) collective-permute-start(f32[128,256]{1,0:T(8,128)S(1)} %collective-permute-done.5.refs_8_), channel_id=1, source_target_pairs={{0,1},{1,0},{2,3},{3,2},{4,5},{5,4},{6,7},{7,6},{8,9},{9,8},{10,11... | collective-permute-start | bytes 393224 | tf_op jit(solution)/shard_map/ppermute | solution.py:160
  28.3 1.4 %collective-permute-start.10 = (f32[128,256]{1,0:T(8,128)S(1)}, f32[128,256]{1,0:T(8,128)S(1)}, u32[]{:S(2)}, u32[]{:S(2)}) collective-permute-start(f32[128,256]{1,0:T(8,128)S(1)} %collective-permute-done.6.refs_9_), channel_id=1, source_target_pairs={{0,1},{1,0},{2,3},{3,2},{4,5},{5,4},{6,7},{7,6},{8,9},{9,8},{10,11... | collective-permute-start | bytes 393224 | tf_op jit(solution)/shard_map/ppermute | solution.py:160
  29.7 8.3 %collective-permute-start.17 = (f32[128,256]{1,0:T(8,128)S(1)}, f32[128,256]{1,0:T(8,128)S(1)}, u32[]{:S(2)}, u32[]{:S(2)}) collective-permute-start(f32[128,256]{1,0:T(8,128)S(1)} %collective-permute-done.16.refs_8_), channel_id=1, source_target_pairs={{0,2},{1,3},{2,4},{3,5},{4,6},{5,7},{6,0},{7,1},{8,10},{9,11},{10,... | collective-permute-start | bytes 393224 | tf_op jit(solution)/shard_map/ppermute | solution.py:159
  36.2 5.5 %collective-permute-start.11 = (f32[128,256]{1,0:T(8,128)S(1)}, f32[128,256]{1,0:T(8,128)S(1)}, u32[]{:S(2)}, u32[]{:S(2)}) collective-permute-start(f32[128,256]{1,0:T(8,128)S(1)} %get-tuple-element.20.refs_0_), channel_id=1, source_target_pairs={{0,8},{8,0},{16,24},{24,16},{1,9},{9,1},{17,25},{25,17},{2,10},{10... | collective-permute-start | bytes 393224 | tf_op jit(solution)/shard_map/ppermute | solution.py:198
  37.0 5.2 %collective-permute-start.12 = (f32[128,256]{1,0:T(8,128)S(1)}, f32[128,256]{1,0:T(8,128)S(1)}, u32[]{:S(2)}, u32[]{:S(2)}) collective-permute-start(f32[128,256]{1,0:T(8,128)S(1)} %get-tuple-element.19.refs_1_), channel_id=1, source_target_pairs={{0,16},{8,24},{16,0},{24,8},{1,17},{9,25},{17,1},{25,9},{2,18},{10... | collective-permute-start | bytes 393224 | tf_op jit(solution)/shard_map/ppermute | solution.py:198
  37.5 5.4 %collective-permute-start.18 = (f32[128,256]{1,0:T(8,128)S(1)}, f32[128,256]{1,0:T(8,128)S(1)}, u32[]{:S(2)}, u32[]{:S(2)}) collective-permute-start(f32[128,256]{1,0:T(8,128)S(1)} %get-tuple-element.17.refs_6_), channel_id=1, source_target_pairs={{0,1},{1,0},{2,3},{3,2},{4,5},{5,4},{6,7},{7,6},{8,9},{9,8},{10,11... | collective-permute-start | bytes 393224 | tf_op jit(solution)/shard_map/ppermute | solution.py:160
  37.5 6.9 %collective-permute-start.19 = (f32[128,256]{1,0:T(8,128)S(1)}, f32[128,256]{1,0:T(8,128)S(1)}, u32[]{:S(2)}, u32[]{:S(2)}) collective-permute-start(f32[128,256]{1,0:T(8,128)S(1)} %collective-permute-done.15.refs_7_), channel_id=1, source_target_pairs={{0,1},{1,0},{2,3},{3,2},{4,5},{5,4},{6,7},{7,6},{8,9},{9,8},{10,11... | collective-permute-start | bytes 393224 | tf_op jit(solution)/shard_map/ppermute | solution.py:160
  38.1 6.4 %collective-permute-start.20 = (f32[128,256]{1,0:T(8,128)S(1)}, f32[128,256]{1,0:T(8,128)S(1)}, u32[]{:S(2)}, u32[]{:S(2)}) collective-permute-start(f32[128,256]{1,0:T(8,128)S(1)} %collective-permute-done.16.refs_8_), channel_id=1, source_target_pairs={{0,1},{1,0},{2,3},{3,2},{4,5},{5,4},{6,7},{7,6},{8,9},{9,8},{10,11... | collective-permute-start | bytes 393224 | tf_op jit(solution)/shard_map/ppermute | solution.py:160
  41.7 2.8 %collective-permute-start.21 = (f32[128,256]{1,0:T(8,128)S(1)}, f32[128,256]{1,0:T(8,128)S(1)}, u32[]{:S(2)}, u32[]{:S(2)}) collective-permute-start(f32[128,256]{1,0:T(8,128)S(1)} %collective-permute-done.17.refs_9_), channel_id=1, source_target_pairs={{0,1},{1,0},{2,3},{3,2},{4,5},{5,4},{6,7},{7,6},{8,9},{9,8},{10,11... | collective-permute-start | bytes 393224 | tf_op jit(solution)/shard_map/ppermute | solution.py:160
  42.4 5.5 %collective-permute-start.13 = (f32[128,256]{1,0:T(8,128)S(1)}, f32[128,256]{1,0:T(8,128)S(1)}, u32[]{:S(2)}, u32[]{:S(2)}) collective-permute-start(f32[128,256]{1,0:T(8,128)S(1)} %get-tuple-element.15.refs_0_), channel_id=1, source_target_pairs={{0,16},{8,24},{16,0},{24,8},{1,17},{9,25},{17,1},{25,9},{2,18},{10... | collective-permute-start | bytes 393224 | tf_op jit(solution)/shard_map/ppermute | solution.py:198
  43.0 5.4 %collective-permute-start.14 = (f32[128,256]{1,0:T(8,128)S(1)}, f32[128,256]{1,0:T(8,128)S(1)}, u32[]{:S(2)}, u32[]{:S(2)}) collective-permute-start(f32[128,256]{1,0:T(8,128)S(1)} %get-tuple-element.16.refs_1_), channel_id=1, source_target_pairs={{0,8},{8,0},{16,24},{24,16},{1,9},{9,1},{17,25},{25,17},{2,10},{10... | collective-permute-start | bytes 393224 | tf_op jit(solution)/shard_map/ppermute | solution.py:198
  (2 other events, 5.3 us)

commit v2 on v0

v2 whole, which is shorter than its diff:
```python
import functools

import jax
import jax.numpy as jnp
from jax import lax
from jax.experimental import pallas as pl
from jax.experimental.pallas import tpu as pltpu
from jax.sharding import PartitionSpec as P

VMEM = pl.BlockSpec(memory_space=pltpu.VMEM)
HBM = pl.BlockSpec(memory_space=pltpu.HBM)
GRANT = pltpu.CompilerParams(vmem_limit_bytes=40 * 1024 * 1024)
F32 = jnp.float32
BF16 = jnp.bfloat16
NOWHERE = -(1 << 24)


def product(left, right):
    return jnp.dot(left, right, preferred_element_type=F32)


def split(values):
    high = values.astype(BF16)
    low = (values - high.astype(F32)).astype(BF16)
    return high, low


def dot(left, right):
    return product(left[0], right[0]) + (product(left[0], right[1]) + product(left[1], right[0]))


def pick(chosen, right):
    return product(chosen, right[0]) + product(chosen, right[1])


def one_hot(left, right):
    return jnp.where(left == right, F32(1), F32(0)).astype(BF16)


def iota(shape, dimension):
    return lax.broadcasted_iota(jnp.int32, shape, dimension)


def column_of(row):
    n = row.shape[1]
    spread = jnp.where(iota((n, n), 0) == iota((n, n), 1), row.astype(F32), F32(0))
    return jnp.sum(spread, axis=1, keepdims=True).astype(jnp.int32)


def local_rows(pivots, step, rows_dev):
    offset = pivots[step : step + 1, :] - lax.axis_index("prow") * rows_dev
    return jnp.where((offset >= 0) & (offset < rows_dev), offset, NOWHERE)


def slot_rows(pivots, step, rows_dev):
    offset = local_rows(pivots, step, rows_dev)
    width = offset.shape[1]
    top = jnp.where(lax.axis_index("prow") == 0, step * width + iota(offset.shape, 1), NOWHERE)
    return jnp.where(offset >= 0, offset, top)


def first_slots(matrix, pivots, out, held, chosen, sems):
    chunks = sems.shape[0] - 1
    rows_dev = held.shape[0]
    rows = rows_dev // chunks
    copies = [pltpu.make_async_copy(pivots, chosen, sems.at[chunks])]
    for c in range(chunks):
        part = pl.ds(c * rows, rows)
        copies.append(pltpu.make_async_copy(matrix.at[part, :], held.at[part, :], sems.at[c]))
    for copy in copies:
        copy.start()
    copies[0].wait()
    place = column_of(slot_rows(chosen, 0, rows_dev))
    total = None
    for c in range(chunks):
        copies[1 + c].wait()
        gather = one_hot(place, iota((place.shape[0], rows), 1) + c * rows)
        term = pick(gather, split(held[c * rows : (c + 1) * rows, :]))
        total = term if total is None else total + term
    out[...] = total


def prepare(matrix, pivots, base, ahead, places):
    rows_dev = matrix.shape[0]
    offset = local_rows(pivots, 0, rows_dev)
    width = offset.shape[1]
    place = column_of(slot_rows(pivots, 1, rows_dev))
    places[...] = jnp.broadcast_to(place, places.shape)
    total = None
    for start in range(0, rows_dev, width):
        hit = jnp.where(offset == iota((width, width), 0) + start, F32(1), F32(0))
        keep = jnp.sum(hit, axis=1, keepdims=True) == 0
        kept = jnp.where(keep, matrix[start : start + width, :], F32(0))
        base[start : start + width, :] = kept
        gather = one_hot(place, iota((width, width), 1) + start)
        term = pick(gather, split(kept))
        total = term if total is None else total + term
    ahead[...] = total


def stage_bits(bits, stage):
    odd = lax.rem(lax.axis_index("pcol"), 2) == 1
    bit = jnp.where(odd, bits[len(bits) - 1 - stage], bits[stage])
    known = jnp.where(odd, sum(bits[len(bits) - stage :]) if stage else 0, sum(bits[:stage]))
    return bit, known


def merge(bits, stage, sent, received, owner, out):
    row = lax.axis_index("prow")
    bit, known = stage_bits(bits, stage)
    partner = row ^ bit
    who = owner[...]
    keep = ~known
    theirs = ((who ^ partner) & keep) == 0
    neither = ((who ^ row) & ~(known | bit)) != 0
    take = theirs | (neither & ((partner & keep) == 0))
    out[...] = jnp.where(take, received[...], sent[...])


def picked_rows(bits, sent, received, owner):
    bit, _ = stage_bits(bits, len(bits) - 1)
    mine = ((owner[...] ^ lax.axis_index("prow")) & bit) == 0
    return jnp.where(mine, sent[...], received[-1][...])


def displaced_rows(bits, received, top):
    row = lax.axis_index("prow")
    value = received[-1][...]
    for stage in reversed(range(len(bits) - 1)):
        bit, known = stage_bits(bits, stage)
        value = jnp.where((row & ~(known | bit)) == 0, received[stage][...], value)
    return jnp.where(row == 0, top, value)


def block_start(position, blocks):
    pairs = len(blocks) // 2
    side, distance = divmod(position, pairs)
    col = lax.axis_index("pcol")
    chip = lax.rem(col // 2 - distance + pairs, pairs)
    core = lax.rem(col, 2) if side == 0 else 1 - lax.rem(col, 2)
    rows = blocks[position].shape[0]
    return pl.multiple_of((chip * 2 + core) * rows, rows)


def solve(bits, step, matrix, pivots, inverse, owner, ahead, places, sent, *refs):
    refs = list(refs)
    received = [refs.pop(0) for _ in bits]
    blocks, (upper_out, displaced_out, slots_out) = refs[:-3], refs[-3:]
    rows_dev = matrix.shape[0]
    picked = picked_rows(bits, sent, received, owner)
    width = picked.shape[0]
    upper = dot(split(inverse[step]), split(picked))
    upper_out[...] = upper
    displaced = displaced_rows(bits, received, matrix[step * width : (step + 1) * width, :])
    displaced_out[...] = displaced
    high = low = None
    for position, block in enumerate(blocks):
        rows = block.shape[0]
        local = places[:, :rows] - block_start(position, blocks)
        gather = one_hot(local, iota((width, rows), 1))
        block_high, block_low = split(block[...])
        term_high, term_low = product(gather, block_high), product(gather, block_low)
        high = term_high if high is None else high + term_high
        low = term_low if low is None else low + term_low
    moved = one_hot(places[...], local_rows(pivots, step, rows_dev))
    factor = (high.astype(BF16), low.astype(BF16))
    slots_out[...] = ahead[...] + (pick(moved, split(displaced)) - dot(factor, split(upper)))


def assemble(step, blocks, rows_dev, width, high, low):
    limit = (step + 1) * width - lax.axis_index("prow") * rows_dev
    for position, block in enumerate(blocks):
        rows = block.shape[0]
        start = block_start(position, blocks)
        below = start + iota(block.shape, 0) >= limit
        block_high, block_low = split(jnp.where(below, -block[...], F32(0)))
        high[pl.ds(start, rows), :] = block_high
        low[pl.ds(start, rows), :] = block_low


def update(step, base, pivots, upper_in, displaced_in, top, *refs):
    blocks, (out, top_out, high, low) = refs[:-4], refs[-4:]
    rows_dev = base.shape[0]
    width = upper_in.shape[0]
    assemble(step, blocks, rows_dev, width, high, low)
    offset = local_rows(pivots, step, rows_dev)
    later = local_rows(pivots, step + 1, rows_dev)
    upper = split(upper_in[...])
    displaced = split(displaced_in[...])
    for start in range(0, rows_dev, width):
        part = slice(start, start + width)
        rows = iota((width, width), 0) + start
        value = base[part, :] + (pick(one_hot(rows, offset), displaced) + dot((high[part, :], low[part, :]), upper))
        if start == step * width:
            value = jnp.where(lax.axis_index("prow") == 0, upper_in[...], value)
        if start == (step + 1) * width:
            top_out[...] = value
        hit = jnp.where(later == rows, F32(1), F32(0))
        out[part, :] = jnp.where(jnp.sum(hit, axis=1, keepdims=True) == 0, value, F32(0))


def finish(bits, step, base, pivots, inverse, owner, top, sent, *refs):
    refs = list(refs)
    received = [refs.pop(0) for _ in bits]
    blocks, (out, high, low, result, sems) = refs[:-5], refs[-5:]
    rows_dev = base.shape[0]
    picked = picked_rows(bits, sent, received, owner)
    width = picked.shape[0]
    upper_full = dot(split(inverse[step]), split(picked))
    assemble(step, blocks, rows_dev, width, high, low)
    offset = local_rows(pivots, step, rows_dev)
    upper = split(upper_full)
    displaced = split(displaced_rows(bits, received, top[...]))
    copies = []
    for start in range(0, rows_dev, width):
        part = slice(start, start + width)
        rows = iota((width, width), 0) + start
        value = base[part, :] + (pick(one_hot(rows, offset), displaced) + dot((high[part, :], low[part, :]), upper))
        if start == step * width:
            value = jnp.where(lax.axis_index("prow") == 0, upper_full, value)
        result[part, :] = value
        copies.append(
            pltpu.make_async_copy(result.at[pl.ds(start, width), :], out.at[pl.ds(start, width), :], sems.at[len(copies)])
        )
        copies[-1].start()
    for copy in copies:
        copy.wait()


def gather_panel(block, count):
    across = [(i, i ^ 1) for i in range(count)]
    own = [block]
    for distance in range(1, count // 2):
        own.append(lax.ppermute(block, "pcol", [(i, (i + 2 * distance) % count) for i in range(count)]))
    return own + [lax.ppermute(piece, "pcol", across) for piece in own]


def per_device(mesh, matrix, l_panels, l_inverse, pivots):
    rows_dev, columns = matrix.shape
    steps, width = pivots.shape
    process_rows, process_columns = mesh.shape["prow"], mesh.shape["pcol"]
    bits = [1 << b for b in range(process_rows.bit_length() - 1)]
    shape = jax.ShapeDtypeStruct
    square = shape((width, columns), F32)
    full = shape((rows_dev, columns), F32)

    def call(kernel, name, operands, outs, specs=None, out_specs=None, scratch=()):
        return pl.pallas_call(
            kernel,
            out_shape=outs,
            in_specs=specs or [VMEM] * len(operands),
            out_specs=out_specs or jax.tree.map(lambda _: VMEM, outs),
            scratch_shapes=scratch,
            compiler_params=GRANT,
            name=name,
        )(*operands)

    def exchange(sent, step):
        received = []
        for stage in range(len(bits)):
            if stage:
                sent = call(functools.partial(merge, bits, stage - 1), "merge", [sent, received[-1], owner[step]], square)
            pairs = []
            for i in range(process_rows):
                for j in range(process_columns):
                    bit = bits[len(bits) - 1 - stage] if j % 2 else bits[stage]
                    pairs.append((i * process_columns + j, (i ^ bit) * process_columns + j))
            received.append(lax.ppermute(sent, ("prow", "pcol"), pairs))
        return sent, received

    owner = jnp.broadcast_to((pivots // rows_dev)[:, :, None], (steps, width, columns))
    chunks = rows_dev // width
    halves = [pltpu.VMEM((rows_dev, l_panels.shape[2]), BF16)] * 2
    slots = call(
        first_slots,
        "first_slots",
        [matrix, pivots],
        square,
        specs=[HBM, HBM],
        scratch=[
            pltpu.VMEM((rows_dev, columns), F32),
            pltpu.VMEM((steps, width), jnp.int32),
            pltpu.SemaphoreType.DMA((chunks + 1,)),
        ],
    )
    sent, received = exchange(slots, 0)
    panels = [gather_panel(l_panels[step], process_columns) for step in range(steps)]
    base, ahead, places = call(
        prepare, "prepare", [matrix, pivots], [full, square, shape((width, width), jnp.int32)]
    )
    upper, displaced, slots = call(
        functools.partial(solve, bits, 0),
        "solve",
        [matrix, pivots, l_inverse, owner[0], ahead, places, sent, *received, *panels[0]],
        [square] * 3,
    )
    sent, received = exchange(slots, 1)
    base, top = call(
        functools.partial(update, 0),
        "update",
        [base, pivots, upper, displaced, matrix, *panels[0]],
        [full, square],
        scratch=halves,
    )
    return call(
        functools.partial(finish, bits, 1),
        "finish",
        [base, pivots, l_inverse, owner[1], top, sent, *received, *panels[1]],
        full,
        out_specs=HBM,
        scratch=halves + [pltpu.VMEM((rows_dev, columns), F32), pltpu.SemaphoreType.DMA((chunks,))],
    )


def solution(mesh):
    placed = (P("prow", "pcol"), P(None, ("prow", "pcol"), None), P(), P())
    return jax.shard_map(
        functools.partial(per_device, mesh), mesh=mesh, in_specs=placed, out_specs=P("prow", "pcol"), check_vma=False
    )
```

time: 131 us -> 40.9 us (0.31)
  waiting for transfers between devices: 92.2 us -> 11.8 us
  starting transfers between devices: 0.13 us -> 19.7 us
  between operations: 15.1 us -> 0.14 us
  local copies, waits for them, and re-layouts: 14.3 us -> 2.43 us
  Pallas kernels: 0 us -> 6.65 us
  matrix products: 6.59 us -> 0 us
  other arithmetic: 2.36 us -> 0.01 us
    psum x2 -> x0, waiting for transfers between devices: 91.6 us -> none  [from_root(): return lax.psum(block, axis)]
    ppermute x0 -> x18, starting transfers between devices: none -> 19.7 us  [the longest x6 10.8 us: gather_panel(): lax.ppermute(block, 'pcol', [(i, (i + 2 * distance) % count) for i in ran...]
    ppermute x0 -> x18, waiting for transfers between devices: none -> 11.8 us  [the longest x4 9.48 us: exchange(): received.append(lax.ppermute(sent, ('prow', 'pcol'), pairs))]
    pallas_call x0 -> x7, Pallas kernels: none -> 6.65 us  [call(): pl.pallas_call(kernel, out_shape=outs, in_specs=specs or [VMEM] * len(ope...]
    dot_general x4 -> x0, matrix products: 6.59 us -> none  [the longest x2 5.65 us: apply_panel(): jnp.dot(factor, upper, precision=lax.Precision.HIGHEST, preferred_element...]
    scatter x4 -> x0, local copies, waits for them, and re-layouts: 4.01 us -> none  [the longest x3 3.99 us: per_device(): current = current.at[target].set(old_top, mode='drop')]
    unnamed x15 -> x8, local copies, waits for them, and re-layouts: 4.73 us -> 1.24 us
    select_n x4 -> x1, other arithmetic: 2.31 us -> 0.01 us  [per_device(): pivots // rows_dev]
  transfers between devices with their start and end apart: 4 -> 18, of which waited for: 2 -> 7; matrix products, arithmetic and copies ran while one was open for 6% -> 0% of each run, Pallas kernels for 0% -> 8%
where the time goes in v2:
time: 40.9 us; the launch traced here: 40.8 us
  starting transfers between devices  19.7 us (48%)
  waiting for transfers between devices  11.8 us (29%)
  Pallas kernels  6.65 us (16%)
  local copies, waits for them, and re-layouts  2.43 us (6%)
    ppermute x6, starting transfers between devices, gather_panel(): lax.ppermute(block, 'pcol', [(i, (i + 2 * distance) % count) for i in ran...  10.8 us
    ppermute x4, waiting for transfers between devices, exchange(): received.append(lax.ppermute(sent, ('prow', 'pcol'), pairs))  9.48 us
    ppermute x4, starting transfers between devices, exchange(): received.append(lax.ppermute(sent, ('prow', 'pcol'), pairs))  6.82 us
    pallas_call x7, Pallas kernels, call(): pl.pallas_call(kernel, out_shape=outs, in_specs=specs or [VMEM] * len(ope...  6.65 us
    ppermute x6, waiting for transfers between devices, gather_panel(): lax.ppermute(block, 'pcol', [(i, (i + 2 * distance) % count) for i in ran...  2.06 us
    ppermute x8, starting transfers between devices, gather_panel(): return own + [lax.ppermute(piece, 'pcol', across) for piece in own]  2.04 us
    unnamed x8, local copies, waits for them, and re-layouts  1.24 us
    squeeze x1, local copies, waits for them, and re-layouts, per_device(): l_panels[step]  1 us
  transfers between devices with their start and end apart: 18, of which 7 were waited for; matrix products, arithmetic and copies ran while one was open for 0% of the time, Pallas kernels for 8%

profile of v2, /device:TPU:0, one launch (start us, length us, event | category | flops | bytes accessed | tf_op | source)
XLA Modules:
  0.0 40.8 jit_solution(13562121445858197863)
XLA Ops:
  0.0 1.0 %slice_bitcast_fusion = (f32[128,256]{1,0:T(8,128)S(1)}, f32[128,256]{1,0:T(8,128)S(1)}) fusion(f32[2,128,256]{2,1,0:T(8,128)} %param.5), kind=kLoop, calls=%fused_computation | loop fusion | bytes 524288 | tf_op jit(solution)/shard_map/squeeze | solution.py:287
  1.0 3.1 %collective-permute-start.2 = (f32[128,256]{1,0:T(8,128)S(1)}, f32[128,256]{1,0:T(8,128)S(1)}, u32[]{:S(2)}, u32[]{:S(2)}) collective-permute-start(f32[128,256]{1,0:T(8,128)S(1)} %get-tuple-element.22.refs_2_.refs_0_), channel_id=1, source_target_pairs={{0,2},{1,3},{2,4},{3,5},{4,6},{5,7},{6,0},{7,1},{8,10},{9,11},{10,... | collective-permute-start | bytes 393224 | tf_op jit(solution)/shard_map/ppermute | solution.py:234
  4.1 2.6 %collective-permute-start.3 = (f32[128,256]{1,0:T(8,128)S(1)}, f32[128,256]{1,0:T(8,128)S(1)}, u32[]{:S(2)}, u32[]{:S(2)}) collective-permute-start(f32[128,256]{1,0:T(8,128)S(1)} %get-tuple-element.22.refs_2_.refs_0_), channel_id=1, source_target_pairs={{0,4},{1,5},{2,6},{3,7},{4,0},{5,1},{6,2},{7,3},{8,12},{9,13},{10,... | collective-permute-start | bytes 393224 | tf_op jit(solution)/shard_map/ppermute | solution.py:234
  6.7 1.3 %collective-permute-start.4 = (f32[128,256]{1,0:T(8,128)S(1)}, f32[128,256]{1,0:T(8,128)S(1)}, u32[]{:S(2)}, u32[]{:S(2)}) collective-permute-start(f32[128,256]{1,0:T(8,128)S(1)} %get-tuple-element.22.refs_2_.refs_0_), channel_id=1, source_target_pairs={{0,6},{1,7},{2,0},{3,1},{4,2},{5,3},{6,4},{7,5},{8,14},{9,15},{10,... | collective-permute-start | bytes 393224 | tf_op jit(solution)/shard_map/ppermute | solution.py:234
  8.0 1.2 %copy-done = f32[1024,256]{1,0:T(8,128)S(1)} copy-done((f32[1024,256]{1,0:T(8,128)S(1)}, f32[1024,256]{1,0:T(8,128)}, u32[]{:S(2)}) %copy-start) | copy-done | bytes 1048600
  9.2 1.2 %first_slots.1.sent = f32[256,256]{1,0:T(8,128)S(1)} custom-call(f32[1024,256]{1,0:T(8,128)S(1)} %copy-done, s32[2,256]{1,0:T(2,128)S(1)} %copy-done.3), custom_call_target="tpu_custom_call" | custom-call | tf_op jit(solution)/shard_map/first_slots/pallas_call | solution.py:248
  10.4 1.6 %collective-permute-start = (f32[256,256]{1,0:T(8,128)S(1)}, f32[256,256]{1,0:T(8,128)S(1)}, u32[]{:S(2)}, u32[]{:S(2)}) collective-permute-start(f32[256,256]{1,0:T(8,128)S(1)} %first_slots.1.sent), channel_id=1, source_target_pairs={{0,8},{1,17},{2,10},{3,19},{4,12},{5,21},{6,14},{7,23},{8,0},{9,25... | collective-permute-start | bytes 786440 | tf_op jit(solution)/shard_map/ppermute | solution.py:268
  12.0 4.9 %collective-permute-done.received.refs_0_ = f32[256,256]{1,0:T(8,128)S(1)} collective-permute-done((f32[256,256]{1,0:T(8,128)S(1)}, f32[256,256]{1,0:T(8,128)S(1)}, u32[]{:S(2)}, u32[]{:S(2)}) %collective-permute-start) | collective-permute-done | bytes 262176 | tf_op jit(solution)/shard_map/ppermute | solution.py:268
  17.1 1.6 %collective-permute-start.1 = (f32[256,256]{1,0:T(8,128)S(1)}, f32[256,256]{1,0:T(8,128)S(1)}, u32[]{:S(2)}, u32[]{:S(2)}) collective-permute-start(f32[256,256]{1,0:T(8,128)S(1)} %merge.2.sent), channel_id=1, source_target_pairs={{0,16},{1,9},{2,18},{3,11},{4,20},{5,13},{6,22},{7,15},{8,24},{9,1... | collective-permute-start | bytes 786440 | tf_op jit(solution)/shard_map/ppermute | solution.py:268
  18.7 0.5 %collective-permute-start.6 = (f32[128,256]{1,0:T(8,128)S(1)}, f32[128,256]{1,0:T(8,128)S(1)}, u32[]{:S(2)}, u32[]{:S(2)}) collective-permute-start(f32[128,256]{1,0:T(8,128)S(1)} %collective-permute-done.2.refs_3_.refs_1_), channel_id=1, source_target_pairs={{0,1},{1,0},{2,3},{3,2},{4,5},{5,4},{6,7},{7,6},{8,9},{9,8},{10,11... | collective-permute-start | bytes 393224 | tf_op jit(solution)/shard_map/ppermute | solution.py:235
  19.3 0.4 %collective-permute-start.8 = (f32[128,256]{1,0:T(8,128)S(1)}, f32[128,256]{1,0:T(8,128)S(1)}, u32[]{:S(2)}, u32[]{:S(2)}) collective-permute-start(f32[128,256]{1,0:T(8,128)S(1)} %collective-permute-done.4.refs_5_.refs_3_), channel_id=1, source_target_pairs={{0,1},{1,0},{2,3},{3,2},{4,5},{5,4},{6,7},{7,6},{8,9},{9,8},{10,11... | collective-permute-start | bytes 393224 | tf_op jit(solution)/shard_map/ppermute | solution.py:235
  19.7 0.7 %prepare.1 = (f32[1024,256]{1,0:T(8,128)S(1)}, f32[256,256]{1,0:T(8,128)S(1)}, s32[256,256]{1,0:T(8,128)S(1)}) custom-call(f32[1024,256]{1,0:T(8,128)S(1)} %copy-done.1, s32[2,256]{1,0:T(2,128)S(1)} %copy-done.3), custom_call_target="tpu_custom_call" | custom-call | tf_op jit(solution)/shard_map/prepare/pallas_call | solution.py:248
  20.7 2.8 %collective-permute-done.1.refs_1_ = f32[256,256]{1,0:T(8,128)S(1)} collective-permute-done((f32[256,256]{1,0:T(8,128)S(1)}, f32[256,256]{1,0:T(8,128)S(1)}, u32[]{:S(2)}, u32[]{:S(2)}) %collective-permute-start.1) | collective-permute-done | bytes 262176 | tf_op jit(solution)/shard_map/ppermute | solution.py:268
  23.5 1.3 %solve.1 = (f32[256,256]{1,0:T(8,128)S(1)}, f32[256,256]{1,0:T(8,128)S(1)}, f32[256,256]{1,0:T(8,128)S(1)}) custom-call(f32[1024,256]{1,0:T(8,128)S(1)} %copy-done.1, s32[2,256]{1,0:T(2,128)S(1)} %copy-done.3, f32[2,256,256]{2,1,0:T(8,128)S(1)} %copy-done.2, s32[256,256]{1,0:T(8,128)S(1)} %broadcast_in_dim.13.owner, f32[256,256]{1,0:T(8,128)S(1)} %get-tuple-element.14.ahead, ...), custom_call_target="tpu_custom_call" | custom-call | tf_op jit(solution)/shard_map/solve/pallas_call | solution.py:248
  24.8 1.6 %collective-permute-start.9 = (f32[256,256]{1,0:T(8,128)S(1)}, f32[256,256]{1,0:T(8,128)S(1)}, u32[]{:S(2)}, u32[]{:S(2)}) collective-permute-start(f32[256,256]{1,0:T(8,128)S(1)} %get-tuple-element.20.sent), channel_id=1, source_target_pairs={{0,8},{1,17},{2,10},{3,19},{4,12},{5,21},{6,14},{7,23},{8,0},{9,25... | collective-permute-start | bytes 786440 | tf_op jit(solution)/shard_map/ppermute | solution.py:268
  26.4 0.7 %collective-permute-start.11 = (f32[128,256]{1,0:T(8,128)S(1)}, f32[128,256]{1,0:T(8,128)S(1)}, u32[]{:S(2)}, u32[]{:S(2)}) collective-permute-start(f32[128,256]{1,0:T(8,128)S(1)} %get-tuple-element.21.refs_2_), channel_id=1, source_target_pairs={{0,2},{1,3},{2,4},{3,5},{4,6},{5,7},{6,0},{7,1},{8,10},{9,11},{10,... | collective-permute-start | bytes 393224 | tf_op jit(solution)/shard_map/ppermute | solution.py:234
  27.4 2.8 %collective-permute-start.13 = (f32[128,256]{1,0:T(8,128)S(1)}, f32[128,256]{1,0:T(8,128)S(1)}, u32[]{:S(2)}, u32[]{:S(2)}) collective-permute-start(f32[128,256]{1,0:T(8,128)S(1)} %get-tuple-element.21.refs_2_), channel_id=1, source_target_pairs={{0,6},{1,7},{2,0},{3,1},{4,2},{5,3},{6,4},{7,5},{8,14},{9,15},{10,... | collective-permute-start | bytes 393224 | tf_op jit(solution)/shard_map/ppermute | solution.py:234
  30.2 1.7 %collective-permute-done.9.received.refs_0_ = f32[256,256]{1,0:T(8,128)S(1)} collective-permute-done((f32[256,256]{1,0:T(8,128)S(1)}, f32[256,256]{1,0:T(8,128)S(1)}, u32[]{:S(2)}, u32[]{:S(2)}) %collective-permute-start.9) | collective-permute-done | bytes 262176 | tf_op jit(solution)/shard_map/ppermute | solution.py:268
  32.2 2.1 %collective-permute-start.10 = (f32[256,256]{1,0:T(8,128)S(1)}, f32[256,256]{1,0:T(8,128)S(1)}, u32[]{:S(2)}, u32[]{:S(2)}) collective-permute-start(f32[256,256]{1,0:T(8,128)S(1)} %merge.3.sent), channel_id=1, source_target_pairs={{0,16},{1,9},{2,18},{3,11},{4,20},{5,13},{6,22},{7,15},{8,24},{9,1... | collective-permute-start | bytes 786440 | tf_op jit(solution)/shard_map/ppermute | solution.py:268
  34.3 0.5 %collective-permute-start.15 = (f32[128,256]{1,0:T(8,128)S(1)}, f32[128,256]{1,0:T(8,128)S(1)}, u32[]{:S(2)}, u32[]{:S(2)}) collective-permute-start(f32[128,256]{1,0:T(8,128)S(1)} %collective-permute-done.11.refs_3_), channel_id=1, source_target_pairs={{0,1},{1,0},{2,3},{3,2},{4,5},{5,4},{6,7},{7,6},{8,9},{9,8},{10,11... | collective-permute-start | bytes 393224 | tf_op jit(solution)/shard_map/ppermute | solution.py:235
  34.8 2.0 %collective-permute-done.12.refs_4_ = f32[128,256]{1,0:T(8,128)S(1)} collective-permute-done((f32[128,256]{1,0:T(8,128)S(1)}, f32[128,256]{1,0:T(8,128)S(1)}, u32[]{:S(2)}, u32[]{:S(2)}) %collective-permute-start.12) | collective-permute-done | bytes 131104 | tf_op jit(solution)/shard_map/ppermute | solution.py:234
  36.9 0.5 %collective-permute-start.17 = (f32[128,256]{1,0:T(8,128)S(1)}, f32[128,256]{1,0:T(8,128)S(1)}, u32[]{:S(2)}, u32[]{:S(2)}) collective-permute-start(f32[128,256]{1,0:T(8,128)S(1)} %collective-permute-done.13.refs_5_), channel_id=1, source_target_pairs={{0,1},{1,0},{2,3},{3,2},{4,5},{5,4},{6,7},{7,6},{8,9},{9,8},{10,11... | collective-permute-start | bytes 393224 | tf_op jit(solution)/shard_map/ppermute | solution.py:235
  37.4 1.1 %update.1 = (f32[1024,256]{1,0:T(8,128)S(1)}, f32[256,256]{1,0:T(8,128)S(1)}) custom-call(f32[1024,256]{1,0:T(8,128)S(1)} %get-tuple-element.13.base, s32[2,256]{1,0:T(2,128)S(1)} %copy-done.3, f32[256,256]{1,0:T(8,128)S(1)} %get-tuple-element.16.upper_in, f32[256,256]{1,0:T(8,128)S(1)} %get-tuple-element.17.displaced_in, f32[1024,256]{1,0:T(8,128)S(1)} %copy-done.1, ...), custom_call_target="tpu_custom_call" | custom-call | tf_op jit(solution)/shard_map/update/pallas_call | solution.py:248
  38.6 2.1 %finish.1 = f32[1024,256]{1,0:T(8,128)} custom-call(f32[1024,256]{1,0:T(8,128)S(1)} %get-tuple-element.18.base, s32[2,256]{1,0:T(2,128)S(1)} %copy-done.3, f32[2,256,256]{2,1,0:T(8,128)S(1)} %copy-done.2, s32[256,256]{1,0:T(8,128)S(1)} %broadcast_in_dim.15.owner, f32[256,256]{1,0:T(8,128)S(1)} %get-tuple-element.19.top, f32[256,256]{1,0:T(8,128)S(1)} %merge.3.sent, ...), custom_call_target="tpu_custom_call" | custom-call | tf_op jit(solution)/shard_map/finish/pallas_call | solution.py:248
  (32 shorter events, 1.2 us)
Async XLA Ops:
  0.0 8.0 %copy-start.3 = (s32[2,256]{1,0:T(2,128)S(1)}, s32[2,256]{1,0:T(2,128)}, u32[]{:S(2)}) copy-start(s32[2,256]{1,0:T(2,128)} %pivots.9) | copy-start | bytes 6148
  1.0 17.7 %collective-permute-start.2 = (f32[128,256]{1,0:T(8,128)S(1)}, f32[128,256]{1,0:T(8,128)S(1)}, u32[]{:S(2)}, u32[]{:S(2)}) collective-permute-start(f32[128,256]{1,0:T(8,128)S(1)} %get-tuple-element.22.refs_2_.refs_0_), channel_id=1, source_target_pairs={{0,2},{1,3},{2,4},{3,5},{4,6},{5,7},{6,0},{7,1},{8,10},{9,11},{10,... | collective-permute-start | bytes 393224 | tf_op jit(solution)/shard_map/ppermute | solution.py:234
  4.1 15.1 %collective-permute-start.3 = (f32[128,256]{1,0:T(8,128)S(1)}, f32[128,256]{1,0:T(8,128)S(1)}, u32[]{:S(2)}, u32[]{:S(2)}) collective-permute-start(f32[128,256]{1,0:T(8,128)S(1)} %get-tuple-element.22.refs_2_.refs_0_), channel_id=1, source_target_pairs={{0,4},{1,5},{2,6},{3,7},{4,0},{5,1},{6,2},{7,3},{8,12},{9,13},{10,... | collective-permute-start | bytes 393224 | tf_op jit(solution)/shard_map/ppermute | solution.py:234
  6.7 12.6 %collective-permute-start.4 = (f32[128,256]{1,0:T(8,128)S(1)}, f32[128,256]{1,0:T(8,128)S(1)}, u32[]{:S(2)}, u32[]{:S(2)}) collective-permute-start(f32[128,256]{1,0:T(8,128)S(1)} %get-tuple-element.22.refs_2_.refs_0_), channel_id=1, source_target_pairs={{0,6},{1,7},{2,0},{3,1},{4,2},{5,3},{6,4},{7,5},{8,14},{9,15},{10,... | collective-permute-start | bytes 393224 | tf_op jit(solution)/shard_map/ppermute | solution.py:234
  8.0 1.2 %copy-start = (f32[1024,256]{1,0:T(8,128)S(1)}, f32[1024,256]{1,0:T(8,128)}, u32[]{:S(2)}) copy-start(f32[1024,256]{1,0:T(8,128)} %top.1) | copy-start | bytes 3145732
  9.2 10.4 %copy-start.1 = (f32[1024,256]{1,0:T(8,128)S(1)}, f32[1024,256]{1,0:T(8,128)}, u32[]{:S(2)}) copy-start(f32[1024,256]{1,0:T(8,128)} %top.1) | copy-start | bytes 3145732
  10.4 6.4 %collective-permute-start = (f32[256,256]{1,0:T(8,128)S(1)}, f32[256,256]{1,0:T(8,128)S(1)}, u32[]{:S(2)}, u32[]{:S(2)}) collective-permute-start(f32[256,256]{1,0:T(8,128)S(1)} %first_slots.1.sent), channel_id=1, source_target_pairs={{0,8},{1,17},{2,10},{3,19},{4,12},{5,21},{6,14},{7,23},{8,0},{9,25... | collective-permute-start | bytes 786440 | tf_op jit(solution)/shard_map/ppermute | solution.py:268
  17.1 6.5 %copy-start.2 = (f32[2,256,256]{2,1,0:T(8,128)S(1)}, f32[2,256,256]{2,1,0:T(8,128)}, u32[]{:S(2)}) copy-start(f32[2,256,256]{2,1,0:T(8,128)} %inverse.3) | copy-start | bytes 1572868
  17.1 6.4 %collective-permute-start.1 = (f32[256,256]{1,0:T(8,128)S(1)}, f32[256,256]{1,0:T(8,128)S(1)}, u32[]{:S(2)}, u32[]{:S(2)}) collective-permute-start(f32[256,256]{1,0:T(8,128)S(1)} %merge.2.sent), channel_id=1, source_target_pairs={{0,16},{1,9},{2,18},{3,11},{4,20},{5,13},{6,22},{7,15},{8,24},{9,1... | collective-permute-start | bytes 786440 | tf_op jit(solution)/shard_map/ppermute | solution.py:268
  18.7 1.7 %collective-permute-start.5 = (f32[128,256]{1,0:T(8,128)S(1)}, f32[128,256]{1,0:T(8,128)S(1)}, u32[]{:S(2)}, u32[]{:S(2)}) collective-permute-start(f32[128,256]{1,0:T(8,128)S(1)} %get-tuple-element.22.refs_2_.refs_0_), channel_id=1, source_target_pairs={{0,1},{1,0},{2,3},{3,2},{4,5},{5,4},{6,7},{7,6},{8,9},{9,8},{10,11... | collective-permute-start | bytes 393224 | tf_op jit(solution)/shard_map/ppermute | solution.py:235
  18.7 1.8 %collective-permute-start.6 = (f32[128,256]{1,0:T(8,128)S(1)}, f32[128,256]{1,0:T(8,128)S(1)}, u32[]{:S(2)}, u32[]{:S(2)}) collective-permute-start(f32[128,256]{1,0:T(8,128)S(1)} %collective-permute-done.2.refs_3_.refs_1_), channel_id=1, source_target_pairs={{0,1},{1,0},{2,3},{3,2},{4,5},{5,4},{6,7},{7,6},{8,9},{9,8},{10,11... | collective-permute-start | bytes 393224 | tf_op jit(solution)/shard_map/ppermute | solution.py:235
  19.2 1.3 %collective-permute-start.7 = (f32[128,256]{1,0:T(8,128)S(1)}, f32[128,256]{1,0:T(8,128)S(1)}, u32[]{:S(2)}, u32[]{:S(2)}) collective-permute-start(f32[128,256]{1,0:T(8,128)S(1)} %collective-permute-done.3.refs_4_.refs_2_), channel_id=1, source_target_pairs={{0,1},{1,0},{2,3},{3,2},{4,5},{5,4},{6,7},{7,6},{8,9},{9,8},{10,11... | collective-permute-start | bytes 393224 | tf_op jit(solution)/shard_map/ppermute | solution.py:235
  19.3 1.5 %collective-permute-start.8 = (f32[128,256]{1,0:T(8,128)S(1)}, f32[128,256]{1,0:T(8,128)S(1)}, u32[]{:S(2)}, u32[]{:S(2)}) collective-permute-start(f32[128,256]{1,0:T(8,128)S(1)} %collective-permute-done.4.refs_5_.refs_3_), channel_id=1, source_target_pairs={{0,1},{1,0},{2,3},{3,2},{4,5},{5,4},{6,7},{7,6},{8,9},{9,8},{10,11... | collective-permute-start | bytes 393224 | tf_op jit(solution)/shard_map/ppermute | solution.py:235
  24.8 7.1 %collective-permute-start.9 = (f32[256,256]{1,0:T(8,128)S(1)}, f32[256,256]{1,0:T(8,128)S(1)}, u32[]{:S(2)}, u32[]{:S(2)}) collective-permute-start(f32[256,256]{1,0:T(8,128)S(1)} %get-tuple-element.20.sent), channel_id=1, source_target_pairs={{0,8},{1,17},{2,10},{3,19},{4,12},{5,21},{6,14},{7,23},{8,0},{9,25... | collective-permute-start | bytes 786440 | tf_op jit(solution)/shard_map/ppermute | solution.py:268
  26.4 7.9 %collective-permute-start.11 = (f32[128,256]{1,0:T(8,128)S(1)}, f32[128,256]{1,0:T(8,128)S(1)}, u32[]{:S(2)}, u32[]{:S(2)}) collective-permute-start(f32[128,256]{1,0:T(8,128)S(1)} %get-tuple-element.21.refs_2_), channel_id=1, source_target_pairs={{0,2},{1,3},{2,4},{3,5},{4,6},{5,7},{6,0},{7,1},{8,10},{9,11},{10,... | collective-permute-start | bytes 393224 | tf_op jit(solution)/shard_map/ppermute | solution.py:234
  27.1 9.8 %collective-permute-start.12 = (f32[128,256]{1,0:T(8,128)S(1)}, f32[128,256]{1,0:T(8,128)S(1)}, u32[]{:S(2)}, u32[]{:S(2)}) collective-permute-start(f32[128,256]{1,0:T(8,128)S(1)} %get-tuple-element.21.refs_2_), channel_id=1, source_target_pairs={{0,4},{1,5},{2,6},{3,7},{4,0},{5,1},{6,2},{7,3},{8,12},{9,13},{10,... | collective-permute-start | bytes 393224 | tf_op jit(solution)/shard_map/ppermute | solution.py:234
  27.4 9.5 %collective-permute-start.13 = (f32[128,256]{1,0:T(8,128)S(1)}, f32[128,256]{1,0:T(8,128)S(1)}, u32[]{:S(2)}, u32[]{:S(2)}) collective-permute-start(f32[128,256]{1,0:T(8,128)S(1)} %get-tuple-element.21.refs_2_), channel_id=1, source_target_pairs={{0,6},{1,7},{2,0},{3,1},{4,2},{5,3},{6,4},{7,5},{8,14},{9,15},{10,... | collective-permute-start | bytes 393224 | tf_op jit(solution)/shard_map/ppermute | solution.py:234
  32.2 6.5 %collective-permute-start.10 = (f32[256,256]{1,0:T(8,128)S(1)}, f32[256,256]{1,0:T(8,128)S(1)}, u32[]{:S(2)}, u32[]{:S(2)}) collective-permute-start(f32[256,256]{1,0:T(8,128)S(1)} %merge.3.sent), channel_id=1, source_target_pairs={{0,16},{1,9},{2,18},{3,11},{4,20},{5,13},{6,22},{7,15},{8,24},{9,1... | collective-permute-start | bytes 786440 | tf_op jit(solution)/shard_map/ppermute | solution.py:268
  34.3 4.2 %collective-permute-start.14 = (f32[128,256]{1,0:T(8,128)S(1)}, f32[128,256]{1,0:T(8,128)S(1)}, u32[]{:S(2)}, u32[]{:S(2)}) collective-permute-start(f32[128,256]{1,0:T(8,128)S(1)} %get-tuple-element.21.refs_2_), channel_id=1, source_target_pairs={{0,1},{1,0},{2,3},{3,2},{4,5},{5,4},{6,7},{7,6},{8,9},{9,8},{10,11... | collective-permute-start | bytes 393224 | tf_op jit(solution)/shard_map/ppermute | solution.py:235
  34.3 4.2 %collective-permute-start.15 = (f32[128,256]{1,0:T(8,128)S(1)}, f32[128,256]{1,0:T(8,128)S(1)}, u32[]{:S(2)}, u32[]{:S(2)}) collective-permute-start(f32[128,256]{1,0:T(8,128)S(1)} %collective-permute-done.11.refs_3_), channel_id=1, source_target_pairs={{0,1},{1,0},{2,3},{3,2},{4,5},{5,4},{6,7},{7,6},{8,9},{9,8},{10,11... | collective-permute-start | bytes 393224 | tf_op jit(solution)/shard_map/ppermute | solution.py:235
  36.8 1.7 %collective-permute-start.16 = (f32[128,256]{1,0:T(8,128)S(1)}, f32[128,256]{1,0:T(8,128)S(1)}, u32[]{:S(2)}, u32[]{:S(2)}) collective-permute-start(f32[128,256]{1,0:T(8,128)S(1)} %collective-permute-done.12.refs_4_), channel_id=1, source_target_pairs={{0,1},{1,0},{2,3},{3,2},{4,5},{5,4},{6,7},{7,6},{8,9},{9,8},{10,11... | collective-permute-start | bytes 393224 | tf_op jit(solution)/shard_map/ppermute | solution.py:235
  36.9 1.7 %collective-permute-start.17 = (f32[128,256]{1,0:T(8,128)S(1)}, f32[128,256]{1,0:T(8,128)S(1)}, u32[]{:S(2)}, u32[]{:S(2)}) collective-permute-start(f32[128,256]{1,0:T(8,128)S(1)} %collective-permute-done.13.refs_5_), channel_id=1, source_target_pairs={{0,1},{1,0},{2,3},{3,2},{4,5},{5,4},{6,7},{7,6},{8,9},{9,8},{10,11... | collective-permute-start | bytes 393224 | tf_op jit(solution)/shard_map/ppermute | solution.py:235

commit v3 on v2

--- a/solution.py
+++ b/solution.py
@@ -8,6 +8,7 @@
 from jax.sharding import PartitionSpec as P
 
 VMEM = pl.BlockSpec(memory_space=pltpu.VMEM)
+ANY = pl.BlockSpec(memory_space=pl.ANY)
 HBM = pl.BlockSpec(memory_space=pltpu.HBM)
 GRANT = pltpu.CompilerParams(vmem_limit_bytes=40 * 1024 * 1024)
 F32 = jnp.float32
@@ -59,14 +60,15 @@
     return jnp.where(offset >= 0, offset, top)
 
 
-def first_slots(matrix, pivots, out, held, chosen, sems):
-    chunks = sems.shape[0] - 1
+def first_slots(matrix, pivots, panels, out, panel, held, chosen, sems):
+    chunks = sems.shape[0] - 2
     rows_dev = held.shape[0]
     rows = rows_dev // chunks
     copies = [pltpu.make_async_copy(pivots, chosen, sems.at[chunks])]
     for c in range(chunks):
         part = pl.ds(c * rows, rows)
         copies.append(pltpu.make_async_copy(matrix.at[part, :], held.at[part, :], sems.at[c]))
+    copies.append(pltpu.make_async_copy(panels.at[0], panel, sems.at[chunks + 1]))
     for copy in copies:
         copy.start()
     copies[0].wait()
@@ -78,9 +80,12 @@
         term = pick(gather, split(held[c * rows : (c + 1) * rows, :]))
         total = term if total is None else total + term
     out[...] = total
-
-
-def prepare(matrix, pivots, base, ahead, places):
+    copies[-1].wait()
+
+
+def prepare(matrix, pivots, panels, arrived, base, ahead, places, panel, sem):
+    copy = pltpu.make_async_copy(panels.at[1], panel, sem)
+    copy.start()
     rows_dev = matrix.shape[0]
     offset = local_rows(pivots, 0, rows_dev)
     width = offset.shape[1]
@@ -96,6 +101,7 @@
         term = pick(gather, split(kept))
         total = term if total is None else total + term
     ahead[...] = total
+    copy.wait()
 
 
 def stage_bits(bits, stage):
@@ -227,11 +233,17 @@
         copy.wait()
 
 
-def gather_panel(block, count):
+def release(panel, before, out):
+    out[...] = panel[...]
+
+
+def gather_panel(block, later, count):
     across = [(i, i ^ 1) for i in range(count)]
+    chips = count // 2
     own = [block]
-    for distance in range(1, count // 2):
-        own.append(lax.ppermute(block, "pcol", [(i, (i + 2 * distance) % count) for i in range(count)]))
+    for distance in range(1, chips):
+        sent = block if distance == chips // 2 else later
+        own.append(lax.ppermute(sent, "pcol", [(i, (i + 2 * distance) % count) for i in range(count)]))
     return own + [lax.ppermute(piece, "pcol", across) for piece in own]
 
 
@@ -271,23 +283,27 @@
     owner = jnp.broadcast_to((pivots // rows_dev)[:, :, None], (steps, width, columns))
     chunks = rows_dev // width
     halves = [pltpu.VMEM((rows_dev, l_panels.shape[2]), BF16)] * 2
-    slots = call(
+    panel_block = shape(l_panels.shape[1:], F32)
+    slots, panel, matrix = call(
         first_slots,
         "first_slots",
-        [matrix, pivots],
-        square,
-        specs=[HBM, HBM],
-        scratch=[
-            pltpu.VMEM((rows_dev, columns), F32),
-            pltpu.VMEM((steps, width), jnp.int32),
-            pltpu.SemaphoreType.DMA((chunks + 1,)),
-        ],
-    )
+        [pltpu.with_memory_space_constraint(x, pltpu.HBM) for x in (matrix, pivots, l_panels)],
+        [square, panel_block, full],
+        specs=[HBM] * 3,
+        scratch=[pltpu.VMEM((steps, width), jnp.int32), pltpu.SemaphoreType.DMA((chunks + 2,))],
+    )
+    later = call(release, "release", [panel, slots], panel_block, specs=[VMEM, ANY])
+    panels = [gather_panel(panel, later, process_columns)]
     sent, received = exchange(slots, 0)
-    panels = [gather_panel(l_panels[step], process_columns) for step in range(steps)]
-    base, ahead, places = call(
-        prepare, "prepare", [matrix, pivots], [full, square, shape((width, width), jnp.int32)]
-    )
+    base, ahead, places, panel = call(
+        prepare,
+        "prepare",
+        [matrix, pivots, l_panels, panels[0][process_columns // 4]],
+        [full, square, shape((width, width), jnp.int32), panel_block],
+        specs=[VMEM, VMEM, ANY, ANY],
+        scratch=[pltpu.SemaphoreType.DMA],
+    )
+    panels.append(gather_panel(panel, panel, process_columns))
     upper, displaced, slots = call(
         functools.partial(solve, bits, 0),
         "solve",

time: 40.9 us -> 39.4 us (0.963); the launches traced: 40.8 us -> 38.6 us
  waiting for transfers between devices: 11.8 us -> 9.27 us
  local copies, waits for them, and re-layouts: 2.43 us -> 0.21 us
  starting transfers between devices: 19.7 us -> 21.4 us
  Pallas kernels: 6.65 us -> 7.59 us
    ppermute x4, waiting for transfers between devices: 9.48 us -> 0.97 us  [exchange(): received.append(lax.ppermute(sent, ('prow', 'pcol'), pairs))]
    ppermute x6, waiting for transfers between devices: 2.06 us -> 7.88 us  [gather_panel(): lax.ppermute(sent, 'pcol', [(i, (i + 2 * distance) % count) for i in rang...]
    ppermute x6, starting transfers between devices: 10.8 us -> 14.1 us  [gather_panel(): lax.ppermute(sent, 'pcol', [(i, (i + 2 * distance) % count) for i in rang...]
    unnamed x8 -> x6, local copies, waits for them, and re-layouts: 1.24 us -> 0.01 us
    squeeze x1 -> x0, local copies, waits for them, and re-layouts: 1 us -> none  [per_device(): l_panels[step]]
    pallas_call x7 -> x8, Pallas kernels: 6.65 us -> 7.59 us  [call(): pl.pallas_call(kernel, out_shape=outs, in_specs=specs or [VMEM] * len(ope...]
    ppermute x8, starting transfers between devices: 2.04 us -> 1.11 us  [gather_panel(): return own + [lax.ppermute(piece, 'pcol', across) for piece in own]]
    ppermute x4, starting transfers between devices: 6.82 us -> 6.22 us  [exchange(): received.append(lax.ppermute(sent, ('prow', 'pcol'), pairs))]
  transfers between devices with their start and end apart: 18 -> 18, of which waited for: 7 -> 6; matrix products, arithmetic and copies ran while one was open for 0% -> 1% of each run, Pallas kernels for 8% -> 6%
where the time goes in v3:
time: 39.4 us; the launch traced here: 38.6 us
  starting transfers between devices  21.4 us (54%)
  waiting for transfers between devices  9.27 us (24%)
  Pallas kernels  7.59 us (19%)
    ppermute x6, starting transfers between devices, gather_panel(): lax.ppermute(sent, 'pcol', [(i, (i + 2 * distance) % count) for i in rang...  14.1 us
    ppermute x6, waiting for transfers between devices, gather_panel(): lax.ppermute(sent, 'pcol', [(i, (i + 2 * distance) % count) for i in rang...  7.88 us
    pallas_call x8, Pallas kernels, call(): pl.pallas_call(kernel, out_shape=outs, in_specs=specs or [VMEM] * len(ope...  7.59 us
    ppermute x4, starting transfers between devices, exchange(): received.append(lax.ppermute(sent, ('prow', 'pcol'), pairs))  6.22 us
    ppermute x8, starting transfers between devices, gather_panel(): return own + [lax.ppermute(piece, 'pcol', across) for piece in own]  1.11 us
    ppermute x4, waiting for transfers between devices, exchange(): received.append(lax.ppermute(sent, ('prow', 'pcol'), pairs))  0.97 us
  transfers between devices with their start and end apart: 18, of which 6 were waited for; matrix products, arithmetic and copies ran while one was open for 1% of the time, Pallas kernels for 6%

profile of v3, /device:TPU:0, one launch (start us, length us, event | category | flops | bytes accessed | tf_op | source)
XLA Modules:
  0.0 38.6 jit_solution(4626033625814089619)
XLA Ops:
  0.0 1.9 %first_slots.1 = (f32[256,256]{1,0:T(8,128)S(1)}, f32[128,256]{1,0:T(8,128)S(1)}, f32[1024,256]{1,0:T(8,128)S(1)}) custom-call(f32[1024,256]{1,0:T(8,128)} %matrix.1, s32[2,256]{1,0:T(2,128)} %pivots.9, f32[2,128,256]{2,1,0:T(8,128)} %panels.3), custom_call_target="tpu_custom_call" | custom-call | tf_op jit(solution)/shard_map/first_slots/pallas_call | solution.py:260
  2.0 4.1 %collective-permute-start = (f32[128,256]{1,0:T(8,128)S(1)}, f32[128,256]{1,0:T(8,128)S(1)}, u32[]{:S(2)}, u32[]{:S(2)}) collective-permute-start(f32[128,256]{1,0:T(8,128)S(1)} %get-tuple-element.18.panel.refs_2_.refs_0_), channel_id=1, source_target_pairs={{0,4},{1,5},{2,6},{3,7},{4,0},{5,1},{6,2},{7,3},{8,12},{9,13},{10,... | collective-permute-start | bytes 393224 | tf_op jit(solution)/shard_map/ppermute | solution.py:246
  6.1 1.5 %collective-permute-start.1 = (f32[256,256]{1,0:T(8,128)S(1)}, f32[256,256]{1,0:T(8,128)S(1)}, u32[]{:S(2)}, u32[]{:S(2)}) collective-permute-start(f32[256,256]{1,0:T(8,128)S(1)} %get-tuple-element.22.sent.before), channel_id=1, source_target_pairs={{0,8},{1,17},{2,10},{3,19},{4,12},{5,21},{6,14},{7,23},{8,0},{9,25... | collective-permute-start | bytes 786440 | tf_op jit(solution)/shard_map/ppermute | solution.py:280
  7.6 1.6 %collective-permute-start.3 = (f32[128,256]{1,0:T(8,128)S(1)}, f32[128,256]{1,0:T(8,128)S(1)}, u32[]{:S(2)}, u32[]{:S(2)}) collective-permute-start(f32[128,256]{1,0:T(8,128)S(1)} %release.1), channel_id=1, source_target_pairs={{0,2},{1,3},{2,4},{3,5},{4,6},{5,7},{6,0},{7,1},{8,10},{9,11},{10,... | collective-permute-start | bytes 393224 | tf_op jit(solution)/shard_map/ppermute | solution.py:246
  9.2 2.2 %collective-permute-start.4 = (f32[128,256]{1,0:T(8,128)S(1)}, f32[128,256]{1,0:T(8,128)S(1)}, u32[]{:S(2)}, u32[]{:S(2)}) collective-permute-start(f32[128,256]{1,0:T(8,128)S(1)} %release.1), channel_id=1, source_target_pairs={{0,6},{1,7},{2,0},{3,1},{4,2},{5,3},{6,4},{7,5},{8,14},{9,15},{10,... | collective-permute-start | bytes 393224 | tf_op jit(solution)/shard_map/ppermute | solution.py:246
  11.5 1.0 %collective-permute-done.1.received.refs_0_ = f32[256,256]{1,0:T(8,128)S(1)} collective-permute-done((f32[256,256]{1,0:T(8,128)S(1)}, f32[256,256]{1,0:T(8,128)S(1)}, u32[]{:S(2)}, u32[]{:S(2)}) %collective-permute-start.1) | collective-permute-done | bytes 262176 | tf_op jit(solution)/shard_map/ppermute | solution.py:280
  12.6 1.6 %collective-permute-start.2 = (f32[256,256]{1,0:T(8,128)S(1)}, f32[256,256]{1,0:T(8,128)S(1)}, u32[]{:S(2)}, u32[]{:S(2)}) collective-permute-start(f32[256,256]{1,0:T(8,128)S(1)} %merge.2.sent), channel_id=1, source_target_pairs={{0,16},{1,9},{2,18},{3,11},{4,20},{5,13},{6,22},{7,15},{8,24},{9,1... | collective-permute-start | bytes 786440 | tf_op jit(solution)/shard_map/ppermute | solution.py:280
  14.2 1.4 %collective-permute-done.3.refs_3_.refs_1_ = f32[128,256]{1,0:T(8,128)S(1)} collective-permute-done((f32[128,256]{1,0:T(8,128)S(1)}, f32[128,256]{1,0:T(8,128)S(1)}, u32[]{:S(2)}, u32[]{:S(2)}) %collective-permute-start.3) | collective-permute-done | bytes 131104 | tf_op jit(solution)/shard_map/ppermute | solution.py:246
  15.6 0.4 %collective-permute-done.arrived.refs_4_.refs_2_ = f32[128,256]{1,0:T(8,128)S(1)} collective-permute-done((f32[128,256]{1,0:T(8,128)S(1)}, f32[128,256]{1,0:T(8,128)S(1)}, u32[]{:S(2)}, u32[]{:S(2)}) %collective-permute-start) | collective-permute-done | bytes 131104 | tf_op jit(solution)/shard_map/ppermute | solution.py:246
  16.1 1.9 %collective-permute-done.4.refs_5_.refs_3_ = f32[128,256]{1,0:T(8,128)S(1)} collective-permute-done((f32[128,256]{1,0:T(8,128)S(1)}, f32[128,256]{1,0:T(8,128)S(1)}, u32[]{:S(2)}, u32[]{:S(2)}) %collective-permute-start.4) | collective-permute-done | bytes 131104 | tf_op jit(solution)/shard_map/ppermute | solution.py:246
  18.0 0.9 %prepare.1 = (f32[1024,256]{1,0:T(8,128)S(1)}, f32[256,256]{1,0:T(8,128)S(1)}, s32[256,256]{1,0:T(8,128)S(1)}, f32[128,256]{1,0:T(8,128)S(1)}) custom-call(f32[1024,256]{1,0:T(8,128)S(1)} %get-tuple-element.17.matrix.top, s32[2,256]{1,0:T(2,128)S(1)} %copy-done.2, f32[2,128,256]{2,1,0:T(8,128)S(1)} %copy-done.1, ...), custom_call_target="tpu_custom_call" | custom-call | tf_op jit(solution)/shard_map/prepare/pallas_call | solution.py:260
  18.9 0.4 %collective-permute-done.8.refs_9_.refs_7_ = f32[128,256]{1,0:T(8,128)S(1)} collective-permute-done((f32[128,256]{1,0:T(8,128)S(1)}, f32[128,256]{1,0:T(8,128)S(1)}, u32[]{:S(2)}, u32[]{:S(2)}) %collective-permute-start.8) | collective-permute-done | bytes 131104 | tf_op jit(solution)/shard_map/ppermute | solution.py:247
  19.3 1.3 %solve.1 = (f32[256,256]{1,0:T(8,128)S(1)}, f32[256,256]{1,0:T(8,128)S(1)}, f32[256,256]{1,0:T(8,128)S(1)}) custom-call(f32[1024,256]{1,0:T(8,128)S(1)} %get-tuple-element.17.matrix.top, s32[2,256]{1,0:T(2,128)S(1)} %copy-done.2, f32[2,256,256]{2,1,0:T(8,128)S(1)} %copy-done, s32[256,256]{1,0:T(8,128)S(1)} %broadcast_in_dim.13.owner, ...), custom_call_target="tpu_custom_call" | custom-call | tf_op jit(solution)/shard_map/solve/pallas_call | solution.py:260
  20.6 1.6 %collective-permute-start.9 = (f32[256,256]{1,0:T(8,128)S(1)}, f32[256,256]{1,0:T(8,128)S(1)}, u32[]{:S(2)}, u32[]{:S(2)}) collective-permute-start(f32[256,256]{1,0:T(8,128)S(1)} %get-tuple-element.27.sent), channel_id=1, source_target_pairs={{0,8},{1,17},{2,10},{3,19},{4,12},{5,21},{6,14},{7,23},{8,0},{9,25... | collective-permute-start | bytes 786440 | tf_op jit(solution)/shard_map/ppermute | solution.py:280
  22.2 1.3 %collective-permute-start.11 = (f32[128,256]{1,0:T(8,128)S(1)}, f32[128,256]{1,0:T(8,128)S(1)}, u32[]{:S(2)}, u32[]{:S(2)}) collective-permute-start(f32[128,256]{1,0:T(8,128)S(1)} %get-tuple-element.28.refs_2_), channel_id=1, source_target_pairs={{0,2},{1,3},{2,4},{3,5},{4,6},{5,7},{6,0},{7,1},{8,10},{9,11},{10,... | collective-permute-start | bytes 393224 | tf_op jit(solution)/shard_map/ppermute | solution.py:246
  23.5 1.9 %collective-permute-start.12 = (f32[128,256]{1,0:T(8,128)S(1)}, f32[128,256]{1,0:T(8,128)S(1)}, u32[]{:S(2)}, u32[]{:S(2)}) collective-permute-start(f32[128,256]{1,0:T(8,128)S(1)} %get-tuple-element.28.refs_2_), channel_id=1, source_target_pairs={{0,4},{1,5},{2,6},{3,7},{4,0},{5,1},{6,2},{7,3},{8,12},{9,13},{10,... | collective-permute-start | bytes 393224 | tf_op jit(solution)/shard_map/ppermute | solution.py:246
  25.4 2.9 %collective-permute-start.13 = (f32[128,256]{1,0:T(8,128)S(1)}, f32[128,256]{1,0:T(8,128)S(1)}, u32[]{:S(2)}, u32[]{:S(2)}) collective-permute-start(f32[128,256]{1,0:T(8,128)S(1)} %get-tuple-element.28.refs_2_), channel_id=1, source_target_pairs={{0,6},{1,7},{2,0},{3,1},{4,2},{5,3},{6,4},{7,5},{8,14},{9,15},{10,... | collective-permute-start | bytes 393224 | tf_op jit(solution)/shard_map/ppermute | solution.py:246
  28.3 0.1 broadcast_in_dim.15.owner
  28.5 1.5 %collective-permute-start.10 = (f32[256,256]{1,0:T(8,128)S(1)}, f32[256,256]{1,0:T(8,128)S(1)}, u32[]{:S(2)}, u32[]{:S(2)}) collective-permute-start(f32[256,256]{1,0:T(8,128)S(1)} %merge.3.sent), channel_id=1, source_target_pairs={{0,16},{1,9},{2,18},{3,11},{4,20},{5,13},{6,22},{7,15},{8,24},{9,1... | collective-permute-start | bytes 786440 | tf_op jit(solution)/shard_map/ppermute | solution.py:280
  30.1 0.5 %collective-permute-start.15 = (f32[128,256]{1,0:T(8,128)S(1)}, f32[128,256]{1,0:T(8,128)S(1)}, u32[]{:S(2)}, u32[]{:S(2)}) collective-permute-start(f32[128,256]{1,0:T(8,128)S(1)} %collective-permute-done.11.refs_3_), channel_id=1, source_target_pairs={{0,1},{1,0},{2,3},{3,2},{4,5},{5,4},{6,7},{7,6},{8,9},{9,8},{10,11... | collective-permute-start | bytes 393224 | tf_op jit(solution)/shard_map/ppermute | solution.py:247
  30.6 4.2 %collective-permute-done.12.refs_4_ = f32[128,256]{1,0:T(8,128)S(1)} collective-permute-done((f32[128,256]{1,0:T(8,128)S(1)}, f32[128,256]{1,0:T(8,128)S(1)}, u32[]{:S(2)}, u32[]{:S(2)}) %collective-permute-start.12) | collective-permute-done | bytes 131104 | tf_op jit(solution)/shard_map/ppermute | solution.py:246
  34.8 0.5 %collective-permute-start.17 = (f32[128,256]{1,0:T(8,128)S(1)}, f32[128,256]{1,0:T(8,128)S(1)}, u32[]{:S(2)}, u32[]{:S(2)}) collective-permute-start(f32[128,256]{1,0:T(8,128)S(1)} %collective-permute-done.13.refs_5_), channel_id=1, source_target_pairs={{0,1},{1,0},{2,3},{3,2},{4,5},{5,4},{6,7},{7,6},{8,9},{9,8},{10,11... | collective-permute-start | bytes 393224 | tf_op jit(solution)/shard_map/ppermute | solution.py:247
  35.3 1.1 %update.1 = (f32[1024,256]{1,0:T(8,128)S(1)}, f32[256,256]{1,0:T(8,128)S(1)}) custom-call(f32[1024,256]{1,0:T(8,128)S(1)} %get-tuple-element.19.base, s32[2,256]{1,0:T(2,128)S(1)} %copy-done.2, f32[256,256]{1,0:T(8,128)S(1)} %get-tuple-element.23.upper_in, f32[256,256]{1,0:T(8,128)S(1)} %get-tuple-element.24.displaced_in, ...), custom_call_target="tpu_custom_call" | custom-call | tf_op jit(solution)/shard_map/update/pallas_call | solution.py:260
  36.5 2.1 %finish.1 = f32[1024,256]{1,0:T(8,128)} custom-call(f32[1024,256]{1,0:T(8,128)S(1)} %get-tuple-element.25.base, s32[2,256]{1,0:T(2,128)S(1)} %copy-done.2, f32[2,256,256]{2,1,0:T(8,128)S(1)} %copy-done, s32[256,256]{1,0:T(8,128)S(1)} %broadcast_in_dim.15.owner, f32[256,256]{1,0:T(8,128)S(1)} %get-tuple-element.26.top, f32[256,256]{1,0:T(8,128)S(1)} %merge.3.sent, ...), custom_call_target="tpu_custom_call" | custom-call | tf_op jit(solution)/shard_map/finish/pallas_call | solution.py:260
  (30 shorter events, 0.4 us)
Async XLA Ops:
  2.0 14.1 %collective-permute-start = (f32[128,256]{1,0:T(8,128)S(1)}, f32[128,256]{1,0:T(8,128)S(1)}, u32[]{:S(2)}, u32[]{:S(2)}) collective-permute-start(f32[128,256]{1,0:T(8,128)S(1)} %get-tuple-element.18.panel.refs_2_.refs_0_), channel_id=1, source_target_pairs={{0,4},{1,5},{2,6},{3,7},{4,0},{5,1},{6,2},{7,3},{8,12},{9,13},{10,... | collective-permute-start | bytes 393224 | tf_op jit(solution)/shard_map/ppermute | solution.py:246
  6.1 5.4 %copy-start.2 = (s32[2,256]{1,0:T(2,128)S(1)}, s32[2,256]{1,0:T(2,128)}, u32[]{:S(2)}) copy-start(s32[2,256]{1,0:T(2,128)} %pivots.9) | copy-start | bytes 6148
  6.1 6.4 %collective-permute-start.1 = (f32[256,256]{1,0:T(8,128)S(1)}, f32[256,256]{1,0:T(8,128)S(1)}, u32[]{:S(2)}, u32[]{:S(2)}) collective-permute-start(f32[256,256]{1,0:T(8,128)S(1)} %get-tuple-element.22.sent.before), channel_id=1, source_target_pairs={{0,8},{1,17},{2,10},{3,19},{4,12},{5,21},{6,14},{7,23},{8,0},{9,25... | collective-permute-start | bytes 786440 | tf_op jit(solution)/shard_map/ppermute | solution.py:280
  7.6 8.0 %collective-permute-start.3 = (f32[128,256]{1,0:T(8,128)S(1)}, f32[128,256]{1,0:T(8,128)S(1)}, u32[]{:S(2)}, u32[]{:S(2)}) collective-permute-start(f32[128,256]{1,0:T(8,128)S(1)} %release.1), channel_id=1, source_target_pairs={{0,2},{1,3},{2,4},{3,5},{4,6},{5,7},{6,0},{7,1},{8,10},{9,11},{10,... | collective-permute-start | bytes 393224 | tf_op jit(solution)/shard_map/ppermute | solution.py:246
  9.2 8.8 %collective-permute-start.4 = (f32[128,256]{1,0:T(8,128)S(1)}, f32[128,256]{1,0:T(8,128)S(1)}, u32[]{:S(2)}, u32[]{:S(2)}) collective-permute-start(f32[128,256]{1,0:T(8,128)S(1)} %release.1), channel_id=1, source_target_pairs={{0,6},{1,7},{2,0},{3,1},{4,2},{5,3},{6,4},{7,5},{8,14},{9,15},{10,... | collective-permute-start | bytes 393224 | tf_op jit(solution)/shard_map/ppermute | solution.py:246
  12.5 5.5 %copy-start.1 = (f32[2,128,256]{2,1,0:T(8,128)S(1)}, f32[2,128,256]{2,1,0:T(8,128)}, u32[]{:S(2)}) copy-start(f32[2,128,256]{2,1,0:T(8,128)} %panels.3) | copy-start | bytes 786436
  12.6 6.7 %collective-permute-start.2 = (f32[256,256]{1,0:T(8,128)S(1)}, f32[256,256]{1,0:T(8,128)S(1)}, u32[]{:S(2)}, u32[]{:S(2)}) collective-permute-start(f32[256,256]{1,0:T(8,128)S(1)} %merge.2.sent), channel_id=1, source_target_pairs={{0,16},{1,9},{2,18},{3,11},{4,20},{5,13},{6,22},{7,15},{8,24},{9,1... | collective-permute-start | bytes 786440 | tf_op jit(solution)/shard_map/ppermute | solution.py:280
  14.2 4.7 %collective-permute-start.5 = (f32[128,256]{1,0:T(8,128)S(1)}, f32[128,256]{1,0:T(8,128)S(1)}, u32[]{:S(2)}, u32[]{:S(2)}) collective-permute-start(f32[128,256]{1,0:T(8,128)S(1)} %get-tuple-element.18.panel.refs_2_.refs_0_), channel_id=1, source_target_pairs={{0,1},{1,0},{2,3},{3,2},{4,5},{5,4},{6,7},{7,6},{8,9},{9,8},{10,11... | collective-permute-start | bytes 393224 | tf_op jit(solution)/shard_map/ppermute | solution.py:247
  15.6 3.3 %collective-permute-start.6 = (f32[128,256]{1,0:T(8,128)S(1)}, f32[128,256]{1,0:T(8,128)S(1)}, u32[]{:S(2)}, u32[]{:S(2)}) collective-permute-start(f32[128,256]{1,0:T(8,128)S(1)} %collective-permute-done.3.refs_3_.refs_1_), channel_id=1, source_target_pairs={{0,1},{1,0},{2,3},{3,2},{4,5},{5,4},{6,7},{7,6},{8,9},{9,8},{10,11... | collective-permute-start | bytes 393224 | tf_op jit(solution)/shard_map/ppermute | solution.py:247
  16.0 2.9 %collective-permute-start.7 = (f32[128,256]{1,0:T(8,128)S(1)}, f32[128,256]{1,0:T(8,128)S(1)}, u32[]{:S(2)}, u32[]{:S(2)}) collective-permute-start(f32[128,256]{1,0:T(8,128)S(1)} %collective-permute-done.arrived.refs_4_.refs_2_), channel_id=1, source_target_pairs={{0,1},{1,0},{2,3},{3,2},{4,5},{5,4},{6,7},{7,6},{8,9},{9,8},{10,11... | collective-permute-start | bytes 393224 | tf_op jit(solution)/shard_map/ppermute | solution.py:247
  18.0 1.3 %collective-permute-start.8 = (f32[128,256]{1,0:T(8,128)S(1)}, f32[128,256]{1,0:T(8,128)S(1)}, u32[]{:S(2)}, u32[]{:S(2)}) collective-permute-start(f32[128,256]{1,0:T(8,128)S(1)} %collective-permute-done.4.refs_5_.refs_3_), channel_id=1, source_target_pairs={{0,1},{1,0},{2,3},{3,2},{4,5},{5,4},{6,7},{7,6},{8,9},{9,8},{10,11... | collective-permute-start | bytes 393224 | tf_op jit(solution)/shard_map/ppermute | solution.py:247
  18.0 1.3 %copy-start = (f32[2,256,256]{2,1,0:T(8,128)S(1)}, f32[2,256,256]{2,1,0:T(8,128)}, u32[]{:S(2)}) copy-start(f32[2,256,256]{2,1,0:T(8,128)} %inverse.3) | copy-start | bytes 1572868
  20.6 7.7 %collective-permute-start.9 = (f32[256,256]{1,0:T(8,128)S(1)}, f32[256,256]{1,0:T(8,128)S(1)}, u32[]{:S(2)}, u32[]{:S(2)}) collective-permute-start(f32[256,256]{1,0:T(8,128)S(1)} %get-tuple-element.27.sent), channel_id=1, source_target_pairs={{0,8},{1,17},{2,10},{3,19},{4,12},{5,21},{6,14},{7,23},{8,0},{9,25... | collective-permute-start | bytes 786440 | tf_op jit(solution)/shard_map/ppermute | solution.py:280
  22.2 7.8 %collective-permute-start.11 = (f32[128,256]{1,0:T(8,128)S(1)}, f32[128,256]{1,0:T(8,128)S(1)}, u32[]{:S(2)}, u32[]{:S(2)}) collective-permute-start(f32[128,256]{1,0:T(8,128)S(1)} %get-tuple-element.28.refs_2_), channel_id=1, source_target_pairs={{0,2},{1,3},{2,4},{3,5},{4,6},{5,7},{6,0},{7,1},{8,10},{9,11},{10,... | collective-permute-start | bytes 393224 | tf_op jit(solution)/shard_map/ppermute | solution.py:246
  23.5 11.3 %collective-permute-start.12 = (f32[128,256]{1,0:T(8,128)S(1)}, f32[128,256]{1,0:T(8,128)S(1)}, u32[]{:S(2)}, u32[]{:S(2)}) collective-permute-start(f32[128,256]{1,0:T(8,128)S(1)} %get-tuple-element.28.refs_2_), channel_id=1, source_target_pairs={{0,4},{1,5},{2,6},{3,7},{4,0},{5,1},{6,2},{7,3},{8,12},{9,13},{10,... | collective-permute-start | bytes 393224 | tf_op jit(solution)/shard_map/ppermute | solution.py:246
  25.4 9.4 %collective-permute-start.13 = (f32[128,256]{1,0:T(8,128)S(1)}, f32[128,256]{1,0:T(8,128)S(1)}, u32[]{:S(2)}, u32[]{:S(2)}) collective-permute-start(f32[128,256]{1,0:T(8,128)S(1)} %get-tuple-element.28.refs_2_), channel_id=1, source_target_pairs={{0,6},{1,7},{2,0},{3,1},{4,2},{5,3},{6,4},{7,5},{8,14},{9,15},{10,... | collective-permute-start | bytes 393224 | tf_op jit(solution)/shard_map/ppermute | solution.py:246
  28.5 8.0 %collective-permute-start.10 = (f32[256,256]{1,0:T(8,128)S(1)}, f32[256,256]{1,0:T(8,128)S(1)}, u32[]{:S(2)}, u32[]{:S(2)}) collective-permute-start(f32[256,256]{1,0:T(8,128)S(1)} %merge.3.sent), channel_id=1, source_target_pairs={{0,16},{1,9},{2,18},{3,11},{4,20},{5,13},{6,22},{7,15},{8,24},{9,1... | collective-permute-start | bytes 786440 | tf_op jit(solution)/shard_map/ppermute | solution.py:280
  30.1 6.4 %collective-permute-start.14 = (f32[128,256]{1,0:T(8,128)S(1)}, f32[128,256]{1,0:T(8,128)S(1)}, u32[]{:S(2)}, u32[]{:S(2)}) collective-permute-start(f32[128,256]{1,0:T(8,128)S(1)} %get-tuple-element.28.refs_2_), channel_id=1, source_target_pairs={{0,1},{1,0},{2,3},{3,2},{4,5},{5,4},{6,7},{7,6},{8,9},{9,8},{10,11... | collective-permute-start | bytes 393224 | tf_op jit(solution)/shard_map/ppermute | solution.py:247
  30.1 6.4 %collective-permute-start.15 = (f32[128,256]{1,0:T(8,128)S(1)}, f32[128,256]{1,0:T(8,128)S(1)}, u32[]{:S(2)}, u32[]{:S(2)}) collective-permute-start(f32[128,256]{1,0:T(8,128)S(1)} %collective-permute-done.11.refs_3_), channel_id=1, source_target_pairs={{0,1},{1,0},{2,3},{3,2},{4,5},{5,4},{6,7},{7,6},{8,9},{9,8},{10,11... | collective-permute-start | bytes 393224 | tf_op jit(solution)/shard_map/ppermute | solution.py:247
  34.8 1.7 %collective-permute-start.16 = (f32[128,256]{1,0:T(8,128)S(1)}, f32[128,256]{1,0:T(8,128)S(1)}, u32[]{:S(2)}, u32[]{:S(2)}) collective-permute-start(f32[128,256]{1,0:T(8,128)S(1)} %collective-permute-done.12.refs_4_), channel_id=1, source_target_pairs={{0,1},{1,0},{2,3},{3,2},{4,5},{5,4},{6,7},{7,6},{8,9},{9,8},{10,11... | collective-permute-start | bytes 393224 | tf_op jit(solution)/shard_map/ppermute | solution.py:247
  34.8 1.7 %collective-permute-start.17 = (f32[128,256]{1,0:T(8,128)S(1)}, f32[128,256]{1,0:T(8,128)S(1)}, u32[]{:S(2)}, u32[]{:S(2)}) collective-permute-start(f32[128,256]{1,0:T(8,128)S(1)} %collective-permute-done.13.refs_5_), channel_id=1, source_target_pairs={{0,1},{1,0},{2,3},{3,2},{4,5},{5,4},{6,7},{7,6},{8,9},{9,8},{10,11... | collective-permute-start | bytes 393224 | tf_op jit(solution)/shard_map/ppermute | solution.py:247

commit v4 on v2

--- a/solution.py
+++ b/solution.py
@@ -8,11 +8,13 @@
 from jax.sharding import PartitionSpec as P
 
 VMEM = pl.BlockSpec(memory_space=pltpu.VMEM)
+ANY = pl.BlockSpec(memory_space=pl.ANY)
 HBM = pl.BlockSpec(memory_space=pltpu.HBM)
 GRANT = pltpu.CompilerParams(vmem_limit_bytes=40 * 1024 * 1024)
 F32 = jnp.float32
 BF16 = jnp.bfloat16
 NOWHERE = -(1 << 24)
+COST = {"update": 4 << 20, "halve": 32 << 20}
 
 
 def product(left, right):
@@ -59,14 +61,17 @@
     return jnp.where(offset >= 0, offset, top)
 
 
-def first_slots(matrix, pivots, out, held, chosen, sems):
-    chunks = sems.shape[0] - 1
+def first_slots(matrix, pivots, panels, out, held, *refs):
+    blocks, (chosen, sems) = refs[:-2], refs[-2:]
+    chunks = sems.shape[0] - 1 - len(blocks)
     rows_dev = held.shape[0]
     rows = rows_dev // chunks
     copies = [pltpu.make_async_copy(pivots, chosen, sems.at[chunks])]
     for c in range(chunks):
         part = pl.ds(c * rows, rows)
         copies.append(pltpu.make_async_copy(matrix.at[part, :], held.at[part, :], sems.at[c]))
+    for step, block in enumerate(blocks):
+        copies.append(pltpu.make_async_copy(panels.at[step], block, sems.at[chunks + 1 + step]))
     for copy in copies:
         copy.start()
     copies[0].wait()
@@ -78,6 +83,8 @@
         term = pick(gather, split(held[c * rows : (c + 1) * rows, :]))
         total = term if total is None else total + term
     out[...] = total
+    for copy in copies[1 + chunks :]:
+        copy.wait()
 
 
 def prepare(matrix, pivots, base, ahead, places):
@@ -142,7 +149,7 @@
     return pl.multiple_of((chip * 2 + core) * rows, rows)
 
 
-def solve(bits, step, matrix, pivots, inverse, owner, ahead, places, sent, *refs):
+def solve(bits, step, matrix, pivots, inverse, owner, ahead, places, before, sent, *refs):
     refs = list(refs)
     received = [refs.pop(0) for _ in bits]
     blocks, (upper_out, displaced_out, slots_out) = refs[:-3], refs[-3:]
@@ -178,6 +185,10 @@
         low[pl.ds(start, rows), :] = block_low
 
 
+def halve(step, rows_dev, width, *refs):
+    assemble(step, refs[:-2], rows_dev, width, refs[-2], refs[-1])
+
+
 def update(step, base, pivots, upper_in, displaced_in, top, *refs):
     blocks, (out, top_out, high, low) = refs[:-4], refs[-4:]
     rows_dev = base.shape[0]
@@ -199,15 +210,12 @@
         out[part, :] = jnp.where(jnp.sum(hit, axis=1, keepdims=True) == 0, value, F32(0))
 
 
-def finish(bits, step, base, pivots, inverse, owner, top, sent, *refs):
-    refs = list(refs)
-    received = [refs.pop(0) for _ in bits]
-    blocks, (out, high, low, result, sems) = refs[:-5], refs[-5:]
+def finish(bits, step, base, pivots, inverse, owner, top, high, low, sent, *refs):
+    received, (out, result, sems) = refs[:-3], refs[-3:]
     rows_dev = base.shape[0]
     picked = picked_rows(bits, sent, received, owner)
     width = picked.shape[0]
     upper_full = dot(split(inverse[step]), split(picked))
-    assemble(step, blocks, rows_dev, width, high, low)
     offset = local_rows(pivots, step, rows_dev)
     upper = split(upper_full)
     displaced = split(displaced_rows(bits, received, top[...]))
@@ -227,11 +235,19 @@
         copy.wait()
 
 
-def gather_panel(block, count):
+def release(panel, before, out):
+    out[...] = panel[...]
+
+
+def gather_panel(up, down, count):
     across = [(i, i ^ 1) for i in range(count)]
-    own = [block]
-    for distance in range(1, count // 2):
-        own.append(lax.ppermute(block, "pcol", [(i, (i + 2 * distance) % count) for i in range(count)]))
+    chips = count // 2
+    own = [up] * chips
+    for distance in range(1, chips // 2 + 1):
+        own[distance] = lax.ppermute(own[distance - 1], "pcol", [(i, (i + 2) % count) for i in range(count)])
+    for distance in range(1, (chips - 1) // 2 + 1):
+        sent = down if distance == 1 else own[chips - distance + 1]
+        own[chips - distance] = lax.ppermute(sent, "pcol", [(i, (i - 2) % count) for i in range(count)])
     return own + [lax.ppermute(piece, "pcol", across) for piece in own]
 
 
@@ -244,7 +260,7 @@
     square = shape((width, columns), F32)
     full = shape((rows_dev, columns), F32)
 
-    def call(kernel, name, operands, outs, specs=None, out_specs=None, scratch=()):
+    def call(kernel, name, operands, outs, specs=None, out_specs=None, scratch=(), cost=None):
         return pl.pallas_call(
             kernel,
             out_shape=outs,
@@ -252,6 +268,7 @@
             out_specs=out_specs or jax.tree.map(lambda _: VMEM, outs),
             scratch_shapes=scratch,
             compiler_params=GRANT,
+            cost_estimate=cost and pl.CostEstimate(flops=0, bytes_accessed=cost, transcendentals=0),
             name=name,
         )(*operands)
 
@@ -271,29 +288,31 @@
     owner = jnp.broadcast_to((pivots // rows_dev)[:, :, None], (steps, width, columns))
     chunks = rows_dev // width
     halves = [pltpu.VMEM((rows_dev, l_panels.shape[2]), BF16)] * 2
-    slots = call(
+    block = shape(l_panels.shape[1:], F32)
+    slots, matrix, *own = call(
         first_slots,
         "first_slots",
-        [matrix, pivots],
-        square,
-        specs=[HBM, HBM],
-        scratch=[
-            pltpu.VMEM((rows_dev, columns), F32),
-            pltpu.VMEM((steps, width), jnp.int32),
-            pltpu.SemaphoreType.DMA((chunks + 1,)),
-        ],
-    )
+        [pltpu.with_memory_space_constraint(x, pltpu.HBM) for x in (matrix, pivots, l_panels)],
+        [square, full] + [block] * steps,
+        specs=[HBM] * 3,
+        scratch=[pltpu.VMEM((steps, width), jnp.int32), pltpu.SemaphoreType.DMA((chunks + 1 + steps,))],
+    )
+
+    def after(panel, before):
+        return call(release, "release", [panel, before], block, specs=[VMEM, ANY])
+
+    panels = [gather_panel(own[0], after(own[0], slots), process_columns)]
     sent, received = exchange(slots, 0)
-    panels = [gather_panel(l_panels[step], process_columns) for step in range(steps)]
     base, ahead, places = call(
         prepare, "prepare", [matrix, pivots], [full, square, shape((width, width), jnp.int32)]
     )
-    upper, displaced, slots = call(
-        functools.partial(solve, bits, 0),
-        "solve",
-        [matrix, pivots, l_inverse, owner[0], ahead, places, sent, *received, *panels[0]],
-        [square] * 3,
-    )
+    up = after(own[1], sent)
+    first = lax.ppermute(up, "pcol", [(i, (i + 2) % process_columns) for i in range(process_columns)])
+    operands = [matrix, pivots, l_inverse, owner[0], ahead, places, first, sent, *received, *panels[0]]
+    specs = [VMEM] * len(operands)
+    specs[6] = ANY
+    upper, displaced, slots = call(functools.partial(solve, bits, 0), "solve", operands, [square] * 3, specs=specs)
+    panels.append(gather_panel(up, after(own[1], slots), process_columns))
     sent, received = exchange(slots, 1)
     base, top = call(
         functools.partial(update, 0),
@@ -301,14 +320,22 @@
         [base, pivots, upper, displaced, matrix, *panels[0]],
         [full, square],
         scratch=halves,
+        cost=COST["update"],
+    )
+    high, low = call(
+        functools.partial(halve, 1, rows_dev, width),
+        "halve",
+        panels[1],
+        [shape((rows_dev, l_panels.shape[2]), BF16)] * 2,
+        cost=COST["halve"],
     )
     return call(
         functools.partial(finish, bits, 1),
         "finish",
-        [base, pivots, l_inverse, owner[1], top, sent, *received, *panels[1]],
+        [base, pivots, l_inverse, owner[1], top, high, low, sent, *received],
         full,
         out_specs=HBM,
-        scratch=halves + [pltpu.VMEM((rows_dev, columns), F32), pltpu.SemaphoreType.DMA((chunks,))],
+        scratch=[pltpu.VMEM((rows_dev, columns), F32), pltpu.SemaphoreType.DMA((chunks,))],
     )
 
 

time: 40.9 us -> 37.7 us (0.922)
  local copies, waits for them, and re-layouts: 2.43 us -> 0.2 us
  starting transfers between devices: 19.7 us -> 18.3 us
  Pallas kernels: 6.65 us -> 7.48 us
    ppermute x4, waiting for transfers between devices: 9.48 us -> 3.28 us  [exchange(): received.append(lax.ppermute(sent, ('prow', 'pcol'), pairs))]
    ppermute x6, waiting for transfers between devices: 2.06 us -> 8.09 us  [the longest x3 4.81 us: gather_panel(): lax.ppermute(own[distance - 1], 'pcol', [(i, (i + 2) % count) for i in ra...]
    unnamed x8 -> x4, local copies, waits for them, and re-layouts: 1.24 us -> 0.01 us
    squeeze x1 -> x0, local copies, waits for them, and re-layouts: 1 us -> none  [per_device(): l_panels[step]]
    pallas_call x7 -> x11, Pallas kernels: 6.65 us -> 7.48 us  [call(): pl.pallas_call(kernel, out_shape=outs, in_specs=specs or [VMEM] * len(ope...]
    ppermute x4, starting transfers between devices: 6.82 us -> 6.03 us  [exchange(): received.append(lax.ppermute(sent, ('prow', 'pcol'), pairs))]
    ppermute x8, starting transfers between devices: 2.04 us -> 1.37 us  [gather_panel(): return own + [lax.ppermute(piece, 'pcol', across) for piece in own]]
  transfers between devices with their start and end apart: 18 -> 18, of which waited for: 7 -> 8; matrix products, arithmetic and copies ran while one was open for 0% -> 1% of each run, Pallas kernels for 8% -> 6%
where the time goes in v4:
time: 37.7 us; the launch traced here: 37.5 us
  starting transfers between devices  18.3 us (49%)
  waiting for transfers between devices  11.4 us (30%)
  Pallas kernels  7.48 us (20%)
    pallas_call x11, Pallas kernels, call(): pl.pallas_call(kernel, out_shape=outs, in_specs=specs or [VMEM] * len(ope...  7.48 us
    ppermute x2, starting transfers between devices, gather_panel(): lax.ppermute(sent, 'pcol', [(i, (i - 2) % count) for i in range(count)])  6.17 us
    ppermute x4, starting transfers between devices, exchange(): received.append(lax.ppermute(sent, ('prow', 'pcol'), pairs))  6.03 us
    ppermute x3, waiting for transfers between devices, gather_panel(): lax.ppermute(own[distance - 1], 'pcol', [(i, (i + 2) % count) for i in ra...  4.81 us
    ppermute x4, waiting for transfers between devices, exchange(): received.append(lax.ppermute(sent, ('prow', 'pcol'), pairs))  3.28 us
    ppermute x1, waiting for transfers between devices, per_device(): lax.ppermute(up, 'pcol', [(i, (i + 2) % process_columns) for i in range(p...  3.1 us
    ppermute x3, starting transfers between devices, gather_panel(): lax.ppermute(own[distance - 1], 'pcol', [(i, (i + 2) % count) for i in ra...  3.08 us
    ppermute x1, starting transfers between devices, per_device(): lax.ppermute(up, 'pcol', [(i, (i + 2) % process_columns) for i in range(p...  1.63 us
  transfers between devices with their start and end apart: 18, of which 8 were waited for; matrix products, arithmetic and copies ran while one was open for 1% of the time, Pallas kernels for 6%

profile of v4, /device:TPU:0, one launch (start us, length us, event | category | flops | bytes accessed | tf_op | source)
XLA Modules:
  0.0 37.5 jit_solution(8748272554352016623)
XLA Ops:
  0.0 2.0 %first_slots.1 = (f32[256,256]{1,0:T(8,128)S(1)}, f32[1024,256]{1,0:T(8,128)S(1)}, f32[128,256]{1,0:T(8,128)S(1)}, f32[128,256]{1,0:T(8,128)S(1)}) custom-call(f32[1024,256]{1,0:T(8,128)} %matrix.1, s32[2,256]{1,0:T(2,128)} %pivots.9, f32[2,128,256]{2,1,0:T(8,128)} %panels.1), custom_call_target="tpu_custom_call" | custom-call | tf_op jit(solution)/shard_map/first_slots/pallas_call | solution.py:264
  2.0 3.1 %collective-permute-start.3 = (f32[128,256]{1,0:T(8,128)S(1)}, f32[128,256]{1,0:T(8,128)S(1)}, u32[]{:S(2)}, u32[]{:S(2)}) collective-permute-start(f32[128,256]{1,0:T(8,128)S(1)} %get-tuple-element.25.panel.refs_2_.refs_0_), channel_id=1, source_target_pairs={{0,2},{1,3},{2,4},{3,5},{4,6},{5,7},{6,0},{7,1},{8,10},{9,11},{10,... | collective-permute-start | bytes 393224 | tf_op jit(solution)/shard_map/ppermute | solution.py:247
  5.0 1.5 %collective-permute-start = (f32[256,256]{1,0:T(8,128)S(1)}, f32[256,256]{1,0:T(8,128)S(1)}, u32[]{:S(2)}, u32[]{:S(2)}) collective-permute-start(f32[256,256]{1,0:T(8,128)S(1)} %get-tuple-element.24.sent.before), channel_id=1, source_target_pairs={{0,8},{1,17},{2,10},{3,19},{4,12},{5,21},{6,14},{7,23},{8,0},{9,25... | collective-permute-start | bytes 786440 | tf_op jit(solution)/shard_map/ppermute | solution.py:285
  6.6 2.3 %collective-permute-start.5 = (f32[128,256]{1,0:T(8,128)S(1)}, f32[128,256]{1,0:T(8,128)S(1)}, u32[]{:S(2)}, u32[]{:S(2)}) collective-permute-start(f32[128,256]{1,0:T(8,128)S(1)} %release.4), channel_id=1, source_target_pairs={{0,6},{1,7},{2,0},{3,1},{4,2},{5,3},{6,4},{7,5},{8,14},{9,15},{10,... | collective-permute-start | bytes 393224 | tf_op jit(solution)/shard_map/ppermute | solution.py:250
  8.9 1.8 %collective-permute-done.3.refs_3_.refs_1_ = f32[128,256]{1,0:T(8,128)S(1)} collective-permute-done((f32[128,256]{1,0:T(8,128)S(1)}, f32[128,256]{1,0:T(8,128)S(1)}, u32[]{:S(2)}, u32[]{:S(2)}) %collective-permute-start.3) | collective-permute-done | bytes 131104 | tf_op jit(solution)/shard_map/ppermute | solution.py:247
  10.7 0.7 %collective-permute-done.received.refs_0_ = f32[256,256]{1,0:T(8,128)S(1)} collective-permute-done((f32[256,256]{1,0:T(8,128)S(1)}, f32[256,256]{1,0:T(8,128)S(1)}, u32[]{:S(2)}, u32[]{:S(2)}) %collective-permute-start) | collective-permute-done | bytes 262176 | tf_op jit(solution)/shard_map/ppermute | solution.py:285
  11.6 1.6 %collective-permute-start.2 = (f32[256,256]{1,0:T(8,128)S(1)}, f32[256,256]{1,0:T(8,128)S(1)}, u32[]{:S(2)}, u32[]{:S(2)}) collective-permute-start(f32[256,256]{1,0:T(8,128)S(1)} %merge.2.before.sent), channel_id=1, source_target_pairs={{0,16},{1,9},{2,18},{3,11},{4,20},{5,13},{6,22},{7,15},{8,24},{9,1... | collective-permute-start | bytes 786440 | tf_op jit(solution)/shard_map/ppermute | solution.py:285
  13.4 0.3 collective-permute-start.9
  13.7 1.6 %collective-permute-start.1 = (f32[128,256]{1,0:T(8,128)S(1)}, f32[128,256]{1,0:T(8,128)S(1)}, u32[]{:S(2)}, u32[]{:S(2)}) collective-permute-start(f32[128,256]{1,0:T(8,128)S(1)} %release.3.refs_0_), channel_id=1, source_target_pairs={{0,2},{1,3},{2,4},{3,5},{4,6},{5,7},{6,0},{7,1},{8,10},{9,11},{10,... | collective-permute-start | bytes 393224 | tf_op jit(solution)/shard_map/ppermute | solution.py:310
  15.4 2.1 %collective-permute-done.4.refs_4_.refs_2_ = f32[128,256]{1,0:T(8,128)S(1)} collective-permute-done((f32[128,256]{1,0:T(8,128)S(1)}, f32[128,256]{1,0:T(8,128)S(1)}, u32[]{:S(2)}, u32[]{:S(2)}) %collective-permute-start.4) | collective-permute-done | bytes 131104 | tf_op jit(solution)/shard_map/ppermute | solution.py:247
  17.4 0.7 %prepare.1 = (f32[1024,256]{1,0:T(8,128)S(1)}, f32[256,256]{1,0:T(8,128)S(1)}, s32[256,256]{1,0:T(8,128)S(1)}) custom-call(f32[1024,256]{1,0:T(8,128)S(1)} %get-tuple-element.19.matrix.top, s32[2,256]{1,0:T(2,128)S(1)} %copy-done.1), custom_call_target="tpu_custom_call" | custom-call | tf_op jit(solution)/shard_map/prepare/pallas_call | solution.py:264
  18.2 3.1 %collective-permute-done.1.before.refs_1_ = f32[128,256]{1,0:T(8,128)S(1)} collective-permute-done((f32[128,256]{1,0:T(8,128)S(1)}, f32[128,256]{1,0:T(8,128)S(1)}, u32[]{:S(2)}, u32[]{:S(2)}) %collective-permute-start.1) | collective-permute-done | bytes 131104 | tf_op jit(solution)/shard_map/ppermute | solution.py:310
  21.3 1.3 %solve.1 = (f32[256,256]{1,0:T(8,128)S(1)}, f32[256,256]{1,0:T(8,128)S(1)}, f32[256,256]{1,0:T(8,128)S(1)}) custom-call(f32[1024,256]{1,0:T(8,128)S(1)} %get-tuple-element.19.matrix.top, s32[2,256]{1,0:T(2,128)S(1)} %copy-done.1, f32[2,256,256]{2,1,0:T(8,128)S(1)} %copy-done, s32[256,256]{1,0:T(8,128)S(1)} %broadcast_in_dim.13.owner, ...), custom_call_target="tpu_custom_call" | custom-call | tf_op jit(solution)/shard_map/solve/pallas_call | solution.py:264
  22.6 1.4 %collective-permute-start.16 = (f32[256,256]{1,0:T(8,128)S(1)}, f32[256,256]{1,0:T(8,128)S(1)}, u32[]{:S(2)}, u32[]{:S(2)}) collective-permute-start(f32[256,256]{1,0:T(8,128)S(1)} %get-tuple-element.30.before.sent), channel_id=1, source_target_pairs={{0,8},{1,17},{2,10},{3,19},{4,12},{5,21},{6,14},{7,23},{8,0},{9,25... | collective-permute-start | bytes 786440 | tf_op jit(solution)/shard_map/ppermute | solution.py:285
  24.0 3.9 %collective-permute-start.11 = (f32[128,256]{1,0:T(8,128)S(1)}, f32[128,256]{1,0:T(8,128)S(1)}, u32[]{:S(2)}, u32[]{:S(2)}) collective-permute-start(f32[128,256]{1,0:T(8,128)S(1)} %release.5), channel_id=1, source_target_pairs={{0,6},{1,7},{2,0},{3,1},{4,2},{5,3},{6,4},{7,5},{8,14},{9,15},{10,... | collective-permute-start | bytes 393224 | tf_op jit(solution)/shard_map/ppermute | solution.py:250
  27.9 1.1 %collective-permute-done.16.received.refs_0_ = f32[256,256]{1,0:T(8,128)S(1)} collective-permute-done((f32[256,256]{1,0:T(8,128)S(1)}, f32[256,256]{1,0:T(8,128)S(1)}, u32[]{:S(2)}, u32[]{:S(2)}) %collective-permute-start.16) | collective-permute-done | bytes 262176 | tf_op jit(solution)/shard_map/ppermute | solution.py:285
  29.2 1.5 %collective-permute-start.17 = (f32[256,256]{1,0:T(8,128)S(1)}, f32[256,256]{1,0:T(8,128)S(1)}, u32[]{:S(2)}, u32[]{:S(2)}) collective-permute-start(f32[256,256]{1,0:T(8,128)S(1)} %merge.3.sent), channel_id=1, source_target_pairs={{0,16},{1,9},{2,18},{3,11},{4,20},{5,13},{6,22},{7,15},{8,24},{9,1... | collective-permute-start | bytes 786440 | tf_op jit(solution)/shard_map/ppermute | solution.py:285
  30.8 0.5 %collective-permute-start.13 = (f32[128,256]{1,0:T(8,128)S(1)}, f32[128,256]{1,0:T(8,128)S(1)}, u32[]{:S(2)}, u32[]{:S(2)}) collective-permute-start(f32[128,256]{1,0:T(8,128)S(1)} %collective-permute-done.1.before.refs_1_), channel_id=1, source_target_pairs={{0,1},{1,0},{2,3},{3,2},{4,5},{5,4},{6,7},{7,6},{8,9},{9,8},{10,11... | collective-permute-start | bytes 393224 | tf_op jit(solution)/shard_map/ppermute | solution.py:251
  31.3 1.0 %collective-permute-done.10.refs_2_ = f32[128,256]{1,0:T(8,128)S(1)} collective-permute-done((f32[128,256]{1,0:T(8,128)S(1)}, f32[128,256]{1,0:T(8,128)S(1)}, u32[]{:S(2)}, u32[]{:S(2)}) %collective-permute-start.10) | collective-permute-done | bytes 131104 | tf_op jit(solution)/shard_map/ppermute | solution.py:247
  32.2 0.5 %collective-permute-start.15 = (f32[128,256]{1,0:T(8,128)S(1)}, f32[128,256]{1,0:T(8,128)S(1)}, u32[]{:S(2)}, u32[]{:S(2)}) collective-permute-start(f32[128,256]{1,0:T(8,128)S(1)} %collective-permute-done.11.refs_3_), channel_id=1, source_target_pairs={{0,1},{1,0},{2,3},{3,2},{4,5},{5,4},{6,7},{7,6},{8,9},{9,8},{10,11... | collective-permute-start | bytes 393224 | tf_op jit(solution)/shard_map/ppermute | solution.py:251
  32.7 1.1 %update.1 = (f32[1024,256]{1,0:T(8,128)S(1)}, f32[256,256]{1,0:T(8,128)S(1)}) custom-call(f32[1024,256]{1,0:T(8,128)S(1)} %get-tuple-element.20.base, s32[2,256]{1,0:T(2,128)S(1)} %copy-done.1, f32[256,256]{1,0:T(8,128)S(1)} %get-tuple-element.26.upper_in, f32[256,256]{1,0:T(8,128)S(1)} %get-tuple-element.27.displaced_in, ...), custom_call_target="tpu_custom_call" | custom-call | bytes 4194304 | tf_op jit(solution)/shard_map/update/pallas_call | solution.py:264
  33.9 0.3 halve.1
  34.3 1.4 %collective-permute-done.17.refs_1_ = f32[256,256]{1,0:T(8,128)S(1)} collective-permute-done((f32[256,256]{1,0:T(8,128)S(1)}, f32[256,256]{1,0:T(8,128)S(1)}, u32[]{:S(2)}, u32[]{:S(2)}) %collective-permute-start.17) | collective-permute-done | bytes 262176 | tf_op jit(solution)/shard_map/ppermute | solution.py:285
  35.7 1.9 %finish.1 = f32[1024,256]{1,0:T(8,128)} custom-call(f32[1024,256]{1,0:T(8,128)S(1)} %get-tuple-element.28.base, s32[2,256]{1,0:T(2,128)S(1)} %copy-done.1, f32[2,256,256]{2,1,0:T(8,128)S(1)} %copy-done, s32[256,256]{1,0:T(8,128)S(1)} %broadcast_in_dim.15.owner, f32[256,256]{1,0:T(8,128)S(1)} %get-tuple-element.29.top, ...), custom_call_target="tpu_custom_call" | custom-call | tf_op jit(solution)/shard_map/finish/pallas_call | solution.py:264
  (31 shorter events, 0.6 us)
Async XLA Ops:
  2.0 8.7 %collective-permute-start.3 = (f32[128,256]{1,0:T(8,128)S(1)}, f32[128,256]{1,0:T(8,128)S(1)}, u32[]{:S(2)}, u32[]{:S(2)}) collective-permute-start(f32[128,256]{1,0:T(8,128)S(1)} %get-tuple-element.25.panel.refs_2_.refs_0_), channel_id=1, source_target_pairs={{0,2},{1,3},{2,4},{3,5},{4,6},{5,7},{6,0},{7,1},{8,10},{9,11},{10,... | collective-permute-start | bytes 393224 | tf_op jit(solution)/shard_map/ppermute | solution.py:247
  5.0 8.7 %collective-permute-start.6 = (f32[128,256]{1,0:T(8,128)S(1)}, f32[128,256]{1,0:T(8,128)S(1)}, u32[]{:S(2)}, u32[]{:S(2)}) collective-permute-start(f32[128,256]{1,0:T(8,128)S(1)} %get-tuple-element.25.panel.refs_2_.refs_0_), channel_id=1, source_target_pairs={{0,1},{1,0},{2,3},{3,2},{4,5},{5,4},{6,7},{7,6},{8,9},{9,8},{10,11... | collective-permute-start | bytes 393224 | tf_op jit(solution)/shard_map/ppermute | solution.py:251
  5.0 3.8 %copy-start.1 = (s32[2,256]{1,0:T(2,128)S(1)}, s32[2,256]{1,0:T(2,128)}, u32[]{:S(2)}) copy-start(s32[2,256]{1,0:T(2,128)} %pivots.9) | copy-start | bytes 6148
  5.0 6.4 %collective-permute-start = (f32[256,256]{1,0:T(8,128)S(1)}, f32[256,256]{1,0:T(8,128)S(1)}, u32[]{:S(2)}, u32[]{:S(2)}) collective-permute-start(f32[256,256]{1,0:T(8,128)S(1)} %get-tuple-element.24.sent.before), channel_id=1, source_target_pairs={{0,8},{1,17},{2,10},{3,19},{4,12},{5,21},{6,14},{7,23},{8,0},{9,25... | collective-permute-start | bytes 786440 | tf_op jit(solution)/shard_map/ppermute | solution.py:285
  6.6 6.8 %collective-permute-start.5 = (f32[128,256]{1,0:T(8,128)S(1)}, f32[128,256]{1,0:T(8,128)S(1)}, u32[]{:S(2)}, u32[]{:S(2)}) collective-permute-start(f32[128,256]{1,0:T(8,128)S(1)} %release.4), channel_id=1, source_target_pairs={{0,6},{1,7},{2,0},{3,1},{4,2},{5,3},{6,4},{7,5},{8,14},{9,15},{10,... | collective-permute-start | bytes 393224 | tf_op jit(solution)/shard_map/ppermute | solution.py:250
  10.7 6.8 %collective-permute-start.4 = (f32[128,256]{1,0:T(8,128)S(1)}, f32[128,256]{1,0:T(8,128)S(1)}, u32[]{:S(2)}, u32[]{:S(2)}) collective-permute-start(f32[128,256]{1,0:T(8,128)S(1)} %collective-permute-done.3.refs_3_.refs_1_), channel_id=1, source_target_pairs={{0,2},{1,3},{2,4},{3,5},{4,6},{5,7},{6,0},{7,1},{8,10},{9,11},{10,... | collective-permute-start | bytes 393224 | tf_op jit(solution)/shard_map/ppermute | solution.py:247
  11.6 9.7 %collective-permute-start.2 = (f32[256,256]{1,0:T(8,128)S(1)}, f32[256,256]{1,0:T(8,128)S(1)}, u32[]{:S(2)}, u32[]{:S(2)}) collective-permute-start(f32[256,256]{1,0:T(8,128)S(1)} %merge.2.before.sent), channel_id=1, source_target_pairs={{0,16},{1,9},{2,18},{3,11},{4,20},{5,13},{6,22},{7,15},{8,24},{9,1... | collective-permute-start | bytes 786440 | tf_op jit(solution)/shard_map/ppermute | solution.py:285
  13.2 5.0 %collective-permute-start.7 = (f32[128,256]{1,0:T(8,128)S(1)}, f32[128,256]{1,0:T(8,128)S(1)}, u32[]{:S(2)}, u32[]{:S(2)}) collective-permute-start(f32[128,256]{1,0:T(8,128)S(1)} %collective-permute-done.3.refs_3_.refs_1_), channel_id=1, source_target_pairs={{0,1},{1,0},{2,3},{3,2},{4,5},{5,4},{6,7},{7,6},{8,9},{9,8},{10,11... | collective-permute-start | bytes 393224 | tf_op jit(solution)/shard_map/ppermute | solution.py:251
  13.4 4.8 %collective-permute-start.9 = (f32[128,256]{1,0:T(8,128)S(1)}, f32[128,256]{1,0:T(8,128)S(1)}, u32[]{:S(2)}, u32[]{:S(2)}) collective-permute-start(f32[128,256]{1,0:T(8,128)S(1)} %collective-permute-done.5.refs_5_.refs_3_), channel_id=1, source_target_pairs={{0,1},{1,0},{2,3},{3,2},{4,5},{5,4},{6,7},{7,6},{8,9},{9,8},{10,11... | collective-permute-start | bytes 393224 | tf_op jit(solution)/shard_map/ppermute | solution.py:251
  13.7 7.5 %collective-permute-start.1 = (f32[128,256]{1,0:T(8,128)S(1)}, f32[128,256]{1,0:T(8,128)S(1)}, u32[]{:S(2)}, u32[]{:S(2)}) collective-permute-start(f32[128,256]{1,0:T(8,128)S(1)} %release.3.refs_0_), channel_id=1, source_target_pairs={{0,2},{1,3},{2,4},{3,5},{4,6},{5,7},{6,0},{7,1},{8,10},{9,11},{10,... | collective-permute-start | bytes 393224 | tf_op jit(solution)/shard_map/ppermute | solution.py:310
  17.4 3.8 %collective-permute-start.8 = (f32[128,256]{1,0:T(8,128)S(1)}, f32[128,256]{1,0:T(8,128)S(1)}, u32[]{:S(2)}, u32[]{:S(2)}) collective-permute-start(f32[128,256]{1,0:T(8,128)S(1)} %collective-permute-done.4.refs_4_.refs_2_), channel_id=1, source_target_pairs={{0,1},{1,0},{2,3},{3,2},{4,5},{5,4},{6,7},{7,6},{8,9},{9,8},{10,11... | collective-permute-start | bytes 393224 | tf_op jit(solution)/shard_map/ppermute | solution.py:251
  17.4 3.8 %copy-start = (f32[2,256,256]{2,1,0:T(8,128)S(1)}, f32[2,256,256]{2,1,0:T(8,128)}, u32[]{:S(2)}) copy-start(f32[2,256,256]{2,1,0:T(8,128)} %inverse.3) | copy-start | bytes 1572868
  22.6 6.4 %collective-permute-start.16 = (f32[256,256]{1,0:T(8,128)S(1)}, f32[256,256]{1,0:T(8,128)S(1)}, u32[]{:S(2)}, u32[]{:S(2)}) collective-permute-start(f32[256,256]{1,0:T(8,128)S(1)} %get-tuple-element.30.before.sent), channel_id=1, source_target_pairs={{0,8},{1,17},{2,10},{3,19},{4,12},{5,21},{6,14},{7,23},{8,0},{9,25... | collective-permute-start | bytes 786440 | tf_op jit(solution)/shard_map/ppermute | solution.py:285
  24.0 8.2 %collective-permute-start.10 = (f32[128,256]{1,0:T(8,128)S(1)}, f32[128,256]{1,0:T(8,128)S(1)}, u32[]{:S(2)}, u32[]{:S(2)}) collective-permute-start(f32[128,256]{1,0:T(8,128)S(1)} %collective-permute-done.1.before.refs_1_), channel_id=1, source_target_pairs={{0,2},{1,3},{2,4},{3,5},{4,6},{5,7},{6,0},{7,1},{8,10},{9,11},{10,... | collective-permute-start | bytes 393224 | tf_op jit(solution)/shard_map/ppermute | solution.py:247
  24.0 8.2 %collective-permute-start.11 = (f32[128,256]{1,0:T(8,128)S(1)}, f32[128,256]{1,0:T(8,128)S(1)}, u32[]{:S(2)}, u32[]{:S(2)}) collective-permute-start(f32[128,256]{1,0:T(8,128)S(1)} %release.5), channel_id=1, source_target_pairs={{0,6},{1,7},{2,0},{3,1},{4,2},{5,3},{6,4},{7,5},{8,14},{9,15},{10,... | collective-permute-start | bytes 393224 | tf_op jit(solution)/shard_map/ppermute | solution.py:250
  29.2 6.4 %collective-permute-start.17 = (f32[256,256]{1,0:T(8,128)S(1)}, f32[256,256]{1,0:T(8,128)S(1)}, u32[]{:S(2)}, u32[]{:S(2)}) collective-permute-start(f32[256,256]{1,0:T(8,128)S(1)} %merge.3.sent), channel_id=1, source_target_pairs={{0,16},{1,9},{2,18},{3,11},{4,20},{5,13},{6,22},{7,15},{8,24},{9,1... | collective-permute-start | bytes 786440 | tf_op jit(solution)/shard_map/ppermute | solution.py:285
  30.8 3.1 %collective-permute-start.12 = (f32[128,256]{1,0:T(8,128)S(1)}, f32[128,256]{1,0:T(8,128)S(1)}, u32[]{:S(2)}, u32[]{:S(2)}) collective-permute-start(f32[128,256]{1,0:T(8,128)S(1)} %release.3.refs_0_), channel_id=1, source_target_pairs={{0,1},{1,0},{2,3},{3,2},{4,5},{5,4},{6,7},{7,6},{8,9},{9,8},{10,11... | collective-permute-start | bytes 393224 | tf_op jit(solution)/shard_map/ppermute | solution.py:251
  30.8 3.1 %collective-permute-start.13 = (f32[128,256]{1,0:T(8,128)S(1)}, f32[128,256]{1,0:T(8,128)S(1)}, u32[]{:S(2)}, u32[]{:S(2)}) collective-permute-start(f32[128,256]{1,0:T(8,128)S(1)} %collective-permute-done.1.before.refs_1_), channel_id=1, source_target_pairs={{0,1},{1,0},{2,3},{3,2},{4,5},{5,4},{6,7},{7,6},{8,9},{9,8},{10,11... | collective-permute-start | bytes 393224 | tf_op jit(solution)/shard_map/ppermute | solution.py:251
  32.2 1.7 %collective-permute-start.14 = (f32[128,256]{1,0:T(8,128)S(1)}, f32[128,256]{1,0:T(8,128)S(1)}, u32[]{:S(2)}, u32[]{:S(2)}) collective-permute-start(f32[128,256]{1,0:T(8,128)S(1)} %collective-permute-done.10.refs_2_), channel_id=1, source_target_pairs={{0,1},{1,0},{2,3},{3,2},{4,5},{5,4},{6,7},{7,6},{8,9},{9,8},{10,11... | collective-permute-start | bytes 393224 | tf_op jit(solution)/shard_map/ppermute | solution.py:251
  32.2 1.7 %collective-permute-start.15 = (f32[128,256]{1,0:T(8,128)S(1)}, f32[128,256]{1,0:T(8,128)S(1)}, u32[]{:S(2)}, u32[]{:S(2)}) collective-permute-start(f32[128,256]{1,0:T(8,128)S(1)} %collective-permute-done.11.refs_3_), channel_id=1, source_target_pairs={{0,1},{1,0},{2,3},{3,2},{4,5},{5,4},{6,7},{7,6},{8,9},{9,8},{10,11... | collective-permute-start | bytes 393224 | tf_op jit(solution)/shard_map/ppermute | solution.py:251

commit v5 on v4

--- a/solution.py
+++ b/solution.py
@@ -14,7 +14,6 @@
 F32 = jnp.float32
 BF16 = jnp.bfloat16
 NOWHERE = -(1 << 24)
-COST = {"update": 4 << 20, "halve": 32 << 20}
 
 
 def product(left, right):
@@ -112,7 +111,7 @@
     return bit, known
 
 
-def merge(bits, stage, sent, received, owner, out):
+def merge(bits, stage, sent, received, owner, *refs):
     row = lax.axis_index("prow")
     bit, known = stage_bits(bits, stage)
     partner = row ^ bit
@@ -121,7 +120,7 @@
     theirs = ((who ^ partner) & keep) == 0
     neither = ((who ^ row) & ~(known | bit)) != 0
     take = theirs | (neither & ((partner & keep) == 0))
-    out[...] = jnp.where(take, received[...], sent[...])
+    refs[-1][...] = jnp.where(take, received[...], sent[...])
 
 
 def picked_rows(bits, sent, received, owner):
@@ -139,17 +138,39 @@
     return jnp.where(row == 0, top, value)
 
 
-def block_start(position, blocks):
-    pairs = len(blocks) // 2
-    side, distance = divmod(position, pairs)
-    col = lax.axis_index("pcol")
-    chip = lax.rem(col // 2 - distance + pairs, pairs)
-    core = lax.rem(col, 2) if side == 0 else 1 - lax.rem(col, 2)
-    rows = blocks[position].shape[0]
-    return pl.multiple_of((chip * 2 + core) * rows, rows)
-
-
-def solve(bits, step, matrix, pivots, inverse, owner, ahead, places, before, sent, *refs):
+def place_of(chip, core, chips, rows):
+    return pl.multiple_of((lax.rem(chip + chips, chips) * 2 + core) * rows, rows)
+
+
+def ring_blocks(refs):
+    chips = len(refs) // 2
+    chip, core = lax.axis_index("pcol") // 2, lax.rem(lax.axis_index("pcol"), 2)
+    found = []
+    for position, ref in enumerate(refs):
+        side, distance = divmod(position, chips)
+        found.append((ref, place_of(chip - distance, 1 - core if side else core, chips, ref.shape[0])))
+    return found
+
+
+def pair_blocks(refs):
+    chips, rows = len(refs) - 2, refs[0].shape[0]
+    chip, core = lax.axis_index("pcol") // 2, lax.rem(lax.axis_index("pcol"), 2)
+    found = []
+    for position, ref in enumerate(refs[:4]):
+        side, far = position % 2, position // 2
+        found.append((ref, place_of(chip + far * (chips // 2), 1 - core if side else core, chips, rows)))
+    hops = chips // 2 - 1
+    for position, ref in enumerate(refs[4:]):
+        side, distance = divmod(position, hops)
+        along = (distance + 1) * (1 - 2 * core)
+        for half in range(2):
+            owner = core if side == half else 1 - core
+            place = place_of(chip + along if side else chip - along, owner, chips, rows)
+            found.append((ref.at[pl.ds(half * rows, rows), :], place))
+    return found
+
+
+def solve(bits, step, matrix, pivots, inverse, owner, ahead, places, sent, *refs):
     refs = list(refs)
     received = [refs.pop(0) for _ in bits]
     blocks, (upper_out, displaced_out, slots_out) = refs[:-3], refs[-3:]
@@ -161,9 +182,9 @@
     displaced = displaced_rows(bits, received, matrix[step * width : (step + 1) * width, :])
     displaced_out[...] = displaced
     high = low = None
-    for position, block in enumerate(blocks):
+    for block, start in ring_blocks(blocks):
         rows = block.shape[0]
-        local = places[:, :rows] - block_start(position, blocks)
+        local = places[:, :rows] - start
         gather = one_hot(local, iota((width, rows), 1))
         block_high, block_low = split(block[...])
         term_high, term_low = product(gather, block_high), product(gather, block_low)
@@ -176,9 +197,8 @@
 
 def assemble(step, blocks, rows_dev, width, high, low):
     limit = (step + 1) * width - lax.axis_index("prow") * rows_dev
-    for position, block in enumerate(blocks):
+    for block, start in blocks:
         rows = block.shape[0]
-        start = block_start(position, blocks)
         below = start + iota(block.shape, 0) >= limit
         block_high, block_low = split(jnp.where(below, -block[...], F32(0)))
         high[pl.ds(start, rows), :] = block_high
@@ -186,14 +206,14 @@
 
 
 def halve(step, rows_dev, width, *refs):
-    assemble(step, refs[:-2], rows_dev, width, refs[-2], refs[-1])
-
-
-def update(step, base, pivots, upper_in, displaced_in, top, *refs):
+    assemble(step, pair_blocks(refs[:-2]), rows_dev, width, refs[-2], refs[-1])
+
+
+def update(step, base, pivots, upper_in, displaced_in, *refs):
     blocks, (out, top_out, high, low) = refs[:-4], refs[-4:]
     rows_dev = base.shape[0]
     width = upper_in.shape[0]
-    assemble(step, blocks, rows_dev, width, high, low)
+    assemble(step, ring_blocks(blocks), rows_dev, width, high, low)
     offset = local_rows(pivots, step, rows_dev)
     later = local_rows(pivots, step + 1, rows_dev)
     upper = split(upper_in[...])
@@ -235,20 +255,42 @@
         copy.wait()
 
 
+def pack(own, other, before, out):
+    rows = own.shape[0]
+    out[:rows, :] = own[...]
+    out[rows:, :] = other[...]
+
+
 def release(panel, before, out):
     out[...] = panel[...]
 
 
-def gather_panel(up, down, count):
-    across = [(i, i ^ 1) for i in range(count)]
+def shift(block, distance, count):
+    return lax.ppermute(block, "pcol", [(i, (i + 2 * distance) % count) for i in range(count)])
+
+
+def across(block, count):
+    return lax.ppermute(block, "pcol", [(i, i ^ 1) for i in range(count)])
+
+
+def forwarded(up, down, count):
     chips = count // 2
     own = [up] * chips
     for distance in range(1, chips // 2 + 1):
-        own[distance] = lax.ppermute(own[distance - 1], "pcol", [(i, (i + 2) % count) for i in range(count)])
+        own[distance] = shift(own[distance - 1], 1, count)
     for distance in range(1, (chips - 1) // 2 + 1):
-        sent = down if distance == 1 else own[chips - distance + 1]
-        own[chips - distance] = lax.ppermute(sent, "pcol", [(i, (i - 2) % count) for i in range(count)])
-    return own + [lax.ppermute(piece, "pcol", across) for piece in own]
+        own[chips - distance] = shift(down if distance == 1 else own[chips - distance + 1], -1, count)
+    return own + [across(piece, count) for piece in own]
+
+
+def paired(own, other, pair, far, count):
+    chips = count // 2
+    onward = [(i, (i + (2 if i % 2 == 0 else -2)) % count) for i in range(count)]
+    passed = [pair]
+    for _ in range(chips // 2 - 1):
+        passed.append(lax.ppermute(passed[-1], "pcol", onward))
+    back = [across(piece, count) for piece in passed[1:]]
+    return [own, other, far, across(far, count)] + passed[1:] + back
 
 
 def per_device(mesh, matrix, l_panels, l_inverse, pivots):
@@ -260,7 +302,7 @@
     square = shape((width, columns), F32)
     full = shape((rows_dev, columns), F32)
 
-    def call(kernel, name, operands, outs, specs=None, out_specs=None, scratch=(), cost=None):
+    def call(kernel, name, operands, outs, specs=None, out_specs=None, scratch=()):
         return pl.pallas_call(
             kernel,
             out_shape=outs,
@@ -268,15 +310,16 @@
             out_specs=out_specs or jax.tree.map(lambda _: VMEM, outs),
             scratch_shapes=scratch,
             compiler_params=GRANT,
-            cost_estimate=cost and pl.CostEstimate(flops=0, bytes_accessed=cost, transcendentals=0),
             name=name,
         )(*operands)
 
-    def exchange(sent, step):
+    def exchange(sent, step, before=()):
         received = []
         for stage in range(len(bits)):
             if stage:
-                sent = call(functools.partial(merge, bits, stage - 1), "merge", [sent, received[-1], owner[step]], square)
+                operands = [sent, received[-1], owner[step], *before]
+                specs = [VMEM] * 3 + [ANY] * len(before)
+                sent = call(functools.partial(merge, bits, stage - 1), "merge", operands, square, specs=specs)
             pairs = []
             for i in range(process_rows):
                 for j in range(process_columns):
@@ -301,33 +344,31 @@
     def after(panel, before):
         return call(release, "release", [panel, before], block, specs=[VMEM, ANY])
 
-    panels = [gather_panel(own[0], after(own[0], slots), process_columns)]
-    sent, received = exchange(slots, 0)
+    panels = [forwarded(own[0], after(own[0], slots), process_columns)]
     base, ahead, places = call(
         prepare, "prepare", [matrix, pivots], [full, square, shape((width, width), jnp.int32)]
     )
-    up = after(own[1], sent)
-    first = lax.ppermute(up, "pcol", [(i, (i + 2) % process_columns) for i in range(process_columns)])
-    operands = [matrix, pivots, l_inverse, owner[0], ahead, places, first, sent, *received, *panels[0]]
-    specs = [VMEM] * len(operands)
-    specs[6] = ANY
-    upper, displaced, slots = call(functools.partial(solve, bits, 0), "solve", operands, [square] * 3, specs=specs)
-    panels.append(gather_panel(up, after(own[1], slots), process_columns))
-    sent, received = exchange(slots, 1)
+    sent, received = exchange(slots, 0, [places])
+    other = across(own[1], process_columns)
+    two = shape((2 * block.shape[0], block.shape[1]), F32)
+    pair = call(pack, "pack", [own[1], other, sent], two, specs=[VMEM, VMEM, ANY])
+    operands = [matrix, pivots, l_inverse, owner[0], ahead, places, sent, *received, *panels[0]]
+    upper, displaced, slots = call(functools.partial(solve, bits, 0), "solve", operands, [square] * 3)
+    far = shift(after(own[1], slots), process_columns // 4, process_columns)
+    panels.append(paired(own[1], other, pair, far, process_columns))
     base, top = call(
         functools.partial(update, 0),
         "update",
-        [base, pivots, upper, displaced, matrix, *panels[0]],
+        [base, pivots, upper, displaced, *panels[0]],
         [full, square],
         scratch=halves,
-        cost=COST["update"],
-    )
+    )
+    sent, received = exchange(slots, 1)
     high, low = call(
         functools.partial(halve, 1, rows_dev, width),
         "halve",
         panels[1],
         [shape((rows_dev, l_panels.shape[2]), BF16)] * 2,
-        cost=COST["halve"],
     )
     return call(
         functools.partial(finish, bits, 1),

time: 37.7 us -> 37.8 us (level)
  waiting for transfers between devices: 11.4 us -> 16.4 us
  starting transfers between devices: 18.3 us -> 13.4 us
    ppermute x14 -> x12, waiting for transfers between devices: 8.11 us -> 16.1 us  [the longest x4 12.1 us: shift(): lax.ppermute(block, 'pcol', [(i, (i + 2 * distance) % count) for i in ran...]
    ppermute x14 -> x12, starting transfers between devices: 12.3 us -> 7.54 us  [the longest x4 6.87 us: shift(): lax.ppermute(block, 'pcol', [(i, (i + 2 * distance) % count) for i in ran...]
    ppermute x4, waiting for transfers between devices: 3.28 us -> 0.34 us  [exchange(): received.append(lax.ppermute(sent, ('prow', 'pcol'), pairs))]
  transfers between devices with their start and end apart: 18 -> 16, of which waited for: 8 -> 7; matrix products, arithmetic and copies ran while one was open for 1% -> 1% of each run, Pallas kernels for 6% -> 10%
where the time goes in v5:
time: 37.8 us; the launch traced here: 37.6 us
  waiting for transfers between devices  16.4 us (43%)
  starting transfers between devices  13.4 us (35%)
  Pallas kernels  7.48 us (20%)
    ppermute x4, waiting for transfers between devices, shift(): lax.ppermute(block, 'pcol', [(i, (i + 2 * distance) % count) for i in ran...  12.1 us
    pallas_call x11, Pallas kernels, call(): pl.pallas_call(kernel, out_shape=outs, in_specs=specs or [VMEM] * len(ope...  7.48 us
    ppermute x4, starting transfers between devices, shift(): lax.ppermute(block, 'pcol', [(i, (i + 2 * distance) % count) for i in ran...  6.87 us
    ppermute x4, starting transfers between devices, exchange(): received.append(lax.ppermute(sent, ('prow', 'pcol'), pairs))  5.85 us
    ppermute x1, waiting for transfers between devices, paired(): passed.append(lax.ppermute(passed[-1], 'pcol', onward))  2.6 us
    ppermute x7, waiting for transfers between devices, across(): return lax.ppermute(block, 'pcol', [(i, i ^ 1) for i in range(count)])  1.42 us
  transfers between devices with their start and end apart: 16, of which 7 were waited for; matrix products, arithmetic and copies ran while one was open for 1% of the time, Pallas kernels for 10%

profile of v5, /device:TPU:0, one launch (start us, length us, event | category | flops | bytes accessed | tf_op | source)
XLA Modules:
  0.0 37.6 jit_solution(11735847931825858682)
XLA Ops:
  0.0 2.0 %first_slots.1 = (f32[256,256]{1,0:T(8,128)S(1)}, f32[1024,256]{1,0:T(8,128)S(1)}, f32[128,256]{1,0:T(8,128)S(1)}, f32[128,256]{1,0:T(8,128)S(1)}) custom-call(f32[1024,256]{1,0:T(8,128)} %matrix.1, s32[2,256]{1,0:T(2,128)} %pivots.9, f32[2,128,256]{2,1,0:T(8,128)} %panels.1), custom_call_target="tpu_custom_call" | custom-call | tf_op jit(solution)/shard_map/first_slots/pallas_call | solution.py:306
  2.0 3.0 %collective-permute-start = (f32[256,256]{1,0:T(8,128)S(1)}, f32[256,256]{1,0:T(8,128)S(1)}, u32[]{:S(2)}, u32[]{:S(2)}) collective-permute-start(f32[256,256]{1,0:T(8,128)S(1)} %get-tuple-element.23.sent.before), channel_id=1, source_target_pairs={{0,8},{1,17},{2,10},{3,19},{4,12},{5,21},{6,14},{7,23},{8,0},{9,25... | collective-permute-start | bytes 786440 | tf_op jit(solution)/shard_map/ppermute | solution.py:328
  5.0 1.6 %collective-permute-start.2 = (f32[128,256]{1,0:T(8,128)S(1)}, f32[128,256]{1,0:T(8,128)S(1)}, u32[]{:S(2)}, u32[]{:S(2)}) collective-permute-start(f32[128,256]{1,0:T(8,128)S(1)} %get-tuple-element.24.panel.refs_2_.refs_0_), channel_id=1, source_target_pairs={{0,2},{1,3},{2,4},{3,5},{4,6},{5,7},{6,0},{7,1},{8,10},{9,11},{10,... | collective-permute-start | bytes 393224 | tf_op jit(solution)/shard_map/ppermute | solution.py:269
  6.6 2.3 %collective-permute-start.4 = (f32[128,256]{1,0:T(8,128)S(1)}, f32[128,256]{1,0:T(8,128)S(1)}, u32[]{:S(2)}, u32[]{:S(2)}) collective-permute-start(f32[128,256]{1,0:T(8,128)S(1)} %release.2), channel_id=1, source_target_pairs={{0,6},{1,7},{2,0},{3,1},{4,2},{5,3},{6,4},{7,5},{8,14},{9,15},{10,... | collective-permute-start | bytes 393224 | tf_op jit(solution)/shard_map/ppermute | solution.py:269
  8.9 0.7 %prepare.1 = (f32[1024,256]{1,0:T(8,128)S(1)}, f32[256,256]{1,0:T(8,128)S(1)}, s32[256,256]{1,0:T(8,128)S(1)}) custom-call(f32[1024,256]{1,0:T(8,128)S(1)} %get-tuple-element.19.matrix, s32[2,256]{1,0:T(2,128)S(1)} %copy-done.1), custom_call_target="tpu_custom_call" | custom-call | tf_op jit(solution)/shard_map/prepare/pallas_call | solution.py:306
  9.6 3.5 %collective-permute-done.2.refs_3_.refs_1_ = f32[128,256]{1,0:T(8,128)S(1)} collective-permute-done((f32[128,256]{1,0:T(8,128)S(1)}, f32[128,256]{1,0:T(8,128)S(1)}, u32[]{:S(2)}, u32[]{:S(2)}) %collective-permute-start.2) | collective-permute-done | bytes 131104 | tf_op jit(solution)/shard_map/ppermute | solution.py:269
  13.1 0.1 broadcast_in_dim.13.owner
  13.2 0.1 merge.2.sent.before
  13.3 1.1 %collective-permute-start.1 = (f32[256,256]{1,0:T(8,128)S(1)}, f32[256,256]{1,0:T(8,128)S(1)}, u32[]{:S(2)}, u32[]{:S(2)}) collective-permute-start(f32[256,256]{1,0:T(8,128)S(1)} %merge.2.sent.before), channel_id=1, source_target_pairs={{0,16},{1,9},{2,18},{3,11},{4,20},{5,13},{6,22},{7,15},{8,24},{9,1... | collective-permute-start | bytes 786440 | tf_op jit(solution)/shard_map/ppermute | solution.py:328
  14.4 0.5 %collective-permute-start.6 = (f32[128,256]{1,0:T(8,128)S(1)}, f32[128,256]{1,0:T(8,128)S(1)}, u32[]{:S(2)}, u32[]{:S(2)}) collective-permute-start(f32[128,256]{1,0:T(8,128)S(1)} %collective-permute-done.2.refs_3_.refs_1_), channel_id=1, source_target_pairs={{0,1},{1,0},{2,3},{3,2},{4,5},{5,4},{6,7},{7,6},{8,9},{9,8},{10,11... | collective-permute-start | bytes 393224 | tf_op jit(solution)/shard_map/ppermute | solution.py:273
  15.0 4.8 %collective-permute-done.3.refs_4_.refs_2_ = f32[128,256]{1,0:T(8,128)S(1)} collective-permute-done((f32[128,256]{1,0:T(8,128)S(1)}, f32[128,256]{1,0:T(8,128)S(1)}, u32[]{:S(2)}, u32[]{:S(2)}) %collective-permute-start.3) | collective-permute-done | bytes 131104 | tf_op jit(solution)/shard_map/ppermute | solution.py:269
  20.0 1.2 %collective-permute-done.7.refs_8_.refs_6_ = f32[128,256]{1,0:T(8,128)S(1)} collective-permute-done((f32[128,256]{1,0:T(8,128)S(1)}, f32[128,256]{1,0:T(8,128)S(1)}, u32[]{:S(2)}, u32[]{:S(2)}) %collective-permute-start.7) | collective-permute-done | bytes 131104 | tf_op jit(solution)/shard_map/ppermute | solution.py:273
  21.2 1.3 %solve.1 = (f32[256,256]{1,0:T(8,128)S(1)}, f32[256,256]{1,0:T(8,128)S(1)}, f32[256,256]{1,0:T(8,128)S(1)}) custom-call(f32[1024,256]{1,0:T(8,128)S(1)} %get-tuple-element.19.matrix, s32[2,256]{1,0:T(2,128)S(1)} %copy-done.1, f32[2,256,256]{2,1,0:T(8,128)S(1)} %copy-done, s32[256,256]{1,0:T(8,128)S(1)} %broadcast_in_dim.13.owner, ...), custom_call_target="tpu_custom_call" | custom-call | tf_op jit(solution)/shard_map/solve/pallas_call | solution.py:306
  22.5 1.0 %collective-permute-start.14 = (f32[256,256]{1,0:T(8,128)S(1)}, f32[256,256]{1,0:T(8,128)S(1)}, u32[]{:S(2)}, u32[]{:S(2)}) collective-permute-start(f32[256,256]{1,0:T(8,128)S(1)} %get-tuple-element.30.before.sent), channel_id=1, source_target_pairs={{0,8},{1,17},{2,10},{3,19},{4,12},{5,21},{6,14},{7,23},{8,0},{9,25... | collective-permute-start | bytes 786440 | tf_op jit(solution)/shard_map/ppermute | solution.py:328
  23.5 3.0 %collective-permute-start.10 = (f32[128,256]{1,0:T(8,128)S(1)}, f32[128,256]{1,0:T(8,128)S(1)}, u32[]{:S(2)}, u32[]{:S(2)}) collective-permute-start(f32[128,256]{1,0:T(8,128)S(1)} %release.3), channel_id=1, source_target_pairs={{0,4},{1,5},{2,6},{3,7},{4,0},{5,1},{6,2},{7,3},{8,12},{9,13},{10,... | collective-permute-start | bytes 393224 | tf_op jit(solution)/shard_map/ppermute | solution.py:269
  26.5 2.6 %collective-permute-done.12.refs_4_ = f32[256,256]{1,0:T(8,128)S(1)} collective-permute-done((f32[256,256]{1,0:T(8,128)S(1)}, f32[256,256]{1,0:T(8,128)S(1)}, u32[]{:S(2)}, u32[]{:S(2)}) %collective-permute-start.12) | collective-permute-done | bytes 262176 | tf_op jit(solution)/shard_map/ppermute | solution.py:291
  29.1 0.1 broadcast_in_dim.15.owner
  29.3 0.7 %collective-permute-start.15 = (f32[256,256]{1,0:T(8,128)S(1)}, f32[256,256]{1,0:T(8,128)S(1)}, u32[]{:S(2)}, u32[]{:S(2)}) collective-permute-start(f32[256,256]{1,0:T(8,128)S(1)} %merge.3.sent), channel_id=1, source_target_pairs={{0,16},{1,9},{2,18},{3,11},{4,20},{5,13},{6,22},{7,15},{8,24},{9,1... | collective-permute-start | bytes 786440 | tf_op jit(solution)/shard_map/ppermute | solution.py:328
  30.1 3.7 %collective-permute-done.10.refs_2_ = f32[128,256]{1,0:T(8,128)S(1)} collective-permute-done((f32[128,256]{1,0:T(8,128)S(1)}, f32[128,256]{1,0:T(8,128)S(1)}, u32[]{:S(2)}, u32[]{:S(2)}) %collective-permute-start.10) | collective-permute-done | bytes 131104 | tf_op jit(solution)/shard_map/ppermute | solution.py:269
  33.8 1.1 %update.1 = (f32[1024,256]{1,0:T(8,128)S(1)}, f32[256,256]{1,0:T(8,128)S(1)}) custom-call(f32[1024,256]{1,0:T(8,128)S(1)} %get-tuple-element.20.base, s32[2,256]{1,0:T(2,128)S(1)} %copy-done.1, f32[256,256]{1,0:T(8,128)S(1)} %get-tuple-element.25.upper_in, f32[256,256]{1,0:T(8,128)S(1)} %get-tuple-element.26.displaced_in, ...), custom_call_target="tpu_custom_call" | custom-call | tf_op jit(solution)/shard_map/update/pallas_call | solution.py:306
  34.9 0.2 collective-permute-done.11.refs_3_
  35.1 0.3 halve.1
  35.4 0.3 collective-permute-done.15.refs_1_
  35.8 1.9 %finish.1 = f32[1024,256]{1,0:T(8,128)} custom-call(f32[1024,256]{1,0:T(8,128)S(1)} %get-tuple-element.27.base, s32[2,256]{1,0:T(2,128)S(1)} %copy-done.1, f32[2,256,256]{2,1,0:T(8,128)S(1)} %copy-done, s32[256,256]{1,0:T(8,128)S(1)} %broadcast_in_dim.15.owner, f32[256,256]{1,0:T(8,128)S(1)} %get-tuple-element.28.top, ...), custom_call_target="tpu_custom_call" | custom-call | tf_op jit(solution)/shard_map/finish/pallas_call | solution.py:306
  (27 shorter events, 0.3 us)
Async XLA Ops:
  2.0 11.1 %collective-permute-start = (f32[256,256]{1,0:T(8,128)S(1)}, f32[256,256]{1,0:T(8,128)S(1)}, u32[]{:S(2)}, u32[]{:S(2)}) collective-permute-start(f32[256,256]{1,0:T(8,128)S(1)} %get-tuple-element.23.sent.before), channel_id=1, source_target_pairs={{0,8},{1,17},{2,10},{3,19},{4,12},{5,21},{6,14},{7,23},{8,0},{9,25... | collective-permute-start | bytes 786440 | tf_op jit(solution)/shard_map/ppermute | solution.py:328
  5.0 8.1 %collective-permute-start.2 = (f32[128,256]{1,0:T(8,128)S(1)}, f32[128,256]{1,0:T(8,128)S(1)}, u32[]{:S(2)}, u32[]{:S(2)}) collective-permute-start(f32[128,256]{1,0:T(8,128)S(1)} %get-tuple-element.24.panel.refs_2_.refs_0_), channel_id=1, source_target_pairs={{0,2},{1,3},{2,4},{3,5},{4,6},{5,7},{6,0},{7,1},{8,10},{9,11},{10,... | collective-permute-start | bytes 393224 | tf_op jit(solution)/shard_map/ppermute | solution.py:269
  6.5 2.3 %copy-start.1 = (s32[2,256]{1,0:T(2,128)S(1)}, s32[2,256]{1,0:T(2,128)}, u32[]{:S(2)}) copy-start(s32[2,256]{1,0:T(2,128)} %pivots.9) | copy-start | bytes 6148
  6.6 7.9 %collective-permute-start.4 = (f32[128,256]{1,0:T(8,128)S(1)}, f32[128,256]{1,0:T(8,128)S(1)}, u32[]{:S(2)}, u32[]{:S(2)}) collective-permute-start(f32[128,256]{1,0:T(8,128)S(1)} %release.2), channel_id=1, source_target_pairs={{0,6},{1,7},{2,0},{3,1},{4,2},{5,3},{6,4},{7,5},{8,14},{9,15},{10,... | collective-permute-start | bytes 393224 | tf_op jit(solution)/shard_map/ppermute | solution.py:269
  8.9 6.1 %collective-permute-start.9 = (f32[128,256]{1,0:T(8,128)S(1)}, f32[128,256]{1,0:T(8,128)S(1)}, u32[]{:S(2)}, u32[]{:S(2)}) collective-permute-start(f32[128,256]{1,0:T(8,128)S(1)} %get-tuple-element.29.panel.own.refs_0_), channel_id=1, source_target_pairs={{0,1},{1,0},{2,3},{3,2},{4,5},{5,4},{6,7},{7,6},{8,9},{9,8},{10,11... | collective-permute-start | bytes 393224 | tf_op jit(solution)/shard_map/ppermute | solution.py:273
  13.1 6.8 %collective-permute-start.3 = (f32[128,256]{1,0:T(8,128)S(1)}, f32[128,256]{1,0:T(8,128)S(1)}, u32[]{:S(2)}, u32[]{:S(2)}) collective-permute-start(f32[128,256]{1,0:T(8,128)S(1)} %collective-permute-done.2.refs_3_.refs_1_), channel_id=1, source_target_pairs={{0,2},{1,3},{2,4},{3,5},{4,6},{5,7},{6,0},{7,1},{8,10},{9,11},{10,... | collective-permute-start | bytes 393224 | tf_op jit(solution)/shard_map/ppermute | solution.py:269
  13.3 7.9 %copy-start = (f32[2,256,256]{2,1,0:T(8,128)S(1)}, f32[2,256,256]{2,1,0:T(8,128)}, u32[]{:S(2)}) copy-start(f32[2,256,256]{2,1,0:T(8,128)} %inverse.3) | copy-start | bytes 1572868
  13.3 7.9 %collective-permute-start.1 = (f32[256,256]{1,0:T(8,128)S(1)}, f32[256,256]{1,0:T(8,128)S(1)}, u32[]{:S(2)}, u32[]{:S(2)}) collective-permute-start(f32[256,256]{1,0:T(8,128)S(1)} %merge.2.sent.before), channel_id=1, source_target_pairs={{0,16},{1,9},{2,18},{3,11},{4,20},{5,13},{6,22},{7,15},{8,24},{9,1... | collective-permute-start | bytes 786440 | tf_op jit(solution)/shard_map/ppermute | solution.py:328
  14.4 5.5 %collective-permute-start.5 = (f32[128,256]{1,0:T(8,128)S(1)}, f32[128,256]{1,0:T(8,128)S(1)}, u32[]{:S(2)}, u32[]{:S(2)}) collective-permute-start(f32[128,256]{1,0:T(8,128)S(1)} %get-tuple-element.24.panel.refs_2_.refs_0_), channel_id=1, source_target_pairs={{0,1},{1,0},{2,3},{3,2},{4,5},{5,4},{6,7},{7,6},{8,9},{9,8},{10,11... | collective-permute-start | bytes 393224 | tf_op jit(solution)/shard_map/ppermute | solution.py:273
  14.4 5.5 %collective-permute-start.6 = (f32[128,256]{1,0:T(8,128)S(1)}, f32[128,256]{1,0:T(8,128)S(1)}, u32[]{:S(2)}, u32[]{:S(2)}) collective-permute-start(f32[128,256]{1,0:T(8,128)S(1)} %collective-permute-done.2.refs_3_.refs_1_), channel_id=1, source_target_pairs={{0,1},{1,0},{2,3},{3,2},{4,5},{5,4},{6,7},{7,6},{8,9},{9,8},{10,11... | collective-permute-start | bytes 393224 | tf_op jit(solution)/shard_map/ppermute | solution.py:273
  14.9 5.0 %collective-permute-start.8 = (f32[128,256]{1,0:T(8,128)S(1)}, f32[128,256]{1,0:T(8,128)S(1)}, u32[]{:S(2)}, u32[]{:S(2)}) collective-permute-start(f32[128,256]{1,0:T(8,128)S(1)} %collective-permute-done.4.refs_5_.refs_3_), channel_id=1, source_target_pairs={{0,1},{1,0},{2,3},{3,2},{4,5},{5,4},{6,7},{7,6},{8,9},{9,8},{10,11... | collective-permute-start | bytes 393224 | tf_op jit(solution)/shard_map/ppermute | solution.py:273
  19.9 1.3 %collective-permute-start.7 = (f32[128,256]{1,0:T(8,128)S(1)}, f32[128,256]{1,0:T(8,128)S(1)}, u32[]{:S(2)}, u32[]{:S(2)}) collective-permute-start(f32[128,256]{1,0:T(8,128)S(1)} %collective-permute-done.3.refs_4_.refs_2_), channel_id=1, source_target_pairs={{0,1},{1,0},{2,3},{3,2},{4,5},{5,4},{6,7},{7,6},{8,9},{9,8},{10,11... | collective-permute-start | bytes 393224 | tf_op jit(solution)/shard_map/ppermute | solution.py:273
  19.9 9.2 %collective-permute-start.12 = (f32[256,256]{1,0:T(8,128)S(1)}, f32[256,256]{1,0:T(8,128)S(1)}, u32[]{:S(2)}, u32[]{:S(2)}) collective-permute-start(f32[256,256]{1,0:T(8,128)S(1)} %pack.1), channel_id=1, source_target_pairs={{0,2},{1,7},{2,4},{3,1},{4,6},{5,3},{6,0},{7,5},{8,10},{9,15},{10,... | collective-permute-start | bytes 786440 | tf_op jit(solution)/shard_map/ppermute | solution.py:291
  22.5 6.6 %collective-permute-start.14 = (f32[256,256]{1,0:T(8,128)S(1)}, f32[256,256]{1,0:T(8,128)S(1)}, u32[]{:S(2)}, u32[]{:S(2)}) collective-permute-start(f32[256,256]{1,0:T(8,128)S(1)} %get-tuple-element.30.before.sent), channel_id=1, source_target_pairs={{0,8},{1,17},{2,10},{3,19},{4,12},{5,21},{6,14},{7,23},{8,0},{9,25... | collective-permute-start | bytes 786440 | tf_op jit(solution)/shard_map/ppermute | solution.py:328
  23.5 10.2 %collective-permute-start.10 = (f32[128,256]{1,0:T(8,128)S(1)}, f32[128,256]{1,0:T(8,128)S(1)}, u32[]{:S(2)}, u32[]{:S(2)}) collective-permute-start(f32[128,256]{1,0:T(8,128)S(1)} %release.3), channel_id=1, source_target_pairs={{0,4},{1,5},{2,6},{3,7},{4,0},{5,1},{6,2},{7,3},{8,12},{9,13},{10,... | collective-permute-start | bytes 393224 | tf_op jit(solution)/shard_map/ppermute | solution.py:269
  29.1 5.8 %collective-permute-start.13 = (f32[256,256]{1,0:T(8,128)S(1)}, f32[256,256]{1,0:T(8,128)S(1)}, u32[]{:S(2)}, u32[]{:S(2)}) collective-permute-start(f32[256,256]{1,0:T(8,128)S(1)} %collective-permute-done.12.refs_4_), channel_id=1, source_target_pairs={{0,1},{1,0},{2,3},{3,2},{4,5},{5,4},{6,7},{7,6},{8,9},{9,8},{10,11... | collective-permute-start | bytes 786440 | tf_op jit(solution)/shard_map/ppermute | solution.py:273
  29.3 6.4 %collective-permute-start.15 = (f32[256,256]{1,0:T(8,128)S(1)}, f32[256,256]{1,0:T(8,128)S(1)}, u32[]{:S(2)}, u32[]{:S(2)}) collective-permute-start(f32[256,256]{1,0:T(8,128)S(1)} %merge.3.sent), channel_id=1, source_target_pairs={{0,16},{1,9},{2,18},{3,11},{4,20},{5,13},{6,22},{7,15},{8,24},{9,1... | collective-permute-start | bytes 786440 | tf_op jit(solution)/shard_map/ppermute | solution.py:328
  33.8 1.3 %collective-permute-start.11 = (f32[128,256]{1,0:T(8,128)S(1)}, f32[128,256]{1,0:T(8,128)S(1)}, u32[]{:S(2)}, u32[]{:S(2)}) collective-permute-start(f32[128,256]{1,0:T(8,128)S(1)} %collective-permute-done.10.refs_2_), channel_id=1, source_target_pairs={{0,1},{1,0},{2,3},{3,2},{4,5},{5,4},{6,7},{7,6},{8,9},{9,8},{10,11... | collective-permute-start | bytes 393224 | tf_op jit(solution)/shard_map/ppermute | solution.py:273

commit v6 on v5

--- a/solution.py
+++ b/solution.py
@@ -142,31 +142,45 @@
     return pl.multiple_of((lax.rem(chip + chips, chips) * 2 + core) * rows, rows)
 
 
+def rows_of(ref, index, count=1):
+    rows = ref.shape[0] // count
+    return ref.at[pl.ds(index * rows, rows), :]
+
+
 def ring_blocks(refs):
-    chips = len(refs) // 2
+    chips, rows = (len(refs) + 1) // 2, refs[0].shape[0]
+    mine, near, rest = refs[:chips], refs[chips], refs[chips + 1 :]
     chip, core = lax.axis_index("pcol") // 2, lax.rem(lax.axis_index("pcol"), 2)
     found = []
-    for position, ref in enumerate(refs):
-        side, distance = divmod(position, chips)
-        found.append((ref, place_of(chip - distance, 1 - core if side else core, chips, ref.shape[0])))
+    for order, distance in enumerate(ring_order(chips)):
+        found.append((mine[order], place_of(chip - distance, core, chips, rows)))
+        if order < 2:
+            ref = rows_of(near, order, 3)
+        else:
+            ref = rest[order - 2]
+        found.append((ref, place_of(chip - distance, 1 - core, chips, rows)))
     return found
 
 
 def pair_blocks(refs):
-    chips, rows = len(refs) - 2, refs[0].shape[0]
+    own, near, far, far_back, *pairs = refs
+    rows = own.shape[0]
+    chips = len(pairs) + 2
+    hops = len(pairs) // 2
     chip, core = lax.axis_index("pcol") // 2, lax.rem(lax.axis_index("pcol"), 2)
-    found = []
-    for position, ref in enumerate(refs[:4]):
-        side, far = position % 2, position // 2
-        found.append((ref, place_of(chip + far * (chips // 2), 1 - core if side else core, chips, rows)))
-    hops = chips // 2 - 1
-    for position, ref in enumerate(refs[4:]):
-        side, distance = divmod(position, hops)
-        along = (distance + 1) * (1 - 2 * core)
+    opposite = chip + chips // 2
+    found = [
+        (own, place_of(chip, core, chips, rows)),
+        (rows_of(near, 2, 3), place_of(chip, 1 - core, chips, rows)),
+        (far, place_of(opposite, core, chips, rows)),
+        (far_back, place_of(opposite, 1 - core, chips, rows)),
+    ]
+    for hop in range(hops):
+        along = (hop + 1) * (1 - 2 * core)
         for half in range(2):
-            owner = core if side == half else 1 - core
-            place = place_of(chip + along if side else chip - along, owner, chips, rows)
-            found.append((ref.at[pl.ds(half * rows, rows), :], place))
+            owner = core if half == 0 else 1 - core
+            found.append((rows_of(pairs[hop], half, 2), place_of(chip - along, owner, chips, rows)))
+            found.append((rows_of(pairs[hops + hop], half, 2), place_of(chip + along, 1 - owner, chips, rows)))
     return found
 
 
@@ -255,10 +269,22 @@
         copy.wait()
 
 
-def pack(own, other, before, out):
+def stack(*refs):
+    out = refs[-1]
+    start = 0
+    for ref in refs[:-1]:
+        out[start : start + ref.shape[0], :] = ref[...]
+        start += ref.shape[0]
+
+
+def pack(own, near, before, out):
     rows = own.shape[0]
     out[:rows, :] = own[...]
-    out[rows:, :] = other[...]
+    out[rows:, :] = near[2 * rows :, :]
+
+
+def ring_order(chips):
+    return [0] + list(range(1, chips // 2 + 1)) + list(range(chips - 1, chips // 2, -1))
 
 
 def release(panel, before, out):
@@ -273,24 +299,23 @@
     return lax.ppermute(block, "pcol", [(i, i ^ 1) for i in range(count)])
 
 
-def forwarded(up, down, count):
+def forwarded(block, down, count):
     chips = count // 2
-    own = [up] * chips
-    for distance in range(1, chips // 2 + 1):
-        own[distance] = shift(own[distance - 1], 1, count)
-    for distance in range(1, (chips - 1) // 2 + 1):
-        own[chips - distance] = shift(down if distance == 1 else own[chips - distance + 1], -1, count)
-    return own + [across(piece, count) for piece in own]
-
-
-def paired(own, other, pair, far, count):
-    chips = count // 2
+    own = [block]
+    for distance in ring_order(chips)[1:]:
+        if distance <= chips // 2:
+            own.append(shift(own[-1], 1, count))
+        else:
+            own.append(shift(down if distance == chips - 1 else own[-1], -1, count))
+    return own
+
+
+def passed(pair, count):
     onward = [(i, (i + (2 if i % 2 == 0 else -2)) % count) for i in range(count)]
-    passed = [pair]
-    for _ in range(chips // 2 - 1):
-        passed.append(lax.ppermute(passed[-1], "pcol", onward))
-    back = [across(piece, count) for piece in passed[1:]]
-    return [own, other, far, across(far, count)] + passed[1:] + back
+    pairs = [pair]
+    for _ in range(count // 4 - 1):
+        pairs.append(lax.ppermute(pairs[-1], "pcol", onward))
+    return pairs[1:]
 
 
 def per_device(mesh, matrix, l_panels, l_inverse, pivots):
@@ -344,22 +369,29 @@
     def after(panel, before):
         return call(release, "release", [panel, before], block, specs=[VMEM, ANY])
 
-    panels = [forwarded(own[0], after(own[0], slots), process_columns)]
+    def stacked(blocks):
+        rows = sum(piece.shape[0] for piece in blocks)
+        return call(stack, "stack", blocks, shape((rows, block.shape[1]), F32))
+
     base, ahead, places = call(
         prepare, "prepare", [matrix, pivots], [full, square, shape((width, width), jnp.int32)]
     )
-    sent, received = exchange(slots, 0, [places])
-    other = across(own[1], process_columns)
+    first = forwarded(own[0], after(own[0], places), process_columns)
+    near = across(stacked([*first[:2], own[1]]), process_columns)
+    first += [near] + [across(piece, process_columns) for piece in first[2:]]
+    sent, received = exchange(slots, 0, [near])
     two = shape((2 * block.shape[0], block.shape[1]), F32)
-    pair = call(pack, "pack", [own[1], other, sent], two, specs=[VMEM, VMEM, ANY])
-    operands = [matrix, pivots, l_inverse, owner[0], ahead, places, sent, *received, *panels[0]]
+    pair = call(pack, "pack", [own[1], near, sent], two, specs=[VMEM, VMEM, ANY])
+    operands = [matrix, pivots, l_inverse, owner[0], ahead, places, sent, *received, *first]
     upper, displaced, slots = call(functools.partial(solve, bits, 0), "solve", operands, [square] * 3)
     far = shift(after(own[1], slots), process_columns // 4, process_columns)
-    panels.append(paired(own[1], other, pair, far, process_columns))
+    pairs = passed(pair, process_columns)
+    second = [own[1], near, far, across(far, process_columns)]
+    second += pairs + [across(piece, process_columns) for piece in pairs]
     base, top = call(
         functools.partial(update, 0),
         "update",
-        [base, pivots, upper, displaced, *panels[0]],
+        [base, pivots, upper, displaced, *first],
         [full, square],
         scratch=halves,
     )
@@ -367,7 +399,7 @@
     high, low = call(
         functools.partial(halve, 1, rows_dev, width),
         "halve",
-        panels[1],
+        second,
         [shape((rows_dev, l_panels.shape[2]), BF16)] * 2,
     )
     return call(

time: 37.8 us -> 36.7 us (0.971)
  waiting for transfers between devices: 16.4 us -> 14.3 us
  starting transfers between devices: 13.4 us -> 14.3 us
    ppermute x4, waiting for transfers between devices: 12.1 us -> 7.32 us  [shift(): lax.ppermute(block, 'pcol', [(i, (i + 2 * distance) % count) for i in ran...]
    ppermute x4, starting transfers between devices: 5.85 us -> 7.28 us  [exchange(): received.append(lax.ppermute(sent, ('prow', 'pcol'), pairs))]
    ppermute x7 -> x5, waiting for transfers between devices: 1.42 us -> 2.51 us  [across(): return lax.ppermute(block, 'pcol', [(i, i ^ 1) for i in range(count)])]
    ppermute x4, waiting for transfers between devices: 0.34 us -> 1.16 us  [exchange(): received.append(lax.ppermute(sent, ('prow', 'pcol'), pairs))]
    ppermute x1, waiting for transfers between devices: 2.6 us -> 3.35 us  [passed(): pairs.append(lax.ppermute(pairs[-1], 'pcol', onward))]
    ppermute x4, starting transfers between devices: 6.87 us -> 6.27 us  [shift(): lax.ppermute(block, 'pcol', [(i, (i + 2 * distance) % count) for i in ran...]
    pallas_call x11 -> x12, Pallas kernels: 7.48 us -> 7.51 us  [call(): pl.pallas_call(kernel, out_shape=outs, in_specs=specs or [VMEM] * len(ope...]
  transfers between devices with their start and end apart: 16 -> 14, of which waited for: 7 -> 10; matrix products, arithmetic and copies ran while one was open for 1% -> 1% of each run, Pallas kernels for 10% -> 10%
where the time goes in v6:
time: 36.7 us; the launch traced here: 36.5 us
  starting transfers between devices  14.3 us (39%)
  waiting for transfers between devices  14.3 us (39%)
  Pallas kernels  7.51 us (20%)
    pallas_call x12, Pallas kernels, call(): pl.pallas_call(kernel, out_shape=outs, in_specs=specs or [VMEM] * len(ope...  7.51 us
    ppermute x4, waiting for transfers between devices, shift(): lax.ppermute(block, 'pcol', [(i, (i + 2 * distance) % count) for i in ran...  7.32 us
    ppermute x4, starting transfers between devices, exchange(): received.append(lax.ppermute(sent, ('prow', 'pcol'), pairs))  7.28 us
    ppermute x4, starting transfers between devices, shift(): lax.ppermute(block, 'pcol', [(i, (i + 2 * distance) % count) for i in ran...  6.27 us
    ppermute x1, waiting for transfers between devices, passed(): pairs.append(lax.ppermute(pairs[-1], 'pcol', onward))  3.35 us
    ppermute x5, waiting for transfers between devices, across(): return lax.ppermute(block, 'pcol', [(i, i ^ 1) for i in range(count)])  2.51 us
    ppermute x4, waiting for transfers between devices, exchange(): received.append(lax.ppermute(sent, ('prow', 'pcol'), pairs))  1.16 us
  transfers between devices with their start and end apart: 14, of which 10 were waited for; matrix products, arithmetic and copies ran while one was open for 1% of the time, Pallas kernels for 10%

profile of v6, /device:TPU:0, one launch (start us, length us, event | category | flops | bytes accessed | tf_op | source)
XLA Modules:
  0.0 36.5 jit_solution(6041414752606871142)
XLA Ops:
  0.0 2.0 %first_slots.1 = (f32[256,256]{1,0:T(8,128)S(1)}, f32[1024,256]{1,0:T(8,128)S(1)}, f32[128,256]{1,0:T(8,128)S(1)}, f32[128,256]{1,0:T(8,128)S(1)}) custom-call(f32[1024,256]{1,0:T(8,128)} %matrix.1, s32[2,256]{1,0:T(2,128)} %pivots.9, f32[2,128,256]{2,1,0:T(8,128)} %panels.1), custom_call_target="tpu_custom_call" | custom-call | tf_op jit(solution)/shard_map/first_slots/pallas_call | solution.py:331
  2.0 3.1 %collective-permute-start.1 = (f32[128,256]{1,0:T(8,128)S(1)}, f32[128,256]{1,0:T(8,128)S(1)}, u32[]{:S(2)}, u32[]{:S(2)}) collective-permute-start(f32[128,256]{1,0:T(8,128)S(1)} %get-tuple-element.24.refs_0_.panel.refs_2_), channel_id=1, source_target_pairs={{0,2},{1,3},{2,4},{3,5},{4,6},{5,7},{6,0},{7,1},{8,10},{9,11},{10,... | collective-permute-start | bytes 393224 | tf_op jit(solution)/shard_map/ppermute | solution.py:295
  5.1 1.5 %collective-permute-start = (f32[256,256]{1,0:T(8,128)S(1)}, f32[256,256]{1,0:T(8,128)S(1)}, u32[]{:S(2)}, u32[]{:S(2)}) collective-permute-start(f32[256,256]{1,0:T(8,128)S(1)} %get-tuple-element.23.sent), channel_id=1, source_target_pairs={{0,8},{1,17},{2,10},{3,19},{4,12},{5,21},{6,14},{7,23},{8,0},{9,25... | collective-permute-start | bytes 786440 | tf_op jit(solution)/shard_map/ppermute | solution.py:353
  6.5 0.7 %prepare.1 = (f32[1024,256]{1,0:T(8,128)S(1)}, f32[256,256]{1,0:T(8,128)S(1)}, s32[256,256]{1,0:T(8,128)S(1)}) custom-call(f32[1024,256]{1,0:T(8,128)S(1)} %get-tuple-element.19.matrix, s32[2,256]{1,0:T(2,128)S(1)} %copy-done.1), custom_call_target="tpu_custom_call" | custom-call | tf_op jit(solution)/shard_map/prepare/pallas_call | solution.py:331
  7.3 2.3 %collective-permute-start.5 = (f32[128,256]{1,0:T(8,128)S(1)}, f32[128,256]{1,0:T(8,128)S(1)}, u32[]{:S(2)}, u32[]{:S(2)}) collective-permute-start(f32[128,256]{1,0:T(8,128)S(1)} %release.2), channel_id=1, source_target_pairs={{0,6},{1,7},{2,0},{3,1},{4,2},{5,3},{6,4},{7,5},{8,14},{9,15},{10,... | collective-permute-start | bytes 393224 | tf_op jit(solution)/shard_map/ppermute | solution.py:295
  9.6 1.1 %collective-permute-done.1.refs_1_.refs_3_ = f32[128,256]{1,0:T(8,128)S(1)} collective-permute-done((f32[128,256]{1,0:T(8,128)S(1)}, f32[128,256]{1,0:T(8,128)S(1)}, u32[]{:S(2)}, u32[]{:S(2)}) %collective-permute-start.1) | collective-permute-done | bytes 131104 | tf_op jit(solution)/shard_map/ppermute | solution.py:295
  10.9 0.5 %collective-permute-done.received.refs_0_ = f32[256,256]{1,0:T(8,128)S(1)} collective-permute-done((f32[256,256]{1,0:T(8,128)S(1)}, f32[256,256]{1,0:T(8,128)S(1)}, u32[]{:S(2)}, u32[]{:S(2)}) %collective-permute-start) | collective-permute-done | bytes 262176 | tf_op jit(solution)/shard_map/ppermute | solution.py:353
  11.4 1.1 %collective-permute-done.2.refs_0_.refs_6_.refs_4_.near.refs_1_ = f32[384,256]{1,0:T(8,128)S(1)} collective-permute-done((f32[384,256]{1,0:T(8,128)S(1)}, f32[384,256]{1,0:T(8,128)S(1)}, u32[]{:S(2)}, u32[]{:S(2)}) %collective-permute-start.2) | collective-permute-done | bytes 393248 | tf_op jit(solution)/shard_map/ppermute | solution.py:299
  12.6 0.1 merge.2.sent.before
  12.7 1.8 %collective-permute-start.3 = (f32[256,256]{1,0:T(8,128)S(1)}, f32[256,256]{1,0:T(8,128)S(1)}, u32[]{:S(2)}, u32[]{:S(2)}) collective-permute-start(f32[256,256]{1,0:T(8,128)S(1)} %merge.2.sent.before), channel_id=1, source_target_pairs={{0,16},{1,9},{2,18},{3,11},{4,20},{5,13},{6,22},{7,15},{8,24},{9,1... | collective-permute-start | bytes 786440 | tf_op jit(solution)/shard_map/ppermute | solution.py:353
  14.5 4.1 %collective-permute-done.4.refs_4_.refs_2_ = f32[128,256]{1,0:T(8,128)S(1)} collective-permute-done((f32[128,256]{1,0:T(8,128)S(1)}, f32[128,256]{1,0:T(8,128)S(1)}, u32[]{:S(2)}, u32[]{:S(2)}) %collective-permute-start.4) | collective-permute-done | bytes 131104 | tf_op jit(solution)/shard_map/ppermute | solution.py:295
  18.7 1.2 %collective-permute-done.6.refs_7_.refs_5_ = f32[128,256]{1,0:T(8,128)S(1)} collective-permute-done((f32[128,256]{1,0:T(8,128)S(1)}, f32[128,256]{1,0:T(8,128)S(1)}, u32[]{:S(2)}, u32[]{:S(2)}) %collective-permute-start.6) | collective-permute-done | bytes 131104 | tf_op jit(solution)/shard_map/ppermute | solution.py:299
  19.9 1.3 %solve.1 = (f32[256,256]{1,0:T(8,128)S(1)}, f32[256,256]{1,0:T(8,128)S(1)}, f32[256,256]{1,0:T(8,128)S(1)}) custom-call(f32[1024,256]{1,0:T(8,128)S(1)} %get-tuple-element.19.matrix, s32[2,256]{1,0:T(2,128)S(1)} %copy-done.1, f32[2,256,256]{2,1,0:T(8,128)S(1)} %copy-done, s32[256,256]{1,0:T(8,128)S(1)} %broadcast_in_dim.13.owner, ...), custom_call_target="tpu_custom_call" | custom-call | tf_op jit(solution)/shard_map/solve/pallas_call | solution.py:331
  21.2 1.6 %collective-permute-start.12 = (f32[256,256]{1,0:T(8,128)S(1)}, f32[256,256]{1,0:T(8,128)S(1)}, u32[]{:S(2)}, u32[]{:S(2)}) collective-permute-start(f32[256,256]{1,0:T(8,128)S(1)} %get-tuple-element.30.before.sent), channel_id=1, source_target_pairs={{0,8},{1,17},{2,10},{3,19},{4,12},{5,21},{6,14},{7,23},{8,0},{9,25... | collective-permute-start | bytes 786440 | tf_op jit(solution)/shard_map/ppermute | solution.py:353
  22.8 0.8 %collective-permute-start.8 = (f32[128,256]{1,0:T(8,128)S(1)}, f32[128,256]{1,0:T(8,128)S(1)}, u32[]{:S(2)}, u32[]{:S(2)}) collective-permute-start(f32[128,256]{1,0:T(8,128)S(1)} %release.3), channel_id=1, source_target_pairs={{0,4},{1,5},{2,6},{3,7},{4,0},{5,1},{6,2},{7,3},{8,12},{9,13},{10,... | collective-permute-start | bytes 393224 | tf_op jit(solution)/shard_map/ppermute | solution.py:295
  23.6 3.3 %collective-permute-done.10.refs_4_ = f32[256,256]{1,0:T(8,128)S(1)} collective-permute-done((f32[256,256]{1,0:T(8,128)S(1)}, f32[256,256]{1,0:T(8,128)S(1)}, u32[]{:S(2)}, u32[]{:S(2)}) %collective-permute-start.10) | collective-permute-done | bytes 262176 | tf_op jit(solution)/shard_map/ppermute | solution.py:317
  27.0 0.6 %collective-permute-start.11 = (f32[256,256]{1,0:T(8,128)S(1)}, f32[256,256]{1,0:T(8,128)S(1)}, u32[]{:S(2)}, u32[]{:S(2)}) collective-permute-start(f32[256,256]{1,0:T(8,128)S(1)} %collective-permute-done.10.refs_4_), channel_id=1, source_target_pairs={{0,1},{1,0},{2,3},{3,2},{4,5},{5,4},{6,7},{7,6},{8,9},{9,8},{10,11... | collective-permute-start | bytes 786440 | tf_op jit(solution)/shard_map/ppermute | solution.py:299
  27.8 2.5 %collective-permute-start.13 = (f32[256,256]{1,0:T(8,128)S(1)}, f32[256,256]{1,0:T(8,128)S(1)}, u32[]{:S(2)}, u32[]{:S(2)}) collective-permute-start(f32[256,256]{1,0:T(8,128)S(1)} %merge.3.sent), channel_id=1, source_target_pairs={{0,16},{1,9},{2,18},{3,11},{4,20},{5,13},{6,22},{7,15},{8,24},{9,1... | collective-permute-start | bytes 786440 | tf_op jit(solution)/shard_map/ppermute | solution.py:353
  30.3 2.2 %collective-permute-done.8.refs_2_ = f32[128,256]{1,0:T(8,128)S(1)} collective-permute-done((f32[128,256]{1,0:T(8,128)S(1)}, f32[128,256]{1,0:T(8,128)S(1)}, u32[]{:S(2)}, u32[]{:S(2)}) %collective-permute-start.8) | collective-permute-done | bytes 131104 | tf_op jit(solution)/shard_map/ppermute | solution.py:295
  32.5 1.1 %update.1 = (f32[1024,256]{1,0:T(8,128)S(1)}, f32[256,256]{1,0:T(8,128)S(1)}) custom-call(f32[1024,256]{1,0:T(8,128)S(1)} %get-tuple-element.20.base, s32[2,256]{1,0:T(2,128)S(1)} %copy-done.1, f32[256,256]{1,0:T(8,128)S(1)} %get-tuple-element.26.upper_in, f32[256,256]{1,0:T(8,128)S(1)} %get-tuple-element.27.displaced_in, ...), custom_call_target="tpu_custom_call" | custom-call | tf_op jit(solution)/shard_map/update/pallas_call | solution.py:331
  33.6 0.2 collective-permute-done.9.refs_3_
  33.8 0.3 halve.1
  34.1 0.5 %collective-permute-done.13.refs_1_ = f32[256,256]{1,0:T(8,128)S(1)} collective-permute-done((f32[256,256]{1,0:T(8,128)S(1)}, f32[256,256]{1,0:T(8,128)S(1)}, u32[]{:S(2)}, u32[]{:S(2)}) %collective-permute-start.13) | collective-permute-done | bytes 262176 | tf_op jit(solution)/shard_map/ppermute | solution.py:353
  34.7 1.9 %finish.1 = f32[1024,256]{1,0:T(8,128)} custom-call(f32[1024,256]{1,0:T(8,128)S(1)} %get-tuple-element.28.base, s32[2,256]{1,0:T(2,128)S(1)} %copy-done.1, f32[2,256,256]{2,1,0:T(8,128)S(1)} %copy-done, s32[256,256]{1,0:T(8,128)S(1)} %broadcast_in_dim.15.owner, f32[256,256]{1,0:T(8,128)S(1)} %get-tuple-element.29.top, ...), custom_call_target="tpu_custom_call" | custom-call | tf_op jit(solution)/shard_map/finish/pallas_call | solution.py:331
  (24 shorter events, 0.7 us)
Async XLA Ops:
  2.0 4.6 %copy-start.1 = (s32[2,256]{1,0:T(2,128)S(1)}, s32[2,256]{1,0:T(2,128)}, u32[]{:S(2)}) copy-start(s32[2,256]{1,0:T(2,128)} %pivots.9) | copy-start | bytes 6148
  2.0 8.7 %collective-permute-start.1 = (f32[128,256]{1,0:T(8,128)S(1)}, f32[128,256]{1,0:T(8,128)S(1)}, u32[]{:S(2)}, u32[]{:S(2)}) collective-permute-start(f32[128,256]{1,0:T(8,128)S(1)} %get-tuple-element.24.refs_0_.panel.refs_2_), channel_id=1, source_target_pairs={{0,2},{1,3},{2,4},{3,5},{4,6},{5,7},{6,0},{7,1},{8,10},{9,11},{10,... | collective-permute-start | bytes 393224 | tf_op jit(solution)/shard_map/ppermute | solution.py:295
  5.1 6.4 %collective-permute-start = (f32[256,256]{1,0:T(8,128)S(1)}, f32[256,256]{1,0:T(8,128)S(1)}, u32[]{:S(2)}, u32[]{:S(2)}) collective-permute-start(f32[256,256]{1,0:T(8,128)S(1)} %get-tuple-element.23.sent), channel_id=1, source_target_pairs={{0,8},{1,17},{2,10},{3,19},{4,12},{5,21},{6,14},{7,23},{8,0},{9,25... | collective-permute-start | bytes 786440 | tf_op jit(solution)/shard_map/ppermute | solution.py:353
  7.3 7.2 %collective-permute-start.5 = (f32[128,256]{1,0:T(8,128)S(1)}, f32[128,256]{1,0:T(8,128)S(1)}, u32[]{:S(2)}, u32[]{:S(2)}) collective-permute-start(f32[128,256]{1,0:T(8,128)S(1)} %release.2), channel_id=1, source_target_pairs={{0,6},{1,7},{2,0},{3,1},{4,2},{5,3},{6,4},{7,5},{8,14},{9,15},{10,... | collective-permute-start | bytes 393224 | tf_op jit(solution)/shard_map/ppermute | solution.py:295
  10.7 1.8 %collective-permute-start.2 = (f32[384,256]{1,0:T(8,128)S(1)}, f32[384,256]{1,0:T(8,128)S(1)}, u32[]{:S(2)}, u32[]{:S(2)}) collective-permute-start(f32[384,256]{1,0:T(8,128)S(1)} %stack.1), channel_id=1, source_target_pairs={{0,1},{1,0},{2,3},{3,2},{4,5},{5,4},{6,7},{7,6},{8,9},{9,8},{10,11... | collective-permute-start | bytes 1179656 | tf_op jit(solution)/shard_map/ppermute | solution.py:299
  10.8 7.7 %collective-permute-start.4 = (f32[128,256]{1,0:T(8,128)S(1)}, f32[128,256]{1,0:T(8,128)S(1)}, u32[]{:S(2)}, u32[]{:S(2)}) collective-permute-start(f32[128,256]{1,0:T(8,128)S(1)} %collective-permute-done.1.refs_1_.refs_3_), channel_id=1, source_target_pairs={{0,2},{1,3},{2,4},{3,5},{4,6},{5,7},{6,0},{7,1},{8,10},{9,11},{10,... | collective-permute-start | bytes 393224 | tf_op jit(solution)/shard_map/ppermute | solution.py:295
  12.7 7.2 %copy-start = (f32[2,256,256]{2,1,0:T(8,128)S(1)}, f32[2,256,256]{2,1,0:T(8,128)}, u32[]{:S(2)}) copy-start(f32[2,256,256]{2,1,0:T(8,128)} %inverse.3) | copy-start | bytes 1572868
  12.7 7.2 %collective-permute-start.3 = (f32[256,256]{1,0:T(8,128)S(1)}, f32[256,256]{1,0:T(8,128)S(1)}, u32[]{:S(2)}, u32[]{:S(2)}) collective-permute-start(f32[256,256]{1,0:T(8,128)S(1)} %merge.2.sent.before), channel_id=1, source_target_pairs={{0,16},{1,9},{2,18},{3,11},{4,20},{5,13},{6,22},{7,15},{8,24},{9,1... | collective-permute-start | bytes 786440 | tf_op jit(solution)/shard_map/ppermute | solution.py:353
  14.5 4.2 %collective-permute-start.7 = (f32[128,256]{1,0:T(8,128)S(1)}, f32[128,256]{1,0:T(8,128)S(1)}, u32[]{:S(2)}, u32[]{:S(2)}) collective-permute-start(f32[128,256]{1,0:T(8,128)S(1)} %collective-permute-done.5.refs_5_.refs_3_), channel_id=1, source_target_pairs={{0,1},{1,0},{2,3},{3,2},{4,5},{5,4},{6,7},{7,6},{8,9},{9,8},{10,11... | collective-permute-start | bytes 393224 | tf_op jit(solution)/shard_map/ppermute | solution.py:299
  18.6 1.3 %collective-permute-start.6 = (f32[128,256]{1,0:T(8,128)S(1)}, f32[128,256]{1,0:T(8,128)S(1)}, u32[]{:S(2)}, u32[]{:S(2)}) collective-permute-start(f32[128,256]{1,0:T(8,128)S(1)} %collective-permute-done.4.refs_4_.refs_2_), channel_id=1, source_target_pairs={{0,1},{1,0},{2,3},{3,2},{4,5},{5,4},{6,7},{7,6},{8,9},{9,8},{10,11... | collective-permute-start | bytes 393224 | tf_op jit(solution)/shard_map/ppermute | solution.py:299
  18.6 8.4 %collective-permute-start.10 = (f32[256,256]{1,0:T(8,128)S(1)}, f32[256,256]{1,0:T(8,128)S(1)}, u32[]{:S(2)}, u32[]{:S(2)}) collective-permute-start(f32[256,256]{1,0:T(8,128)S(1)} %pack.1), channel_id=1, source_target_pairs={{0,2},{1,7},{2,4},{3,1},{4,6},{5,3},{6,0},{7,5},{8,10},{9,15},{10,... | collective-permute-start | bytes 786440 | tf_op jit(solution)/shard_map/ppermute | solution.py:317
  21.2 6.4 %collective-permute-start.12 = (f32[256,256]{1,0:T(8,128)S(1)}, f32[256,256]{1,0:T(8,128)S(1)}, u32[]{:S(2)}, u32[]{:S(2)}) collective-permute-start(f32[256,256]{1,0:T(8,128)S(1)} %get-tuple-element.30.before.sent), channel_id=1, source_target_pairs={{0,8},{1,17},{2,10},{3,19},{4,12},{5,21},{6,14},{7,23},{8,0},{9,25... | collective-permute-start | bytes 786440 | tf_op jit(solution)/shard_map/ppermute | solution.py:353
  22.8 9.7 %collective-permute-start.8 = (f32[128,256]{1,0:T(8,128)S(1)}, f32[128,256]{1,0:T(8,128)S(1)}, u32[]{:S(2)}, u32[]{:S(2)}) collective-permute-start(f32[128,256]{1,0:T(8,128)S(1)} %release.3), channel_id=1, source_target_pairs={{0,4},{1,5},{2,6},{3,7},{4,0},{5,1},{6,2},{7,3},{8,12},{9,13},{10,... | collective-permute-start | bytes 393224 | tf_op jit(solution)/shard_map/ppermute | solution.py:295
  27.0 6.9 %collective-permute-start.11 = (f32[256,256]{1,0:T(8,128)S(1)}, f32[256,256]{1,0:T(8,128)S(1)}, u32[]{:S(2)}, u32[]{:S(2)}) collective-permute-start(f32[256,256]{1,0:T(8,128)S(1)} %collective-permute-done.10.refs_4_), channel_id=1, source_target_pairs={{0,1},{1,0},{2,3},{3,2},{4,5},{5,4},{6,7},{7,6},{8,9},{9,8},{10,11... | collective-permute-start | bytes 786440 | tf_op jit(solution)/shard_map/ppermute | solution.py:299
  27.8 6.8 %collective-permute-start.13 = (f32[256,256]{1,0:T(8,128)S(1)}, f32[256,256]{1,0:T(8,128)S(1)}, u32[]{:S(2)}, u32[]{:S(2)}) collective-permute-start(f32[256,256]{1,0:T(8,128)S(1)} %merge.3.sent), channel_id=1, source_target_pairs={{0,16},{1,9},{2,18},{3,11},{4,20},{5,13},{6,22},{7,15},{8,24},{9,1... | collective-permute-start | bytes 786440 | tf_op jit(solution)/shard_map/ppermute | solution.py:353
  32.5 1.3 %collective-permute-start.9 = (f32[128,256]{1,0:T(8,128)S(1)}, f32[128,256]{1,0:T(8,128)S(1)}, u32[]{:S(2)}, u32[]{:S(2)}) collective-permute-start(f32[128,256]{1,0:T(8,128)S(1)} %collective-permute-done.8.refs_2_), channel_id=1, source_target_pairs={{0,1},{1,0},{2,3},{3,2},{4,5},{5,4},{6,7},{7,6},{8,9},{9,8},{10,11... | collective-permute-start | bytes 393224 | tf_op jit(solution)/shard_map/ppermute | solution.py:299

commit v7 on v6

--- a/solution.py
+++ b/solution.py
@@ -147,22 +147,7 @@
     return ref.at[pl.ds(index * rows, rows), :]
 
 
-def ring_blocks(refs):
-    chips, rows = (len(refs) + 1) // 2, refs[0].shape[0]
-    mine, near, rest = refs[:chips], refs[chips], refs[chips + 1 :]
-    chip, core = lax.axis_index("pcol") // 2, lax.rem(lax.axis_index("pcol"), 2)
-    found = []
-    for order, distance in enumerate(ring_order(chips)):
-        found.append((mine[order], place_of(chip - distance, core, chips, rows)))
-        if order < 2:
-            ref = rows_of(near, order, 3)
-        else:
-            ref = rest[order - 2]
-        found.append((ref, place_of(chip - distance, 1 - core, chips, rows)))
-    return found
-
-
-def pair_blocks(refs):
+def panel_blocks(step, steps, refs):
     own, near, far, far_back, *pairs = refs
     rows = own.shape[0]
     chips = len(pairs) + 2
@@ -171,7 +156,7 @@
     opposite = chip + chips // 2
     found = [
         (own, place_of(chip, core, chips, rows)),
-        (rows_of(near, 2, 3), place_of(chip, 1 - core, chips, rows)),
+        (rows_of(near, step, steps), place_of(chip, 1 - core, chips, rows)),
         (far, place_of(opposite, core, chips, rows)),
         (far_back, place_of(opposite, 1 - core, chips, rows)),
     ]
@@ -196,7 +181,7 @@
     displaced = displaced_rows(bits, received, matrix[step * width : (step + 1) * width, :])
     displaced_out[...] = displaced
     high = low = None
-    for block, start in ring_blocks(blocks):
+    for block, start in panel_blocks(step, pivots.shape[0], blocks):
         rows = block.shape[0]
         local = places[:, :rows] - start
         gather = one_hot(local, iota((width, rows), 1))
@@ -219,15 +204,15 @@
         low[pl.ds(start, rows), :] = block_low
 
 
-def halve(step, rows_dev, width, *refs):
-    assemble(step, pair_blocks(refs[:-2]), rows_dev, width, refs[-2], refs[-1])
+def halve(step, steps, rows_dev, width, *refs):
+    assemble(step, panel_blocks(step, steps, refs[:-2]), rows_dev, width, refs[-2], refs[-1])
 
 
 def update(step, base, pivots, upper_in, displaced_in, *refs):
     blocks, (out, top_out, high, low) = refs[:-4], refs[-4:]
     rows_dev = base.shape[0]
     width = upper_in.shape[0]
-    assemble(step, ring_blocks(blocks), rows_dev, width, high, low)
+    assemble(step, panel_blocks(step, pivots.shape[0], blocks), rows_dev, width, high, low)
     offset = local_rows(pivots, step, rows_dev)
     later = local_rows(pivots, step + 1, rows_dev)
     upper = split(upper_in[...])
@@ -269,22 +254,10 @@
         copy.wait()
 
 
-def stack(*refs):
-    out = refs[-1]
-    start = 0
-    for ref in refs[:-1]:
-        out[start : start + ref.shape[0], :] = ref[...]
-        start += ref.shape[0]
-
-
-def pack(own, near, before, out):
+def pack(step, own, near, before, out):
     rows = own.shape[0]
     out[:rows, :] = own[...]
-    out[rows:, :] = near[2 * rows :, :]
-
-
-def ring_order(chips):
-    return [0] + list(range(1, chips // 2 + 1)) + list(range(chips - 1, chips // 2, -1))
+    out[rows:, :] = near[step * rows : (step + 1) * rows, :]
 
 
 def release(panel, before, out):
@@ -297,17 +270,6 @@
 
 def across(block, count):
     return lax.ppermute(block, "pcol", [(i, i ^ 1) for i in range(count)])
-
-
-def forwarded(block, down, count):
-    chips = count // 2
-    own = [block]
-    for distance in ring_order(chips)[1:]:
-        if distance <= chips // 2:
-            own.append(shift(own[-1], 1, count))
-        else:
-            own.append(shift(down if distance == chips - 1 else own[-1], -1, count))
-    return own
 
 
 def passed(pair, count):
@@ -369,25 +331,26 @@
     def after(panel, before):
         return call(release, "release", [panel, before], block, specs=[VMEM, ANY])
 
-    def stacked(blocks):
-        rows = sum(piece.shape[0] for piece in blocks)
-        return call(stack, "stack", blocks, shape((rows, block.shape[1]), F32))
+    near = across(l_panels.reshape(-1, l_panels.shape[2]), process_columns)
+
+    def gather(step, before_pair, before_far):
+        two = shape((2 * block.shape[0], block.shape[1]), F32)
+        specs = [VMEM, VMEM, ANY]
+        pair = call(functools.partial(pack, step), "pack", [own[step], near, before_pair], two, specs=specs)
+        far = shift(after(own[step], before_far), process_columns // 4, process_columns)
+        pairs = passed(pair, process_columns)
+        back = [across(piece, process_columns) for piece in pairs]
+        return [own[step], near, far, across(far, process_columns), *pairs, *back]
 
     base, ahead, places = call(
         prepare, "prepare", [matrix, pivots], [full, square, shape((width, width), jnp.int32)]
     )
-    first = forwarded(own[0], after(own[0], places), process_columns)
-    near = across(stacked([*first[:2], own[1]]), process_columns)
-    first += [near] + [across(piece, process_columns) for piece in first[2:]]
-    sent, received = exchange(slots, 0, [near])
-    two = shape((2 * block.shape[0], block.shape[1]), F32)
-    pair = call(pack, "pack", [own[1], near, sent], two, specs=[VMEM, VMEM, ANY])
+    later = call(release, "release", [slots, near], square, specs=[VMEM, ANY])
+    first = gather(0, later, own[1])
+    sent, received = exchange(later, 0, [places])
     operands = [matrix, pivots, l_inverse, owner[0], ahead, places, sent, *received, *first]
     upper, displaced, slots = call(functools.partial(solve, bits, 0), "solve", operands, [square] * 3)
-    far = shift(after(own[1], slots), process_columns // 4, process_columns)
-    pairs = passed(pair, process_columns)
-    second = [own[1], near, far, across(far, process_columns)]
-    second += pairs + [across(piece, process_columns) for piece in pairs]
+    second = gather(1, sent, slots)
     base, top = call(
         functools.partial(update, 0),
         "update",
@@ -397,7 +360,7 @@
     )
     sent, received = exchange(slots, 1)
     high, low = call(
-        functools.partial(halve, 1, rows_dev, width),
+        functools.partial(halve, 1, steps, rows_dev, width),
         "halve",
         second,
         [shape((rows_dev, l_panels.shape[2]), BF16)] * 2,

time: 36.7 us -> 39.7 us (1.082)
  the two profiles are of different devices: /device:TPU:0 before, /device:TPU:20 now
where the time goes in v7:
time: 39.7 us; the launch traced here: 39.6 us
  waiting for transfers between devices  24.3 us (61%)
  Pallas kernels  7.5 us (19%)
  starting transfers between devices  7.42 us (19%)
    ppermute x2, waiting for transfers between devices, passed(): pairs.append(lax.ppermute(pairs[-1], 'pcol', onward))  17.1 us
    pallas_call x13, Pallas kernels, call(): pl.pallas_call(kernel, out_shape=outs, in_specs=specs or [VMEM] * len(ope...  7.5 us
    ppermute x4, waiting for transfers between devices, exchange(): received.append(lax.ppermute(sent, ('prow', 'pcol'), pairs))  6.27 us
    ppermute x4, starting transfers between devices, exchange(): received.append(lax.ppermute(sent, ('prow', 'pcol'), pairs))  3.82 us
    ppermute x2, starting transfers between devices, passed(): pairs.append(lax.ppermute(pairs[-1], 'pcol', onward))  1.87 us
    ppermute x5, starting transfers between devices, across(): return lax.ppermute(block, 'pcol', [(i, i ^ 1) for i in range(count)])  1.25 us
    ppermute x5, waiting for transfers between devices, across(): return lax.ppermute(block, 'pcol', [(i, i ^ 1) for i in range(count)])  0.95 us
  transfers between devices with their start and end apart: 13, of which 5 were waited for; matrix products, arithmetic and copies ran while one was open for 1% of the time, Pallas kernels for 14%

profile of v7, /device:TPU:20, one launch (start us, length us, event | category | flops | bytes accessed | tf_op | source)
XLA Modules:
  0.0 39.6 jit_solution(3974172964091645174)
XLA Ops:
  0.0 2.0 %first_slots.1 = (f32[256,256]{1,0:T(8,128)S(1)}, f32[1024,256]{1,0:T(8,128)S(1)}, f32[128,256]{1,0:T(8,128)S(1)}, f32[128,256]{1,0:T(8,128)S(1)}) custom-call(f32[1024,256]{1,0:T(8,128)} %matrix.1, s32[2,256]{1,0:T(2,128)} %pivots.9, f32[2,128,256]{2,1,0:T(8,128)} %panels.1), custom_call_target="tpu_custom_call" | custom-call | tf_op jit(solution)/shard_map/first_slots/pallas_call | solution.py:293
  2.0 0.4 %collective-permute-start.3 = (f32[128,256]{1,0:T(8,128)S(1)}, f32[128,256]{1,0:T(8,128)S(1)}, u32[]{:S(2)}, u32[]{:S(2)}) collective-permute-start(f32[128,256]{1,0:T(8,128)S(1)} %release.4), channel_id=1, source_target_pairs={{0,4},{1,5},{2,6},{3,7},{4,0},{5,1},{6,2},{7,3},{8,12},{9,13},{10,... | collective-permute-start | bytes 393224 | tf_op jit(solution)/shard_map/ppermute | solution.py:268
  2.4 1.6 %collective-permute-start.1 = (f32[256,256]{1,0:T(8,128)S(1)}, f32[256,256]{1,0:T(8,128)S(1)}, u32[]{:S(2)}, u32[]{:S(2)}) collective-permute-start(f32[256,256]{1,0:T(8,128)S(1)} %release.3.sent.before), channel_id=1, source_target_pairs={{0,8},{1,17},{2,10},{3,19},{4,12},{5,21},{6,14},{7,23},{8,0},{9,25... | collective-permute-start | bytes 786440 | tf_op jit(solution)/shard_map/ppermute | solution.py:315
  4.0 1.6 %collective-permute-start.5 = (f32[256,256]{1,0:T(8,128)S(1)}, f32[256,256]{1,0:T(8,128)S(1)}, u32[]{:S(2)}, u32[]{:S(2)}) collective-permute-start(f32[256,256]{1,0:T(8,128)S(1)} %pack.2), channel_id=1, source_target_pairs={{0,2},{1,7},{2,4},{3,1},{4,6},{5,3},{6,0},{7,5},{8,10},{9,15},{10,... | collective-permute-start | bytes 786440 | tf_op jit(solution)/shard_map/ppermute | solution.py:279
  5.6 0.7 %prepare.1 = (f32[1024,256]{1,0:T(8,128)S(1)}, f32[256,256]{1,0:T(8,128)S(1)}, s32[256,256]{1,0:T(8,128)S(1)}) custom-call(f32[1024,256]{1,0:T(8,128)S(1)} %get-tuple-element.19.matrix, s32[2,256]{1,0:T(2,128)S(1)} %copy-done.1), custom_call_target="tpu_custom_call" | custom-call | tf_op jit(solution)/shard_map/prepare/pallas_call | solution.py:293
  6.4 2.5 %collective-permute-done.1.received.refs_0_ = f32[256,256]{1,0:T(8,128)S(1)} collective-permute-done((f32[256,256]{1,0:T(8,128)S(1)}, f32[256,256]{1,0:T(8,128)S(1)}, u32[]{:S(2)}, u32[]{:S(2)}) %collective-permute-start.1) | collective-permute-done | bytes 262176 | tf_op jit(solution)/shard_map/ppermute | solution.py:315
  8.9 0.1 broadcast_in_dim.13.owner
  9.0 0.1 merge.2.sent.before
  9.1 0.3 collective-permute-start.2
  9.3 8.0 %collective-permute-done.5.refs_6_.refs_4_ = f32[256,256]{1,0:T(8,128)S(1)} collective-permute-done((f32[256,256]{1,0:T(8,128)S(1)}, f32[256,256]{1,0:T(8,128)S(1)}, u32[]{:S(2)}, u32[]{:S(2)}) %collective-permute-start.5) | collective-permute-done | bytes 262176 | tf_op jit(solution)/shard_map/ppermute | solution.py:279
  17.3 0.5 %collective-permute-start.4 = (f32[128,256]{1,0:T(8,128)S(1)}, f32[128,256]{1,0:T(8,128)S(1)}, u32[]{:S(2)}, u32[]{:S(2)}) collective-permute-start(f32[128,256]{1,0:T(8,128)S(1)} %collective-permute-done.3.refs_4_.refs_2_), channel_id=1, source_target_pairs={{0,1},{1,0},{2,3},{3,2},{4,5},{5,4},{6,7},{7,6},{8,9},{9,8},{10,11... | collective-permute-start | bytes 393224 | tf_op jit(solution)/shard_map/ppermute | solution.py:272
  17.9 0.2 collective-permute-start.9
  18.1 0.9 %collective-permute-done.4.refs_5_.refs_3_ = f32[128,256]{1,0:T(8,128)S(1)} collective-permute-done((f32[128,256]{1,0:T(8,128)S(1)}, f32[128,256]{1,0:T(8,128)S(1)}, u32[]{:S(2)}, u32[]{:S(2)}) %collective-permute-start.4) | collective-permute-done | bytes 131104 | tf_op jit(solution)/shard_map/ppermute | solution.py:272
  19.1 1.3 %solve.1 = (f32[256,256]{1,0:T(8,128)S(1)}, f32[256,256]{1,0:T(8,128)S(1)}, f32[256,256]{1,0:T(8,128)S(1)}) custom-call(f32[1024,256]{1,0:T(8,128)S(1)} %get-tuple-element.19.matrix, s32[2,256]{1,0:T(2,128)S(1)} %copy-done.1, f32[2,256,256]{2,1,0:T(8,128)S(1)} %copy-done, s32[256,256]{1,0:T(8,128)S(1)} %broadcast_in_dim.13.owner, ...), custom_call_target="tpu_custom_call" | custom-call | tf_op jit(solution)/shard_map/solve/pallas_call | solution.py:293
  20.4 1.6 %collective-permute-start.11 = (f32[256,256]{1,0:T(8,128)S(1)}, f32[256,256]{1,0:T(8,128)S(1)}, u32[]{:S(2)}, u32[]{:S(2)}) collective-permute-start(f32[256,256]{1,0:T(8,128)S(1)} %get-tuple-element.30.before.sent), channel_id=1, source_target_pairs={{0,8},{1,17},{2,10},{3,19},{4,12},{5,21},{6,14},{7,23},{8,0},{9,25... | collective-permute-start | bytes 786440 | tf_op jit(solution)/shard_map/ppermute | solution.py:315
  22.0 9.1 %collective-permute-done.9.refs_4_ = f32[256,256]{1,0:T(8,128)S(1)} collective-permute-done((f32[256,256]{1,0:T(8,128)S(1)}, f32[256,256]{1,0:T(8,128)S(1)}, u32[]{:S(2)}, u32[]{:S(2)}) %collective-permute-start.9) | collective-permute-done | bytes 262176 | tf_op jit(solution)/shard_map/ppermute | solution.py:279
  31.1 0.1 broadcast_in_dim.15.owner
  31.2 0.1 merge.3.sent
  31.3 0.5 %collective-permute-start.12 = (f32[256,256]{1,0:T(8,128)S(1)}, f32[256,256]{1,0:T(8,128)S(1)}, u32[]{:S(2)}, u32[]{:S(2)}) collective-permute-start(f32[256,256]{1,0:T(8,128)S(1)} %merge.3.sent), channel_id=1, source_target_pairs={{0,16},{1,9},{2,18},{3,11},{4,20},{5,13},{6,22},{7,15},{8,24},{9,1... | collective-permute-start | bytes 786440 | tf_op jit(solution)/shard_map/ppermute | solution.py:315
  31.7 0.7 %collective-permute-start.8 = (f32[128,256]{1,0:T(8,128)S(1)}, f32[128,256]{1,0:T(8,128)S(1)}, u32[]{:S(2)}, u32[]{:S(2)}) collective-permute-start(f32[128,256]{1,0:T(8,128)S(1)} %collective-permute-done.7.refs_2_), channel_id=1, source_target_pairs={{0,1},{1,0},{2,3},{3,2},{4,5},{5,4},{6,7},{7,6},{8,9},{9,8},{10,11... | collective-permute-start | bytes 393224 | tf_op jit(solution)/shard_map/ppermute | solution.py:272
  32.5 1.1 %update.1 = (f32[1024,256]{1,0:T(8,128)S(1)}, f32[256,256]{1,0:T(8,128)S(1)}) custom-call(f32[1024,256]{1,0:T(8,128)S(1)} %get-tuple-element.20.base, s32[2,256]{1,0:T(2,128)S(1)} %copy-done.1, f32[256,256]{1,0:T(8,128)S(1)} %get-tuple-element.26.upper_in, f32[256,256]{1,0:T(8,128)S(1)} %get-tuple-element.27.displaced_in, ...), custom_call_target="tpu_custom_call" | custom-call | tf_op jit(solution)/shard_map/update/pallas_call | solution.py:293
  33.6 0.3 halve.1
  33.9 3.8 %collective-permute-done.12.refs_1_ = f32[256,256]{1,0:T(8,128)S(1)} collective-permute-done((f32[256,256]{1,0:T(8,128)S(1)}, f32[256,256]{1,0:T(8,128)S(1)}, u32[]{:S(2)}, u32[]{:S(2)}) %collective-permute-start.12) | collective-permute-done | bytes 262176 | tf_op jit(solution)/shard_map/ppermute | solution.py:315
  37.7 1.9 %finish.1 = f32[1024,256]{1,0:T(8,128)} custom-call(f32[1024,256]{1,0:T(8,128)S(1)} %get-tuple-element.28.base, s32[2,256]{1,0:T(2,128)S(1)} %copy-done.1, f32[2,256,256]{2,1,0:T(8,128)S(1)} %copy-done, s32[256,256]{1,0:T(8,128)S(1)} %broadcast_in_dim.15.owner, f32[256,256]{1,0:T(8,128)S(1)} %get-tuple-element.29.top, ...), custom_call_target="tpu_custom_call" | custom-call | tf_op jit(solution)/shard_map/finish/pallas_call | solution.py:293
  (23 shorter events, 0.2 us)
Async XLA Ops:
  0.0 2.4 %collective-permute-start = (f32[256,256]{1,0:T(8,128)}, f32[256,256]{1,0:T(8,128)S(1)}, u32[]{:S(2)}, u32[]{:S(2)}) collective-permute-start(f32[256,256]{1,0:T(8,128)} %bitcast.3), channel_id=1, source_target_pairs={{0,1},{1,0},{2,3},{3,2},{4,5},{5,4},{6,7},{7,6},{8,9},{9,8},{10,11... | collective-permute-start | bytes 786440 | tf_op jit(solution)/shard_map/ppermute | solution.py:272
  2.0 15.4 %collective-permute-start.3 = (f32[128,256]{1,0:T(8,128)S(1)}, f32[128,256]{1,0:T(8,128)S(1)}, u32[]{:S(2)}, u32[]{:S(2)}) collective-permute-start(f32[128,256]{1,0:T(8,128)S(1)} %release.4), channel_id=1, source_target_pairs={{0,4},{1,5},{2,6},{3,7},{4,0},{5,1},{6,2},{7,3},{8,12},{9,13},{10,... | collective-permute-start | bytes 393224 | tf_op jit(solution)/shard_map/ppermute | solution.py:268
  2.4 3.2 %copy-start.1 = (s32[2,256]{1,0:T(2,128)S(1)}, s32[2,256]{1,0:T(2,128)}, u32[]{:S(2)}) copy-start(s32[2,256]{1,0:T(2,128)} %pivots.9) | copy-start | bytes 6148
  2.4 6.4 %collective-permute-start.1 = (f32[256,256]{1,0:T(8,128)S(1)}, f32[256,256]{1,0:T(8,128)S(1)}, u32[]{:S(2)}, u32[]{:S(2)}) collective-permute-start(f32[256,256]{1,0:T(8,128)S(1)} %release.3.sent.before), channel_id=1, source_target_pairs={{0,8},{1,17},{2,10},{3,19},{4,12},{5,21},{6,14},{7,23},{8,0},{9,25... | collective-permute-start | bytes 786440 | tf_op jit(solution)/shard_map/ppermute | solution.py:315
  4.0 13.3 %collective-permute-start.5 = (f32[256,256]{1,0:T(8,128)S(1)}, f32[256,256]{1,0:T(8,128)S(1)}, u32[]{:S(2)}, u32[]{:S(2)}) collective-permute-start(f32[256,256]{1,0:T(8,128)S(1)} %pack.2), channel_id=1, source_target_pairs={{0,2},{1,7},{2,4},{3,1},{4,6},{5,3},{6,0},{7,5},{8,10},{9,15},{10,... | collective-permute-start | bytes 786440 | tf_op jit(solution)/shard_map/ppermute | solution.py:279
  9.1 10.0 %copy-start = (f32[2,256,256]{2,1,0:T(8,128)S(1)}, f32[2,256,256]{2,1,0:T(8,128)}, u32[]{:S(2)}) copy-start(f32[2,256,256]{2,1,0:T(8,128)} %inverse.3) | copy-start | bytes 1572868
  9.1 10.0 %collective-permute-start.2 = (f32[256,256]{1,0:T(8,128)S(1)}, f32[256,256]{1,0:T(8,128)S(1)}, u32[]{:S(2)}, u32[]{:S(2)}) collective-permute-start(f32[256,256]{1,0:T(8,128)S(1)} %merge.2.sent.before), channel_id=1, source_target_pairs={{0,16},{1,9},{2,18},{3,11},{4,20},{5,13},{6,22},{7,15},{8,24},{9,1... | collective-permute-start | bytes 786440 | tf_op jit(solution)/shard_map/ppermute | solution.py:315
  17.3 1.7 %collective-permute-start.6 = (f32[256,256]{1,0:T(8,128)S(1)}, f32[256,256]{1,0:T(8,128)S(1)}, u32[]{:S(2)}, u32[]{:S(2)}) collective-permute-start(f32[256,256]{1,0:T(8,128)S(1)} %collective-permute-done.5.refs_6_.refs_4_), channel_id=1, source_target_pairs={{0,1},{1,0},{2,3},{3,2},{4,5},{5,4},{6,7},{7,6},{8,9},{9,8},{10,11... | collective-permute-start | bytes 786440 | tf_op jit(solution)/shard_map/ppermute | solution.py:272
  17.3 1.7 %collective-permute-start.4 = (f32[128,256]{1,0:T(8,128)S(1)}, f32[128,256]{1,0:T(8,128)S(1)}, u32[]{:S(2)}, u32[]{:S(2)}) collective-permute-start(f32[128,256]{1,0:T(8,128)S(1)} %collective-permute-done.3.refs_4_.refs_2_), channel_id=1, source_target_pairs={{0,1},{1,0},{2,3},{3,2},{4,5},{5,4},{6,7},{7,6},{8,9},{9,8},{10,11... | collective-permute-start | bytes 393224 | tf_op jit(solution)/shard_map/ppermute | solution.py:272
  17.9 13.2 %collective-permute-start.9 = (f32[256,256]{1,0:T(8,128)S(1)}, f32[256,256]{1,0:T(8,128)S(1)}, u32[]{:S(2)}, u32[]{:S(2)}) collective-permute-start(f32[256,256]{1,0:T(8,128)S(1)} %pack.3), channel_id=1, source_target_pairs={{0,2},{1,7},{2,4},{3,1},{4,6},{5,3},{6,0},{7,5},{8,10},{9,15},{10,... | collective-permute-start | bytes 786440 | tf_op jit(solution)/shard_map/ppermute | solution.py:279
  20.4 10.7 %collective-permute-start.11 = (f32[256,256]{1,0:T(8,128)S(1)}, f32[256,256]{1,0:T(8,128)S(1)}, u32[]{:S(2)}, u32[]{:S(2)}) collective-permute-start(f32[256,256]{1,0:T(8,128)S(1)} %get-tuple-element.30.before.sent), channel_id=1, source_target_pairs={{0,8},{1,17},{2,10},{3,19},{4,12},{5,21},{6,14},{7,23},{8,0},{9,25... | collective-permute-start | bytes 786440 | tf_op jit(solution)/shard_map/ppermute | solution.py:315
  21.9 9.8 %collective-permute-start.7 = (f32[128,256]{1,0:T(8,128)S(1)}, f32[128,256]{1,0:T(8,128)S(1)}, u32[]{:S(2)}, u32[]{:S(2)}) collective-permute-start(f32[128,256]{1,0:T(8,128)S(1)} %release.5), channel_id=1, source_target_pairs={{0,4},{1,5},{2,6},{3,7},{4,0},{5,1},{6,2},{7,3},{8,12},{9,13},{10,... | collective-permute-start | bytes 393224 | tf_op jit(solution)/shard_map/ppermute | solution.py:268
  31.1 2.5 %collective-permute-start.10 = (f32[256,256]{1,0:T(8,128)S(1)}, f32[256,256]{1,0:T(8,128)S(1)}, u32[]{:S(2)}, u32[]{:S(2)}) collective-permute-start(f32[256,256]{1,0:T(8,128)S(1)} %collective-permute-done.9.refs_4_), channel_id=1, source_target_pairs={{0,1},{1,0},{2,3},{3,2},{4,5},{5,4},{6,7},{7,6},{8,9},{9,8},{10,11... | collective-permute-start | bytes 786440 | tf_op jit(solution)/shard_map/ppermute | solution.py:272
  31.3 6.4 %collective-permute-start.12 = (f32[256,256]{1,0:T(8,128)S(1)}, f32[256,256]{1,0:T(8,128)S(1)}, u32[]{:S(2)}, u32[]{:S(2)}) collective-permute-start(f32[256,256]{1,0:T(8,128)S(1)} %merge.3.sent), channel_id=1, source_target_pairs={{0,16},{1,9},{2,18},{3,11},{4,20},{5,13},{6,22},{7,15},{8,24},{9,1... | collective-permute-start | bytes 786440 | tf_op jit(solution)/shard_map/ppermute | solution.py:315
  31.7 1.9 %collective-permute-start.8 = (f32[128,256]{1,0:T(8,128)S(1)}, f32[128,256]{1,0:T(8,128)S(1)}, u32[]{:S(2)}, u32[]{:S(2)}) collective-permute-start(f32[128,256]{1,0:T(8,128)S(1)} %collective-permute-done.7.refs_2_), channel_id=1, source_target_pairs={{0,1},{1,0},{2,3},{3,2},{4,5},{5,4},{6,7},{7,6},{8,9},{9,8},{10,11... | collective-permute-start | bytes 393224 | tf_op jit(solution)/shard_map/ppermute | solution.py:272

commit v8 on v6

--- a/solution.py
+++ b/solution.py
@@ -60,30 +60,27 @@
     return jnp.where(offset >= 0, offset, top)
 
 
-def first_slots(matrix, pivots, panels, out, held, *refs):
-    blocks, (chosen, sems) = refs[:-2], refs[-2:]
-    chunks = sems.shape[0] - 1 - len(blocks)
-    rows_dev = held.shape[0]
-    rows = rows_dev // chunks
-    copies = [pltpu.make_async_copy(pivots, chosen, sems.at[chunks])]
-    for c in range(chunks):
-        part = pl.ds(c * rows, rows)
-        copies.append(pltpu.make_async_copy(matrix.at[part, :], held.at[part, :], sems.at[c]))
-    for step, block in enumerate(blocks):
-        copies.append(pltpu.make_async_copy(panels.at[step], block, sems.at[chunks + 1 + step]))
+def load(matrix, pivots, panels, held, chosen, *refs):
+    blocks, sems = refs[:-1], refs[-1]
+    sources = [panels.at[step] for step in range(len(blocks))] + [pivots, matrix]
+    targets = [*blocks, chosen, held]
+    copies = [pltpu.make_async_copy(*pair, sems.at[i]) for i, pair in enumerate(zip(sources, targets))]
     for copy in copies:
         copy.start()
-    copies[0].wait()
-    place = column_of(slot_rows(chosen, 0, rows_dev))
+    for copy in copies:
+        copy.wait()
+
+
+def first_slots(matrix, pivots, out):
+    rows_dev = matrix.shape[0]
+    place = column_of(slot_rows(pivots, 0, rows_dev))
+    width = place.shape[0]
     total = None
-    for c in range(chunks):
-        copies[1 + c].wait()
-        gather = one_hot(place, iota((place.shape[0], rows), 1) + c * rows)
-        term = pick(gather, split(held[c * rows : (c + 1) * rows, :]))
+    for start in range(0, rows_dev, width):
+        gather = one_hot(place, iota((width, width), 1) + start)
+        term = pick(gather, split(matrix[start : start + width, :]))
         total = term if total is None else total + term
     out[...] = total
-    for copy in copies[1 + chunks :]:
-        copy.wait()
 
 
 def prepare(matrix, pivots, base, ahead, places):
@@ -148,17 +145,15 @@
 
 
 def ring_blocks(refs):
-    chips, rows = (len(refs) + 1) // 2, refs[0].shape[0]
-    mine, near, rest = refs[:chips], refs[chips], refs[chips + 1 :]
+    chips = (len(refs) + 1) // 2
+    mine, joint, rest = refs[:chips], refs[chips], refs[chips + 1 :]
+    rows = mine[0].shape[0]
+    others = [rows_of(joint, 0, 2), rows_of(joint, 1, 2), *rest]
     chip, core = lax.axis_index("pcol") // 2, lax.rem(lax.axis_index("pcol"), 2)
     found = []
     for order, distance in enumerate(ring_order(chips)):
         found.append((mine[order], place_of(chip - distance, core, chips, rows)))
-        if order < 2:
-            ref = rows_of(near, order, 3)
-        else:
-            ref = rest[order - 2]
-        found.append((ref, place_of(chip - distance, 1 - core, chips, rows)))
+        found.append((others[order], place_of(chip - distance, 1 - core, chips, rows)))
     return found
 
 
@@ -171,7 +166,7 @@
     opposite = chip + chips // 2
     found = [
         (own, place_of(chip, core, chips, rows)),
-        (rows_of(near, 2, 3), place_of(chip, 1 - core, chips, rows)),
+        (near, place_of(chip, 1 - core, chips, rows)),
         (far, place_of(opposite, core, chips, rows)),
         (far_back, place_of(opposite, 1 - core, chips, rows)),
     ]
@@ -269,18 +264,16 @@
         copy.wait()
 
 
-def stack(*refs):
-    out = refs[-1]
-    start = 0
-    for ref in refs[:-1]:
-        out[start : start + ref.shape[0], :] = ref[...]
-        start += ref.shape[0]
+def stack(one, other, out):
+    rows = one.shape[0]
+    out[:rows, :] = one[...]
+    out[rows:, :] = other[...]
 
 
 def pack(own, near, before, out):
     rows = own.shape[0]
     out[:rows, :] = own[...]
-    out[rows:, :] = near[2 * rows :, :]
+    out[rows:, :] = near[...]
 
 
 def ring_order(chips):
@@ -353,33 +346,34 @@
             received.append(lax.ppermute(sent, ("prow", "pcol"), pairs))
         return sent, received
 
-    owner = jnp.broadcast_to((pivots // rows_dev)[:, :, None], (steps, width, columns))
     chunks = rows_dev // width
     halves = [pltpu.VMEM((rows_dev, l_panels.shape[2]), BF16)] * 2
     block = shape(l_panels.shape[1:], F32)
-    slots, matrix, *own = call(
-        first_slots,
-        "first_slots",
+    matrix, pivots, *own = call(
+        load,
+        "load",
         [pltpu.with_memory_space_constraint(x, pltpu.HBM) for x in (matrix, pivots, l_panels)],
-        [square, full] + [block] * steps,
+        [full, shape(pivots.shape, pivots.dtype)] + [block] * steps,
         specs=[HBM] * 3,
-        scratch=[pltpu.VMEM((steps, width), jnp.int32), pltpu.SemaphoreType.DMA((chunks + 1 + steps,))],
-    )
+        scratch=[pltpu.SemaphoreType.DMA((2 + steps,))],
+    )
+    slots = call(first_slots, "first_slots", [matrix, pivots], square)
+
+    owner = jnp.broadcast_to((pivots // rows_dev)[:, :, None], (steps, width, columns))
+
+    near = across(own[1], process_columns)
 
     def after(panel, before):
         return call(release, "release", [panel, before], block, specs=[VMEM, ANY])
 
-    def stacked(blocks):
-        rows = sum(piece.shape[0] for piece in blocks)
-        return call(stack, "stack", blocks, shape((rows, block.shape[1]), F32))
-
     base, ahead, places = call(
         prepare, "prepare", [matrix, pivots], [full, square, shape((width, width), jnp.int32)]
     )
     first = forwarded(own[0], after(own[0], places), process_columns)
-    near = across(stacked([*first[:2], own[1]]), process_columns)
-    first += [near] + [across(piece, process_columns) for piece in first[2:]]
-    sent, received = exchange(slots, 0, [near])
+    joint = call(stack, "stack", first[:2], shape((2 * block.shape[0], block.shape[1]), F32))
+    joint = across(joint, process_columns)
+    first += [joint] + [across(piece, process_columns) for piece in first[2:]]
+    sent, received = exchange(slots, 0, [joint])
     two = shape((2 * block.shape[0], block.shape[1]), F32)
     pair = call(pack, "pack", [own[1], near, sent], two, specs=[VMEM, VMEM, ANY])
     operands = [matrix, pivots, l_inverse, owner[0], ahead, places, sent, *received, *first]

time: 36.7 us -> 36.2 us (0.986)
  waiting for transfers between devices: 14.3 us -> 13.3 us
  starting transfers between devices: 14.3 us -> 14.9 us
    ppermute x5 -> x6, waiting for transfers between devices: 2.51 us -> 1.67 us  [across(): return lax.ppermute(block, 'pcol', [(i, i ^ 1) for i in range(count)])]
    ppermute x4, waiting for transfers between devices: 7.32 us -> 6.64 us  [shift(): lax.ppermute(block, 'pcol', [(i, (i + 2 * distance) % count) for i in ran...]
    ppermute x4, starting transfers between devices: 6.27 us -> 6.92 us  [shift(): lax.ppermute(block, 'pcol', [(i, (i + 2 * distance) % count) for i in ran...]
    ppermute x4, waiting for transfers between devices: 1.16 us -> 1.62 us  [exchange(): received.append(lax.ppermute(sent, ('prow', 'pcol'), pairs))]
    pallas_call x12 -> x13, Pallas kernels: 7.51 us -> 7.5 us  [call(): pl.pallas_call(kernel, out_shape=outs, in_specs=specs or [VMEM] * len(ope...]
  transfers between devices with their start and end apart: 14 -> 15, of which waited for: 10 -> 10; matrix products, arithmetic and copies ran while one was open for 1% -> 1% of each run, Pallas kernels for 10% -> 12%
where the time goes in v8:
time: 36.2 us; the launch traced here: 36 us
  starting transfers between devices  14.9 us (41%)
  waiting for transfers between devices  13.3 us (37%)
  Pallas kernels  7.5 us (21%)
    pallas_call x13, Pallas kernels, call(): pl.pallas_call(kernel, out_shape=outs, in_specs=specs or [VMEM] * len(ope...  7.5 us
    ppermute x4, starting transfers between devices, exchange(): received.append(lax.ppermute(sent, ('prow', 'pcol'), pairs))  7.31 us
    ppermute x4, starting transfers between devices, shift(): lax.ppermute(block, 'pcol', [(i, (i + 2 * distance) % count) for i in ran...  6.92 us
    ppermute x4, waiting for transfers between devices, shift(): lax.ppermute(block, 'pcol', [(i, (i + 2 * distance) % count) for i in ran...  6.64 us
    ppermute x1, waiting for transfers between devices, passed(): pairs.append(lax.ppermute(pairs[-1], 'pcol', onward))  3.33 us
    ppermute x6, waiting for transfers between devices, across(): return lax.ppermute(block, 'pcol', [(i, i ^ 1) for i in range(count)])  1.67 us
    ppermute x4, waiting for transfers between devices, exchange(): received.append(lax.ppermute(sent, ('prow', 'pcol'), pairs))  1.62 us
  transfers between devices with their start and end apart: 15, of which 10 were waited for; matrix products, arithmetic and copies ran while one was open for 1% of the time, Pallas kernels for 12%

profile of v8, /device:TPU:0, one launch (start us, length us, event | category | flops | bytes accessed | tf_op | source)
XLA Modules:
  0.0 36.0 jit_solution(14652975749790373220)
XLA Ops:
  0.0 1.4 %load.1 = (f32[1024,256]{1,0:T(8,128)S(1)}, s32[2,256]{1,0:T(2,128)S(1)}, f32[128,256]{1,0:T(8,128)S(1)}, f32[128,256]{1,0:T(8,128)S(1)}) custom-call(f32[1024,256]{1,0:T(8,128)} %matrix.1, s32[2,256]{1,0:T(2,128)} %pivots.1, f32[2,128,256]{2,1,0:T(8,128)} %panels.1), custom_call_target="tpu_custom_call" | custom-call | tf_op jit(solution)/shard_map/load/pallas_call | solution.py:324
  1.4 3.1 %collective-permute-start.1 = (f32[128,256]{1,0:T(8,128)S(1)}, f32[128,256]{1,0:T(8,128)S(1)}, u32[]{:S(2)}, u32[]{:S(2)}) collective-permute-start(f32[128,256]{1,0:T(8,128)S(1)} %get-tuple-element.24.one.panel.refs_2_.refs_0_), channel_id=1, source_target_pairs={{0,2},{1,3},{2,4},{3,5},{4,6},{5,7},{6,0},{7,1},{8,10},{9,11},{10,... | collective-permute-start | bytes 393224 | tf_op jit(solution)/shard_map/ppermute | solution.py:288
  4.5 0.5 %first_slots.1.sent = f32[256,256]{1,0:T(8,128)S(1)} custom-call(f32[1024,256]{1,0:T(8,128)S(1)} %get-tuple-element.19.matrix, s32[2,256]{1,0:T(2,128)S(1)} %get-tuple-element.20.pivots), custom_call_target="tpu_custom_call" | custom-call | tf_op jit(solution)/shard_map/first_slots/pallas_call | solution.py:324
  5.0 1.6 %collective-permute-start = (f32[256,256]{1,0:T(8,128)S(1)}, f32[256,256]{1,0:T(8,128)S(1)}, u32[]{:S(2)}, u32[]{:S(2)}) collective-permute-start(f32[256,256]{1,0:T(8,128)S(1)} %first_slots.1.sent), channel_id=1, source_target_pairs={{0,8},{1,17},{2,10},{3,19},{4,12},{5,21},{6,14},{7,23},{8,0},{9,25... | collective-permute-start | bytes 786440 | tf_op jit(solution)/shard_map/ppermute | solution.py:346
  6.6 0.7 %prepare.1 = (f32[1024,256]{1,0:T(8,128)S(1)}, f32[256,256]{1,0:T(8,128)S(1)}, s32[256,256]{1,0:T(8,128)S(1)}) custom-call(f32[1024,256]{1,0:T(8,128)S(1)} %get-tuple-element.19.matrix, s32[2,256]{1,0:T(2,128)S(1)} %get-tuple-element.20.pivots), custom_call_target="tpu_custom_call" | custom-call | tf_op jit(solution)/shard_map/prepare/pallas_call | solution.py:324
  7.3 2.3 %collective-permute-start.5 = (f32[128,256]{1,0:T(8,128)S(1)}, f32[128,256]{1,0:T(8,128)S(1)}, u32[]{:S(2)}, u32[]{:S(2)}) collective-permute-start(f32[128,256]{1,0:T(8,128)S(1)} %release.2), channel_id=1, source_target_pairs={{0,6},{1,7},{2,0},{3,1},{4,2},{5,3},{6,4},{7,5},{8,14},{9,15},{10,... | collective-permute-start | bytes 393224 | tf_op jit(solution)/shard_map/ppermute | solution.py:288
  9.6 0.5 %collective-permute-done.1.other.refs_3_.refs_1_ = f32[128,256]{1,0:T(8,128)S(1)} collective-permute-done((f32[128,256]{1,0:T(8,128)S(1)}, f32[128,256]{1,0:T(8,128)S(1)}, u32[]{:S(2)}, u32[]{:S(2)}) %collective-permute-start.1) | collective-permute-done | bytes 131104 | tf_op jit(solution)/shard_map/ppermute | solution.py:288
  10.3 1.2 %collective-permute-done.received.refs_0_ = f32[256,256]{1,0:T(8,128)S(1)} collective-permute-done((f32[256,256]{1,0:T(8,128)S(1)}, f32[256,256]{1,0:T(8,128)S(1)}, u32[]{:S(2)}, u32[]{:S(2)}) %collective-permute-start) | collective-permute-done | bytes 262176 | tf_op jit(solution)/shard_map/ppermute | solution.py:346
  11.5 0.2 collective-permute-done.2.refs_0_.refs_6_.refs_4_
  11.9 1.6 %collective-permute-start.3 = (f32[256,256]{1,0:T(8,128)S(1)}, f32[256,256]{1,0:T(8,128)S(1)}, u32[]{:S(2)}, u32[]{:S(2)}) collective-permute-start(f32[256,256]{1,0:T(8,128)S(1)} %merge.2.sent.before), channel_id=1, source_target_pairs={{0,16},{1,9},{2,18},{3,11},{4,20},{5,13},{6,22},{7,15},{8,24},{9,1... | collective-permute-start | bytes 786440 | tf_op jit(solution)/shard_map/ppermute | solution.py:346
  13.6 0.5 %collective-permute-start.7 = (f32[128,256]{1,0:T(8,128)S(1)}, f32[128,256]{1,0:T(8,128)S(1)}, u32[]{:S(2)}, u32[]{:S(2)}) collective-permute-start(f32[128,256]{1,0:T(8,128)S(1)} %collective-permute-done.5.refs_5_.refs_3_), channel_id=1, source_target_pairs={{0,1},{1,0},{2,3},{3,2},{4,5},{5,4},{6,7},{7,6},{8,9},{9,8},{10,11... | collective-permute-start | bytes 393224 | tf_op jit(solution)/shard_map/ppermute | solution.py:292
  14.1 3.9 %collective-permute-done.4.refs_4_.refs_2_ = f32[128,256]{1,0:T(8,128)S(1)} collective-permute-done((f32[128,256]{1,0:T(8,128)S(1)}, f32[128,256]{1,0:T(8,128)S(1)}, u32[]{:S(2)}, u32[]{:S(2)}) %collective-permute-start.4) | collective-permute-done | bytes 131104 | tf_op jit(solution)/shard_map/ppermute | solution.py:288
  18.1 1.2 %collective-permute-done.6.refs_7_.refs_5_ = f32[128,256]{1,0:T(8,128)S(1)} collective-permute-done((f32[128,256]{1,0:T(8,128)S(1)}, f32[128,256]{1,0:T(8,128)S(1)}, u32[]{:S(2)}, u32[]{:S(2)}) %collective-permute-start.6) | collective-permute-done | bytes 131104 | tf_op jit(solution)/shard_map/ppermute | solution.py:292
  19.3 1.3 %solve.1 = (f32[256,256]{1,0:T(8,128)S(1)}, f32[256,256]{1,0:T(8,128)S(1)}, f32[256,256]{1,0:T(8,128)S(1)}) custom-call(f32[1024,256]{1,0:T(8,128)S(1)} %get-tuple-element.19.matrix, s32[2,256]{1,0:T(2,128)S(1)} %get-tuple-element.20.pivots, f32[2,256,256]{2,1,0:T(8,128)S(1)} %copy-done, s32[256,256]{1,0:T(8,128)S(1)} %broadcast_in_dim.13.owner, ...), custom_call_target="tpu_custom_call" | custom-call | tf_op jit(solution)/shard_map/solve/pallas_call | solution.py:324
  20.6 1.6 %collective-permute-start.13 = (f32[256,256]{1,0:T(8,128)S(1)}, f32[256,256]{1,0:T(8,128)S(1)}, u32[]{:S(2)}, u32[]{:S(2)}) collective-permute-start(f32[256,256]{1,0:T(8,128)S(1)} %get-tuple-element.30.before.sent), channel_id=1, source_target_pairs={{0,8},{1,17},{2,10},{3,19},{4,12},{5,21},{6,14},{7,23},{8,0},{9,25... | collective-permute-start | bytes 786440 | tf_op jit(solution)/shard_map/ppermute | solution.py:346
  22.2 1.5 %collective-permute-start.9 = (f32[128,256]{1,0:T(8,128)S(1)}, f32[128,256]{1,0:T(8,128)S(1)}, u32[]{:S(2)}, u32[]{:S(2)}) collective-permute-start(f32[128,256]{1,0:T(8,128)S(1)} %release.3), channel_id=1, source_target_pairs={{0,4},{1,5},{2,6},{3,7},{4,0},{5,1},{6,2},{7,3},{8,12},{9,13},{10,... | collective-permute-start | bytes 393224 | tf_op jit(solution)/shard_map/ppermute | solution.py:288
  23.7 3.3 %collective-permute-done.11.refs_4_ = f32[256,256]{1,0:T(8,128)S(1)} collective-permute-done((f32[256,256]{1,0:T(8,128)S(1)}, f32[256,256]{1,0:T(8,128)S(1)}, u32[]{:S(2)}, u32[]{:S(2)}) %collective-permute-start.11) | collective-permute-done | bytes 262176 | tf_op jit(solution)/shard_map/ppermute | solution.py:310
  27.3 2.6 %collective-permute-start.14 = (f32[256,256]{1,0:T(8,128)S(1)}, f32[256,256]{1,0:T(8,128)S(1)}, u32[]{:S(2)}, u32[]{:S(2)}) collective-permute-start(f32[256,256]{1,0:T(8,128)S(1)} %merge.3.sent), channel_id=1, source_target_pairs={{0,16},{1,9},{2,18},{3,11},{4,20},{5,13},{6,22},{7,15},{8,24},{9,1... | collective-permute-start | bytes 786440 | tf_op jit(solution)/shard_map/ppermute | solution.py:346
  29.8 2.3 %collective-permute-done.9.refs_2_ = f32[128,256]{1,0:T(8,128)S(1)} collective-permute-done((f32[128,256]{1,0:T(8,128)S(1)}, f32[128,256]{1,0:T(8,128)S(1)}, u32[]{:S(2)}, u32[]{:S(2)}) %collective-permute-start.9) | collective-permute-done | bytes 131104 | tf_op jit(solution)/shard_map/ppermute | solution.py:288
  32.1 1.1 %update.1 = (f32[1024,256]{1,0:T(8,128)S(1)}, f32[256,256]{1,0:T(8,128)S(1)}) custom-call(f32[1024,256]{1,0:T(8,128)S(1)} %get-tuple-element.21.base, s32[2,256]{1,0:T(2,128)S(1)} %get-tuple-element.20.pivots, f32[256,256]{1,0:T(8,128)S(1)} %get-tuple-element.25.upper_in, f32[256,256]{1,0:T(8,128)S(1)} %get-tuple-element.26.displaced_in, ...), custom_call_target="tpu_custom_call" | custom-call | tf_op jit(solution)/shard_map/update/pallas_call | solution.py:324
  33.3 0.2 collective-permute-done.10.refs_3_
  33.5 0.3 halve.1
  33.8 0.4 %collective-permute-done.14.refs_1_ = f32[256,256]{1,0:T(8,128)S(1)} collective-permute-done((f32[256,256]{1,0:T(8,128)S(1)}, f32[256,256]{1,0:T(8,128)S(1)}, u32[]{:S(2)}, u32[]{:S(2)}) %collective-permute-start.14) | collective-permute-done | bytes 262176 | tf_op jit(solution)/shard_map/ppermute | solution.py:346
  34.2 1.9 %finish.1 = f32[1024,256]{1,0:T(8,128)} custom-call(f32[1024,256]{1,0:T(8,128)S(1)} %get-tuple-element.27.base, s32[2,256]{1,0:T(2,128)S(1)} %get-tuple-element.20.pivots, f32[2,256,256]{2,1,0:T(8,128)S(1)} %copy-done, s32[256,256]{1,0:T(8,128)S(1)} %broadcast_in_dim.15.owner, f32[256,256]{1,0:T(8,128)S(1)} %get-tuple-element.28.top, ...), custom_call_target="tpu_custom_call" | custom-call | tf_op jit(solution)/shard_map/finish/pallas_call | solution.py:324
  (25 shorter events, 0.8 us)
Async XLA Ops:
  1.4 8.7 %collective-permute-start.1 = (f32[128,256]{1,0:T(8,128)S(1)}, f32[128,256]{1,0:T(8,128)S(1)}, u32[]{:S(2)}, u32[]{:S(2)}) collective-permute-start(f32[128,256]{1,0:T(8,128)S(1)} %get-tuple-element.24.one.panel.refs_2_.refs_0_), channel_id=1, source_target_pairs={{0,2},{1,3},{2,4},{3,5},{4,6},{5,7},{6,0},{7,1},{8,10},{9,11},{10,... | collective-permute-start | bytes 393224 | tf_op jit(solution)/shard_map/ppermute | solution.py:288
  5.0 6.4 %collective-permute-start = (f32[256,256]{1,0:T(8,128)S(1)}, f32[256,256]{1,0:T(8,128)S(1)}, u32[]{:S(2)}, u32[]{:S(2)}) collective-permute-start(f32[256,256]{1,0:T(8,128)S(1)} %first_slots.1.sent), channel_id=1, source_target_pairs={{0,8},{1,17},{2,10},{3,19},{4,12},{5,21},{6,14},{7,23},{8,0},{9,25... | collective-permute-start | bytes 786440 | tf_op jit(solution)/shard_map/ppermute | solution.py:346
  7.3 6.3 %collective-permute-start.5 = (f32[128,256]{1,0:T(8,128)S(1)}, f32[128,256]{1,0:T(8,128)S(1)}, u32[]{:S(2)}, u32[]{:S(2)}) collective-permute-start(f32[128,256]{1,0:T(8,128)S(1)} %release.2), channel_id=1, source_target_pairs={{0,6},{1,7},{2,0},{3,1},{4,2},{5,3},{6,4},{7,5},{8,14},{9,15},{10,... | collective-permute-start | bytes 393224 | tf_op jit(solution)/shard_map/ppermute | solution.py:288
  10.1 1.6 %collective-permute-start.2 = (f32[256,256]{1,0:T(8,128)S(1)}, f32[256,256]{1,0:T(8,128)S(1)}, u32[]{:S(2)}, u32[]{:S(2)}) collective-permute-start(f32[256,256]{1,0:T(8,128)S(1)} %stack.1), channel_id=1, source_target_pairs={{0,1},{1,0},{2,3},{3,2},{4,5},{5,4},{6,7},{7,6},{8,9},{9,8},{10,11... | collective-permute-start | bytes 786440 | tf_op jit(solution)/shard_map/ppermute | solution.py:292
  10.2 7.7 %collective-permute-start.4 = (f32[128,256]{1,0:T(8,128)S(1)}, f32[128,256]{1,0:T(8,128)S(1)}, u32[]{:S(2)}, u32[]{:S(2)}) collective-permute-start(f32[128,256]{1,0:T(8,128)S(1)} %collective-permute-done.1.other.refs_3_.refs_1_), channel_id=1, source_target_pairs={{0,2},{1,3},{2,4},{3,5},{4,6},{5,7},{6,0},{7,1},{8,10},{9,11},{10,... | collective-permute-start | bytes 393224 | tf_op jit(solution)/shard_map/ppermute | solution.py:288
  11.9 7.4 %copy-start = (f32[2,256,256]{2,1,0:T(8,128)S(1)}, f32[2,256,256]{2,1,0:T(8,128)}, u32[]{:S(2)}) copy-start(f32[2,256,256]{2,1,0:T(8,128)} %inverse.3) | copy-start | bytes 1572868
  11.9 7.4 %collective-permute-start.3 = (f32[256,256]{1,0:T(8,128)S(1)}, f32[256,256]{1,0:T(8,128)S(1)}, u32[]{:S(2)}, u32[]{:S(2)}) collective-permute-start(f32[256,256]{1,0:T(8,128)S(1)} %merge.2.sent.before), channel_id=1, source_target_pairs={{0,16},{1,9},{2,18},{3,11},{4,20},{5,13},{6,22},{7,15},{8,24},{9,1... | collective-permute-start | bytes 786440 | tf_op jit(solution)/shard_map/ppermute | solution.py:346
  13.6 4.4 %collective-permute-start.8 = (f32[128,256]{1,0:T(8,128)S(1)}, f32[128,256]{1,0:T(8,128)S(1)}, u32[]{:S(2)}, u32[]{:S(2)}) collective-permute-start(f32[128,256]{1,0:T(8,128)S(1)} %get-tuple-element.29.panel.own.refs_0_), channel_id=1, source_target_pairs={{0,1},{1,0},{2,3},{3,2},{4,5},{5,4},{6,7},{7,6},{8,9},{9,8},{10,11... | collective-permute-start | bytes 393224 | tf_op jit(solution)/shard_map/ppermute | solution.py:292
  13.6 4.5 %collective-permute-start.7 = (f32[128,256]{1,0:T(8,128)S(1)}, f32[128,256]{1,0:T(8,128)S(1)}, u32[]{:S(2)}, u32[]{:S(2)}) collective-permute-start(f32[128,256]{1,0:T(8,128)S(1)} %collective-permute-done.5.refs_5_.refs_3_), channel_id=1, source_target_pairs={{0,1},{1,0},{2,3},{3,2},{4,5},{5,4},{6,7},{7,6},{8,9},{9,8},{10,11... | collective-permute-start | bytes 393224 | tf_op jit(solution)/shard_map/ppermute | solution.py:292
  18.0 1.3 %collective-permute-start.6 = (f32[128,256]{1,0:T(8,128)S(1)}, f32[128,256]{1,0:T(8,128)S(1)}, u32[]{:S(2)}, u32[]{:S(2)}) collective-permute-start(f32[128,256]{1,0:T(8,128)S(1)} %collective-permute-done.4.refs_4_.refs_2_), channel_id=1, source_target_pairs={{0,1},{1,0},{2,3},{3,2},{4,5},{5,4},{6,7},{7,6},{8,9},{9,8},{10,11... | collective-permute-start | bytes 393224 | tf_op jit(solution)/shard_map/ppermute | solution.py:292
  18.0 9.0 %collective-permute-start.11 = (f32[256,256]{1,0:T(8,128)S(1)}, f32[256,256]{1,0:T(8,128)S(1)}, u32[]{:S(2)}, u32[]{:S(2)}) collective-permute-start(f32[256,256]{1,0:T(8,128)S(1)} %pack.1), channel_id=1, source_target_pairs={{0,2},{1,7},{2,4},{3,1},{4,6},{5,3},{6,0},{7,5},{8,10},{9,15},{10,... | collective-permute-start | bytes 786440 | tf_op jit(solution)/shard_map/ppermute | solution.py:310
  20.6 6.4 %collective-permute-start.13 = (f32[256,256]{1,0:T(8,128)S(1)}, f32[256,256]{1,0:T(8,128)S(1)}, u32[]{:S(2)}, u32[]{:S(2)}) collective-permute-start(f32[256,256]{1,0:T(8,128)S(1)} %get-tuple-element.30.before.sent), channel_id=1, source_target_pairs={{0,8},{1,17},{2,10},{3,19},{4,12},{5,21},{6,14},{7,23},{8,0},{9,25... | collective-permute-start | bytes 786440 | tf_op jit(solution)/shard_map/ppermute | solution.py:346
  22.2 9.9 %collective-permute-start.9 = (f32[128,256]{1,0:T(8,128)S(1)}, f32[128,256]{1,0:T(8,128)S(1)}, u32[]{:S(2)}, u32[]{:S(2)}) collective-permute-start(f32[128,256]{1,0:T(8,128)S(1)} %release.3), channel_id=1, source_target_pairs={{0,4},{1,5},{2,6},{3,7},{4,0},{5,1},{6,2},{7,3},{8,12},{9,13},{10,... | collective-permute-start | bytes 393224 | tf_op jit(solution)/shard_map/ppermute | solution.py:288
  27.0 6.5 %collective-permute-start.12 = (f32[256,256]{1,0:T(8,128)S(1)}, f32[256,256]{1,0:T(8,128)S(1)}, u32[]{:S(2)}, u32[]{:S(2)}) collective-permute-start(f32[256,256]{1,0:T(8,128)S(1)} %collective-permute-done.11.refs_4_), channel_id=1, source_target_pairs={{0,1},{1,0},{2,3},{3,2},{4,5},{5,4},{6,7},{7,6},{8,9},{9,8},{10,11... | collective-permute-start | bytes 786440 | tf_op jit(solution)/shard_map/ppermute | solution.py:292
  27.3 6.9 %collective-permute-start.14 = (f32[256,256]{1,0:T(8,128)S(1)}, f32[256,256]{1,0:T(8,128)S(1)}, u32[]{:S(2)}, u32[]{:S(2)}) collective-permute-start(f32[256,256]{1,0:T(8,128)S(1)} %merge.3.sent), channel_id=1, source_target_pairs={{0,16},{1,9},{2,18},{3,11},{4,20},{5,13},{6,22},{7,15},{8,24},{9,1... | collective-permute-start | bytes 786440 | tf_op jit(solution)/shard_map/ppermute | solution.py:346
  32.1 1.3 %collective-permute-start.10 = (f32[128,256]{1,0:T(8,128)S(1)}, f32[128,256]{1,0:T(8,128)S(1)}, u32[]{:S(2)}, u32[]{:S(2)}) collective-permute-start(f32[128,256]{1,0:T(8,128)S(1)} %collective-permute-done.9.refs_2_), channel_id=1, source_target_pairs={{0,1},{1,0},{2,3},{3,2},{4,5},{5,4},{6,7},{7,6},{8,9},{9,8},{10,11... | collective-permute-start | bytes 393224 | tf_op jit(solution)/shard_map/ppermute | solution.py:292

commit v9 on v8

--- a/solution.py
+++ b/solution.py
@@ -14,6 +14,8 @@
 F32 = jnp.float32
 BF16 = jnp.bfloat16
 NOWHERE = -(1 << 24)
+TAIL = 16
+SPARE = 16
 
 
 def product(left, right):
@@ -158,24 +160,29 @@
 
 
 def pair_blocks(refs):
-    own, near, far, far_back, *pairs = refs
+    own, near, far, far_back, *rest = refs
     rows = own.shape[0]
-    chips = len(pairs) + 2
-    hops = len(pairs) // 2
+    hops, tail = len(rest) // 2, tail_of(rows)
+    pairs, back = rest[:hops], rest[hops:]
+    chips = 2 * hops + 2
     chip, core = lax.axis_index("pcol") // 2, lax.rem(lax.axis_index("pcol"), 2)
     opposite = chip + chips // 2
     found = [
         (own, place_of(chip, core, chips, rows)),
         (near, place_of(chip, 1 - core, chips, rows)),
         (far, place_of(opposite, core, chips, rows)),
-        (far_back, place_of(opposite, 1 - core, chips, rows)),
+        (far_back.at[pl.ds(0, rows), :], place_of(opposite, 1 - core, chips, rows)),
     ]
     for hop in range(hops):
         along = (hop + 1) * (1 - 2 * core)
         for half in range(2):
-            owner = core if half == 0 else 1 - core
-            found.append((rows_of(pairs[hop], half, 2), place_of(chip - along, owner, chips, rows)))
-            found.append((rows_of(pairs[hops + hop], half, 2), place_of(chip + along, 1 - owner, chips, rows)))
+            place = place_of(chip - along, core if half == 0 else 1 - core, chips, rows)
+            found.append((pairs[hop].at[pl.ds(half * rows, rows), :], place))
+            place = place_of(chip + along, 1 - core if half == 0 else core, chips, rows)
+            held = rows - half * tail
+            found.append((back[hop].at[pl.ds(half * rows, held), :], place))
+        if tail:
+            found.append((far_back.at[pl.ds(rows + hop * tail, tail), :], pl.multiple_of(place + held, tail)))
     return found
 
 
@@ -273,15 +280,30 @@
 def pack(own, near, before, out):
     rows = own.shape[0]
     out[:rows, :] = own[...]
-    out[rows:, :] = near[...]
+    out[rows : 2 * rows, :] = near[...]
+    out[2 * rows :, :] = own[: out.shape[0] - 2 * rows, :]
 
 
 def ring_order(chips):
     return [0] + list(range(1, chips // 2 + 1)) + list(range(chips - 1, chips // 2, -1))
 
 
+def tail_of(rows):
+    return TAIL if rows > TAIL else 0
+
+
+def tails(far, *refs):
+    pairs, out = refs[:-1], refs[-1]
+    rows = far.shape[0]
+    out[:rows, :] = far[...]
+    for hop, pair in enumerate(pairs):
+        start, tail = rows + hop * tail_of(rows), tail_of(rows)
+        if tail:
+            out[start : start + tail, :] = pair[2 * rows - tail : 2 * rows, :]
+
+
 def release(panel, before, out):
-    out[...] = panel[...]
+    out[...] = panel[: out.shape[0], :]
 
 
 def shift(block, distance, count):
@@ -363,8 +385,8 @@
 
     near = across(own[1], process_columns)
 
-    def after(panel, before):
-        return call(release, "release", [panel, before], block, specs=[VMEM, ANY])
+    def after(panel, before, rows=block.shape[0]):
+        return call(release, "release", [panel, before], shape((rows, block.shape[1]), F32), specs=[VMEM, ANY])
 
     base, ahead, places = call(
         prepare, "prepare", [matrix, pivots], [full, square, shape((width, width), jnp.int32)]
@@ -374,14 +396,16 @@
     joint = across(joint, process_columns)
     first += [joint] + [across(piece, process_columns) for piece in first[2:]]
     sent, received = exchange(slots, 0, [joint])
-    two = shape((2 * block.shape[0], block.shape[1]), F32)
+    two = shape((2 * block.shape[0] + SPARE, block.shape[1]), F32)
     pair = call(pack, "pack", [own[1], near, sent], two, specs=[VMEM, VMEM, ANY])
     operands = [matrix, pivots, l_inverse, owner[0], ahead, places, sent, *received, *first]
     upper, displaced, slots = call(functools.partial(solve, bits, 0), "solve", operands, [square] * 3)
     far = shift(after(own[1], slots), process_columns // 4, process_columns)
     pairs = passed(pair, process_columns)
-    second = [own[1], near, far, across(far, process_columns)]
-    second += pairs + [across(piece, process_columns) for piece in pairs]
+    rows = block.shape[0]
+    joint = call(tails, "tails", [far, *pairs], shape((rows + tail_of(rows) * len(pairs), block.shape[1]), F32))
+    second = [own[1], near, far, across(joint, process_columns)]
+    second += pairs + [across(after(piece, own[1], 2 * rows - tail_of(rows)), process_columns) for piece in pairs]
     base, top = call(
         functools.partial(update, 0),
         "update",

time: 36.2 us -> 36.3 us (level)
  starting transfers between devices: 14.9 us -> 14.1 us
  waiting for transfers between devices: 13.3 us -> 14.1 us
    ppermute x1, waiting for transfers between devices: 3.33 us -> 0.01 us  [passed(): pairs.append(lax.ppermute(pairs[-1], 'pcol', onward))]
    ppermute x4, waiting for transfers between devices: 1.62 us -> 4.59 us  [exchange(): received.append(lax.ppermute(sent, ('prow', 'pcol'), pairs))]
    ppermute x4, waiting for transfers between devices: 6.64 us -> 7.84 us  [shift(): lax.ppermute(block, 'pcol', [(i, (i + 2 * distance) % count) for i in ran...]
    ppermute x4, starting transfers between devices: 7.31 us -> 6.41 us  [exchange(): received.append(lax.ppermute(sent, ('prow', 'pcol'), pairs))]
    pallas_call x13 -> x15, Pallas kernels: 7.5 us -> 7.49 us  [call(): pl.pallas_call(kernel, out_shape=outs, in_specs=specs or [VMEM] * len(ope...]
  transfers between devices with their start and end apart: 15 -> 15, of which waited for: 10 -> 8; matrix products, arithmetic and copies ran while one was open for 1% -> 1% of each run, Pallas kernels for 12% -> 12%
where the time goes in v9:
time: 36.3 us; the launch traced here: 36.1 us
  starting transfers between devices  14.1 us (39%)
  waiting for transfers between devices  14.1 us (39%)
  Pallas kernels  7.49 us (21%)
    ppermute x4, waiting for transfers between devices, shift(): lax.ppermute(block, 'pcol', [(i, (i + 2 * distance) % count) for i in ran...  7.84 us
    pallas_call x15, Pallas kernels, call(): pl.pallas_call(kernel, out_shape=outs, in_specs=specs or [VMEM] * len(ope...  7.49 us
    ppermute x4, starting transfers between devices, shift(): lax.ppermute(block, 'pcol', [(i, (i + 2 * distance) % count) for i in ran...  6.9 us
    ppermute x4, starting transfers between devices, exchange(): received.append(lax.ppermute(sent, ('prow', 'pcol'), pairs))  6.41 us
    ppermute x4, waiting for transfers between devices, exchange(): received.append(lax.ppermute(sent, ('prow', 'pcol'), pairs))  4.59 us
    ppermute x6, waiting for transfers between devices, across(): return lax.ppermute(block, 'pcol', [(i, i ^ 1) for i in range(count)])  1.69 us
    ppermute x6, starting transfers between devices, across(): return lax.ppermute(block, 'pcol', [(i, i ^ 1) for i in range(count)])  0.74 us
  transfers between devices with their start and end apart: 15, of which 8 were waited for; matrix products, arithmetic and copies ran while one was open for 1% of the time, Pallas kernels for 12%

profile of v9, /device:TPU:0, one launch (start us, length us, event | category | flops | bytes accessed | tf_op | source)
XLA Modules:
  0.0 36.1 jit_solution(7301176935438684780)
XLA Ops:
  0.0 1.4 %load.1 = (f32[1024,256]{1,0:T(8,128)S(1)}, s32[2,256]{1,0:T(2,128)S(1)}, f32[128,256]{1,0:T(8,128)S(1)}, f32[128,256]{1,0:T(8,128)S(1)}) custom-call(f32[1024,256]{1,0:T(8,128)} %matrix.1, s32[2,256]{1,0:T(2,128)} %pivots.1, f32[2,128,256]{2,1,0:T(8,128)} %panels.1), custom_call_target="tpu_custom_call" | custom-call | tf_op jit(solution)/shard_map/load/pallas_call | solution.py:346
  1.4 3.1 %collective-permute-start.1 = (f32[128,256]{1,0:T(8,128)S(1)}, f32[128,256]{1,0:T(8,128)S(1)}, u32[]{:S(2)}, u32[]{:S(2)}) collective-permute-start(f32[128,256]{1,0:T(8,128)S(1)} %get-tuple-element.24.one.panel.refs_2_.refs_0_), channel_id=1, source_target_pairs={{0,2},{1,3},{2,4},{3,5},{4,6},{5,7},{6,0},{7,1},{8,10},{9,11},{10,... | collective-permute-start | bytes 393224 | tf_op jit(solution)/shard_map/ppermute | solution.py:310
  4.5 0.5 %first_slots.1.sent = f32[256,256]{1,0:T(8,128)S(1)} custom-call(f32[1024,256]{1,0:T(8,128)S(1)} %get-tuple-element.19.matrix, s32[2,256]{1,0:T(2,128)S(1)} %get-tuple-element.20.pivots), custom_call_target="tpu_custom_call" | custom-call | tf_op jit(solution)/shard_map/first_slots/pallas_call | solution.py:346
  5.0 1.6 %collective-permute-start = (f32[256,256]{1,0:T(8,128)S(1)}, f32[256,256]{1,0:T(8,128)S(1)}, u32[]{:S(2)}, u32[]{:S(2)}) collective-permute-start(f32[256,256]{1,0:T(8,128)S(1)} %first_slots.1.sent), channel_id=1, source_target_pairs={{0,8},{1,17},{2,10},{3,19},{4,12},{5,21},{6,14},{7,23},{8,0},{9,25... | collective-permute-start | bytes 786440 | tf_op jit(solution)/shard_map/ppermute | solution.py:368
  6.6 0.7 %prepare.1 = (f32[1024,256]{1,0:T(8,128)S(1)}, f32[256,256]{1,0:T(8,128)S(1)}, s32[256,256]{1,0:T(8,128)S(1)}) custom-call(f32[1024,256]{1,0:T(8,128)S(1)} %get-tuple-element.19.matrix, s32[2,256]{1,0:T(2,128)S(1)} %get-tuple-element.20.pivots), custom_call_target="tpu_custom_call" | custom-call | tf_op jit(solution)/shard_map/prepare/pallas_call | solution.py:346
  7.3 2.3 %collective-permute-start.5 = (f32[128,256]{1,0:T(8,128)S(1)}, f32[128,256]{1,0:T(8,128)S(1)}, u32[]{:S(2)}, u32[]{:S(2)}) collective-permute-start(f32[128,256]{1,0:T(8,128)S(1)} %release.3), channel_id=1, source_target_pairs={{0,6},{1,7},{2,0},{3,1},{4,2},{5,3},{6,4},{7,5},{8,14},{9,15},{10,... | collective-permute-start | bytes 393224 | tf_op jit(solution)/shard_map/ppermute | solution.py:310
  9.6 0.5 %collective-permute-done.1.other.refs_3_.refs_1_ = f32[128,256]{1,0:T(8,128)S(1)} collective-permute-done((f32[128,256]{1,0:T(8,128)S(1)}, f32[128,256]{1,0:T(8,128)S(1)}, u32[]{:S(2)}, u32[]{:S(2)}) %collective-permute-start.1) | collective-permute-done | bytes 131104 | tf_op jit(solution)/shard_map/ppermute | solution.py:310
  10.3 1.2 %collective-permute-done.received.refs_0_ = f32[256,256]{1,0:T(8,128)S(1)} collective-permute-done((f32[256,256]{1,0:T(8,128)S(1)}, f32[256,256]{1,0:T(8,128)S(1)}, u32[]{:S(2)}, u32[]{:S(2)}) %collective-permute-start) | collective-permute-done | bytes 262176 | tf_op jit(solution)/shard_map/ppermute | solution.py:368
  11.5 0.2 collective-permute-done.2.refs_0_.refs_6_.refs_4_
  11.7 0.1 broadcast_in_dim.13.owner
  11.9 1.6 %collective-permute-start.3 = (f32[256,256]{1,0:T(8,128)S(1)}, f32[256,256]{1,0:T(8,128)S(1)}, u32[]{:S(2)}, u32[]{:S(2)}) collective-permute-start(f32[256,256]{1,0:T(8,128)S(1)} %merge.2.sent.before), channel_id=1, source_target_pairs={{0,16},{1,9},{2,18},{3,11},{4,20},{5,13},{6,22},{7,15},{8,24},{9,1... | collective-permute-start | bytes 786440 | tf_op jit(solution)/shard_map/ppermute | solution.py:368
  13.6 0.5 %collective-permute-start.7 = (f32[128,256]{1,0:T(8,128)S(1)}, f32[128,256]{1,0:T(8,128)S(1)}, u32[]{:S(2)}, u32[]{:S(2)}) collective-permute-start(f32[128,256]{1,0:T(8,128)S(1)} %collective-permute-done.5.refs_5_.refs_3_), channel_id=1, source_target_pairs={{0,1},{1,0},{2,3},{3,2},{4,5},{5,4},{6,7},{7,6},{8,9},{9,8},{10,11... | collective-permute-start | bytes 393224 | tf_op jit(solution)/shard_map/ppermute | solution.py:314
  14.1 3.9 %collective-permute-done.4.refs_4_.refs_2_ = f32[128,256]{1,0:T(8,128)S(1)} collective-permute-done((f32[128,256]{1,0:T(8,128)S(1)}, f32[128,256]{1,0:T(8,128)S(1)}, u32[]{:S(2)}, u32[]{:S(2)}) %collective-permute-start.4) | collective-permute-done | bytes 131104 | tf_op jit(solution)/shard_map/ppermute | solution.py:310
  18.1 1.2 %collective-permute-done.6.refs_7_.refs_5_ = f32[128,256]{1,0:T(8,128)S(1)} collective-permute-done((f32[128,256]{1,0:T(8,128)S(1)}, f32[128,256]{1,0:T(8,128)S(1)}, u32[]{:S(2)}, u32[]{:S(2)}) %collective-permute-start.6) | collective-permute-done | bytes 131104 | tf_op jit(solution)/shard_map/ppermute | solution.py:314
  19.3 1.3 %solve.1 = (f32[256,256]{1,0:T(8,128)S(1)}, f32[256,256]{1,0:T(8,128)S(1)}, f32[256,256]{1,0:T(8,128)S(1)}) custom-call(f32[1024,256]{1,0:T(8,128)S(1)} %get-tuple-element.19.matrix, s32[2,256]{1,0:T(2,128)S(1)} %get-tuple-element.20.pivots, f32[2,256,256]{2,1,0:T(8,128)S(1)} %copy-done, s32[256,256]{1,0:T(8,128)S(1)} %broadcast_in_dim.13.owner, ...), custom_call_target="tpu_custom_call" | custom-call | tf_op jit(solution)/shard_map/solve/pallas_call | solution.py:346
  20.6 1.6 %collective-permute-start.13 = (f32[256,256]{1,0:T(8,128)S(1)}, f32[256,256]{1,0:T(8,128)S(1)}, u32[]{:S(2)}, u32[]{:S(2)}) collective-permute-start(f32[256,256]{1,0:T(8,128)S(1)} %get-tuple-element.30.before.sent), channel_id=1, source_target_pairs={{0,8},{1,17},{2,10},{3,19},{4,12},{5,21},{6,14},{7,23},{8,0},{9,25... | collective-permute-start | bytes 786440 | tf_op jit(solution)/shard_map/ppermute | solution.py:368
  22.2 1.5 %collective-permute-start.9 = (f32[128,256]{1,0:T(8,128)S(1)}, f32[128,256]{1,0:T(8,128)S(1)}, u32[]{:S(2)}, u32[]{:S(2)}) collective-permute-start(f32[128,256]{1,0:T(8,128)S(1)} %release.4), channel_id=1, source_target_pairs={{0,4},{1,5},{2,6},{3,7},{4,0},{5,1},{6,2},{7,3},{8,12},{9,13},{10,... | collective-permute-start | bytes 393224 | tf_op jit(solution)/shard_map/ppermute | solution.py:310
  23.6 3.4 %collective-permute-done.13.received.refs_0_ = f32[256,256]{1,0:T(8,128)S(1)} collective-permute-done((f32[256,256]{1,0:T(8,128)S(1)}, f32[256,256]{1,0:T(8,128)S(1)}, u32[]{:S(2)}, u32[]{:S(2)}) %collective-permute-start.13) | collective-permute-done | bytes 262176 | tf_op jit(solution)/shard_map/ppermute | solution.py:368
  27.2 1.6 %collective-permute-start.14 = (f32[256,256]{1,0:T(8,128)S(1)}, f32[256,256]{1,0:T(8,128)S(1)}, u32[]{:S(2)}, u32[]{:S(2)}) collective-permute-start(f32[256,256]{1,0:T(8,128)S(1)} %merge.3.sent), channel_id=1, source_target_pairs={{0,16},{1,9},{2,18},{3,11},{4,20},{5,13},{6,22},{7,15},{8,24},{9,1... | collective-permute-start | bytes 786440 | tf_op jit(solution)/shard_map/ppermute | solution.py:368
  29.0 3.5 %collective-permute-done.9.far.refs_2_ = f32[128,256]{1,0:T(8,128)S(1)} collective-permute-done((f32[128,256]{1,0:T(8,128)S(1)}, f32[128,256]{1,0:T(8,128)S(1)}, u32[]{:S(2)}, u32[]{:S(2)}) %collective-permute-start.9) | collective-permute-done | bytes 131104 | tf_op jit(solution)/shard_map/ppermute | solution.py:310
  32.6 1.1 %update.1 = (f32[1024,256]{1,0:T(8,128)S(1)}, f32[256,256]{1,0:T(8,128)S(1)}) custom-call(f32[1024,256]{1,0:T(8,128)S(1)} %get-tuple-element.21.base, s32[2,256]{1,0:T(2,128)S(1)} %get-tuple-element.20.pivots, f32[256,256]{1,0:T(8,128)S(1)} %get-tuple-element.25.upper_in, f32[256,256]{1,0:T(8,128)S(1)} %get-tuple-element.26.displaced_in, ...), custom_call_target="tpu_custom_call" | custom-call | tf_op jit(solution)/shard_map/update/pallas_call | solution.py:346
  33.7 0.2 collective-permute-done.11.refs_3_
  33.9 0.3 halve.1
  34.3 1.9 %finish.1 = f32[1024,256]{1,0:T(8,128)} custom-call(f32[1024,256]{1,0:T(8,128)S(1)} %get-tuple-element.27.base, s32[2,256]{1,0:T(2,128)S(1)} %get-tuple-element.20.pivots, f32[2,256,256]{2,1,0:T(8,128)S(1)} %copy-done, s32[256,256]{1,0:T(8,128)S(1)} %broadcast_in_dim.15.owner, f32[256,256]{1,0:T(8,128)S(1)} %get-tuple-element.28.top, ...), custom_call_target="tpu_custom_call" | custom-call | tf_op jit(solution)/shard_map/finish/pallas_call | solution.py:346
  (27 shorter events, 0.7 us)
Async XLA Ops:
  1.4 8.7 %collective-permute-start.1 = (f32[128,256]{1,0:T(8,128)S(1)}, f32[128,256]{1,0:T(8,128)S(1)}, u32[]{:S(2)}, u32[]{:S(2)}) collective-permute-start(f32[128,256]{1,0:T(8,128)S(1)} %get-tuple-element.24.one.panel.refs_2_.refs_0_), channel_id=1, source_target_pairs={{0,2},{1,3},{2,4},{3,5},{4,6},{5,7},{6,0},{7,1},{8,10},{9,11},{10,... | collective-permute-start | bytes 393224 | tf_op jit(solution)/shard_map/ppermute | solution.py:310
  5.0 6.4 %collective-permute-start = (f32[256,256]{1,0:T(8,128)S(1)}, f32[256,256]{1,0:T(8,128)S(1)}, u32[]{:S(2)}, u32[]{:S(2)}) collective-permute-start(f32[256,256]{1,0:T(8,128)S(1)} %first_slots.1.sent), channel_id=1, source_target_pairs={{0,8},{1,17},{2,10},{3,19},{4,12},{5,21},{6,14},{7,23},{8,0},{9,25... | collective-permute-start | bytes 786440 | tf_op jit(solution)/shard_map/ppermute | solution.py:368
  7.3 6.3 %collective-permute-start.5 = (f32[128,256]{1,0:T(8,128)S(1)}, f32[128,256]{1,0:T(8,128)S(1)}, u32[]{:S(2)}, u32[]{:S(2)}) collective-permute-start(f32[128,256]{1,0:T(8,128)S(1)} %release.3), channel_id=1, source_target_pairs={{0,6},{1,7},{2,0},{3,1},{4,2},{5,3},{6,4},{7,5},{8,14},{9,15},{10,... | collective-permute-start | bytes 393224 | tf_op jit(solution)/shard_map/ppermute | solution.py:310
  10.1 1.6 %collective-permute-start.2 = (f32[256,256]{1,0:T(8,128)S(1)}, f32[256,256]{1,0:T(8,128)S(1)}, u32[]{:S(2)}, u32[]{:S(2)}) collective-permute-start(f32[256,256]{1,0:T(8,128)S(1)} %stack.1), channel_id=1, source_target_pairs={{0,1},{1,0},{2,3},{3,2},{4,5},{5,4},{6,7},{7,6},{8,9},{9,8},{10,11... | collective-permute-start | bytes 786440 | tf_op jit(solution)/shard_map/ppermute | solution.py:314
  10.2 7.7 %collective-permute-start.4 = (f32[128,256]{1,0:T(8,128)S(1)}, f32[128,256]{1,0:T(8,128)S(1)}, u32[]{:S(2)}, u32[]{:S(2)}) collective-permute-start(f32[128,256]{1,0:T(8,128)S(1)} %collective-permute-done.1.other.refs_3_.refs_1_), channel_id=1, source_target_pairs={{0,2},{1,3},{2,4},{3,5},{4,6},{5,7},{6,0},{7,1},{8,10},{9,11},{10,... | collective-permute-start | bytes 393224 | tf_op jit(solution)/shard_map/ppermute | solution.py:310
  11.9 7.4 %copy-start = (f32[2,256,256]{2,1,0:T(8,128)S(1)}, f32[2,256,256]{2,1,0:T(8,128)}, u32[]{:S(2)}) copy-start(f32[2,256,256]{2,1,0:T(8,128)} %inverse.3) | copy-start | bytes 1572868
  11.9 7.4 %collective-permute-start.3 = (f32[256,256]{1,0:T(8,128)S(1)}, f32[256,256]{1,0:T(8,128)S(1)}, u32[]{:S(2)}, u32[]{:S(2)}) collective-permute-start(f32[256,256]{1,0:T(8,128)S(1)} %merge.2.sent.before), channel_id=1, source_target_pairs={{0,16},{1,9},{2,18},{3,11},{4,20},{5,13},{6,22},{7,15},{8,24},{9,1... | collective-permute-start | bytes 786440 | tf_op jit(solution)/shard_map/ppermute | solution.py:368
  13.6 4.4 %collective-permute-start.8 = (f32[128,256]{1,0:T(8,128)S(1)}, f32[128,256]{1,0:T(8,128)S(1)}, u32[]{:S(2)}, u32[]{:S(2)}) collective-permute-start(f32[128,256]{1,0:T(8,128)S(1)} %get-tuple-element.29.panel.own.before.refs_0_), channel_id=1, source_target_pairs={{0,1},{1,0},{2,3},{3,2},{4,5},{5,4},{6,7},{7,6},{8,9},{9,8},{10,11... | collective-permute-start | bytes 393224 | tf_op jit(solution)/shard_map/ppermute | solution.py:314
  13.6 4.5 %collective-permute-start.7 = (f32[128,256]{1,0:T(8,128)S(1)}, f32[128,256]{1,0:T(8,128)S(1)}, u32[]{:S(2)}, u32[]{:S(2)}) collective-permute-start(f32[128,256]{1,0:T(8,128)S(1)} %collective-permute-done.5.refs_5_.refs_3_), channel_id=1, source_target_pairs={{0,1},{1,0},{2,3},{3,2},{4,5},{5,4},{6,7},{7,6},{8,9},{9,8},{10,11... | collective-permute-start | bytes 393224 | tf_op jit(solution)/shard_map/ppermute | solution.py:314
  18.0 1.3 %collective-permute-start.6 = (f32[128,256]{1,0:T(8,128)S(1)}, f32[128,256]{1,0:T(8,128)S(1)}, u32[]{:S(2)}, u32[]{:S(2)}) collective-permute-start(f32[128,256]{1,0:T(8,128)S(1)} %collective-permute-done.4.refs_4_.refs_2_), channel_id=1, source_target_pairs={{0,1},{1,0},{2,3},{3,2},{4,5},{5,4},{6,7},{7,6},{8,9},{9,8},{10,11... | collective-permute-start | bytes 393224 | tf_op jit(solution)/shard_map/ppermute | solution.py:314
  18.0 10.9 %collective-permute-start.10 = (f32[272,256]{1,0:T(8,128)S(1)}, f32[272,256]{1,0:T(8,128)S(1)}, u32[]{:S(2)}, u32[]{:S(2)}) collective-permute-start(f32[272,256]{1,0:T(8,128)S(1)} %pack.1), channel_id=1, source_target_pairs={{0,2},{1,7},{2,4},{3,1},{4,6},{5,3},{6,0},{7,5},{8,10},{9,15},{10,... | collective-permute-start | bytes 835592 | tf_op jit(solution)/shard_map/ppermute | solution.py:332
  20.6 6.4 %collective-permute-start.13 = (f32[256,256]{1,0:T(8,128)S(1)}, f32[256,256]{1,0:T(8,128)S(1)}, u32[]{:S(2)}, u32[]{:S(2)}) collective-permute-start(f32[256,256]{1,0:T(8,128)S(1)} %get-tuple-element.30.before.sent), channel_id=1, source_target_pairs={{0,8},{1,17},{2,10},{3,19},{4,12},{5,21},{6,14},{7,23},{8,0},{9,25... | collective-permute-start | bytes 786440 | tf_op jit(solution)/shard_map/ppermute | solution.py:368
  22.2 10.3 %collective-permute-start.9 = (f32[128,256]{1,0:T(8,128)S(1)}, f32[128,256]{1,0:T(8,128)S(1)}, u32[]{:S(2)}, u32[]{:S(2)}) collective-permute-start(f32[128,256]{1,0:T(8,128)S(1)} %release.4), channel_id=1, source_target_pairs={{0,4},{1,5},{2,6},{3,7},{4,0},{5,1},{6,2},{7,3},{8,12},{9,13},{10,... | collective-permute-start | bytes 393224 | tf_op jit(solution)/shard_map/ppermute | solution.py:310
  27.2 7.0 %collective-permute-start.14 = (f32[256,256]{1,0:T(8,128)S(1)}, f32[256,256]{1,0:T(8,128)S(1)}, u32[]{:S(2)}, u32[]{:S(2)}) collective-permute-start(f32[256,256]{1,0:T(8,128)S(1)} %merge.3.sent), channel_id=1, source_target_pairs={{0,16},{1,9},{2,18},{3,11},{4,20},{5,13},{6,22},{7,15},{8,24},{9,1... | collective-permute-start | bytes 786440 | tf_op jit(solution)/shard_map/ppermute | solution.py:368
  28.9 4.8 %collective-permute-start.12 = (f32[240,256]{1,0:T(8,128)S(1)}, f32[240,256]{1,0:T(8,128)S(1)}, u32[]{:S(2)}, u32[]{:S(2)}) collective-permute-start(f32[240,256]{1,0:T(8,128)S(1)} %release.5), channel_id=1, source_target_pairs={{0,1},{1,0},{2,3},{3,2},{4,5},{5,4},{6,7},{7,6},{8,9},{9,8},{10,11... | collective-permute-start | bytes 737288 | tf_op jit(solution)/shard_map/ppermute | solution.py:314
  32.5 1.4 %collective-permute-start.11 = (f32[144,256]{1,0:T(8,128)S(1)}, f32[144,256]{1,0:T(8,128)S(1)}, u32[]{:S(2)}, u32[]{:S(2)}) collective-permute-start(f32[144,256]{1,0:T(8,128)S(1)} %tails.1), channel_id=1, source_target_pairs={{0,1},{1,0},{2,3},{3,2},{4,5},{5,4},{6,7},{7,6},{8,9},{9,8},{10,11... | collective-permute-start | bytes 442376 | tf_op jit(solution)/shard_map/ppermute | solution.py:314

commit v10 on v9

--- a/solution.py
+++ b/solution.py
@@ -15,6 +15,8 @@
 BF16 = jnp.bfloat16
 NOWHERE = -(1 << 24)
 TAIL = 16
+COST = {"holders": 3 * 10**9}
+PARTS = 4
 SPARE = 16
 
 
@@ -64,8 +66,10 @@
 
 def load(matrix, pivots, panels, held, chosen, *refs):
     blocks, sems = refs[:-1], refs[-1]
-    sources = [panels.at[step] for step in range(len(blocks))] + [pivots, matrix]
-    targets = [*blocks, chosen, held]
+    rows = held.shape[0] // PARTS
+    parts = [pl.ds(part * rows, rows) for part in range(PARTS)]
+    sources = [panels.at[step] for step in range(len(blocks))] + [pivots] + [matrix.at[part, :] for part in parts]
+    targets = [*blocks, chosen] + [held.at[part, :] for part in parts]
     copies = [pltpu.make_async_copy(*pair, sems.at[i]) for i, pair in enumerate(zip(sources, targets))]
     for copy in copies:
         copy.start()
@@ -83,6 +87,11 @@
         term = pick(gather, split(matrix[start : start + width, :]))
         total = term if total is None else total + term
     out[...] = total
+
+
+def holders(rows_dev, pivots, *owners):
+    for step, owner in enumerate(owners):
+        owner[...] = jnp.broadcast_to(column_of(pivots[step : step + 1, :]) // rows_dev, owner.shape)
 
 
 def prepare(matrix, pivots, base, ahead, places):
@@ -149,8 +158,8 @@
 def ring_blocks(refs):
     chips = (len(refs) + 1) // 2
     mine, joint, rest = refs[:chips], refs[chips], refs[chips + 1 :]
-    rows = mine[0].shape[0]
-    others = [rows_of(joint, 0, 2), rows_of(joint, 1, 2), *rest]
+    rows = next(ref for ref in [*mine, *rest] if ref is not None).shape[0]
+    others = [joint if joint is None else rows_of(joint, half, 2) for half in range(2)] + list(rest)
     chip, core = lax.axis_index("pcol") // 2, lax.rem(lax.axis_index("pcol"), 2)
     found = []
     for order, distance in enumerate(ring_order(chips)):
@@ -186,10 +195,35 @@
     return found
 
 
-def solve(bits, step, matrix, pivots, inverse, owner, ahead, places, sent, *refs):
+def panel_rows(places, blocks):
+    high = low = None
+    for block, start in blocks:
+        rows = block.shape[0]
+        gather = one_hot(places[:, :rows] - start, iota((places.shape[0], rows), 1))
+        block_high, block_low = split(block[...])
+        term_high, term_low = product(gather, block_high), product(gather, block_low)
+        high = term_high if high is None else high + term_high
+        low = term_low if low is None else low + term_low
+    return high, low
+
+
+def late_blocks(chips):
+    return [chips + chips // 2 - 1, 2 * chips - 2]
+
+
+def collect(late, places, *refs):
+    blocks, (high, low) = list(refs[:-2]), refs[-2:]
+    for position in late:
+        blocks.insert(position, None)
+    found_high, found_low = panel_rows(places, [pair for pair in ring_blocks(blocks) if pair[0] is not None])
+    high[...] = found_high.astype(BF16)
+    low[...] = found_low.astype(BF16)
+
+
+def solve(bits, step, late, matrix, pivots, inverse, owner, ahead, places, sent, *refs):
     refs = list(refs)
     received = [refs.pop(0) for _ in bits]
-    blocks, (upper_out, displaced_out, slots_out) = refs[:-3], refs[-3:]
+    high, low, *found, upper_out, displaced_out, slots = refs
     rows_dev = matrix.shape[0]
     picked = picked_rows(bits, sent, received, owner)
     width = picked.shape[0]
@@ -197,18 +231,13 @@
     upper_out[...] = upper
     displaced = displaced_rows(bits, received, matrix[step * width : (step + 1) * width, :])
     displaced_out[...] = displaced
-    high = low = None
-    for block, start in ring_blocks(blocks):
-        rows = block.shape[0]
-        local = places[:, :rows] - start
-        gather = one_hot(local, iota((width, rows), 1))
-        block_high, block_low = split(block[...])
-        term_high, term_low = product(gather, block_high), product(gather, block_low)
-        high = term_high if high is None else high + term_high
-        low = term_low if low is None else low + term_low
     moved = one_hot(places[...], local_rows(pivots, step, rows_dev))
-    factor = (high.astype(BF16), low.astype(BF16))
-    slots_out[...] = ahead[...] + (pick(moved, split(displaced)) - dot(factor, split(upper)))
+    blocks = [None] * (rows_dev // found[0].shape[0] - 1)
+    for position, block in zip(late, found):
+        blocks[position] = block
+    rest_high, rest_low = panel_rows(places, [pair for pair in ring_blocks(blocks) if pair[0] is not None])
+    factor = ((high[...].astype(F32) + rest_high).astype(BF16), (low[...].astype(F32) + rest_low).astype(BF16))
+    slots[...] = ahead[...] + (pick(moved, split(displaced)) - dot(factor, split(upper)))
 
 
 def assemble(step, blocks, rows_dev, width, high, low):
@@ -350,6 +379,7 @@
             out_specs=out_specs or jax.tree.map(lambda _: VMEM, outs),
             scratch_shapes=scratch,
             compiler_params=GRANT,
+            cost_estimate=pl.CostEstimate(COST[name], 0, 0) if name in COST else None,
             name=name,
         )(*operands)
 
@@ -377,17 +407,17 @@
         [pltpu.with_memory_space_constraint(x, pltpu.HBM) for x in (matrix, pivots, l_panels)],
         [full, shape(pivots.shape, pivots.dtype)] + [block] * steps,
         specs=[HBM] * 3,
-        scratch=[pltpu.SemaphoreType.DMA((2 + steps,))],
+        scratch=[pltpu.SemaphoreType.DMA((1 + steps + PARTS,))],
     )
     slots = call(first_slots, "first_slots", [matrix, pivots], square)
-
-    owner = jnp.broadcast_to((pivots // rows_dev)[:, :, None], (steps, width, columns))
 
     near = across(own[1], process_columns)
 
     def after(panel, before, rows=block.shape[0]):
         return call(release, "release", [panel, before], shape((rows, block.shape[1]), F32), specs=[VMEM, ANY])
 
+    indices = shape((width, columns), jnp.int32)
+    owner = call(functools.partial(holders, rows_dev), "holders", [pivots], [indices] * steps)
     base, ahead, places = call(
         prepare, "prepare", [matrix, pivots], [full, square, shape((width, width), jnp.int32)]
     )
@@ -398,8 +428,11 @@
     sent, received = exchange(slots, 0, [joint])
     two = shape((2 * block.shape[0] + SPARE, block.shape[1]), F32)
     pair = call(pack, "pack", [own[1], near, sent], two, specs=[VMEM, VMEM, ANY])
-    operands = [matrix, pivots, l_inverse, owner[0], ahead, places, sent, *received, *first]
-    upper, displaced, slots = call(functools.partial(solve, bits, 0), "solve", operands, [square] * 3)
+    late = late_blocks(process_columns // 2)
+    early = [piece for position, piece in enumerate(first) if position not in late]
+    factor = call(functools.partial(collect, late), "collect", [places, *early], [shape((width, width), BF16)] * 2)
+    operands = [matrix, pivots, l_inverse, owner[0], ahead, places, sent, *received, *factor, *[first[position] for position in late]]
+    upper, displaced, slots = call(functools.partial(solve, bits, 0, late), "solve", operands, [square] * 3)
     far = shift(after(own[1], slots), process_columns // 4, process_columns)
     pairs = passed(pair, process_columns)
     rows = block.shape[0]
@@ -413,7 +446,7 @@
         [full, square],
         scratch=halves,
     )
-    sent, received = exchange(slots, 1)
+    sent, received = exchange(slots, 1, [top])
     high, low = call(
         functools.partial(halve, 1, rows_dev, width),
         "halve",

time: 36.3 us -> 36.3 us (level)
  waiting for transfers between devices: 14.1 us -> 14.6 us
    ppermute x4, waiting for transfers between devices: 4.59 us -> 3.59 us  [exchange(): received.append(lax.ppermute(sent, ('prow', 'pcol'), pairs))]
    ppermute x4, waiting for transfers between devices: 7.84 us -> 8.77 us  [shift(): lax.ppermute(block, 'pcol', [(i, (i + 2 * distance) % count) for i in ran...]
    ppermute x6, waiting for transfers between devices: 1.69 us -> 2.22 us  [across(): return lax.ppermute(block, 'pcol', [(i, i ^ 1) for i in range(count)])]
    ppermute x4, starting transfers between devices: 6.9 us -> 6.54 us  [shift(): lax.ppermute(block, 'pcol', [(i, (i + 2 * distance) % count) for i in ran...]
    pallas_call x15 -> x17, Pallas kernels: 7.49 us -> 7.69 us  [call(): pl.pallas_call(kernel, out_shape=outs, in_specs=specs or [VMEM] * len(ope...]
  transfers between devices with their start and end apart: 15 -> 15, of which waited for: 8 -> 8; matrix products, arithmetic and copies ran while one was open for 1% -> 0% of each run, Pallas kernels for 12% -> 12%
where the time goes in v10:
time: 36.3 us; the launch traced here: 36.2 us
  waiting for transfers between devices  14.6 us (40%)
  starting transfers between devices  13.8 us (38%)
  Pallas kernels  7.69 us (21%)
    ppermute x4, waiting for transfers between devices, shift(): lax.ppermute(block, 'pcol', [(i, (i + 2 * distance) % count) for i in ran...  8.77 us
    pallas_call x17, Pallas kernels, call(): pl.pallas_call(kernel, out_shape=outs, in_specs=specs or [VMEM] * len(ope...  7.69 us
    ppermute x4, starting transfers between devices, shift(): lax.ppermute(block, 'pcol', [(i, (i + 2 * distance) % count) for i in ran...  6.54 us
    ppermute x4, starting transfers between devices, exchange(): received.append(lax.ppermute(sent, ('prow', 'pcol'), pairs))  6.39 us
    ppermute x4, waiting for transfers between devices, exchange(): received.append(lax.ppermute(sent, ('prow', 'pcol'), pairs))  3.59 us
    ppermute x6, waiting for transfers between devices, across(): return lax.ppermute(block, 'pcol', [(i, i ^ 1) for i in range(count)])  2.22 us
    ppermute x6, starting transfers between devices, across(): return lax.ppermute(block, 'pcol', [(i, i ^ 1) for i in range(count)])  0.78 us
  transfers between devices with their start and end apart: 15, of which 8 were waited for; matrix products, arithmetic and copies ran while one was open for 0% of the time, Pallas kernels for 12%

profile of v10, /device:TPU:0, one launch (start us, length us, event | category | flops | bytes accessed | tf_op | source)
XLA Modules:
  0.0 36.2 jit_solution(399683477458750602)
XLA Ops:
  0.0 1.4 %load.1 = (f32[1024,256]{1,0:T(8,128)S(1)}, s32[2,256]{1,0:T(2,128)S(1)}, f32[128,256]{1,0:T(8,128)S(1)}, f32[128,256]{1,0:T(8,128)S(1)}) custom-call(f32[1024,256]{1,0:T(8,128)} %matrix.1, s32[2,256]{1,0:T(2,128)} %pivots.1, f32[2,128,256]{2,1,0:T(8,128)} %panels.1), custom_call_target="tpu_custom_call" | custom-call | tf_op jit(solution)/shard_map/load/pallas_call | solution.py:375
  1.4 3.1 %collective-permute-start.1 = (f32[128,256]{1,0:T(8,128)S(1)}, f32[128,256]{1,0:T(8,128)S(1)}, u32[]{:S(2)}, u32[]{:S(2)}) collective-permute-start(f32[128,256]{1,0:T(8,128)S(1)} %get-tuple-element.29.one.panel.refs_0_), channel_id=1, source_target_pairs={{0,2},{1,3},{2,4},{3,5},{4,6},{5,7},{6,0},{7,1},{8,10},{9,11},{10,... | collective-permute-start | bytes 393224 | tf_op jit(solution)/shard_map/ppermute | solution.py:339
  4.5 0.5 %first_slots.1.sent = f32[256,256]{1,0:T(8,128)S(1)} custom-call(f32[1024,256]{1,0:T(8,128)S(1)} %get-tuple-element.23.matrix, s32[2,256]{1,0:T(2,128)S(1)} %get-tuple-element.24.pivots), custom_call_target="tpu_custom_call" | custom-call | tf_op jit(solution)/shard_map/first_slots/pallas_call | solution.py:375
  5.0 1.6 %collective-permute-start = (f32[256,256]{1,0:T(8,128)S(1)}, f32[256,256]{1,0:T(8,128)S(1)}, u32[]{:S(2)}, u32[]{:S(2)}) collective-permute-start(f32[256,256]{1,0:T(8,128)S(1)} %first_slots.1.sent), channel_id=1, source_target_pairs={{0,8},{1,17},{2,10},{3,19},{4,12},{5,21},{6,14},{7,23},{8,0},{9,25... | collective-permute-start | bytes 786440 | tf_op jit(solution)/shard_map/ppermute | solution.py:398
  6.6 0.7 %prepare.1 = (f32[1024,256]{1,0:T(8,128)S(1)}, f32[256,256]{1,0:T(8,128)S(1)}, s32[256,256]{1,0:T(8,128)S(1)}) custom-call(f32[1024,256]{1,0:T(8,128)S(1)} %get-tuple-element.23.matrix, s32[2,256]{1,0:T(2,128)S(1)} %get-tuple-element.24.pivots), custom_call_target="tpu_custom_call" | custom-call | tf_op jit(solution)/shard_map/prepare/pallas_call | solution.py:375
  7.3 2.3 %collective-permute-start.5 = (f32[128,256]{1,0:T(8,128)S(1)}, f32[128,256]{1,0:T(8,128)S(1)}, u32[]{:S(2)}, u32[]{:S(2)}) collective-permute-start(f32[128,256]{1,0:T(8,128)S(1)} %release.3), channel_id=1, source_target_pairs={{0,6},{1,7},{2,0},{3,1},{4,2},{5,3},{6,4},{7,5},{8,14},{9,15},{10,... | collective-permute-start | bytes 393224 | tf_op jit(solution)/shard_map/ppermute | solution.py:339
  9.6 0.5 %collective-permute-done.1.other.refs_1_ = f32[128,256]{1,0:T(8,128)S(1)} collective-permute-done((f32[128,256]{1,0:T(8,128)S(1)}, f32[128,256]{1,0:T(8,128)S(1)}, u32[]{:S(2)}, u32[]{:S(2)}) %collective-permute-start.1) | collective-permute-done | bytes 131104 | tf_op jit(solution)/shard_map/ppermute | solution.py:339
  10.2 0.3 holders.1
  10.5 1.0 %collective-permute-done.received.refs_0_ = f32[256,256]{1,0:T(8,128)S(1)} collective-permute-done((f32[256,256]{1,0:T(8,128)S(1)}, f32[256,256]{1,0:T(8,128)S(1)}, u32[]{:S(2)}, u32[]{:S(2)}) %collective-permute-start) | collective-permute-done | bytes 262176 | tf_op jit(solution)/shard_map/ppermute | solution.py:398
  11.8 1.6 %collective-permute-start.3 = (f32[256,256]{1,0:T(8,128)S(1)}, f32[256,256]{1,0:T(8,128)S(1)}, u32[]{:S(2)}, u32[]{:S(2)}) collective-permute-start(f32[256,256]{1,0:T(8,128)S(1)} %merge.2.sent.before), channel_id=1, source_target_pairs={{0,16},{1,9},{2,18},{3,11},{4,20},{5,13},{6,22},{7,15},{8,24},{9,1... | collective-permute-start | bytes 786440 | tf_op jit(solution)/shard_map/ppermute | solution.py:398
  13.4 0.5 %collective-permute-start.7 = (f32[128,256]{1,0:T(8,128)S(1)}, f32[128,256]{1,0:T(8,128)S(1)}, u32[]{:S(2)}, u32[]{:S(2)}) collective-permute-start(f32[128,256]{1,0:T(8,128)S(1)} %collective-permute-done.5.refs_3_), channel_id=1, source_target_pairs={{0,1},{1,0},{2,3},{3,2},{4,5},{5,4},{6,7},{7,6},{8,9},{9,8},{10,11... | collective-permute-start | bytes 393224 | tf_op jit(solution)/shard_map/ppermute | solution.py:343
  13.9 4.2 %collective-permute-done.4.refs_2_ = f32[128,256]{1,0:T(8,128)S(1)} collective-permute-done((f32[128,256]{1,0:T(8,128)S(1)}, f32[128,256]{1,0:T(8,128)S(1)}, u32[]{:S(2)}, u32[]{:S(2)}) %collective-permute-start.4) | collective-permute-done | bytes 131104 | tf_op jit(solution)/shard_map/ppermute | solution.py:339
  18.3 0.6 %collect.1 = (bf16[256,256]{1,0:T(8,128)(2,1)S(1)}, bf16[256,256]{1,0:T(8,128)(2,1)S(1)}) custom-call(s32[256,256]{1,0:T(8,128)S(1)} %get-tuple-element.28.before.places, f32[128,256]{1,0:T(8,128)S(1)} %get-tuple-element.29.one.panel.refs_0_, f32[128,256]{1,0:T(8,128)S(1)} %collective-permute-done.1.other.refs_1_, ...), custom_call_target="tpu_custom_call" | custom-call | tf_op jit(solution)/shard_map/collect/pallas_call | solution.py:375
  18.9 0.7 %collective-permute-done.6.refs_4_.refs_5_ = f32[128,256]{1,0:T(8,128)S(1)} collective-permute-done((f32[128,256]{1,0:T(8,128)S(1)}, f32[128,256]{1,0:T(8,128)S(1)}, u32[]{:S(2)}, u32[]{:S(2)}) %collective-permute-start.6) | collective-permute-done | bytes 131104 | tf_op jit(solution)/shard_map/ppermute | solution.py:343
  19.5 0.7 %solve.1 = (f32[256,256]{1,0:T(8,128)S(1)}, f32[256,256]{1,0:T(8,128)S(1)}, f32[256,256]{1,0:T(8,128)S(1)}) custom-call(f32[1024,256]{1,0:T(8,128)S(1)} %get-tuple-element.23.matrix, s32[2,256]{1,0:T(2,128)S(1)} %get-tuple-element.24.pivots, f32[2,256,256]{2,1,0:T(8,128)S(1)} %copy-done, s32[256,256]{1,0:T(8,128)S(1)} %get-tuple-element.26.owner, ...), custom_call_target="tpu_custom_call" | custom-call | tf_op jit(solution)/shard_map/solve/pallas_call | solution.py:375
  20.2 1.6 %collective-permute-start.13 = (f32[256,256]{1,0:T(8,128)S(1)}, f32[256,256]{1,0:T(8,128)S(1)}, u32[]{:S(2)}, u32[]{:S(2)}) collective-permute-start(f32[256,256]{1,0:T(8,128)S(1)} %get-tuple-element.38.before.sent), channel_id=1, source_target_pairs={{0,8},{1,17},{2,10},{3,19},{4,12},{5,21},{6,14},{7,23},{8,0},{9,25... | collective-permute-start | bytes 786440 | tf_op jit(solution)/shard_map/ppermute | solution.py:398
  21.8 1.1 %collective-permute-start.9 = (f32[128,256]{1,0:T(8,128)S(1)}, f32[128,256]{1,0:T(8,128)S(1)}, u32[]{:S(2)}, u32[]{:S(2)}) collective-permute-start(f32[128,256]{1,0:T(8,128)S(1)} %release.4), channel_id=1, source_target_pairs={{0,4},{1,5},{2,6},{3,7},{4,0},{5,1},{6,2},{7,3},{8,12},{9,13},{10,... | collective-permute-start | bytes 393224 | tf_op jit(solution)/shard_map/ppermute | solution.py:339
  22.9 1.1 %update.1 = (f32[1024,256]{1,0:T(8,128)S(1)}, f32[256,256]{1,0:T(8,128)S(1)}) custom-call(f32[1024,256]{1,0:T(8,128)S(1)} %get-tuple-element.25.base, s32[2,256]{1,0:T(2,128)S(1)} %get-tuple-element.24.pivots, f32[256,256]{1,0:T(8,128)S(1)} %get-tuple-element.32.upper_in, f32[256,256]{1,0:T(8,128)S(1)} %get-tuple-element.33.displaced_in, ...), custom_call_target="tpu_custom_call" | custom-call | tf_op jit(solution)/shard_map/update/pallas_call | solution.py:375
  24.0 2.6 %collective-permute-done.13.received.refs_0_ = f32[256,256]{1,0:T(8,128)S(1)} collective-permute-done((f32[256,256]{1,0:T(8,128)S(1)}, f32[256,256]{1,0:T(8,128)S(1)}, u32[]{:S(2)}, u32[]{:S(2)}) %collective-permute-start.13) | collective-permute-done | bytes 262176 | tf_op jit(solution)/shard_map/ppermute | solution.py:398
  26.8 1.6 %collective-permute-start.14 = (f32[256,256]{1,0:T(8,128)S(1)}, f32[256,256]{1,0:T(8,128)S(1)}, u32[]{:S(2)}, u32[]{:S(2)}) collective-permute-start(f32[256,256]{1,0:T(8,128)S(1)} %merge.3.sent), channel_id=1, source_target_pairs={{0,16},{1,9},{2,18},{3,11},{4,20},{5,13},{6,22},{7,15},{8,24},{9,1... | collective-permute-start | bytes 786440 | tf_op jit(solution)/shard_map/ppermute | solution.py:398
  28.5 4.1 %collective-permute-done.9.far.refs_2_ = f32[128,256]{1,0:T(8,128)S(1)} collective-permute-done((f32[128,256]{1,0:T(8,128)S(1)}, f32[128,256]{1,0:T(8,128)S(1)}, u32[]{:S(2)}, u32[]{:S(2)}) %collective-permute-start.9) | collective-permute-done | bytes 131104 | tf_op jit(solution)/shard_map/ppermute | solution.py:339
  32.7 1.3 %collective-permute-done.11.refs_3_ = f32[144,256]{1,0:T(8,128)S(1)} collective-permute-done((f32[144,256]{1,0:T(8,128)S(1)}, f32[144,256]{1,0:T(8,128)S(1)}, u32[]{:S(2)}, u32[]{:S(2)}) %collective-permute-start.11) | collective-permute-done | bytes 147488 | tf_op jit(solution)/shard_map/ppermute | solution.py:343
  34.0 0.3 halve.1
  34.3 1.9 %finish.1 = f32[1024,256]{1,0:T(8,128)} custom-call(f32[1024,256]{1,0:T(8,128)S(1)} %get-tuple-element.34.base, s32[2,256]{1,0:T(2,128)S(1)} %get-tuple-element.24.pivots, f32[2,256,256]{2,1,0:T(8,128)S(1)} %copy-done, s32[256,256]{1,0:T(8,128)S(1)} %get-tuple-element.35.owner, f32[256,256]{1,0:T(8,128)S(1)} %get-tuple-element.36.refs_0_.top, ...), custom_call_target="tpu_custom_call" | custom-call | tf_op jit(solution)/shard_map/finish/pallas_call | solution.py:375
  (25 shorter events, 0.9 us)
Async XLA Ops:
  1.4 8.7 %collective-permute-start.1 = (f32[128,256]{1,0:T(8,128)S(1)}, f32[128,256]{1,0:T(8,128)S(1)}, u32[]{:S(2)}, u32[]{:S(2)}) collective-permute-start(f32[128,256]{1,0:T(8,128)S(1)} %get-tuple-element.29.one.panel.refs_0_), channel_id=1, source_target_pairs={{0,2},{1,3},{2,4},{3,5},{4,6},{5,7},{6,0},{7,1},{8,10},{9,11},{10,... | collective-permute-start | bytes 393224 | tf_op jit(solution)/shard_map/ppermute | solution.py:339
  5.0 6.4 %collective-permute-start = (f32[256,256]{1,0:T(8,128)S(1)}, f32[256,256]{1,0:T(8,128)S(1)}, u32[]{:S(2)}, u32[]{:S(2)}) collective-permute-start(f32[256,256]{1,0:T(8,128)S(1)} %first_slots.1.sent), channel_id=1, source_target_pairs={{0,8},{1,17},{2,10},{3,19},{4,12},{5,21},{6,14},{7,23},{8,0},{9,25... | collective-permute-start | bytes 786440 | tf_op jit(solution)/shard_map/ppermute | solution.py:398
  7.3 6.1 %collective-permute-start.5 = (f32[128,256]{1,0:T(8,128)S(1)}, f32[128,256]{1,0:T(8,128)S(1)}, u32[]{:S(2)}, u32[]{:S(2)}) collective-permute-start(f32[128,256]{1,0:T(8,128)S(1)} %release.3), channel_id=1, source_target_pairs={{0,6},{1,7},{2,0},{3,1},{4,2},{5,3},{6,4},{7,5},{8,14},{9,15},{10,... | collective-permute-start | bytes 393224 | tf_op jit(solution)/shard_map/ppermute | solution.py:339
  10.1 1.6 %collective-permute-start.2 = (f32[256,256]{1,0:T(8,128)S(1)}, f32[256,256]{1,0:T(8,128)S(1)}, u32[]{:S(2)}, u32[]{:S(2)}) collective-permute-start(f32[256,256]{1,0:T(8,128)S(1)} %stack.1), channel_id=1, source_target_pairs={{0,1},{1,0},{2,3},{3,2},{4,5},{5,4},{6,7},{7,6},{8,9},{9,8},{10,11... | collective-permute-start | bytes 786440 | tf_op jit(solution)/shard_map/ppermute | solution.py:343
  10.4 7.7 %collective-permute-start.4 = (f32[128,256]{1,0:T(8,128)S(1)}, f32[128,256]{1,0:T(8,128)S(1)}, u32[]{:S(2)}, u32[]{:S(2)}) collective-permute-start(f32[128,256]{1,0:T(8,128)S(1)} %collective-permute-done.1.other.refs_1_), channel_id=1, source_target_pairs={{0,2},{1,3},{2,4},{3,5},{4,6},{5,7},{6,0},{7,1},{8,10},{9,11},{10,... | collective-permute-start | bytes 393224 | tf_op jit(solution)/shard_map/ppermute | solution.py:339
  11.8 7.8 %collective-permute-start.3 = (f32[256,256]{1,0:T(8,128)S(1)}, f32[256,256]{1,0:T(8,128)S(1)}, u32[]{:S(2)}, u32[]{:S(2)}) collective-permute-start(f32[256,256]{1,0:T(8,128)S(1)} %merge.2.sent.before), channel_id=1, source_target_pairs={{0,16},{1,9},{2,18},{3,11},{4,20},{5,13},{6,22},{7,15},{8,24},{9,1... | collective-permute-start | bytes 786440 | tf_op jit(solution)/shard_map/ppermute | solution.py:398
  13.4 4.8 %collective-permute-start.8 = (f32[128,256]{1,0:T(8,128)S(1)}, f32[128,256]{1,0:T(8,128)S(1)}, u32[]{:S(2)}, u32[]{:S(2)}) collective-permute-start(f32[128,256]{1,0:T(8,128)S(1)} %get-tuple-element.37.panel.own.before.refs_0_), channel_id=1, source_target_pairs={{0,1},{1,0},{2,3},{3,2},{4,5},{5,4},{6,7},{7,6},{8,9},{9,8},{10,11... | collective-permute-start | bytes 393224 | tf_op jit(solution)/shard_map/ppermute | solution.py:343
  13.4 5.4 %collective-permute-start.7 = (f32[128,256]{1,0:T(8,128)S(1)}, f32[128,256]{1,0:T(8,128)S(1)}, u32[]{:S(2)}, u32[]{:S(2)}) collective-permute-start(f32[128,256]{1,0:T(8,128)S(1)} %collective-permute-done.5.refs_3_), channel_id=1, source_target_pairs={{0,1},{1,0},{2,3},{3,2},{4,5},{5,4},{6,7},{7,6},{8,9},{9,8},{10,11... | collective-permute-start | bytes 393224 | tf_op jit(solution)/shard_map/ppermute | solution.py:343
  18.2 1.3 %collective-permute-start.6 = (f32[128,256]{1,0:T(8,128)S(1)}, f32[128,256]{1,0:T(8,128)S(1)}, u32[]{:S(2)}, u32[]{:S(2)}) collective-permute-start(f32[128,256]{1,0:T(8,128)S(1)} %collective-permute-done.4.refs_2_), channel_id=1, source_target_pairs={{0,1},{1,0},{2,3},{3,2},{4,5},{5,4},{6,7},{7,6},{8,9},{9,8},{10,11... | collective-permute-start | bytes 393224 | tf_op jit(solution)/shard_map/ppermute | solution.py:343
  18.2 1.3 %copy-start = (f32[2,256,256]{2,1,0:T(8,128)S(1)}, f32[2,256,256]{2,1,0:T(8,128)}, u32[]{:S(2)}) copy-start(f32[2,256,256]{2,1,0:T(8,128)} %inverse.3) | copy-start | bytes 1572868
  18.2 10.2 %collective-permute-start.10 = (f32[272,256]{1,0:T(8,128)S(1)}, f32[272,256]{1,0:T(8,128)S(1)}, u32[]{:S(2)}, u32[]{:S(2)}) collective-permute-start(f32[272,256]{1,0:T(8,128)S(1)} %pack.1), channel_id=1, source_target_pairs={{0,2},{1,7},{2,4},{3,1},{4,6},{5,3},{6,0},{7,5},{8,10},{9,15},{10,... | collective-permute-start | bytes 835592 | tf_op jit(solution)/shard_map/ppermute | solution.py:361
  20.2 6.4 %collective-permute-start.13 = (f32[256,256]{1,0:T(8,128)S(1)}, f32[256,256]{1,0:T(8,128)S(1)}, u32[]{:S(2)}, u32[]{:S(2)}) collective-permute-start(f32[256,256]{1,0:T(8,128)S(1)} %get-tuple-element.38.before.sent), channel_id=1, source_target_pairs={{0,8},{1,17},{2,10},{3,19},{4,12},{5,21},{6,14},{7,23},{8,0},{9,25... | collective-permute-start | bytes 786440 | tf_op jit(solution)/shard_map/ppermute | solution.py:398
  21.8 10.7 %collective-permute-start.9 = (f32[128,256]{1,0:T(8,128)S(1)}, f32[128,256]{1,0:T(8,128)S(1)}, u32[]{:S(2)}, u32[]{:S(2)}) collective-permute-start(f32[128,256]{1,0:T(8,128)S(1)} %release.4), channel_id=1, source_target_pairs={{0,4},{1,5},{2,6},{3,7},{4,0},{5,1},{6,2},{7,3},{8,12},{9,13},{10,... | collective-permute-start | bytes 393224 | tf_op jit(solution)/shard_map/ppermute | solution.py:339
  26.8 7.6 %collective-permute-start.14 = (f32[256,256]{1,0:T(8,128)S(1)}, f32[256,256]{1,0:T(8,128)S(1)}, u32[]{:S(2)}, u32[]{:S(2)}) collective-permute-start(f32[256,256]{1,0:T(8,128)S(1)} %merge.3.sent), channel_id=1, source_target_pairs={{0,16},{1,9},{2,18},{3,11},{4,20},{5,13},{6,22},{7,15},{8,24},{9,1... | collective-permute-start | bytes 786440 | tf_op jit(solution)/shard_map/ppermute | solution.py:398
  28.4 4.3 %collective-permute-start.12 = (f32[240,256]{1,0:T(8,128)S(1)}, f32[240,256]{1,0:T(8,128)S(1)}, u32[]{:S(2)}, u32[]{:S(2)}) collective-permute-start(f32[240,256]{1,0:T(8,128)S(1)} %release.5), channel_id=1, source_target_pairs={{0,1},{1,0},{2,3},{3,2},{4,5},{5,4},{6,7},{7,6},{8,9},{9,8},{10,11... | collective-permute-start | bytes 737288 | tf_op jit(solution)/shard_map/ppermute | solution.py:343
  32.6 1.4 %collective-permute-start.11 = (f32[144,256]{1,0:T(8,128)S(1)}, f32[144,256]{1,0:T(8,128)S(1)}, u32[]{:S(2)}, u32[]{:S(2)}) collective-permute-start(f32[144,256]{1,0:T(8,128)S(1)} %tails.1), channel_id=1, source_target_pairs={{0,1},{1,0},{2,3},{3,2},{4,5},{5,4},{6,7},{7,6},{8,9},{9,8},{10,11... | collective-permute-start | bytes 442376 | tf_op jit(solution)/shard_map/ppermute | solution.py:343

commit v11 on v10

--- a/solution.py
+++ b/solution.py
@@ -14,10 +14,8 @@
 F32 = jnp.float32
 BF16 = jnp.bfloat16
 NOWHERE = -(1 << 24)
-TAIL = 16
-COST = {"holders": 3 * 10**9}
+COST = {"holders": 3 * 10**9, "update": 5 * 10**9, "down_piece": 15 * 10**8}
 PARTS = 4
-SPARE = 16
 
 
 def product(left, right):
@@ -64,27 +62,29 @@
     return jnp.where(offset >= 0, offset, top)
 
 
-def load(matrix, pivots, panels, held, chosen, *refs):
+def load(pivots, panels, chosen, *refs):
     blocks, sems = refs[:-1], refs[-1]
-    rows = held.shape[0] // PARTS
-    parts = [pl.ds(part * rows, rows) for part in range(PARTS)]
-    sources = [panels.at[step] for step in range(len(blocks))] + [pivots] + [matrix.at[part, :] for part in parts]
-    targets = [*blocks, chosen] + [held.at[part, :] for part in parts]
-    copies = [pltpu.make_async_copy(*pair, sems.at[i]) for i, pair in enumerate(zip(sources, targets))]
+    sources = [panels.at[step] for step in range(len(blocks))] + [pivots]
+    copies = [pltpu.make_async_copy(*pair, sems.at[i]) for i, pair in enumerate(zip(sources, [*blocks, chosen]))]
     for copy in copies:
         copy.start()
     for copy in copies:
         copy.wait()
 
 
-def first_slots(matrix, pivots, out):
-    rows_dev = matrix.shape[0]
+def first_slots(pivots, matrix, out, held, sems):
+    chunks, rows_dev = sems.shape[0], held.shape[0]
+    rows = rows_dev // chunks
+    parts = [pl.ds(part * rows, rows) for part in range(chunks)]
+    copies = [pltpu.make_async_copy(matrix.at[part, :], held.at[part, :], sems.at[i]) for i, part in enumerate(parts)]
+    for copy in copies:
+        copy.start()
     place = column_of(slot_rows(pivots, 0, rows_dev))
-    width = place.shape[0]
     total = None
-    for start in range(0, rows_dev, width):
-        gather = one_hot(place, iota((width, width), 1) + start)
-        term = pick(gather, split(matrix[start : start + width, :]))
+    for part, copy in enumerate(copies):
+        copy.wait()
+        gather = one_hot(place, iota((place.shape[0], rows), 1) + part * rows)
+        term = pick(gather, split(held[part * rows : (part + 1) * rows, :]))
         total = term if total is None else total + term
     out[...] = total
 
@@ -165,33 +165,6 @@
     for order, distance in enumerate(ring_order(chips)):
         found.append((mine[order], place_of(chip - distance, core, chips, rows)))
         found.append((others[order], place_of(chip - distance, 1 - core, chips, rows)))
-    return found
-
-
-def pair_blocks(refs):
-    own, near, far, far_back, *rest = refs
-    rows = own.shape[0]
-    hops, tail = len(rest) // 2, tail_of(rows)
-    pairs, back = rest[:hops], rest[hops:]
-    chips = 2 * hops + 2
-    chip, core = lax.axis_index("pcol") // 2, lax.rem(lax.axis_index("pcol"), 2)
-    opposite = chip + chips // 2
-    found = [
-        (own, place_of(chip, core, chips, rows)),
-        (near, place_of(chip, 1 - core, chips, rows)),
-        (far, place_of(opposite, core, chips, rows)),
-        (far_back.at[pl.ds(0, rows), :], place_of(opposite, 1 - core, chips, rows)),
-    ]
-    for hop in range(hops):
-        along = (hop + 1) * (1 - 2 * core)
-        for half in range(2):
-            place = place_of(chip - along, core if half == 0 else 1 - core, chips, rows)
-            found.append((pairs[hop].at[pl.ds(half * rows, rows), :], place))
-            place = place_of(chip + along, 1 - core if half == 0 else core, chips, rows)
-            held = rows - half * tail
-            found.append((back[hop].at[pl.ds(half * rows, held), :], place))
-        if tail:
-            found.append((far_back.at[pl.ds(rows + hop * tail, tail), :], pl.multiple_of(place + held, tail)))
     return found
 
 
@@ -251,7 +224,7 @@
 
 
 def halve(step, rows_dev, width, *refs):
-    assemble(step, pair_blocks(refs[:-2]), rows_dev, width, refs[-2], refs[-1])
+    assemble(step, ring_blocks(refs[:-2]), rows_dev, width, refs[-2], refs[-1])
 
 
 def update(step, base, pivots, upper_in, displaced_in, *refs):
@@ -306,33 +279,12 @@
     out[rows:, :] = other[...]
 
 
-def pack(own, near, before, out):
-    rows = own.shape[0]
-    out[:rows, :] = own[...]
-    out[rows : 2 * rows, :] = near[...]
-    out[2 * rows :, :] = own[: out.shape[0] - 2 * rows, :]
-
-
 def ring_order(chips):
     return [0] + list(range(1, chips // 2 + 1)) + list(range(chips - 1, chips // 2, -1))
 
 
-def tail_of(rows):
-    return TAIL if rows > TAIL else 0
-
-
-def tails(far, *refs):
-    pairs, out = refs[:-1], refs[-1]
-    rows = far.shape[0]
-    out[:rows, :] = far[...]
-    for hop, pair in enumerate(pairs):
-        start, tail = rows + hop * tail_of(rows), tail_of(rows)
-        if tail:
-            out[start : start + tail, :] = pair[2 * rows - tail : 2 * rows, :]
-
-
 def release(panel, before, out):
-    out[...] = panel[: out.shape[0], :]
+    out[...] = panel[...]
 
 
 def shift(block, distance, count):
@@ -343,23 +295,15 @@
     return lax.ppermute(block, "pcol", [(i, i ^ 1) for i in range(count)])
 
 
-def forwarded(block, down, count):
+def forwarded(block, up, down, count, held=lambda piece: piece):
     chips = count // 2
     own = [block]
     for distance in ring_order(chips)[1:]:
         if distance <= chips // 2:
-            own.append(shift(own[-1], 1, count))
+            own.append(held(shift(up, 1, count)) if distance == 1 else shift(own[-1], 1, count))
         else:
             own.append(shift(down if distance == chips - 1 else own[-1], -1, count))
     return own
-
-
-def passed(pair, count):
-    onward = [(i, (i + (2 if i % 2 == 0 else -2)) % count) for i in range(count)]
-    pairs = [pair]
-    for _ in range(count // 4 - 1):
-        pairs.append(lax.ppermute(pairs[-1], "pcol", onward))
-    return pairs[1:]
 
 
 def per_device(mesh, matrix, l_panels, l_inverse, pivots):
@@ -401,44 +345,43 @@
     chunks = rows_dev // width
     halves = [pltpu.VMEM((rows_dev, l_panels.shape[2]), BF16)] * 2
     block = shape(l_panels.shape[1:], F32)
-    matrix, pivots, *own = call(
+    chosen, *own = call(
         load,
         "load",
-        [pltpu.with_memory_space_constraint(x, pltpu.HBM) for x in (matrix, pivots, l_panels)],
-        [full, shape(pivots.shape, pivots.dtype)] + [block] * steps,
-        specs=[HBM] * 3,
-        scratch=[pltpu.SemaphoreType.DMA((1 + steps + PARTS,))],
-    )
-    slots = call(first_slots, "first_slots", [matrix, pivots], square)
-
-    near = across(own[1], process_columns)
-
-    def after(panel, before, rows=block.shape[0]):
-        return call(release, "release", [panel, before], shape((rows, block.shape[1]), F32), specs=[VMEM, ANY])
+        [pltpu.with_memory_space_constraint(x, pltpu.HBM) for x in (pivots, l_panels)],
+        [shape(pivots.shape, pivots.dtype)] + [block] * steps,
+        specs=[HBM] * 2,
+        scratch=[pltpu.SemaphoreType.DMA((1 + steps,))],
+    )
+    pivots = chosen
+    slots, matrix = call(
+        first_slots,
+        "first_slots",
+        [pivots, pltpu.with_memory_space_constraint(matrix, pltpu.HBM)],
+        [square, full],
+        specs=[VMEM, HBM],
+        scratch=[pltpu.SemaphoreType.DMA((PARTS,))],
+    )
+
+    def after(panel, before, name):
+        return call(release, name, [panel, before], block, specs=[VMEM, ANY])
+
+    def with_other_core(mine, name):
+        joint = call(stack, name, mine[:2], shape((2 * block.shape[0], block.shape[1]), F32))
+        return mine + [across(piece, process_columns) for piece in [joint, *mine[2:]]]
 
     indices = shape((width, columns), jnp.int32)
     owner = call(functools.partial(holders, rows_dev), "holders", [pivots], [indices] * steps)
     base, ahead, places = call(
         prepare, "prepare", [matrix, pivots], [full, square, shape((width, width), jnp.int32)]
     )
-    first = forwarded(own[0], after(own[0], places), process_columns)
-    joint = call(stack, "stack", first[:2], shape((2 * block.shape[0], block.shape[1]), F32))
-    joint = across(joint, process_columns)
-    first += [joint] + [across(piece, process_columns) for piece in first[2:]]
-    sent, received = exchange(slots, 0, [joint])
-    two = shape((2 * block.shape[0] + SPARE, block.shape[1]), F32)
-    pair = call(pack, "pack", [own[1], near, sent], two, specs=[VMEM, VMEM, ANY])
+    first = with_other_core(forwarded(own[0], own[0], after(own[0], places, "down_first"), process_columns), "stack_first")
+    sent, received = exchange(slots, 0, [first[process_columns // 2]])
     late = late_blocks(process_columns // 2)
     early = [piece for position, piece in enumerate(first) if position not in late]
     factor = call(functools.partial(collect, late), "collect", [places, *early], [shape((width, width), BF16)] * 2)
     operands = [matrix, pivots, l_inverse, owner[0], ahead, places, sent, *received, *factor, *[first[position] for position in late]]
     upper, displaced, slots = call(functools.partial(solve, bits, 0, late), "solve", operands, [square] * 3)
-    far = shift(after(own[1], slots), process_columns // 4, process_columns)
-    pairs = passed(pair, process_columns)
-    rows = block.shape[0]
-    joint = call(tails, "tails", [far, *pairs], shape((rows + tail_of(rows) * len(pairs), block.shape[1]), F32))
-    second = [own[1], near, far, across(joint, process_columns)]
-    second += pairs + [across(after(piece, own[1], 2 * rows - tail_of(rows)), process_columns) for piece in pairs]
     base, top = call(
         functools.partial(update, 0),
         "update",
@@ -446,6 +389,11 @@
         [full, square],
         scratch=halves,
     )
+    up = after(own[1], sent, "up_second")
+    down = after(own[1], slots, "down_second")
+    second = forwarded(own[1], up, down, process_columns, lambda piece: after(piece, top, "onward"))
+    second[-1] = after(second[-1], slots, "down_piece")
+    second = with_other_core(second, "stack_second")
     sent, received = exchange(slots, 1, [top])
     high, low = call(
         functools.partial(halve, 1, rows_dev, width),

time: 36.3 us -> 37.5 us (1.033)
  starting transfers between devices: 13.8 us -> 14.8 us
  waiting for transfers between devices: 14.6 us -> 13.6 us
  Pallas kernels: 7.69 us -> 8.66 us
    ppermute x4 -> x6, starting transfers between devices: 6.54 us -> 8.71 us  [shift(): lax.ppermute(block, 'pcol', [(i, (i + 2 * distance) % count) for i in ran...]
    ppermute x4, waiting for transfers between devices: 3.59 us -> 1.78 us  [exchange(): received.append(lax.ppermute(sent, ('prow', 'pcol'), pairs))]
    ppermute x4 -> x6, waiting for transfers between devices: 8.77 us -> 10.2 us  [shift(): lax.ppermute(block, 'pcol', [(i, (i + 2 * distance) % count) for i in ran...]
    pallas_call x17 -> x18, Pallas kernels: 7.69 us -> 8.66 us  [call(): pl.pallas_call(kernel, out_shape=outs, in_specs=specs or [VMEM] * len(ope...]
    ppermute x4, starting transfers between devices: 6.39 us -> 5.46 us  [exchange(): received.append(lax.ppermute(sent, ('prow', 'pcol'), pairs))]
    ppermute x6, waiting for transfers between devices: 2.22 us -> 1.7 us  [across(): return lax.ppermute(block, 'pcol', [(i, i ^ 1) for i in range(count)])]
  transfers between devices with their start and end apart: 15 -> 16, of which waited for: 8 -> 10; matrix products, arithmetic and copies ran while one was open for 0% -> 0% of each run, Pallas kernels for 12% -> 16%
where the time goes in v11:
time: 37.5 us; the launch traced here: 37.3 us
  starting transfers between devices  14.8 us (39%)
  waiting for transfers between devices  13.6 us (36%)
  Pallas kernels  8.66 us (23%)
    ppermute x6, waiting for transfers between devices, shift(): lax.ppermute(block, 'pcol', [(i, (i + 2 * distance) % count) for i in ran...  10.2 us
    ppermute x6, starting transfers between devices, shift(): lax.ppermute(block, 'pcol', [(i, (i + 2 * distance) % count) for i in ran...  8.71 us
    pallas_call x18, Pallas kernels, call(): pl.pallas_call(kernel, out_shape=outs, in_specs=specs or [VMEM] * len(ope...  8.66 us
    ppermute x4, starting transfers between devices, exchange(): received.append(lax.ppermute(sent, ('prow', 'pcol'), pairs))  5.46 us
    ppermute x4, waiting for transfers between devices, exchange(): received.append(lax.ppermute(sent, ('prow', 'pcol'), pairs))  1.78 us
    ppermute x6, waiting for transfers between devices, across(): return lax.ppermute(block, 'pcol', [(i, i ^ 1) for i in range(count)])  1.7 us
  transfers between devices with their start and end apart: 16, of which 10 were waited for; matrix products, arithmetic and copies ran while one was open for 0% of the time, Pallas kernels for 16%

profile of v11, /device:TPU:0, one launch (start us, length us, event | category | flops | bytes accessed | tf_op | source)
XLA Modules:
  0.0 37.3 jit_solution(2704684854517196012)
XLA Ops:
  0.0 1.0 %load.1 = (s32[2,256]{1,0:T(2,128)S(1)}, f32[128,256]{1,0:T(8,128)S(1)}, f32[128,256]{1,0:T(8,128)S(1)}) custom-call(s32[2,256]{1,0:T(2,128)} %pivots.1, f32[2,128,256]{2,1,0:T(8,128)} %panels.1), custom_call_target="tpu_custom_call" | custom-call | tf_op jit(solution)/shard_map/load/pallas_call | solution.py:319
  1.0 3.1 %collective-permute-start.1 = (f32[128,256]{1,0:T(8,128)S(1)}, f32[128,256]{1,0:T(8,128)S(1)}, u32[]{:S(2)}, u32[]{:S(2)}) collective-permute-start(f32[128,256]{1,0:T(8,128)S(1)} %get-tuple-element.31.one.panel.refs_0_), channel_id=1, source_target_pairs={{0,2},{1,3},{2,4},{3,5},{4,6},{5,7},{6,0},{7,1},{8,10},{9,11},{10,... | collective-permute-start | bytes 393224 | tf_op jit(solution)/shard_map/ppermute | solution.py:291
  4.1 1.9 %first_slots.1 = (f32[256,256]{1,0:T(8,128)S(1)}, f32[1024,256]{1,0:T(8,128)S(1)}) custom-call(s32[2,256]{1,0:T(2,128)S(1)} %get-tuple-element.24.pivots, f32[1024,256]{1,0:T(8,128)} %matrix.1), custom_call_target="tpu_custom_call" | custom-call | tf_op jit(solution)/shard_map/first_slots/pallas_call | solution.py:319
  6.0 1.6 %collective-permute-start = (f32[256,256]{1,0:T(8,128)S(1)}, f32[256,256]{1,0:T(8,128)S(1)}, u32[]{:S(2)}, u32[]{:S(2)}) collective-permute-start(f32[256,256]{1,0:T(8,128)S(1)} %get-tuple-element.30.sent), channel_id=1, source_target_pairs={{0,8},{1,17},{2,10},{3,19},{4,12},{5,21},{6,14},{7,23},{8,0},{9,25... | collective-permute-start | bytes 786440 | tf_op jit(solution)/shard_map/ppermute | solution.py:342
  7.6 0.7 %prepare.1 = (f32[1024,256]{1,0:T(8,128)S(1)}, f32[256,256]{1,0:T(8,128)S(1)}, s32[256,256]{1,0:T(8,128)S(1)}) custom-call(f32[1024,256]{1,0:T(8,128)S(1)} %get-tuple-element.25.matrix, s32[2,256]{1,0:T(2,128)S(1)} %get-tuple-element.24.pivots), custom_call_target="tpu_custom_call" | custom-call | tf_op jit(solution)/shard_map/prepare/pallas_call | solution.py:319
  8.3 2.3 %collective-permute-start.5 = (f32[128,256]{1,0:T(8,128)S(1)}, f32[128,256]{1,0:T(8,128)S(1)}, u32[]{:S(2)}, u32[]{:S(2)}) collective-permute-start(f32[128,256]{1,0:T(8,128)S(1)} %down_first.1), channel_id=1, source_target_pairs={{0,6},{1,7},{2,0},{3,1},{4,2},{5,3},{6,4},{7,5},{8,14},{9,15},{10,... | collective-permute-start | bytes 393224 | tf_op jit(solution)/shard_map/ppermute | solution.py:291
  11.0 1.4 %collective-permute-done.received.refs_0_ = f32[256,256]{1,0:T(8,128)S(1)} collective-permute-done((f32[256,256]{1,0:T(8,128)S(1)}, f32[256,256]{1,0:T(8,128)S(1)}, u32[]{:S(2)}, u32[]{:S(2)}) %collective-permute-start) | collective-permute-done | bytes 262176 | tf_op jit(solution)/shard_map/ppermute | solution.py:342
  12.5 1.6 %collective-permute-start.3 = (f32[256,256]{1,0:T(8,128)S(1)}, f32[256,256]{1,0:T(8,128)S(1)}, u32[]{:S(2)}, u32[]{:S(2)}) collective-permute-start(f32[256,256]{1,0:T(8,128)S(1)} %merge.2.sent.before), channel_id=1, source_target_pairs={{0,16},{1,9},{2,18},{3,11},{4,20},{5,13},{6,22},{7,15},{8,24},{9,1... | collective-permute-start | bytes 786440 | tf_op jit(solution)/shard_map/ppermute | solution.py:342
  14.3 4.4 %collective-permute-done.4.refs_2_ = f32[128,256]{1,0:T(8,128)S(1)} collective-permute-done((f32[128,256]{1,0:T(8,128)S(1)}, f32[128,256]{1,0:T(8,128)S(1)}, u32[]{:S(2)}, u32[]{:S(2)}) %collective-permute-start.4) | collective-permute-done | bytes 131104 | tf_op jit(solution)/shard_map/ppermute | solution.py:291
  18.8 0.6 %collect.1 = (bf16[256,256]{1,0:T(8,128)(2,1)S(1)}, bf16[256,256]{1,0:T(8,128)(2,1)S(1)}) custom-call(s32[256,256]{1,0:T(8,128)S(1)} %get-tuple-element.29.before.places, f32[128,256]{1,0:T(8,128)S(1)} %get-tuple-element.31.one.panel.refs_0_, f32[128,256]{1,0:T(8,128)S(1)} %collective-permute-done.1.other.refs_1_, ...), custom_call_target="tpu_custom_call" | custom-call | tf_op jit(solution)/shard_map/collect/pallas_call | solution.py:319
  19.4 0.7 %collective-permute-done.6.refs_4_.refs_5_ = f32[128,256]{1,0:T(8,128)S(1)} collective-permute-done((f32[128,256]{1,0:T(8,128)S(1)}, f32[128,256]{1,0:T(8,128)S(1)}, u32[]{:S(2)}, u32[]{:S(2)}) %collective-permute-start.6) | collective-permute-done | bytes 131104 | tf_op jit(solution)/shard_map/ppermute | solution.py:295
  20.1 0.7 %solve.1 = (f32[256,256]{1,0:T(8,128)S(1)}, f32[256,256]{1,0:T(8,128)S(1)}, f32[256,256]{1,0:T(8,128)S(1)}) custom-call(f32[1024,256]{1,0:T(8,128)S(1)} %get-tuple-element.25.matrix, s32[2,256]{1,0:T(2,128)S(1)} %get-tuple-element.24.pivots, f32[2,256,256]{2,1,0:T(8,128)S(1)} %copy-done, s32[256,256]{1,0:T(8,128)S(1)} %get-tuple-element.27.owner, ...), custom_call_target="tpu_custom_call" | custom-call | tf_op jit(solution)/shard_map/solve/pallas_call | solution.py:319
  20.8 0.7 %collective-permute-start.14 = (f32[256,256]{1,0:T(8,128)S(1)}, f32[256,256]{1,0:T(8,128)S(1)}, u32[]{:S(2)}, u32[]{:S(2)}) collective-permute-start(f32[256,256]{1,0:T(8,128)S(1)} %get-tuple-element.40.before.sent), channel_id=1, source_target_pairs={{0,8},{1,17},{2,10},{3,19},{4,12},{5,21},{6,14},{7,23},{8,0},{9,25... | collective-permute-start | bytes 786440 | tf_op jit(solution)/shard_map/ppermute | solution.py:342
  21.5 3.2 %collective-permute-start.10 = (f32[128,256]{1,0:T(8,128)S(1)}, f32[128,256]{1,0:T(8,128)S(1)}, u32[]{:S(2)}, u32[]{:S(2)}) collective-permute-start(f32[128,256]{1,0:T(8,128)S(1)} %down_second.1), channel_id=1, source_target_pairs={{0,6},{1,7},{2,0},{3,1},{4,2},{5,3},{6,4},{7,5},{8,14},{9,15},{10,... | collective-permute-start | bytes 393224 | tf_op jit(solution)/shard_map/ppermute | solution.py:291
  24.7 1.1 %update.1 = (f32[1024,256]{1,0:T(8,128)S(1)}, f32[256,256]{1,0:T(8,128)S(1)}) custom-call(f32[1024,256]{1,0:T(8,128)S(1)} %get-tuple-element.26.base, s32[2,256]{1,0:T(2,128)S(1)} %get-tuple-element.24.pivots, f32[256,256]{1,0:T(8,128)S(1)} %get-tuple-element.34.upper_in, f32[256,256]{1,0:T(8,128)S(1)} %get-tuple-element.35.displaced_in, ...), custom_call_target="tpu_custom_call" | custom-call | flops 5000000000 | tf_op jit(solution)/shard_map/update/pallas_call | solution.py:319
  25.8 0.9 %collective-permute-done.8.panel = f32[128,256]{1,0:T(8,128)S(1)} collective-permute-done((f32[128,256]{1,0:T(8,128)S(1)}, f32[128,256]{1,0:T(8,128)S(1)}, u32[]{:S(2)}, u32[]{:S(2)}) %collective-permute-start.8) | collective-permute-done | bytes 131104 | tf_op jit(solution)/shard_map/ppermute | solution.py:291
  26.8 0.4 collective-permute-done.14.received.refs_0_
  27.3 1.6 %collective-permute-start.15 = (f32[256,256]{1,0:T(8,128)S(1)}, f32[256,256]{1,0:T(8,128)S(1)}, u32[]{:S(2)}, u32[]{:S(2)}) collective-permute-start(f32[256,256]{1,0:T(8,128)S(1)} %merge.3.sent), channel_id=1, source_target_pairs={{0,16},{1,9},{2,18},{3,11},{4,20},{5,13},{6,22},{7,15},{8,24},{9,1... | collective-permute-start | bytes 786440 | tf_op jit(solution)/shard_map/ppermute | solution.py:342
  28.9 0.5 %collective-permute-done.10.panel = f32[128,256]{1,0:T(8,128)S(1)} collective-permute-done((f32[128,256]{1,0:T(8,128)S(1)}, f32[128,256]{1,0:T(8,128)S(1)}, u32[]{:S(2)}, u32[]{:S(2)}) %collective-permute-start.10) | collective-permute-done | bytes 131104 | tf_op jit(solution)/shard_map/ppermute | solution.py:291
  29.3 4.3 %collective-permute-done.9.refs_2_ = f32[128,256]{1,0:T(8,128)S(1)} collective-permute-done((f32[128,256]{1,0:T(8,128)S(1)}, f32[128,256]{1,0:T(8,128)S(1)}, u32[]{:S(2)}, u32[]{:S(2)}) %collective-permute-start.9) | collective-permute-done | bytes 131104 | tf_op jit(solution)/shard_map/ppermute | solution.py:291
  33.6 0.5 %collective-permute-start.13 = (f32[128,256]{1,0:T(8,128)S(1)}, f32[128,256]{1,0:T(8,128)S(1)}, u32[]{:S(2)}, u32[]{:S(2)}) collective-permute-start(f32[128,256]{1,0:T(8,128)S(1)} %down_piece.1.refs_3_), channel_id=1, source_target_pairs={{0,1},{1,0},{2,3},{3,2},{4,5},{5,4},{6,7},{7,6},{8,9},{9,8},{10,11... | collective-permute-start | bytes 393224 | tf_op jit(solution)/shard_map/ppermute | solution.py:295
  34.1 0.8 %collective-permute-done.12.refs_5_ = f32[128,256]{1,0:T(8,128)S(1)} collective-permute-done((f32[128,256]{1,0:T(8,128)S(1)}, f32[128,256]{1,0:T(8,128)S(1)}, u32[]{:S(2)}, u32[]{:S(2)}) %collective-permute-start.12) | collective-permute-done | bytes 131104 | tf_op jit(solution)/shard_map/ppermute | solution.py:295
  35.1 0.3 halve.1
  35.4 1.9 %finish.1 = f32[1024,256]{1,0:T(8,128)} custom-call(f32[1024,256]{1,0:T(8,128)S(1)} %get-tuple-element.36.base, s32[2,256]{1,0:T(2,128)S(1)} %get-tuple-element.24.pivots, f32[2,256,256]{2,1,0:T(8,128)S(1)} %copy-done, s32[256,256]{1,0:T(8,128)S(1)} %get-tuple-element.37.owner, f32[256,256]{1,0:T(8,128)S(1)} %get-tuple-element.38.before.refs_0_.top, ...), custom_call_target="tpu_custom_call" | custom-call | tf_op jit(solution)/shard_map/finish/pallas_call | solution.py:319
  (28 shorter events, 1.2 us)
Async XLA Ops:
  1.0 9.6 %collective-permute-start.1 = (f32[128,256]{1,0:T(8,128)S(1)}, f32[128,256]{1,0:T(8,128)S(1)}, u32[]{:S(2)}, u32[]{:S(2)}) collective-permute-start(f32[128,256]{1,0:T(8,128)S(1)} %get-tuple-element.31.one.panel.refs_0_), channel_id=1, source_target_pairs={{0,2},{1,3},{2,4},{3,5},{4,6},{5,7},{6,0},{7,1},{8,10},{9,11},{10,... | collective-permute-start | bytes 393224 | tf_op jit(solution)/shard_map/ppermute | solution.py:291
  6.0 6.4 %collective-permute-start = (f32[256,256]{1,0:T(8,128)S(1)}, f32[256,256]{1,0:T(8,128)S(1)}, u32[]{:S(2)}, u32[]{:S(2)}) collective-permute-start(f32[256,256]{1,0:T(8,128)S(1)} %get-tuple-element.30.sent), channel_id=1, source_target_pairs={{0,8},{1,17},{2,10},{3,19},{4,12},{5,21},{6,14},{7,23},{8,0},{9,25... | collective-permute-start | bytes 786440 | tf_op jit(solution)/shard_map/ppermute | solution.py:342
  8.3 6.0 %collective-permute-start.5 = (f32[128,256]{1,0:T(8,128)S(1)}, f32[128,256]{1,0:T(8,128)S(1)}, u32[]{:S(2)}, u32[]{:S(2)}) collective-permute-start(f32[128,256]{1,0:T(8,128)S(1)} %down_first.1), channel_id=1, source_target_pairs={{0,6},{1,7},{2,0},{3,1},{4,2},{5,3},{6,4},{7,5},{8,14},{9,15},{10,... | collective-permute-start | bytes 393224 | tf_op jit(solution)/shard_map/ppermute | solution.py:291
  10.6 1.8 %collective-permute-start.2 = (f32[256,256]{1,0:T(8,128)S(1)}, f32[256,256]{1,0:T(8,128)S(1)}, u32[]{:S(2)}, u32[]{:S(2)}) collective-permute-start(f32[256,256]{1,0:T(8,128)S(1)} %stack_first.1), channel_id=1, source_target_pairs={{0,1},{1,0},{2,3},{3,2},{4,5},{5,4},{6,7},{7,6},{8,9},{9,8},{10,11... | collective-permute-start | bytes 786440 | tf_op jit(solution)/shard_map/ppermute | solution.py:295
  10.9 7.7 %collective-permute-start.4 = (f32[128,256]{1,0:T(8,128)S(1)}, f32[128,256]{1,0:T(8,128)S(1)}, u32[]{:S(2)}, u32[]{:S(2)}) collective-permute-start(f32[128,256]{1,0:T(8,128)S(1)} %collective-permute-done.1.other.refs_1_), channel_id=1, source_target_pairs={{0,2},{1,3},{2,4},{3,5},{4,6},{5,7},{6,0},{7,1},{8,10},{9,11},{10,... | collective-permute-start | bytes 393224 | tf_op jit(solution)/shard_map/ppermute | solution.py:291
  12.5 7.5 %collective-permute-start.3 = (f32[256,256]{1,0:T(8,128)S(1)}, f32[256,256]{1,0:T(8,128)S(1)}, u32[]{:S(2)}, u32[]{:S(2)}) collective-permute-start(f32[256,256]{1,0:T(8,128)S(1)} %merge.2.sent.before), channel_id=1, source_target_pairs={{0,16},{1,9},{2,18},{3,11},{4,20},{5,13},{6,22},{7,15},{8,24},{9,1... | collective-permute-start | bytes 786440 | tf_op jit(solution)/shard_map/ppermute | solution.py:342
  14.2 5.1 %collective-permute-start.7 = (f32[128,256]{1,0:T(8,128)S(1)}, f32[128,256]{1,0:T(8,128)S(1)}, u32[]{:S(2)}, u32[]{:S(2)}) collective-permute-start(f32[128,256]{1,0:T(8,128)S(1)} %collective-permute-done.5.refs_3_), channel_id=1, source_target_pairs={{0,1},{1,0},{2,3},{3,2},{4,5},{5,4},{6,7},{7,6},{8,9},{9,8},{10,11... | collective-permute-start | bytes 393224 | tf_op jit(solution)/shard_map/ppermute | solution.py:295
  18.7 1.3 %collective-permute-start.6 = (f32[128,256]{1,0:T(8,128)S(1)}, f32[128,256]{1,0:T(8,128)S(1)}, u32[]{:S(2)}, u32[]{:S(2)}) collective-permute-start(f32[128,256]{1,0:T(8,128)S(1)} %collective-permute-done.4.refs_2_), channel_id=1, source_target_pairs={{0,1},{1,0},{2,3},{3,2},{4,5},{5,4},{6,7},{7,6},{8,9},{9,8},{10,11... | collective-permute-start | bytes 393224 | tf_op jit(solution)/shard_map/ppermute | solution.py:295
  18.7 1.3 %copy-start = (f32[2,256,256]{2,1,0:T(8,128)S(1)}, f32[2,256,256]{2,1,0:T(8,128)}, u32[]{:S(2)}) copy-start(f32[2,256,256]{2,1,0:T(8,128)} %inverse.3) | copy-start | bytes 1572868
  18.7 7.9 %collective-permute-start.8 = (f32[128,256]{1,0:T(8,128)S(1)}, f32[128,256]{1,0:T(8,128)S(1)}, u32[]{:S(2)}, u32[]{:S(2)}) collective-permute-start(f32[128,256]{1,0:T(8,128)S(1)} %up_second.1), channel_id=1, source_target_pairs={{0,2},{1,3},{2,4},{3,5},{4,6},{5,7},{6,0},{7,1},{8,10},{9,11},{10,... | collective-permute-start | bytes 393224 | tf_op jit(solution)/shard_map/ppermute | solution.py:291
  20.8 6.4 %collective-permute-start.14 = (f32[256,256]{1,0:T(8,128)S(1)}, f32[256,256]{1,0:T(8,128)S(1)}, u32[]{:S(2)}, u32[]{:S(2)}) collective-permute-start(f32[256,256]{1,0:T(8,128)S(1)} %get-tuple-element.40.before.sent), channel_id=1, source_target_pairs={{0,8},{1,17},{2,10},{3,19},{4,12},{5,21},{6,14},{7,23},{8,0},{9,25... | collective-permute-start | bytes 786440 | tf_op jit(solution)/shard_map/ppermute | solution.py:342
  21.5 7.8 %collective-permute-start.10 = (f32[128,256]{1,0:T(8,128)S(1)}, f32[128,256]{1,0:T(8,128)S(1)}, u32[]{:S(2)}, u32[]{:S(2)}) collective-permute-start(f32[128,256]{1,0:T(8,128)S(1)} %down_second.1), channel_id=1, source_target_pairs={{0,6},{1,7},{2,0},{3,1},{4,2},{5,3},{6,4},{7,5},{8,14},{9,15},{10,... | collective-permute-start | bytes 393224 | tf_op jit(solution)/shard_map/ppermute | solution.py:291
  26.7 6.9 %collective-permute-start.9 = (f32[128,256]{1,0:T(8,128)S(1)}, f32[128,256]{1,0:T(8,128)S(1)}, u32[]{:S(2)}, u32[]{:S(2)}) collective-permute-start(f32[128,256]{1,0:T(8,128)S(1)} %onward.1.other.refs_1_), channel_id=1, source_target_pairs={{0,2},{1,3},{2,4},{3,5},{4,6},{5,7},{6,0},{7,1},{8,10},{9,11},{10,... | collective-permute-start | bytes 393224 | tf_op jit(solution)/shard_map/ppermute | solution.py:291
  26.8 7.3 %collective-permute-start.11 = (f32[256,256]{1,0:T(8,128)S(1)}, f32[256,256]{1,0:T(8,128)S(1)}, u32[]{:S(2)}, u32[]{:S(2)}) collective-permute-start(f32[256,256]{1,0:T(8,128)S(1)} %stack_second.1), channel_id=1, source_target_pairs={{0,1},{1,0},{2,3},{3,2},{4,5},{5,4},{6,7},{7,6},{8,9},{9,8},{10,11... | collective-permute-start | bytes 786440 | tf_op jit(solution)/shard_map/ppermute | solution.py:295
  27.3 8.2 %collective-permute-start.15 = (f32[256,256]{1,0:T(8,128)S(1)}, f32[256,256]{1,0:T(8,128)S(1)}, u32[]{:S(2)}, u32[]{:S(2)}) collective-permute-start(f32[256,256]{1,0:T(8,128)S(1)} %merge.3.sent), channel_id=1, source_target_pairs={{0,16},{1,9},{2,18},{3,11},{4,20},{5,13},{6,22},{7,15},{8,24},{9,1... | collective-permute-start | bytes 786440 | tf_op jit(solution)/shard_map/ppermute | solution.py:342
  33.6 1.3 %collective-permute-start.12 = (f32[128,256]{1,0:T(8,128)S(1)}, f32[128,256]{1,0:T(8,128)S(1)}, u32[]{:S(2)}, u32[]{:S(2)}) collective-permute-start(f32[128,256]{1,0:T(8,128)S(1)} %collective-permute-done.9.refs_2_), channel_id=1, source_target_pairs={{0,1},{1,0},{2,3},{3,2},{4,5},{5,4},{6,7},{7,6},{8,9},{9,8},{10,11... | collective-permute-start | bytes 393224 | tf_op jit(solution)/shard_map/ppermute | solution.py:295
  33.6 1.5 %collective-permute-start.13 = (f32[128,256]{1,0:T(8,128)S(1)}, f32[128,256]{1,0:T(8,128)S(1)}, u32[]{:S(2)}, u32[]{:S(2)}) collective-permute-start(f32[128,256]{1,0:T(8,128)S(1)} %down_piece.1.refs_3_), channel_id=1, source_target_pairs={{0,1},{1,0},{2,3},{3,2},{4,5},{5,4},{6,7},{7,6},{8,9},{9,8},{10,11... | collective-permute-start | bytes 393224 | tf_op jit(solution)/shard_map/ppermute | solution.py:295

commit v12 on v10

--- a/solution.py
+++ b/solution.py
@@ -14,10 +14,18 @@
 F32 = jnp.float32
 BF16 = jnp.bfloat16
 NOWHERE = -(1 << 24)
-TAIL = 16
-COST = {"holders": 3 * 10**9}
+COST = {
+    "holders": 3000 * 10**6,
+    "update": 5000 * 10**6,
+    "pair_piece": 2000 * 10**6,
+    "stack": 5000 * 10**6,
+    "far_piece": 3000 * 10**6,
+    "far_block": 5000 * 10**6,
+    "prepare": 600 * 10**6,
+    "down_block": 300 * 10**6,
+    "collect": 1 * 10**6,
+}
 PARTS = 4
-SPARE = 16
 
 
 def product(left, right):
@@ -171,8 +179,7 @@
 def pair_blocks(refs):
     own, near, far, far_back, *rest = refs
     rows = own.shape[0]
-    hops, tail = len(rest) // 2, tail_of(rows)
-    pairs, back = rest[:hops], rest[hops:]
+    hops = len(rest) // 2
     chips = 2 * hops + 2
     chip, core = lax.axis_index("pcol") // 2, lax.rem(lax.axis_index("pcol"), 2)
     opposite = chip + chips // 2
@@ -180,18 +187,14 @@
         (own, place_of(chip, core, chips, rows)),
         (near, place_of(chip, 1 - core, chips, rows)),
         (far, place_of(opposite, core, chips, rows)),
-        (far_back.at[pl.ds(0, rows), :], place_of(opposite, 1 - core, chips, rows)),
+        (far_back, place_of(opposite, 1 - core, chips, rows)),
     ]
     for hop in range(hops):
         along = (hop + 1) * (1 - 2 * core)
         for half in range(2):
-            place = place_of(chip - along, core if half == 0 else 1 - core, chips, rows)
-            found.append((pairs[hop].at[pl.ds(half * rows, rows), :], place))
-            place = place_of(chip + along, 1 - core if half == 0 else core, chips, rows)
-            held = rows - half * tail
-            found.append((back[hop].at[pl.ds(half * rows, held), :], place))
-        if tail:
-            found.append((far_back.at[pl.ds(rows + hop * tail, tail), :], pl.multiple_of(place + held, tail)))
+            owner = core if half == 0 else 1 - core
+            found.append((rows_of(rest[hop], half, 2), place_of(chip - along, owner, chips, rows)))
+            found.append((rows_of(rest[hops + hop], half, 2), place_of(chip + along, 1 - owner, chips, rows)))
     return found
 
 
@@ -285,16 +288,17 @@
     upper = split(upper_full)
     displaced = split(displaced_rows(bits, received, top[...]))
     copies = []
-    for start in range(0, rows_dev, width):
-        part = slice(start, start + width)
-        rows = iota((width, width), 0) + start
-        value = base[part, :] + (pick(one_hot(rows, offset), displaced) + dot((high[part, :], low[part, :]), upper))
-        if start == step * width:
-            value = jnp.where(lax.axis_index("prow") == 0, upper_full, value)
-        result[part, :] = value
-        copies.append(
-            pltpu.make_async_copy(result.at[pl.ds(start, width), :], out.at[pl.ds(start, width), :], sems.at[len(copies)])
-        )
+    part = rows_dev // sems.shape[0]
+    for start in range(0, rows_dev, part):
+        rows = slice(start, start + part)
+        gather = one_hot(iota((part, width), 0) + start, offset)
+        value = base[rows, :] + (pick(gather, displaced) + dot((high[rows, :], low[rows, :]), upper))
+        inside = start - step * width
+        if 0 <= inside < width:
+            value = jnp.where(lax.axis_index("prow") == 0, upper_full[inside : inside + part, :], value)
+        result[rows, :] = value
+        place = pl.ds(start, part)
+        copies.append(pltpu.make_async_copy(result.at[place, :], out.at[place, :], sems.at[len(copies)]))
         copies[-1].start()
     for copy in copies:
         copy.wait()
@@ -309,30 +313,15 @@
 def pack(own, near, before, out):
     rows = own.shape[0]
     out[:rows, :] = own[...]
-    out[rows : 2 * rows, :] = near[...]
-    out[2 * rows :, :] = own[: out.shape[0] - 2 * rows, :]
+    out[rows:, :] = near[...]
 
 
 def ring_order(chips):
     return [0] + list(range(1, chips // 2 + 1)) + list(range(chips - 1, chips // 2, -1))
 
 
-def tail_of(rows):
-    return TAIL if rows > TAIL else 0
-
-
-def tails(far, *refs):
-    pairs, out = refs[:-1], refs[-1]
-    rows = far.shape[0]
-    out[:rows, :] = far[...]
-    for hop, pair in enumerate(pairs):
-        start, tail = rows + hop * tail_of(rows), tail_of(rows)
-        if tail:
-            out[start : start + tail, :] = pair[2 * rows - tail : 2 * rows, :]
-
-
 def release(panel, before, out):
-    out[...] = panel[: out.shape[0], :]
+    out[...] = panel[...]
 
 
 def shift(block, distance, count):
@@ -413,32 +402,28 @@
 
     near = across(own[1], process_columns)
 
-    def after(panel, before, rows=block.shape[0]):
-        return call(release, "release", [panel, before], shape((rows, block.shape[1]), F32), specs=[VMEM, ANY])
+    def after(panel, before, name="release"):
+        return call(release, name, [panel, before], shape(panel.shape, F32), specs=[VMEM, ANY])
 
     indices = shape((width, columns), jnp.int32)
     owner = call(functools.partial(holders, rows_dev), "holders", [pivots], [indices] * steps)
     base, ahead, places = call(
         prepare, "prepare", [matrix, pivots], [full, square, shape((width, width), jnp.int32)]
     )
-    first = forwarded(own[0], after(own[0], places), process_columns)
+    first = forwarded(own[0], after(own[0], places, "down_block"), process_columns)
     joint = call(stack, "stack", first[:2], shape((2 * block.shape[0], block.shape[1]), F32))
     joint = across(joint, process_columns)
     first += [joint] + [across(piece, process_columns) for piece in first[2:]]
     sent, received = exchange(slots, 0, [joint])
-    two = shape((2 * block.shape[0] + SPARE, block.shape[1]), F32)
+    two = shape((2 * block.shape[0], block.shape[1]), F32)
     pair = call(pack, "pack", [own[1], near, sent], two, specs=[VMEM, VMEM, ANY])
     late = late_blocks(process_columns // 2)
     early = [piece for position, piece in enumerate(first) if position not in late]
     factor = call(functools.partial(collect, late), "collect", [places, *early], [shape((width, width), BF16)] * 2)
     operands = [matrix, pivots, l_inverse, owner[0], ahead, places, sent, *received, *factor, *[first[position] for position in late]]
     upper, displaced, slots = call(functools.partial(solve, bits, 0, late), "solve", operands, [square] * 3)
-    far = shift(after(own[1], slots), process_columns // 4, process_columns)
+    far = shift(after(own[1], slots, "far_block"), process_columns // 4, process_columns)
     pairs = passed(pair, process_columns)
-    rows = block.shape[0]
-    joint = call(tails, "tails", [far, *pairs], shape((rows + tail_of(rows) * len(pairs), block.shape[1]), F32))
-    second = [own[1], near, far, across(joint, process_columns)]
-    second += pairs + [across(after(piece, own[1], 2 * rows - tail_of(rows)), process_columns) for piece in pairs]
     base, top = call(
         functools.partial(update, 0),
         "update",
@@ -447,6 +432,8 @@
         scratch=halves,
     )
     sent, received = exchange(slots, 1, [top])
+    second = [own[1], near, far, across(after(far, own[1], "far_piece"), process_columns)]
+    second += pairs + [across(after(piece, sent, "pair_piece"), process_columns) for piece in pairs]
     high, low = call(
         functools.partial(halve, 1, rows_dev, width),
         "halve",
@@ -459,7 +446,7 @@
         [base, pivots, l_inverse, owner[1], top, high, low, sent, *received],
         full,
         out_specs=HBM,
-        scratch=[pltpu.VMEM((rows_dev, columns), F32), pltpu.SemaphoreType.DMA((chunks,))],
+        scratch=[pltpu.VMEM((rows_dev, columns), F32), pltpu.SemaphoreType.DMA((2 * chunks,))],
     )
 
 

time: 36.3 us -> 36.2 us (level)
  waiting for transfers between devices: 14.6 us -> 14.2 us
    ppermute x4, waiting for transfers between devices: 8.77 us -> 8.37 us  [shift(): lax.ppermute(block, 'pcol', [(i, (i + 2 * distance) % count) for i in ran...]
where the time goes in v12:
time: 36.2 us; the launch traced here: 36 us
  waiting for transfers between devices  14.2 us (39%)
  starting transfers between devices  13.7 us (38%)
  Pallas kernels  7.94 us (22%)
    ppermute x4, waiting for transfers between devices, shift(): lax.ppermute(block, 'pcol', [(i, (i + 2 * distance) % count) for i in ran...  8.37 us
    pallas_call x17, Pallas kernels, call(): pl.pallas_call(kernel, out_shape=outs, in_specs=specs or [VMEM] * len(ope...  7.94 us
    ppermute x4, starting transfers between devices, shift(): lax.ppermute(block, 'pcol', [(i, (i + 2 * distance) % count) for i in ran...  6.49 us
    ppermute x4, starting transfers between devices, exchange(): received.append(lax.ppermute(sent, ('prow', 'pcol'), pairs))  6.39 us
    ppermute x4, waiting for transfers between devices, exchange(): received.append(lax.ppermute(sent, ('prow', 'pcol'), pairs))  3.64 us
    ppermute x6, waiting for transfers between devices, across(): return lax.ppermute(block, 'pcol', [(i, i ^ 1) for i in range(count)])  2.21 us
    ppermute x6, starting transfers between devices, across(): return lax.ppermute(block, 'pcol', [(i, i ^ 1) for i in range(count)])  0.78 us
  transfers between devices with their start and end apart: 15, of which 8 were waited for; matrix products, arithmetic and copies ran while one was open for 0% of the time, Pallas kernels for 12%

profile of v12, /device:TPU:0, one launch (start us, length us, event | category | flops | bytes accessed | tf_op | source)
XLA Modules:
  0.0 36.0 jit_solution(9505938300510763220)
XLA Ops:
  0.0 1.4 %load.1 = (f32[1024,256]{1,0:T(8,128)S(1)}, s32[2,256]{1,0:T(2,128)S(1)}, f32[128,256]{1,0:T(8,128)S(1)}, f32[128,256]{1,0:T(8,128)S(1)}) custom-call(f32[1024,256]{1,0:T(8,128)} %matrix.1, s32[2,256]{1,0:T(2,128)} %pivots.1, f32[2,128,256]{2,1,0:T(8,128)} %panels.1), custom_call_target="tpu_custom_call" | custom-call | tf_op jit(solution)/shard_map/load/pallas_call | solution.py:364
  1.4 3.1 %collective-permute-start.1 = (f32[128,256]{1,0:T(8,128)S(1)}, f32[128,256]{1,0:T(8,128)S(1)}, u32[]{:S(2)}, u32[]{:S(2)}) collective-permute-start(f32[128,256]{1,0:T(8,128)S(1)} %get-tuple-element.29.one.panel.refs_0_), channel_id=1, source_target_pairs={{0,2},{1,3},{2,4},{3,5},{4,6},{5,7},{6,0},{7,1},{8,10},{9,11},{10,... | collective-permute-start | bytes 393224 | tf_op jit(solution)/shard_map/ppermute | solution.py:328
  4.5 0.5 %first_slots.1.sent = f32[256,256]{1,0:T(8,128)S(1)} custom-call(f32[1024,256]{1,0:T(8,128)S(1)} %get-tuple-element.23.matrix, s32[2,256]{1,0:T(2,128)S(1)} %get-tuple-element.24.pivots), custom_call_target="tpu_custom_call" | custom-call | tf_op jit(solution)/shard_map/first_slots/pallas_call | solution.py:364
  5.0 1.6 %collective-permute-start = (f32[256,256]{1,0:T(8,128)S(1)}, f32[256,256]{1,0:T(8,128)S(1)}, u32[]{:S(2)}, u32[]{:S(2)}) collective-permute-start(f32[256,256]{1,0:T(8,128)S(1)} %first_slots.1.sent), channel_id=1, source_target_pairs={{0,8},{1,17},{2,10},{3,19},{4,12},{5,21},{6,14},{7,23},{8,0},{9,25... | collective-permute-start | bytes 786440 | tf_op jit(solution)/shard_map/ppermute | solution.py:387
  6.6 0.7 %prepare.1 = (f32[1024,256]{1,0:T(8,128)S(1)}, f32[256,256]{1,0:T(8,128)S(1)}, s32[256,256]{1,0:T(8,128)S(1)}) custom-call(f32[1024,256]{1,0:T(8,128)S(1)} %get-tuple-element.23.matrix, s32[2,256]{1,0:T(2,128)S(1)} %get-tuple-element.24.pivots), custom_call_target="tpu_custom_call" | custom-call | flops 600000000 | tf_op jit(solution)/shard_map/prepare/pallas_call | solution.py:364
  7.3 2.3 %collective-permute-start.5 = (f32[128,256]{1,0:T(8,128)S(1)}, f32[128,256]{1,0:T(8,128)S(1)}, u32[]{:S(2)}, u32[]{:S(2)}) collective-permute-start(f32[128,256]{1,0:T(8,128)S(1)} %down_block.1), channel_id=1, source_target_pairs={{0,6},{1,7},{2,0},{3,1},{4,2},{5,3},{6,4},{7,5},{8,14},{9,15},{10,... | collective-permute-start | bytes 393224 | tf_op jit(solution)/shard_map/ppermute | solution.py:328
  9.6 0.5 %collective-permute-done.1.other.refs_1_ = f32[128,256]{1,0:T(8,128)S(1)} collective-permute-done((f32[128,256]{1,0:T(8,128)S(1)}, f32[128,256]{1,0:T(8,128)S(1)}, u32[]{:S(2)}, u32[]{:S(2)}) %collective-permute-start.1) | collective-permute-done | bytes 131104 | tf_op jit(solution)/shard_map/ppermute | solution.py:328
  10.2 0.3 holders.1
  10.5 1.0 %collective-permute-done.received.refs_0_ = f32[256,256]{1,0:T(8,128)S(1)} collective-permute-done((f32[256,256]{1,0:T(8,128)S(1)}, f32[256,256]{1,0:T(8,128)S(1)}, u32[]{:S(2)}, u32[]{:S(2)}) %collective-permute-start) | collective-permute-done | bytes 262176 | tf_op jit(solution)/shard_map/ppermute | solution.py:387
  11.8 1.6 %collective-permute-start.3 = (f32[256,256]{1,0:T(8,128)S(1)}, f32[256,256]{1,0:T(8,128)S(1)}, u32[]{:S(2)}, u32[]{:S(2)}) collective-permute-start(f32[256,256]{1,0:T(8,128)S(1)} %merge.2.sent.before), channel_id=1, source_target_pairs={{0,16},{1,9},{2,18},{3,11},{4,20},{5,13},{6,22},{7,15},{8,24},{9,1... | collective-permute-start | bytes 786440 | tf_op jit(solution)/shard_map/ppermute | solution.py:387
  13.5 0.5 %collective-permute-start.7 = (f32[128,256]{1,0:T(8,128)S(1)}, f32[128,256]{1,0:T(8,128)S(1)}, u32[]{:S(2)}, u32[]{:S(2)}) collective-permute-start(f32[128,256]{1,0:T(8,128)S(1)} %collective-permute-done.5.refs_3_), channel_id=1, source_target_pairs={{0,1},{1,0},{2,3},{3,2},{4,5},{5,4},{6,7},{7,6},{8,9},{9,8},{10,11... | collective-permute-start | bytes 393224 | tf_op jit(solution)/shard_map/ppermute | solution.py:332
  14.0 4.2 %collective-permute-done.4.refs_2_ = f32[128,256]{1,0:T(8,128)S(1)} collective-permute-done((f32[128,256]{1,0:T(8,128)S(1)}, f32[128,256]{1,0:T(8,128)S(1)}, u32[]{:S(2)}, u32[]{:S(2)}) %collective-permute-start.4) | collective-permute-done | bytes 131104 | tf_op jit(solution)/shard_map/ppermute | solution.py:328
  18.3 0.6 %collect.1 = (bf16[256,256]{1,0:T(8,128)(2,1)S(1)}, bf16[256,256]{1,0:T(8,128)(2,1)S(1)}) custom-call(s32[256,256]{1,0:T(8,128)S(1)} %get-tuple-element.28.before.places, f32[128,256]{1,0:T(8,128)S(1)} %get-tuple-element.29.one.panel.refs_0_, f32[128,256]{1,0:T(8,128)S(1)} %collective-permute-done.1.other.refs_1_, ...), custom_call_target="tpu_custom_call" | custom-call | flops 1000000 | tf_op jit(solution)/shard_map/collect/pallas_call | solution.py:364
  18.9 0.7 %collective-permute-done.6.refs_4_.refs_5_ = f32[128,256]{1,0:T(8,128)S(1)} collective-permute-done((f32[128,256]{1,0:T(8,128)S(1)}, f32[128,256]{1,0:T(8,128)S(1)}, u32[]{:S(2)}, u32[]{:S(2)}) %collective-permute-start.6) | collective-permute-done | bytes 131104 | tf_op jit(solution)/shard_map/ppermute | solution.py:332
  19.5 0.7 %solve.1 = (f32[256,256]{1,0:T(8,128)S(1)}, f32[256,256]{1,0:T(8,128)S(1)}, f32[256,256]{1,0:T(8,128)S(1)}) custom-call(f32[1024,256]{1,0:T(8,128)S(1)} %get-tuple-element.23.matrix, s32[2,256]{1,0:T(2,128)S(1)} %get-tuple-element.24.pivots, f32[2,256,256]{2,1,0:T(8,128)S(1)} %copy-done, s32[256,256]{1,0:T(8,128)S(1)} %get-tuple-element.26.owner, ...), custom_call_target="tpu_custom_call" | custom-call | tf_op jit(solution)/shard_map/solve/pallas_call | solution.py:364
  20.3 1.6 %collective-permute-start.12 = (f32[256,256]{1,0:T(8,128)S(1)}, f32[256,256]{1,0:T(8,128)S(1)}, u32[]{:S(2)}, u32[]{:S(2)}) collective-permute-start(f32[256,256]{1,0:T(8,128)S(1)} %get-tuple-element.38.before.sent), channel_id=1, source_target_pairs={{0,8},{1,17},{2,10},{3,19},{4,12},{5,21},{6,14},{7,23},{8,0},{9,25... | collective-permute-start | bytes 786440 | tf_op jit(solution)/shard_map/ppermute | solution.py:387
  21.8 1.1 %collective-permute-start.9 = (f32[128,256]{1,0:T(8,128)S(1)}, f32[128,256]{1,0:T(8,128)S(1)}, u32[]{:S(2)}, u32[]{:S(2)}) collective-permute-start(f32[128,256]{1,0:T(8,128)S(1)} %far_block.1), channel_id=1, source_target_pairs={{0,4},{1,5},{2,6},{3,7},{4,0},{5,1},{6,2},{7,3},{8,12},{9,13},{10,... | collective-permute-start | bytes 393224 | tf_op jit(solution)/shard_map/ppermute | solution.py:328
  22.9 1.1 %update.1 = (f32[1024,256]{1,0:T(8,128)S(1)}, f32[256,256]{1,0:T(8,128)S(1)}) custom-call(f32[1024,256]{1,0:T(8,128)S(1)} %get-tuple-element.25.base, s32[2,256]{1,0:T(2,128)S(1)} %get-tuple-element.24.pivots, f32[256,256]{1,0:T(8,128)S(1)} %get-tuple-element.32.upper_in, f32[256,256]{1,0:T(8,128)S(1)} %get-tuple-element.33.displaced_in, ...), custom_call_target="tpu_custom_call" | custom-call | flops 5000000000 | tf_op jit(solution)/shard_map/update/pallas_call | solution.py:364
  24.0 2.7 %collective-permute-done.12.received.refs_0_ = f32[256,256]{1,0:T(8,128)S(1)} collective-permute-done((f32[256,256]{1,0:T(8,128)S(1)}, f32[256,256]{1,0:T(8,128)S(1)}, u32[]{:S(2)}, u32[]{:S(2)}) %collective-permute-start.12) | collective-permute-done | bytes 262176 | tf_op jit(solution)/shard_map/ppermute | solution.py:387
  26.8 1.6 %collective-permute-start.14 = (f32[256,256]{1,0:T(8,128)S(1)}, f32[256,256]{1,0:T(8,128)S(1)}, u32[]{:S(2)}, u32[]{:S(2)}) collective-permute-start(f32[256,256]{1,0:T(8,128)S(1)} %merge.3.before.sent), channel_id=1, source_target_pairs={{0,16},{1,9},{2,18},{3,11},{4,20},{5,13},{6,22},{7,15},{8,24},{9,1... | collective-permute-start | bytes 786440 | tf_op jit(solution)/shard_map/ppermute | solution.py:387
  28.5 3.7 %collective-permute-done.9.panel.refs_2_ = f32[128,256]{1,0:T(8,128)S(1)} collective-permute-done((f32[128,256]{1,0:T(8,128)S(1)}, f32[128,256]{1,0:T(8,128)S(1)}, u32[]{:S(2)}, u32[]{:S(2)}) %collective-permute-start.9) | collective-permute-done | bytes 131104 | tf_op jit(solution)/shard_map/ppermute | solution.py:328
  32.3 1.3 %collective-permute-done.10.refs_3_ = f32[128,256]{1,0:T(8,128)S(1)} collective-permute-done((f32[128,256]{1,0:T(8,128)S(1)}, f32[128,256]{1,0:T(8,128)S(1)}, u32[]{:S(2)}, u32[]{:S(2)}) %collective-permute-start.10) | collective-permute-done | bytes 131104 | tf_op jit(solution)/shard_map/ppermute | solution.py:332
  33.6 0.3 halve.1
  34.0 2.1 %finish.1 = f32[1024,256]{1,0:T(8,128)} custom-call(f32[1024,256]{1,0:T(8,128)S(1)} %get-tuple-element.34.base, s32[2,256]{1,0:T(2,128)S(1)} %get-tuple-element.24.pivots, f32[2,256,256]{2,1,0:T(8,128)S(1)} %copy-done, s32[256,256]{1,0:T(8,128)S(1)} %get-tuple-element.35.owner, f32[256,256]{1,0:T(8,128)S(1)} %get-tuple-element.36.refs_0_.top, ...), custom_call_target="tpu_custom_call" | custom-call | tf_op jit(solution)/shard_map/finish/pallas_call | solution.py:364
  (25 shorter events, 0.9 us)
Async XLA Ops:
  1.4 8.7 %collective-permute-start.1 = (f32[128,256]{1,0:T(8,128)S(1)}, f32[128,256]{1,0:T(8,128)S(1)}, u32[]{:S(2)}, u32[]{:S(2)}) collective-permute-start(f32[128,256]{1,0:T(8,128)S(1)} %get-tuple-element.29.one.panel.refs_0_), channel_id=1, source_target_pairs={{0,2},{1,3},{2,4},{3,5},{4,6},{5,7},{6,0},{7,1},{8,10},{9,11},{10,... | collective-permute-start | bytes 393224 | tf_op jit(solution)/shard_map/ppermute | solution.py:328
  5.0 6.4 %collective-permute-start = (f32[256,256]{1,0:T(8,128)S(1)}, f32[256,256]{1,0:T(8,128)S(1)}, u32[]{:S(2)}, u32[]{:S(2)}) collective-permute-start(f32[256,256]{1,0:T(8,128)S(1)} %first_slots.1.sent), channel_id=1, source_target_pairs={{0,8},{1,17},{2,10},{3,19},{4,12},{5,21},{6,14},{7,23},{8,0},{9,25... | collective-permute-start | bytes 786440 | tf_op jit(solution)/shard_map/ppermute | solution.py:387
  7.3 6.1 %collective-permute-start.5 = (f32[128,256]{1,0:T(8,128)S(1)}, f32[128,256]{1,0:T(8,128)S(1)}, u32[]{:S(2)}, u32[]{:S(2)}) collective-permute-start(f32[128,256]{1,0:T(8,128)S(1)} %down_block.1), channel_id=1, source_target_pairs={{0,6},{1,7},{2,0},{3,1},{4,2},{5,3},{6,4},{7,5},{8,14},{9,15},{10,... | collective-permute-start | bytes 393224 | tf_op jit(solution)/shard_map/ppermute | solution.py:328
  10.1 1.6 %collective-permute-start.2 = (f32[256,256]{1,0:T(8,128)S(1)}, f32[256,256]{1,0:T(8,128)S(1)}, u32[]{:S(2)}, u32[]{:S(2)}) collective-permute-start(f32[256,256]{1,0:T(8,128)S(1)} %stack.1), channel_id=1, source_target_pairs={{0,1},{1,0},{2,3},{3,2},{4,5},{5,4},{6,7},{7,6},{8,9},{9,8},{10,11... | collective-permute-start | bytes 786440 | tf_op jit(solution)/shard_map/ppermute | solution.py:332
  10.4 7.7 %collective-permute-start.4 = (f32[128,256]{1,0:T(8,128)S(1)}, f32[128,256]{1,0:T(8,128)S(1)}, u32[]{:S(2)}, u32[]{:S(2)}) collective-permute-start(f32[128,256]{1,0:T(8,128)S(1)} %collective-permute-done.1.other.refs_1_), channel_id=1, source_target_pairs={{0,2},{1,3},{2,4},{3,5},{4,6},{5,7},{6,0},{7,1},{8,10},{9,11},{10,... | collective-permute-start | bytes 393224 | tf_op jit(solution)/shard_map/ppermute | solution.py:328
  11.8 7.7 %collective-permute-start.3 = (f32[256,256]{1,0:T(8,128)S(1)}, f32[256,256]{1,0:T(8,128)S(1)}, u32[]{:S(2)}, u32[]{:S(2)}) collective-permute-start(f32[256,256]{1,0:T(8,128)S(1)} %merge.2.sent.before), channel_id=1, source_target_pairs={{0,16},{1,9},{2,18},{3,11},{4,20},{5,13},{6,22},{7,15},{8,24},{9,1... | collective-permute-start | bytes 786440 | tf_op jit(solution)/shard_map/ppermute | solution.py:387
  13.4 4.7 %collective-permute-start.8 = (f32[128,256]{1,0:T(8,128)S(1)}, f32[128,256]{1,0:T(8,128)S(1)}, u32[]{:S(2)}, u32[]{:S(2)}) collective-permute-start(f32[128,256]{1,0:T(8,128)S(1)} %get-tuple-element.37.panel.before.own.refs_0_), channel_id=1, source_target_pairs={{0,1},{1,0},{2,3},{3,2},{4,5},{5,4},{6,7},{7,6},{8,9},{9,8},{10,11... | collective-permute-start | bytes 393224 | tf_op jit(solution)/shard_map/ppermute | solution.py:332
  13.5 5.4 %collective-permute-start.7 = (f32[128,256]{1,0:T(8,128)S(1)}, f32[128,256]{1,0:T(8,128)S(1)}, u32[]{:S(2)}, u32[]{:S(2)}) collective-permute-start(f32[128,256]{1,0:T(8,128)S(1)} %collective-permute-done.5.refs_3_), channel_id=1, source_target_pairs={{0,1},{1,0},{2,3},{3,2},{4,5},{5,4},{6,7},{7,6},{8,9},{9,8},{10,11... | collective-permute-start | bytes 393224 | tf_op jit(solution)/shard_map/ppermute | solution.py:332
  18.2 1.3 %collective-permute-start.6 = (f32[128,256]{1,0:T(8,128)S(1)}, f32[128,256]{1,0:T(8,128)S(1)}, u32[]{:S(2)}, u32[]{:S(2)}) collective-permute-start(f32[128,256]{1,0:T(8,128)S(1)} %collective-permute-done.4.refs_2_), channel_id=1, source_target_pairs={{0,1},{1,0},{2,3},{3,2},{4,5},{5,4},{6,7},{7,6},{8,9},{9,8},{10,11... | collective-permute-start | bytes 393224 | tf_op jit(solution)/shard_map/ppermute | solution.py:332
  18.2 1.3 %copy-start = (f32[2,256,256]{2,1,0:T(8,128)S(1)}, f32[2,256,256]{2,1,0:T(8,128)}, u32[]{:S(2)}) copy-start(f32[2,256,256]{2,1,0:T(8,128)} %inverse.3) | copy-start | bytes 1572868
  18.2 10.2 %collective-permute-start.11 = (f32[256,256]{1,0:T(8,128)S(1)}, f32[256,256]{1,0:T(8,128)S(1)}, u32[]{:S(2)}, u32[]{:S(2)}) collective-permute-start(f32[256,256]{1,0:T(8,128)S(1)} %pack.1), channel_id=1, source_target_pairs={{0,2},{1,7},{2,4},{3,1},{4,6},{5,3},{6,0},{7,5},{8,10},{9,15},{10,... | collective-permute-start | bytes 786440 | tf_op jit(solution)/shard_map/ppermute | solution.py:350
  20.3 6.4 %collective-permute-start.12 = (f32[256,256]{1,0:T(8,128)S(1)}, f32[256,256]{1,0:T(8,128)S(1)}, u32[]{:S(2)}, u32[]{:S(2)}) collective-permute-start(f32[256,256]{1,0:T(8,128)S(1)} %get-tuple-element.38.before.sent), channel_id=1, source_target_pairs={{0,8},{1,17},{2,10},{3,19},{4,12},{5,21},{6,14},{7,23},{8,0},{9,25... | collective-permute-start | bytes 786440 | tf_op jit(solution)/shard_map/ppermute | solution.py:387
  21.8 10.4 %collective-permute-start.9 = (f32[128,256]{1,0:T(8,128)S(1)}, f32[128,256]{1,0:T(8,128)S(1)}, u32[]{:S(2)}, u32[]{:S(2)}) collective-permute-start(f32[128,256]{1,0:T(8,128)S(1)} %far_block.1), channel_id=1, source_target_pairs={{0,4},{1,5},{2,6},{3,7},{4,0},{5,1},{6,2},{7,3},{8,12},{9,13},{10,... | collective-permute-start | bytes 393224 | tf_op jit(solution)/shard_map/ppermute | solution.py:328
  26.8 7.2 %collective-permute-start.14 = (f32[256,256]{1,0:T(8,128)S(1)}, f32[256,256]{1,0:T(8,128)S(1)}, u32[]{:S(2)}, u32[]{:S(2)}) collective-permute-start(f32[256,256]{1,0:T(8,128)S(1)} %merge.3.before.sent), channel_id=1, source_target_pairs={{0,16},{1,9},{2,18},{3,11},{4,20},{5,13},{6,22},{7,15},{8,24},{9,1... | collective-permute-start | bytes 786440 | tf_op jit(solution)/shard_map/ppermute | solution.py:387
  28.4 5.2 %collective-permute-start.13 = (f32[256,256]{1,0:T(8,128)S(1)}, f32[256,256]{1,0:T(8,128)S(1)}, u32[]{:S(2)}, u32[]{:S(2)}) collective-permute-start(f32[256,256]{1,0:T(8,128)S(1)} %pair_piece.1), channel_id=1, source_target_pairs={{0,1},{1,0},{2,3},{3,2},{4,5},{5,4},{6,7},{7,6},{8,9},{9,8},{10,11... | collective-permute-start | bytes 786440 | tf_op jit(solution)/shard_map/ppermute | solution.py:332
  32.2 1.4 %collective-permute-start.10 = (f32[128,256]{1,0:T(8,128)S(1)}, f32[128,256]{1,0:T(8,128)S(1)}, u32[]{:S(2)}, u32[]{:S(2)}) collective-permute-start(f32[128,256]{1,0:T(8,128)S(1)} %far_piece.1), channel_id=1, source_target_pairs={{0,1},{1,0},{2,3},{3,2},{4,5},{5,4},{6,7},{7,6},{8,9},{9,8},{10,11... | collective-permute-start | bytes 393224 | tf_op jit(solution)/shard_map/ppermute | solution.py:332

commit v13 on v12

--- a/solution.py
+++ b/solution.py
@@ -15,15 +15,15 @@
 BF16 = jnp.bfloat16
 NOWHERE = -(1 << 24)
 COST = {
+    "prepare": 1000 * 10**6,
+    "down_block": 300 * 10**6,
+    "far_block": 5000 * 10**6,
+    "collect": 1500 * 10**6,
     "holders": 3000 * 10**6,
     "update": 5000 * 10**6,
-    "pair_piece": 2000 * 10**6,
-    "stack": 5000 * 10**6,
+    "pair_piece": 1000 * 10**6,
+    "stack": 8000 * 10**6,
     "far_piece": 3000 * 10**6,
-    "far_block": 5000 * 10**6,
-    "prepare": 600 * 10**6,
-    "down_block": 300 * 10**6,
-    "collect": 1 * 10**6,
 }
 PARTS = 4
 
@@ -446,7 +446,7 @@
         [base, pivots, l_inverse, owner[1], top, high, low, sent, *received],
         full,
         out_specs=HBM,
-        scratch=[pltpu.VMEM((rows_dev, columns), F32), pltpu.SemaphoreType.DMA((2 * chunks,))],
+        scratch=[pltpu.VMEM((rows_dev, columns), F32), pltpu.SemaphoreType.DMA((chunks,))],
     )
 
 

time: 36.2 us -> 35.8 us (0.989)
    ppermute x6, starting transfers between devices: 0.78 us -> 0.33 us  [across(): return lax.ppermute(block, 'pcol', [(i, i ^ 1) for i in range(count)])]
where the time goes in v13:
time: 35.8 us; the launch traced here: 35.7 us
  waiting for transfers between devices  14.2 us (40%)
  starting transfers between devices  13.6 us (38%)
  Pallas kernels  7.73 us (22%)
    ppermute x4, waiting for transfers between devices, shift(): lax.ppermute(block, 'pcol', [(i, (i + 2 * distance) % count) for i in ran...  8.72 us
    pallas_call x17, Pallas kernels, call(): pl.pallas_call(kernel, out_shape=outs, in_specs=specs or [VMEM] * len(ope...  7.73 us
    ppermute x4, starting transfers between devices, shift(): lax.ppermute(block, 'pcol', [(i, (i + 2 * distance) % count) for i in ran...  6.77 us
    ppermute x4, starting transfers between devices, exchange(): received.append(lax.ppermute(sent, ('prow', 'pcol'), pairs))  6.39 us
    ppermute x4, waiting for transfers between devices, exchange(): received.append(lax.ppermute(sent, ('prow', 'pcol'), pairs))  3.34 us
    ppermute x6, waiting for transfers between devices, across(): return lax.ppermute(block, 'pcol', [(i, i ^ 1) for i in range(count)])  2.18 us
  transfers between devices with their start and end apart: 15, of which 8 were waited for; matrix products, arithmetic and copies ran while one was open for 0% of the time, Pallas kernels for 12%

profile of v13, /device:TPU:0, one launch (start us, length us, event | category | flops | bytes accessed | tf_op | source)
XLA Modules:
  0.0 35.7 jit_solution(17677033738712712128)
XLA Ops:
  0.0 1.4 %load.1 = (f32[1024,256]{1,0:T(8,128)S(1)}, s32[2,256]{1,0:T(2,128)S(1)}, f32[128,256]{1,0:T(8,128)S(1)}, f32[128,256]{1,0:T(8,128)S(1)}) custom-call(f32[1024,256]{1,0:T(8,128)} %matrix.1, s32[2,256]{1,0:T(2,128)} %pivots.1, f32[2,128,256]{2,1,0:T(8,128)} %panels.1), custom_call_target="tpu_custom_call" | custom-call | tf_op jit(solution)/shard_map/load/pallas_call | solution.py:364
  1.4 3.1 %collective-permute-start.1 = (f32[128,256]{1,0:T(8,128)S(1)}, f32[128,256]{1,0:T(8,128)S(1)}, u32[]{:S(2)}, u32[]{:S(2)}) collective-permute-start(f32[128,256]{1,0:T(8,128)S(1)} %get-tuple-element.29.one.panel.refs_0_), channel_id=1, source_target_pairs={{0,2},{1,3},{2,4},{3,5},{4,6},{5,7},{6,0},{7,1},{8,10},{9,11},{10,... | collective-permute-start | bytes 393224 | tf_op jit(solution)/shard_map/ppermute | solution.py:328
  4.5 0.5 %first_slots.1.sent = f32[256,256]{1,0:T(8,128)S(1)} custom-call(f32[1024,256]{1,0:T(8,128)S(1)} %get-tuple-element.23.matrix, s32[2,256]{1,0:T(2,128)S(1)} %get-tuple-element.24.pivots), custom_call_target="tpu_custom_call" | custom-call | tf_op jit(solution)/shard_map/first_slots/pallas_call | solution.py:364
  5.0 1.6 %collective-permute-start = (f32[256,256]{1,0:T(8,128)S(1)}, f32[256,256]{1,0:T(8,128)S(1)}, u32[]{:S(2)}, u32[]{:S(2)}) collective-permute-start(f32[256,256]{1,0:T(8,128)S(1)} %first_slots.1.sent), channel_id=1, source_target_pairs={{0,8},{1,17},{2,10},{3,19},{4,12},{5,21},{6,14},{7,23},{8,0},{9,25... | collective-permute-start | bytes 786440 | tf_op jit(solution)/shard_map/ppermute | solution.py:387
  6.6 0.7 %prepare.1 = (f32[1024,256]{1,0:T(8,128)S(1)}, f32[256,256]{1,0:T(8,128)S(1)}, s32[256,256]{1,0:T(8,128)S(1)}) custom-call(f32[1024,256]{1,0:T(8,128)S(1)} %get-tuple-element.23.matrix, s32[2,256]{1,0:T(2,128)S(1)} %get-tuple-element.24.pivots), custom_call_target="tpu_custom_call" | custom-call | flops 1000000000 | tf_op jit(solution)/shard_map/prepare/pallas_call | solution.py:364
  7.3 2.3 %collective-permute-start.5 = (f32[128,256]{1,0:T(8,128)S(1)}, f32[128,256]{1,0:T(8,128)S(1)}, u32[]{:S(2)}, u32[]{:S(2)}) collective-permute-start(f32[128,256]{1,0:T(8,128)S(1)} %down_block.1), channel_id=1, source_target_pairs={{0,6},{1,7},{2,0},{3,1},{4,2},{5,3},{6,4},{7,5},{8,14},{9,15},{10,... | collective-permute-start | bytes 393224 | tf_op jit(solution)/shard_map/ppermute | solution.py:328
  9.6 0.5 %collective-permute-done.1.other.refs_1_ = f32[128,256]{1,0:T(8,128)S(1)} collective-permute-done((f32[128,256]{1,0:T(8,128)S(1)}, f32[128,256]{1,0:T(8,128)S(1)}, u32[]{:S(2)}, u32[]{:S(2)}) %collective-permute-start.1) | collective-permute-done | bytes 131104 | tf_op jit(solution)/shard_map/ppermute | solution.py:328
  10.2 0.3 holders.1
  10.5 1.0 %collective-permute-done.received.refs_0_ = f32[256,256]{1,0:T(8,128)S(1)} collective-permute-done((f32[256,256]{1,0:T(8,128)S(1)}, f32[256,256]{1,0:T(8,128)S(1)}, u32[]{:S(2)}, u32[]{:S(2)}) %collective-permute-start) | collective-permute-done | bytes 262176 | tf_op jit(solution)/shard_map/ppermute | solution.py:387
  11.5 0.2 collective-permute-done.2.refs_0_.refs_4_
  11.8 1.6 %collective-permute-start.3 = (f32[256,256]{1,0:T(8,128)S(1)}, f32[256,256]{1,0:T(8,128)S(1)}, u32[]{:S(2)}, u32[]{:S(2)}) collective-permute-start(f32[256,256]{1,0:T(8,128)S(1)} %merge.2.sent.before), channel_id=1, source_target_pairs={{0,16},{1,9},{2,18},{3,11},{4,20},{5,13},{6,22},{7,15},{8,24},{9,1... | collective-permute-start | bytes 786440 | tf_op jit(solution)/shard_map/ppermute | solution.py:387
  13.5 4.4 %collective-permute-done.4.refs_2_ = f32[128,256]{1,0:T(8,128)S(1)} collective-permute-done((f32[128,256]{1,0:T(8,128)S(1)}, f32[128,256]{1,0:T(8,128)S(1)}, u32[]{:S(2)}, u32[]{:S(2)}) %collective-permute-start.4) | collective-permute-done | bytes 131104 | tf_op jit(solution)/shard_map/ppermute | solution.py:328
  18.0 0.6 %collect.1 = (bf16[256,256]{1,0:T(8,128)(2,1)S(1)}, bf16[256,256]{1,0:T(8,128)(2,1)S(1)}) custom-call(s32[256,256]{1,0:T(8,128)S(1)} %get-tuple-element.28.before.places, f32[128,256]{1,0:T(8,128)S(1)} %get-tuple-element.29.one.panel.refs_0_, f32[128,256]{1,0:T(8,128)S(1)} %collective-permute-done.1.other.refs_1_, ...), custom_call_target="tpu_custom_call" | custom-call | flops 1500000000 | tf_op jit(solution)/shard_map/collect/pallas_call | solution.py:364
  18.6 0.7 %collective-permute-done.6.refs_4_.refs_5_ = f32[128,256]{1,0:T(8,128)S(1)} collective-permute-done((f32[128,256]{1,0:T(8,128)S(1)}, f32[128,256]{1,0:T(8,128)S(1)}, u32[]{:S(2)}, u32[]{:S(2)}) %collective-permute-start.6) | collective-permute-done | bytes 131104 | tf_op jit(solution)/shard_map/ppermute | solution.py:332
  19.2 0.7 %solve.1 = (f32[256,256]{1,0:T(8,128)S(1)}, f32[256,256]{1,0:T(8,128)S(1)}, f32[256,256]{1,0:T(8,128)S(1)}) custom-call(f32[1024,256]{1,0:T(8,128)S(1)} %get-tuple-element.23.matrix, s32[2,256]{1,0:T(2,128)S(1)} %get-tuple-element.24.pivots, f32[2,256,256]{2,1,0:T(8,128)S(1)} %copy-done, s32[256,256]{1,0:T(8,128)S(1)} %get-tuple-element.26.owner, ...), custom_call_target="tpu_custom_call" | custom-call | tf_op jit(solution)/shard_map/solve/pallas_call | solution.py:364
  20.0 1.6 %collective-permute-start.12 = (f32[256,256]{1,0:T(8,128)S(1)}, f32[256,256]{1,0:T(8,128)S(1)}, u32[]{:S(2)}, u32[]{:S(2)}) collective-permute-start(f32[256,256]{1,0:T(8,128)S(1)} %get-tuple-element.38.before.sent), channel_id=1, source_target_pairs={{0,8},{1,17},{2,10},{3,19},{4,12},{5,21},{6,14},{7,23},{8,0},{9,25... | collective-permute-start | bytes 786440 | tf_op jit(solution)/shard_map/ppermute | solution.py:387
  21.5 1.4 %collective-permute-start.9 = (f32[128,256]{1,0:T(8,128)S(1)}, f32[128,256]{1,0:T(8,128)S(1)}, u32[]{:S(2)}, u32[]{:S(2)}) collective-permute-start(f32[128,256]{1,0:T(8,128)S(1)} %far_block.1), channel_id=1, source_target_pairs={{0,4},{1,5},{2,6},{3,7},{4,0},{5,1},{6,2},{7,3},{8,12},{9,13},{10,... | collective-permute-start | bytes 393224 | tf_op jit(solution)/shard_map/ppermute | solution.py:328
  22.9 1.1 %update.1 = (f32[1024,256]{1,0:T(8,128)S(1)}, f32[256,256]{1,0:T(8,128)S(1)}) custom-call(f32[1024,256]{1,0:T(8,128)S(1)} %get-tuple-element.25.base, s32[2,256]{1,0:T(2,128)S(1)} %get-tuple-element.24.pivots, f32[256,256]{1,0:T(8,128)S(1)} %get-tuple-element.32.upper_in, f32[256,256]{1,0:T(8,128)S(1)} %get-tuple-element.33.displaced_in, ...), custom_call_target="tpu_custom_call" | custom-call | flops 5000000000 | tf_op jit(solution)/shard_map/update/pallas_call | solution.py:364
  24.0 2.4 %collective-permute-done.12.received.refs_0_ = f32[256,256]{1,0:T(8,128)S(1)} collective-permute-done((f32[256,256]{1,0:T(8,128)S(1)}, f32[256,256]{1,0:T(8,128)S(1)}, u32[]{:S(2)}, u32[]{:S(2)}) %collective-permute-start.12) | collective-permute-done | bytes 262176 | tf_op jit(solution)/shard_map/ppermute | solution.py:387
  26.5 1.6 %collective-permute-start.14 = (f32[256,256]{1,0:T(8,128)S(1)}, f32[256,256]{1,0:T(8,128)S(1)}, u32[]{:S(2)}, u32[]{:S(2)}) collective-permute-start(f32[256,256]{1,0:T(8,128)S(1)} %merge.3.before.sent), channel_id=1, source_target_pairs={{0,16},{1,9},{2,18},{3,11},{4,20},{5,13},{6,22},{7,15},{8,24},{9,1... | collective-permute-start | bytes 786440 | tf_op jit(solution)/shard_map/ppermute | solution.py:387
  28.2 3.8 %collective-permute-done.9.panel.refs_2_ = f32[128,256]{1,0:T(8,128)S(1)} collective-permute-done((f32[128,256]{1,0:T(8,128)S(1)}, f32[128,256]{1,0:T(8,128)S(1)}, u32[]{:S(2)}, u32[]{:S(2)}) %collective-permute-start.9) | collective-permute-done | bytes 131104 | tf_op jit(solution)/shard_map/ppermute | solution.py:328
  32.2 1.3 %collective-permute-done.10.refs_3_ = f32[128,256]{1,0:T(8,128)S(1)} collective-permute-done((f32[128,256]{1,0:T(8,128)S(1)}, f32[128,256]{1,0:T(8,128)S(1)}, u32[]{:S(2)}, u32[]{:S(2)}) %collective-permute-start.10) | collective-permute-done | bytes 131104 | tf_op jit(solution)/shard_map/ppermute | solution.py:332
  33.5 0.3 halve.1
  33.8 1.9 %finish.1 = f32[1024,256]{1,0:T(8,128)} custom-call(f32[1024,256]{1,0:T(8,128)S(1)} %get-tuple-element.34.base, s32[2,256]{1,0:T(2,128)S(1)} %get-tuple-element.24.pivots, f32[2,256,256]{2,1,0:T(8,128)S(1)} %copy-done, s32[256,256]{1,0:T(8,128)S(1)} %get-tuple-element.35.owner, f32[256,256]{1,0:T(8,128)S(1)} %get-tuple-element.36.refs_0_.top, ...), custom_call_target="tpu_custom_call" | custom-call | tf_op jit(solution)/shard_map/finish/pallas_call | solution.py:364
  (25 shorter events, 0.7 us)
Async XLA Ops:
  1.4 8.7 %collective-permute-start.1 = (f32[128,256]{1,0:T(8,128)S(1)}, f32[128,256]{1,0:T(8,128)S(1)}, u32[]{:S(2)}, u32[]{:S(2)}) collective-permute-start(f32[128,256]{1,0:T(8,128)S(1)} %get-tuple-element.29.one.panel.refs_0_), channel_id=1, source_target_pairs={{0,2},{1,3},{2,4},{3,5},{4,6},{5,7},{6,0},{7,1},{8,10},{9,11},{10,... | collective-permute-start | bytes 393224 | tf_op jit(solution)/shard_map/ppermute | solution.py:328
  5.0 6.4 %collective-permute-start = (f32[256,256]{1,0:T(8,128)S(1)}, f32[256,256]{1,0:T(8,128)S(1)}, u32[]{:S(2)}, u32[]{:S(2)}) collective-permute-start(f32[256,256]{1,0:T(8,128)S(1)} %first_slots.1.sent), channel_id=1, source_target_pairs={{0,8},{1,17},{2,10},{3,19},{4,12},{5,21},{6,14},{7,23},{8,0},{9,25... | collective-permute-start | bytes 786440 | tf_op jit(solution)/shard_map/ppermute | solution.py:387
  7.3 6.1 %collective-permute-start.5 = (f32[128,256]{1,0:T(8,128)S(1)}, f32[128,256]{1,0:T(8,128)S(1)}, u32[]{:S(2)}, u32[]{:S(2)}) collective-permute-start(f32[128,256]{1,0:T(8,128)S(1)} %down_block.1), channel_id=1, source_target_pairs={{0,6},{1,7},{2,0},{3,1},{4,2},{5,3},{6,4},{7,5},{8,14},{9,15},{10,... | collective-permute-start | bytes 393224 | tf_op jit(solution)/shard_map/ppermute | solution.py:328
  9.6 8.3 %collective-permute-start.8 = (f32[128,256]{1,0:T(8,128)S(1)}, f32[128,256]{1,0:T(8,128)S(1)}, u32[]{:S(2)}, u32[]{:S(2)}) collective-permute-start(f32[128,256]{1,0:T(8,128)S(1)} %get-tuple-element.37.panel.before.own.refs_0_), channel_id=1, source_target_pairs={{0,1},{1,0},{2,3},{3,2},{4,5},{5,4},{6,7},{7,6},{8,9},{9,8},{10,11... | collective-permute-start | bytes 393224 | tf_op jit(solution)/shard_map/ppermute | solution.py:332
  10.1 1.6 %collective-permute-start.2 = (f32[256,256]{1,0:T(8,128)S(1)}, f32[256,256]{1,0:T(8,128)S(1)}, u32[]{:S(2)}, u32[]{:S(2)}) collective-permute-start(f32[256,256]{1,0:T(8,128)S(1)} %stack.1), channel_id=1, source_target_pairs={{0,1},{1,0},{2,3},{3,2},{4,5},{5,4},{6,7},{7,6},{8,9},{9,8},{10,11... | collective-permute-start | bytes 786440 | tf_op jit(solution)/shard_map/ppermute | solution.py:332
  10.2 7.7 %collective-permute-start.4 = (f32[128,256]{1,0:T(8,128)S(1)}, f32[128,256]{1,0:T(8,128)S(1)}, u32[]{:S(2)}, u32[]{:S(2)}) collective-permute-start(f32[128,256]{1,0:T(8,128)S(1)} %collective-permute-done.1.other.refs_1_), channel_id=1, source_target_pairs={{0,2},{1,3},{2,4},{3,5},{4,6},{5,7},{6,0},{7,1},{8,10},{9,11},{10,... | collective-permute-start | bytes 393224 | tf_op jit(solution)/shard_map/ppermute | solution.py:328
  11.8 7.4 %collective-permute-start.3 = (f32[256,256]{1,0:T(8,128)S(1)}, f32[256,256]{1,0:T(8,128)S(1)}, u32[]{:S(2)}, u32[]{:S(2)}) collective-permute-start(f32[256,256]{1,0:T(8,128)S(1)} %merge.2.sent.before), channel_id=1, source_target_pairs={{0,16},{1,9},{2,18},{3,11},{4,20},{5,13},{6,22},{7,15},{8,24},{9,1... | collective-permute-start | bytes 786440 | tf_op jit(solution)/shard_map/ppermute | solution.py:387
  13.4 5.1 %collective-permute-start.7 = (f32[128,256]{1,0:T(8,128)S(1)}, f32[128,256]{1,0:T(8,128)S(1)}, u32[]{:S(2)}, u32[]{:S(2)}) collective-permute-start(f32[128,256]{1,0:T(8,128)S(1)} %collective-permute-done.5.refs_3_), channel_id=1, source_target_pairs={{0,1},{1,0},{2,3},{3,2},{4,5},{5,4},{6,7},{7,6},{8,9},{9,8},{10,11... | collective-permute-start | bytes 393224 | tf_op jit(solution)/shard_map/ppermute | solution.py:332
  17.9 1.3 %collective-permute-start.6 = (f32[128,256]{1,0:T(8,128)S(1)}, f32[128,256]{1,0:T(8,128)S(1)}, u32[]{:S(2)}, u32[]{:S(2)}) collective-permute-start(f32[128,256]{1,0:T(8,128)S(1)} %collective-permute-done.4.refs_2_), channel_id=1, source_target_pairs={{0,1},{1,0},{2,3},{3,2},{4,5},{5,4},{6,7},{7,6},{8,9},{9,8},{10,11... | collective-permute-start | bytes 393224 | tf_op jit(solution)/shard_map/ppermute | solution.py:332
  17.9 1.3 %copy-start = (f32[2,256,256]{2,1,0:T(8,128)S(1)}, f32[2,256,256]{2,1,0:T(8,128)}, u32[]{:S(2)}) copy-start(f32[2,256,256]{2,1,0:T(8,128)} %inverse.3) | copy-start | bytes 1572868
  17.9 10.2 %collective-permute-start.11 = (f32[256,256]{1,0:T(8,128)S(1)}, f32[256,256]{1,0:T(8,128)S(1)}, u32[]{:S(2)}, u32[]{:S(2)}) collective-permute-start(f32[256,256]{1,0:T(8,128)S(1)} %pack.1), channel_id=1, source_target_pairs={{0,2},{1,7},{2,4},{3,1},{4,6},{5,3},{6,0},{7,5},{8,10},{9,15},{10,... | collective-permute-start | bytes 786440 | tf_op jit(solution)/shard_map/ppermute | solution.py:350
  20.0 6.4 %collective-permute-start.12 = (f32[256,256]{1,0:T(8,128)S(1)}, f32[256,256]{1,0:T(8,128)S(1)}, u32[]{:S(2)}, u32[]{:S(2)}) collective-permute-start(f32[256,256]{1,0:T(8,128)S(1)} %get-tuple-element.38.before.sent), channel_id=1, source_target_pairs={{0,8},{1,17},{2,10},{3,19},{4,12},{5,21},{6,14},{7,23},{8,0},{9,25... | collective-permute-start | bytes 786440 | tf_op jit(solution)/shard_map/ppermute | solution.py:387
  21.5 10.5 %collective-permute-start.9 = (f32[128,256]{1,0:T(8,128)S(1)}, f32[128,256]{1,0:T(8,128)S(1)}, u32[]{:S(2)}, u32[]{:S(2)}) collective-permute-start(f32[128,256]{1,0:T(8,128)S(1)} %far_block.1), channel_id=1, source_target_pairs={{0,4},{1,5},{2,6},{3,7},{4,0},{5,1},{6,2},{7,3},{8,12},{9,13},{10,... | collective-permute-start | bytes 393224 | tf_op jit(solution)/shard_map/ppermute | solution.py:328
  26.5 7.3 %collective-permute-start.14 = (f32[256,256]{1,0:T(8,128)S(1)}, f32[256,256]{1,0:T(8,128)S(1)}, u32[]{:S(2)}, u32[]{:S(2)}) collective-permute-start(f32[256,256]{1,0:T(8,128)S(1)} %merge.3.before.sent), channel_id=1, source_target_pairs={{0,16},{1,9},{2,18},{3,11},{4,20},{5,13},{6,22},{7,15},{8,24},{9,1... | collective-permute-start | bytes 786440 | tf_op jit(solution)/shard_map/ppermute | solution.py:387
  28.1 5.3 %collective-permute-start.13 = (f32[256,256]{1,0:T(8,128)S(1)}, f32[256,256]{1,0:T(8,128)S(1)}, u32[]{:S(2)}, u32[]{:S(2)}) collective-permute-start(f32[256,256]{1,0:T(8,128)S(1)} %pair_piece.1), channel_id=1, source_target_pairs={{0,1},{1,0},{2,3},{3,2},{4,5},{5,4},{6,7},{7,6},{8,9},{9,8},{10,11... | collective-permute-start | bytes 786440 | tf_op jit(solution)/shard_map/ppermute | solution.py:332
  32.1 1.4 %collective-permute-start.10 = (f32[128,256]{1,0:T(8,128)S(1)}, f32[128,256]{1,0:T(8,128)S(1)}, u32[]{:S(2)}, u32[]{:S(2)}) collective-permute-start(f32[128,256]{1,0:T(8,128)S(1)} %far_piece.1), channel_id=1, source_target_pairs={{0,1},{1,0},{2,3},{3,2},{4,5},{5,4},{6,7},{7,6},{8,9},{9,8},{10,11... | collective-permute-start | bytes 393224 | tf_op jit(solution)/shard_map/ppermute | solution.py:332

commit v14 on v13

--- a/solution.py
+++ b/solution.py
@@ -246,6 +246,8 @@
 def assemble(step, blocks, rows_dev, width, high, low):
     limit = (step + 1) * width - lax.axis_index("prow") * rows_dev
     for block, start in blocks:
+        if block is None:
+            continue
         rows = block.shape[0]
         below = start + iota(block.shape, 0) >= limit
         block_high, block_low = split(jnp.where(below, -block[...], F32(0)))
@@ -253,8 +255,9 @@
         low[pl.ds(start, rows), :] = block_low
 
 
-def halve(step, rows_dev, width, *refs):
-    assemble(step, pair_blocks(refs[:-2]), rows_dev, width, refs[-2], refs[-1])
+def halve(step, rows_dev, width, own, near, *refs):
+    blocks = pair_blocks([own, near, None, None, *refs[:-2]])
+    assemble(step, blocks, rows_dev, width, refs[-2], refs[-1])
 
 
 def update(step, base, pivots, upper_in, displaced_in, *refs):
@@ -278,30 +281,57 @@
         out[part, :] = jnp.where(jnp.sum(hit, axis=1, keepdims=True) == 0, value, F32(0))
 
 
-def finish(bits, step, base, pivots, inverse, owner, top, high, low, sent, *refs):
-    received, (out, result, sems) = refs[:-3], refs[-3:]
+def opposite_chip(chips):
+    return lax.rem(lax.axis_index("pcol") // 2 + chips // 2, chips)
+
+
+def with_top(step, start, value, upper):
+    part, width = value.shape[0], upper.shape[0]
+    inside = start - step * width
+    chosen = (lax.axis_index("prow") == 0) & (inside >= 0) & (inside < width)
+    place = pl.multiple_of(jnp.clip(inside, 0, width - part), part)
+    return jnp.where(chosen, upper[pl.ds(place, part), :], value)
+
+
+def finish(bits, step, part, base, pivots, inverse, owner, top, high, low, sent, *refs):
+    received, (out, upper_out, partial, result, sems) = refs[:-5], refs[-5:]
     rows_dev = base.shape[0]
+    chips = rows_dev // part
     picked = picked_rows(bits, sent, received, owner)
     width = picked.shape[0]
-    upper_full = dot(split(inverse[step]), split(picked))
+    upper_out[...] = dot(split(inverse[step]), split(picked))
     offset = local_rows(pivots, step, rows_dev)
-    upper = split(upper_full)
+    upper = split(upper_out[...])
     displaced = split(displaced_rows(bits, received, top[...]))
     copies = []
-    part = rows_dev // sems.shape[0]
-    for start in range(0, rows_dev, part):
-        rows = slice(start, start + part)
-        gather = one_hot(iota((part, width), 0) + start, offset)
-        value = base[rows, :] + (pick(gather, displaced) + dot((high[rows, :], low[rows, :]), upper))
-        inside = start - step * width
-        if 0 <= inside < width:
-            value = jnp.where(lax.axis_index("prow") == 0, upper_full[inside : inside + part, :], value)
-        result[rows, :] = value
-        place = pl.ds(start, part)
-        copies.append(pltpu.make_async_copy(result.at[place, :], out.at[place, :], sems.at[len(copies)]))
+    for turn in range(1, chips + 1):
+        start = pl.multiple_of(lax.rem(opposite_chip(chips) + turn, chips) * part, part)
+        rows = pl.ds(start, part)
+        value = base[rows, :] + pick(one_hot(iota((part, width), 0) + start, offset), displaced)
+        if turn == chips:
+            partial[...] = value
+            break
+        value = value + dot((high[rows, :], low[rows, :]), upper)
+        result[rows, :] = with_top(step, start, value, upper_out)
+        copies.append(pltpu.make_async_copy(result.at[rows, :], out.at[rows, :], sems.at[turn - 1]))
         copies[-1].start()
     for copy in copies:
         copy.wait()
+
+
+def far_rows(step, chips, far, far_back, upper, partial, before, out, panel, result, sem):
+    rows, (part, width) = far.shape[0], partial.shape
+    core = lax.rem(lax.axis_index("pcol"), 2)
+    panel[pl.ds(pl.multiple_of(core * rows, rows), rows), :] = far[...]
+    panel[pl.ds(pl.multiple_of((1 - core) * rows, rows), rows), :] = far_back[...]
+    start = pl.multiple_of(opposite_chip(chips) * part, part)
+    limit = (step + 1) * upper.shape[0] - lax.axis_index("prow") * chips * part
+    factor = jnp.where(start + iota(panel.shape, 0) >= limit, -panel[...], F32(0))
+    value = partial[...] + dot(split(factor), split(upper[...]))
+    result[...] = with_top(step, start, value, upper)
+    copy = pltpu.make_async_copy(result, out.at[pl.ds(start, part), :], sem)
+    copy.start()
+    copy.wait()
 
 
 def stack(one, other, out):
@@ -360,13 +390,14 @@
     square = shape((width, columns), F32)
     full = shape((rows_dev, columns), F32)
 
-    def call(kernel, name, operands, outs, specs=None, out_specs=None, scratch=()):
+    def call(kernel, name, operands, outs, specs=None, out_specs=None, scratch=(), aliases=None):
         return pl.pallas_call(
             kernel,
             out_shape=outs,
             in_specs=specs or [VMEM] * len(operands),
             out_specs=out_specs or jax.tree.map(lambda _: VMEM, outs),
             scratch_shapes=scratch,
+            input_output_aliases=aliases or {},
             compiler_params=GRANT,
             cost_estimate=pl.CostEstimate(COST[name], 0, 0) if name in COST else None,
             name=name,
@@ -434,19 +465,30 @@
     sent, received = exchange(slots, 1, [top])
     second = [own[1], near, far, across(after(far, own[1], "far_piece"), process_columns)]
     second += pairs + [across(after(piece, sent, "pair_piece"), process_columns) for piece in pairs]
+    part, depth = 2 * block.shape[0], block.shape[1]
     high, low = call(
         functools.partial(halve, 1, rows_dev, width),
         "halve",
-        second,
-        [shape((rows_dev, l_panels.shape[2]), BF16)] * 2,
-    )
-    return call(
-        functools.partial(finish, bits, 1),
+        second[:2] + second[4:],
+        [shape((rows_dev, depth), BF16)] * 2,
+    )
+    out, upper, partial = call(
+        functools.partial(finish, bits, 1, part),
         "finish",
         [base, pivots, l_inverse, owner[1], top, high, low, sent, *received],
+        [full, square, shape((part, columns), F32)],
+        out_specs=[HBM, VMEM, VMEM],
+        scratch=[pltpu.VMEM((rows_dev, columns), F32), pltpu.SemaphoreType.DMA((rows_dev // part - 1,))],
+    )
+    return call(
+        functools.partial(far_rows, 1, rows_dev // part),
+        "far_rows",
+        [*second[2:4], upper, partial, out],
         full,
+        specs=[VMEM] * 4 + [HBM],
         out_specs=HBM,
-        scratch=[pltpu.VMEM((rows_dev, columns), F32), pltpu.SemaphoreType.DMA((chunks,))],
+        scratch=[pltpu.VMEM((part, depth), F32), pltpu.VMEM((part, columns), F32), pltpu.SemaphoreType.DMA],
+        aliases={4: 0},
     )
 
 

time: 35.8 us -> 35.9 us (level)
  Pallas kernels: 7.73 us -> 8.61 us
  waiting for transfers between devices: 14.2 us -> 13.4 us
    ppermute x6, waiting for transfers between devices: 2.18 us -> 0.92 us  [across(): return lax.ppermute(block, 'pcol', [(i, i ^ 1) for i in range(count)])]
    pallas_call x17 -> x18, Pallas kernels: 7.73 us -> 8.61 us  [call(): pl.pallas_call(kernel, out_shape=outs, in_specs=specs or [VMEM] * len(ope...]
    ppermute x4, waiting for transfers between devices: 3.34 us -> 3.8 us  [exchange(): received.append(lax.ppermute(sent, ('prow', 'pcol'), pairs))]
  transfers between devices with their start and end apart: 15 -> 15, of which waited for: 8 -> 8; matrix products, arithmetic and copies ran while one was open for 0% -> 0% of each run, Pallas kernels for 12% -> 17%
where the time goes in v14:
time: 35.9 us; the launch traced here: 35.8 us
  starting transfers between devices  13.6 us (38%)
  waiting for transfers between devices  13.4 us (37%)
  Pallas kernels  8.61 us (24%)
    ppermute x4, waiting for transfers between devices, shift(): lax.ppermute(block, 'pcol', [(i, (i + 2 * distance) % count) for i in ran...  8.72 us
    pallas_call x18, Pallas kernels, call(): pl.pallas_call(kernel, out_shape=outs, in_specs=specs or [VMEM] * len(ope...  8.61 us
    ppermute x4, starting transfers between devices, shift(): lax.ppermute(block, 'pcol', [(i, (i + 2 * distance) % count) for i in ran...  6.77 us
    ppermute x4, starting transfers between devices, exchange(): received.append(lax.ppermute(sent, ('prow', 'pcol'), pairs))  6.39 us
    ppermute x4, waiting for transfers between devices, exchange(): received.append(lax.ppermute(sent, ('prow', 'pcol'), pairs))  3.8 us
    ppermute x6, waiting for transfers between devices, across(): return lax.ppermute(block, 'pcol', [(i, i ^ 1) for i in range(count)])  0.92 us
  transfers between devices with their start and end apart: 15, of which 8 were waited for; matrix products, arithmetic and copies ran while one was open for 0% of the time, Pallas kernels for 17%

profile of v14, /device:TPU:0, one launch (start us, length us, event | category | flops | bytes accessed | tf_op | source)
XLA Modules:
  0.0 35.8 jit_solution(16608327542179045081)
XLA Ops:
  0.0 1.4 %load.1 = (f32[1024,256]{1,0:T(8,128)S(1)}, s32[2,256]{1,0:T(2,128)S(1)}, f32[128,256]{1,0:T(8,128)S(1)}, f32[128,256]{1,0:T(8,128)S(1)}) custom-call(f32[1024,256]{1,0:T(8,128)} %matrix.1, s32[2,256]{1,0:T(2,128)} %pivots.1, f32[2,128,256]{2,1,0:T(8,128)} %panels.1), custom_call_target="tpu_custom_call" | custom-call | tf_op jit(solution)/shard_map/load/pallas_call | solution.py:394
  1.4 3.1 %collective-permute-start.1 = (f32[128,256]{1,0:T(8,128)S(1)}, f32[128,256]{1,0:T(8,128)S(1)}, u32[]{:S(2)}, u32[]{:S(2)}) collective-permute-start(f32[128,256]{1,0:T(8,128)S(1)} %get-tuple-element.32.one.panel.refs_0_), channel_id=1, source_target_pairs={{0,2},{1,3},{2,4},{3,5},{4,6},{5,7},{6,0},{7,1},{8,10},{9,11},{10,... | collective-permute-start | bytes 393224 | tf_op jit(solution)/shard_map/ppermute | solution.py:358
  4.5 0.5 %first_slots.1.sent = f32[256,256]{1,0:T(8,128)S(1)} custom-call(f32[1024,256]{1,0:T(8,128)S(1)} %get-tuple-element.27.matrix, s32[2,256]{1,0:T(2,128)S(1)} %get-tuple-element.28.pivots), custom_call_target="tpu_custom_call" | custom-call | tf_op jit(solution)/shard_map/first_slots/pallas_call | solution.py:394
  5.0 1.6 %collective-permute-start = (f32[256,256]{1,0:T(8,128)S(1)}, f32[256,256]{1,0:T(8,128)S(1)}, u32[]{:S(2)}, u32[]{:S(2)}) collective-permute-start(f32[256,256]{1,0:T(8,128)S(1)} %first_slots.1.sent), channel_id=1, source_target_pairs={{0,8},{1,17},{2,10},{3,19},{4,12},{5,21},{6,14},{7,23},{8,0},{9,25... | collective-permute-start | bytes 786440 | tf_op jit(solution)/shard_map/ppermute | solution.py:418
  6.6 0.7 %prepare.1 = (f32[1024,256]{1,0:T(8,128)S(1)}, f32[256,256]{1,0:T(8,128)S(1)}, s32[256,256]{1,0:T(8,128)S(1)}) custom-call(f32[1024,256]{1,0:T(8,128)S(1)} %get-tuple-element.27.matrix, s32[2,256]{1,0:T(2,128)S(1)} %get-tuple-element.28.pivots), custom_call_target="tpu_custom_call" | custom-call | flops 1000000000 | tf_op jit(solution)/shard_map/prepare/pallas_call | solution.py:394
  7.3 2.3 %collective-permute-start.5 = (f32[128,256]{1,0:T(8,128)S(1)}, f32[128,256]{1,0:T(8,128)S(1)}, u32[]{:S(2)}, u32[]{:S(2)}) collective-permute-start(f32[128,256]{1,0:T(8,128)S(1)} %down_block.1), channel_id=1, source_target_pairs={{0,6},{1,7},{2,0},{3,1},{4,2},{5,3},{6,4},{7,5},{8,14},{9,15},{10,... | collective-permute-start | bytes 393224 | tf_op jit(solution)/shard_map/ppermute | solution.py:358
  9.6 0.5 %collective-permute-done.1.other.refs_1_ = f32[128,256]{1,0:T(8,128)S(1)} collective-permute-done((f32[128,256]{1,0:T(8,128)S(1)}, f32[128,256]{1,0:T(8,128)S(1)}, u32[]{:S(2)}, u32[]{:S(2)}) %collective-permute-start.1) | collective-permute-done | bytes 131104 | tf_op jit(solution)/shard_map/ppermute | solution.py:358
  10.2 0.3 holders.1
  10.5 1.0 %collective-permute-done.received.refs_0_ = f32[256,256]{1,0:T(8,128)S(1)} collective-permute-done((f32[256,256]{1,0:T(8,128)S(1)}, f32[256,256]{1,0:T(8,128)S(1)}, u32[]{:S(2)}, u32[]{:S(2)}) %collective-permute-start) | collective-permute-done | bytes 262176 | tf_op jit(solution)/shard_map/ppermute | solution.py:418
  11.5 0.2 collective-permute-done.2.refs_0_.refs_4_
  11.8 1.6 %collective-permute-start.3 = (f32[256,256]{1,0:T(8,128)S(1)}, f32[256,256]{1,0:T(8,128)S(1)}, u32[]{:S(2)}, u32[]{:S(2)}) collective-permute-start(f32[256,256]{1,0:T(8,128)S(1)} %merge.2.sent.before), channel_id=1, source_target_pairs={{0,16},{1,9},{2,18},{3,11},{4,20},{5,13},{6,22},{7,15},{8,24},{9,1... | collective-permute-start | bytes 786440 | tf_op jit(solution)/shard_map/ppermute | solution.py:418
  13.5 4.4 %collective-permute-done.4.refs_2_ = f32[128,256]{1,0:T(8,128)S(1)} collective-permute-done((f32[128,256]{1,0:T(8,128)S(1)}, f32[128,256]{1,0:T(8,128)S(1)}, u32[]{:S(2)}, u32[]{:S(2)}) %collective-permute-start.4) | collective-permute-done | bytes 131104 | tf_op jit(solution)/shard_map/ppermute | solution.py:358
  18.0 0.6 %collect.1 = (bf16[256,256]{1,0:T(8,128)(2,1)S(1)}, bf16[256,256]{1,0:T(8,128)(2,1)S(1)}) custom-call(s32[256,256]{1,0:T(8,128)S(1)} %get-tuple-element.31.before.places, f32[128,256]{1,0:T(8,128)S(1)} %get-tuple-element.32.one.panel.refs_0_, f32[128,256]{1,0:T(8,128)S(1)} %collective-permute-done.1.other.refs_1_, ...), custom_call_target="tpu_custom_call" | custom-call | flops 1500000000 | tf_op jit(solution)/shard_map/collect/pallas_call | solution.py:394
  18.6 0.7 %collective-permute-done.6.refs_4_.refs_5_ = f32[128,256]{1,0:T(8,128)S(1)} collective-permute-done((f32[128,256]{1,0:T(8,128)S(1)}, f32[128,256]{1,0:T(8,128)S(1)}, u32[]{:S(2)}, u32[]{:S(2)}) %collective-permute-start.6) | collective-permute-done | bytes 131104 | tf_op jit(solution)/shard_map/ppermute | solution.py:362
  19.2 0.7 %solve.1 = (f32[256,256]{1,0:T(8,128)S(1)}, f32[256,256]{1,0:T(8,128)S(1)}, f32[256,256]{1,0:T(8,128)S(1)}) custom-call(f32[1024,256]{1,0:T(8,128)S(1)} %get-tuple-element.27.matrix, s32[2,256]{1,0:T(2,128)S(1)} %get-tuple-element.28.pivots, f32[2,256,256]{2,1,0:T(8,128)S(1)} %copy-done, s32[256,256]{1,0:T(8,128)S(1)} %get-tuple-element.29.owner, ...), custom_call_target="tpu_custom_call" | custom-call | tf_op jit(solution)/shard_map/solve/pallas_call | solution.py:394
  20.0 1.6 %collective-permute-start.12 = (f32[256,256]{1,0:T(8,128)S(1)}, f32[256,256]{1,0:T(8,128)S(1)}, u32[]{:S(2)}, u32[]{:S(2)}) collective-permute-start(f32[256,256]{1,0:T(8,128)S(1)} %get-tuple-element.35.before.sent), channel_id=1, source_target_pairs={{0,8},{1,17},{2,10},{3,19},{4,12},{5,21},{6,14},{7,23},{8,0},{9,25... | collective-permute-start | bytes 786440 | tf_op jit(solution)/shard_map/ppermute | solution.py:418
  21.5 1.4 %collective-permute-start.8 = (f32[128,256]{1,0:T(8,128)S(1)}, f32[128,256]{1,0:T(8,128)S(1)}, u32[]{:S(2)}, u32[]{:S(2)}) collective-permute-start(f32[128,256]{1,0:T(8,128)S(1)} %far_block.1), channel_id=1, source_target_pairs={{0,4},{1,5},{2,6},{3,7},{4,0},{5,1},{6,2},{7,3},{8,12},{9,13},{10,... | collective-permute-start | bytes 393224 | tf_op jit(solution)/shard_map/ppermute | solution.py:358
  22.9 1.1 %update.1 = (f32[1024,256]{1,0:T(8,128)S(1)}, f32[256,256]{1,0:T(8,128)S(1)}) custom-call(f32[1024,256]{1,0:T(8,128)S(1)} %get-tuple-element.36.base, s32[2,256]{1,0:T(2,128)S(1)} %get-tuple-element.28.pivots, f32[256,256]{1,0:T(8,128)S(1)} %get-tuple-element.37.upper_in, f32[256,256]{1,0:T(8,128)S(1)} %get-tuple-element.38.displaced_in, ...), custom_call_target="tpu_custom_call" | custom-call | flops 5000000000 | tf_op jit(solution)/shard_map/update/pallas_call | solution.py:394
  24.0 2.4 %collective-permute-done.12.received.refs_0_ = f32[256,256]{1,0:T(8,128)S(1)} collective-permute-done((f32[256,256]{1,0:T(8,128)S(1)}, f32[256,256]{1,0:T(8,128)S(1)}, u32[]{:S(2)}, u32[]{:S(2)}) %collective-permute-start.12) | collective-permute-done | bytes 262176 | tf_op jit(solution)/shard_map/ppermute | solution.py:418
  26.5 1.6 %collective-permute-start.14 = (f32[256,256]{1,0:T(8,128)S(1)}, f32[256,256]{1,0:T(8,128)S(1)}, u32[]{:S(2)}, u32[]{:S(2)}) collective-permute-start(f32[256,256]{1,0:T(8,128)S(1)} %merge.3.before.sent), channel_id=1, source_target_pairs={{0,16},{1,9},{2,18},{3,11},{4,20},{5,13},{6,22},{7,15},{8,24},{9,1... | collective-permute-start | bytes 786440 | tf_op jit(solution)/shard_map/ppermute | solution.py:418
  28.2 3.8 %collective-permute-done.8.panel.far = f32[128,256]{1,0:T(8,128)S(1)} collective-permute-done((f32[128,256]{1,0:T(8,128)S(1)}, f32[128,256]{1,0:T(8,128)S(1)}, u32[]{:S(2)}, u32[]{:S(2)}) %collective-permute-start.8) | collective-permute-done | bytes 131104 | tf_op jit(solution)/shard_map/ppermute | solution.py:358
  32.4 0.5 %collective-permute-done.14.refs_1_ = f32[256,256]{1,0:T(8,128)S(1)} collective-permute-done((f32[256,256]{1,0:T(8,128)S(1)}, f32[256,256]{1,0:T(8,128)S(1)}, u32[]{:S(2)}, u32[]{:S(2)}) %collective-permute-start.14) | collective-permute-done | bytes 262176 | tf_op jit(solution)/shard_map/ppermute | solution.py:418
  32.9 1.8 %finish.1 = (f32[1024,256]{1,0:T(8,128)}, f32[256,256]{1,0:T(8,128)S(1)}, f32[256,256]{1,0:T(8,128)S(1)}) custom-call(f32[1024,256]{1,0:T(8,128)S(1)} %get-tuple-element.39.base, s32[2,256]{1,0:T(2,128)S(1)} %get-tuple-element.28.pivots, f32[2,256,256]{2,1,0:T(8,128)S(1)} %copy-done, s32[256,256]{1,0:T(8,128)S(1)} %get-tuple-element.40.owner, ...), custom_call_target="tpu_custom_call" | custom-call | tf_op jit(solution)/shard_map/finish/pallas_call | solution.py:394
  34.8 1.0 %far_rows.1 = f32[1024,256]{1,0:T(8,128)} custom-call(f32[128,256]{1,0:T(8,128)S(1)} %collective-permute-done.8.panel.far, f32[128,256]{1,0:T(8,128)S(1)} %collective-permute-done.9.far_back, f32[256,256]{1,0:T(8,128)S(1)} %get-tuple-element.44.upper, f32[256,256]{1,0:T(8,128)S(1)} %get-tuple-element.45.partial, ...), custom_call_target="tpu_custom_call", output_to_operand_aliasing={{}: (4, {})} | custom-call | tf_op jit(solution)/shard_map/far_rows/pallas_call | solution.py:394
  (26 shorter events, 0.9 us)
Async XLA Ops:
  1.4 8.7 %collective-permute-start.1 = (f32[128,256]{1,0:T(8,128)S(1)}, f32[128,256]{1,0:T(8,128)S(1)}, u32[]{:S(2)}, u32[]{:S(2)}) collective-permute-start(f32[128,256]{1,0:T(8,128)S(1)} %get-tuple-element.32.one.panel.refs_0_), channel_id=1, source_target_pairs={{0,2},{1,3},{2,4},{3,5},{4,6},{5,7},{6,0},{7,1},{8,10},{9,11},{10,... | collective-permute-start | bytes 393224 | tf_op jit(solution)/shard_map/ppermute | solution.py:358
  5.0 6.4 %collective-permute-start = (f32[256,256]{1,0:T(8,128)S(1)}, f32[256,256]{1,0:T(8,128)S(1)}, u32[]{:S(2)}, u32[]{:S(2)}) collective-permute-start(f32[256,256]{1,0:T(8,128)S(1)} %first_slots.1.sent), channel_id=1, source_target_pairs={{0,8},{1,17},{2,10},{3,19},{4,12},{5,21},{6,14},{7,23},{8,0},{9,25... | collective-permute-start | bytes 786440 | tf_op jit(solution)/shard_map/ppermute | solution.py:418
  7.3 6.1 %collective-permute-start.5 = (f32[128,256]{1,0:T(8,128)S(1)}, f32[128,256]{1,0:T(8,128)S(1)}, u32[]{:S(2)}, u32[]{:S(2)}) collective-permute-start(f32[128,256]{1,0:T(8,128)S(1)} %down_block.1), channel_id=1, source_target_pairs={{0,6},{1,7},{2,0},{3,1},{4,2},{5,3},{6,4},{7,5},{8,14},{9,15},{10,... | collective-permute-start | bytes 393224 | tf_op jit(solution)/shard_map/ppermute | solution.py:358
  9.6 8.3 %collective-permute-start.10 = (f32[128,256]{1,0:T(8,128)S(1)}, f32[128,256]{1,0:T(8,128)S(1)}, u32[]{:S(2)}, u32[]{:S(2)}) collective-permute-start(f32[128,256]{1,0:T(8,128)S(1)} %get-tuple-element.26.panel.before.own), channel_id=1, source_target_pairs={{0,1},{1,0},{2,3},{3,2},{4,5},{5,4},{6,7},{7,6},{8,9},{9,8},{10,11... | collective-permute-start | bytes 393224 | tf_op jit(solution)/shard_map/ppermute | solution.py:362
  10.1 1.6 %collective-permute-start.2 = (f32[256,256]{1,0:T(8,128)S(1)}, f32[256,256]{1,0:T(8,128)S(1)}, u32[]{:S(2)}, u32[]{:S(2)}) collective-permute-start(f32[256,256]{1,0:T(8,128)S(1)} %stack.1), channel_id=1, source_target_pairs={{0,1},{1,0},{2,3},{3,2},{4,5},{5,4},{6,7},{7,6},{8,9},{9,8},{10,11... | collective-permute-start | bytes 786440 | tf_op jit(solution)/shard_map/ppermute | solution.py:362
  10.2 7.7 %collective-permute-start.4 = (f32[128,256]{1,0:T(8,128)S(1)}, f32[128,256]{1,0:T(8,128)S(1)}, u32[]{:S(2)}, u32[]{:S(2)}) collective-permute-start(f32[128,256]{1,0:T(8,128)S(1)} %collective-permute-done.1.other.refs_1_), channel_id=1, source_target_pairs={{0,2},{1,3},{2,4},{3,5},{4,6},{5,7},{6,0},{7,1},{8,10},{9,11},{10,... | collective-permute-start | bytes 393224 | tf_op jit(solution)/shard_map/ppermute | solution.py:358
  11.8 7.4 %collective-permute-start.3 = (f32[256,256]{1,0:T(8,128)S(1)}, f32[256,256]{1,0:T(8,128)S(1)}, u32[]{:S(2)}, u32[]{:S(2)}) collective-permute-start(f32[256,256]{1,0:T(8,128)S(1)} %merge.2.sent.before), channel_id=1, source_target_pairs={{0,16},{1,9},{2,18},{3,11},{4,20},{5,13},{6,22},{7,15},{8,24},{9,1... | collective-permute-start | bytes 786440 | tf_op jit(solution)/shard_map/ppermute | solution.py:418
  13.4 5.1 %collective-permute-start.7 = (f32[128,256]{1,0:T(8,128)S(1)}, f32[128,256]{1,0:T(8,128)S(1)}, u32[]{:S(2)}, u32[]{:S(2)}) collective-permute-start(f32[128,256]{1,0:T(8,128)S(1)} %collective-permute-done.5.refs_3_), channel_id=1, source_target_pairs={{0,1},{1,0},{2,3},{3,2},{4,5},{5,4},{6,7},{7,6},{8,9},{9,8},{10,11... | collective-permute-start | bytes 393224 | tf_op jit(solution)/shard_map/ppermute | solution.py:362
  17.9 1.3 %collective-permute-start.6 = (f32[128,256]{1,0:T(8,128)S(1)}, f32[128,256]{1,0:T(8,128)S(1)}, u32[]{:S(2)}, u32[]{:S(2)}) collective-permute-start(f32[128,256]{1,0:T(8,128)S(1)} %collective-permute-done.4.refs_2_), channel_id=1, source_target_pairs={{0,1},{1,0},{2,3},{3,2},{4,5},{5,4},{6,7},{7,6},{8,9},{9,8},{10,11... | collective-permute-start | bytes 393224 | tf_op jit(solution)/shard_map/ppermute | solution.py:362
  17.9 1.3 %copy-start = (f32[2,256,256]{2,1,0:T(8,128)S(1)}, f32[2,256,256]{2,1,0:T(8,128)}, u32[]{:S(2)}) copy-start(f32[2,256,256]{2,1,0:T(8,128)} %inverse.3) | copy-start | bytes 1572868
  17.9 10.2 %collective-permute-start.11 = (f32[256,256]{1,0:T(8,128)S(1)}, f32[256,256]{1,0:T(8,128)S(1)}, u32[]{:S(2)}, u32[]{:S(2)}) collective-permute-start(f32[256,256]{1,0:T(8,128)S(1)} %pack.1), channel_id=1, source_target_pairs={{0,2},{1,7},{2,4},{3,1},{4,6},{5,3},{6,0},{7,5},{8,10},{9,15},{10,... | collective-permute-start | bytes 786440 | tf_op jit(solution)/shard_map/ppermute | solution.py:380
  20.0 6.4 %collective-permute-start.12 = (f32[256,256]{1,0:T(8,128)S(1)}, f32[256,256]{1,0:T(8,128)S(1)}, u32[]{:S(2)}, u32[]{:S(2)}) collective-permute-start(f32[256,256]{1,0:T(8,128)S(1)} %get-tuple-element.35.before.sent), channel_id=1, source_target_pairs={{0,8},{1,17},{2,10},{3,19},{4,12},{5,21},{6,14},{7,23},{8,0},{9,25... | collective-permute-start | bytes 786440 | tf_op jit(solution)/shard_map/ppermute | solution.py:418
  21.5 10.5 %collective-permute-start.8 = (f32[128,256]{1,0:T(8,128)S(1)}, f32[128,256]{1,0:T(8,128)S(1)}, u32[]{:S(2)}, u32[]{:S(2)}) collective-permute-start(f32[128,256]{1,0:T(8,128)S(1)} %far_block.1), channel_id=1, source_target_pairs={{0,4},{1,5},{2,6},{3,7},{4,0},{5,1},{6,2},{7,3},{8,12},{9,13},{10,... | collective-permute-start | bytes 393224 | tf_op jit(solution)/shard_map/ppermute | solution.py:358
  26.5 6.4 %collective-permute-start.14 = (f32[256,256]{1,0:T(8,128)S(1)}, f32[256,256]{1,0:T(8,128)S(1)}, u32[]{:S(2)}, u32[]{:S(2)}) collective-permute-start(f32[256,256]{1,0:T(8,128)S(1)} %merge.3.before.sent), channel_id=1, source_target_pairs={{0,16},{1,9},{2,18},{3,11},{4,20},{5,13},{6,22},{7,15},{8,24},{9,1... | collective-permute-start | bytes 786440 | tf_op jit(solution)/shard_map/ppermute | solution.py:418
  28.1 4.1 %collective-permute-start.13 = (f32[256,256]{1,0:T(8,128)S(1)}, f32[256,256]{1,0:T(8,128)S(1)}, u32[]{:S(2)}, u32[]{:S(2)}) collective-permute-start(f32[256,256]{1,0:T(8,128)S(1)} %pair_piece.1), channel_id=1, source_target_pairs={{0,1},{1,0},{2,3},{3,2},{4,5},{5,4},{6,7},{7,6},{8,9},{9,8},{10,11... | collective-permute-start | bytes 786440 | tf_op jit(solution)/shard_map/ppermute | solution.py:362
  32.1 2.7 %collective-permute-start.9 = (f32[128,256]{1,0:T(8,128)S(1)}, f32[128,256]{1,0:T(8,128)S(1)}, u32[]{:S(2)}, u32[]{:S(2)}) collective-permute-start(f32[128,256]{1,0:T(8,128)S(1)} %far_piece.1), channel_id=1, source_target_pairs={{0,1},{1,0},{2,3},{3,2},{4,5},{5,4},{6,7},{7,6},{8,9},{9,8},{10,11... | collective-permute-start | bytes 393224 | tf_op jit(solution)/shard_map/ppermute | solution.py:362

commit v15 on v13

--- a/solution.py
+++ b/solution.py
@@ -246,6 +246,8 @@
 def assemble(step, blocks, rows_dev, width, high, low):
     limit = (step + 1) * width - lax.axis_index("prow") * rows_dev
     for block, start in blocks:
+        if block is None:
+            continue
         rows = block.shape[0]
         below = start + iota(block.shape, 0) >= limit
         block_high, block_low = split(jnp.where(below, -block[...], F32(0)))
@@ -253,8 +255,9 @@
         low[pl.ds(start, rows), :] = block_low
 
 
-def halve(step, rows_dev, width, *refs):
-    assemble(step, pair_blocks(refs[:-2]), rows_dev, width, refs[-2], refs[-1])
+def halve(step, rows_dev, width, own, near, *refs):
+    blocks = pair_blocks([own, near, None, None, *refs[:-2]])
+    assemble(step, blocks, rows_dev, width, refs[-2], refs[-1])
 
 
 def update(step, base, pivots, upper_in, displaced_in, *refs):
@@ -278,27 +281,45 @@
         out[part, :] = jnp.where(jnp.sum(hit, axis=1, keepdims=True) == 0, value, F32(0))
 
 
-def finish(bits, step, base, pivots, inverse, owner, top, high, low, sent, *refs):
-    received, (out, result, sems) = refs[:-3], refs[-3:]
-    rows_dev = base.shape[0]
+def opposite_chip(chips):
+    return lax.rem(lax.axis_index("pcol") // 2 + chips // 2, chips)
+
+
+def with_top(step, start, value, upper):
+    part, width = value.shape[0], upper.shape[0]
+    inside = start - step * width
+    chosen = (lax.axis_index("prow") == 0) & (inside >= 0) & (inside < width)
+    place = pl.multiple_of(jnp.clip(inside, 0, width - part), part)
+    return jnp.where(chosen, upper[pl.ds(place, part), :], value)
+
+
+def finish(bits, step, base, pivots, inverse, owner, top, high, low, far, far_back, sent, *refs):
+    received, (out, panel, upper_ref, result, sems) = refs[:-5], refs[-5:]
+    rows_dev, chips = base.shape[0], sems.shape[0]
+    part = rows_dev // chips
     picked = picked_rows(bits, sent, received, owner)
     width = picked.shape[0]
-    upper_full = dot(split(inverse[step]), split(picked))
+    upper_ref[...] = dot(split(inverse[step]), split(picked))
     offset = local_rows(pivots, step, rows_dev)
-    upper = split(upper_full)
+    upper = split(upper_ref[...])
     displaced = split(displaced_rows(bits, received, top[...]))
+    rows = far.shape[0]
+    core = lax.rem(lax.axis_index("pcol"), 2)
+    panel[pl.ds(pl.multiple_of(core * rows, rows), rows), :] = far[...]
+    panel[pl.ds(pl.multiple_of((1 - core) * rows, rows), rows), :] = far_back[...]
+    limit = (step + 1) * width - lax.axis_index("prow") * rows_dev
     copies = []
-    part = rows_dev // sems.shape[0]
-    for start in range(0, rows_dev, part):
-        rows = slice(start, start + part)
+    for turn in range(1, chips + 1):
+        start = pl.multiple_of(lax.rem(opposite_chip(chips) + turn, chips) * part, part)
+        rows = pl.ds(start, part)
+        if turn < chips:
+            factor = (high[rows, :], low[rows, :])
+        else:
+            factor = split(jnp.where(start + iota(panel.shape, 0) >= limit, -panel[...], F32(0)))
         gather = one_hot(iota((part, width), 0) + start, offset)
-        value = base[rows, :] + (pick(gather, displaced) + dot((high[rows, :], low[rows, :]), upper))
-        inside = start - step * width
-        if 0 <= inside < width:
-            value = jnp.where(lax.axis_index("prow") == 0, upper_full[inside : inside + part, :], value)
-        result[rows, :] = value
-        place = pl.ds(start, part)
-        copies.append(pltpu.make_async_copy(result.at[place, :], out.at[place, :], sems.at[len(copies)]))
+        value = base[rows, :] + (pick(gather, displaced) + dot(factor, upper))
+        result[rows, :] = with_top(step, start, value, upper_ref)
+        copies.append(pltpu.make_async_copy(result.at[rows, :], out.at[rows, :], sems.at[turn - 1]))
         copies[-1].start()
     for copy in copies:
         copy.wait()
@@ -434,19 +455,25 @@
     sent, received = exchange(slots, 1, [top])
     second = [own[1], near, far, across(after(far, own[1], "far_piece"), process_columns)]
     second += pairs + [across(after(piece, sent, "pair_piece"), process_columns) for piece in pairs]
+    part, depth = 2 * block.shape[0], block.shape[1]
     high, low = call(
         functools.partial(halve, 1, rows_dev, width),
         "halve",
-        second,
-        [shape((rows_dev, l_panels.shape[2]), BF16)] * 2,
+        second[:2] + second[4:],
+        [shape((rows_dev, depth), BF16)] * 2,
     )
     return call(
         functools.partial(finish, bits, 1),
         "finish",
-        [base, pivots, l_inverse, owner[1], top, high, low, sent, *received],
+        [base, pivots, l_inverse, owner[1], top, high, low, *second[2:4], sent, *received],
         full,
         out_specs=HBM,
-        scratch=[pltpu.VMEM((rows_dev, columns), F32), pltpu.SemaphoreType.DMA((chunks,))],
+        scratch=[
+            pltpu.VMEM((part, depth), F32),
+            pltpu.VMEM((width, columns), F32),
+            pltpu.VMEM((rows_dev, columns), F32),
+            pltpu.SemaphoreType.DMA((rows_dev // part,)),
+        ],
     )
 
 

time: 35.8 us -> 35.5 us (level)
  no operation moved by 1% of the time
where the time goes in v15:
time: 35.5 us; the launch traced here: 35.4 us
  waiting for transfers between devices  13.9 us (39%)
  starting transfers between devices  13.6 us (38%)
  Pallas kernels  7.67 us (22%)
    ppermute x4, waiting for transfers between devices, shift(): lax.ppermute(block, 'pcol', [(i, (i + 2 * distance) % count) for i in ran...  8.74 us
    pallas_call x17, Pallas kernels, call(): pl.pallas_call(kernel, out_shape=outs, in_specs=specs or [VMEM] * len(ope...  7.67 us
    ppermute x4, starting transfers between devices, shift(): lax.ppermute(block, 'pcol', [(i, (i + 2 * distance) % count) for i in ran...  6.83 us
    ppermute x4, starting transfers between devices, exchange(): received.append(lax.ppermute(sent, ('prow', 'pcol'), pairs))  6.39 us
    ppermute x4, waiting for transfers between devices, exchange(): received.append(lax.ppermute(sent, ('prow', 'pcol'), pairs))  3.25 us
    ppermute x6, waiting for transfers between devices, across(): return lax.ppermute(block, 'pcol', [(i, i ^ 1) for i in range(count)])  1.94 us
  transfers between devices with their start and end apart: 15, of which 8 were waited for; matrix products, arithmetic and copies ran while one was open for 0% of the time, Pallas kernels for 12%

profile of v15, /device:TPU:0, one launch (start us, length us, event | category | flops | bytes accessed | tf_op | source)
XLA Modules:
  0.0 35.4 jit_solution(16284300700405694870)
XLA Ops:
  0.0 1.4 %load.1 = (f32[1024,256]{1,0:T(8,128)S(1)}, s32[2,256]{1,0:T(2,128)S(1)}, f32[128,256]{1,0:T(8,128)S(1)}, f32[128,256]{1,0:T(8,128)S(1)}) custom-call(f32[1024,256]{1,0:T(8,128)} %matrix.1, s32[2,256]{1,0:T(2,128)} %pivots.1, f32[2,128,256]{2,1,0:T(8,128)} %panels.1), custom_call_target="tpu_custom_call" | custom-call | tf_op jit(solution)/shard_map/load/pallas_call | solution.py:385
  1.4 3.1 %collective-permute-start.1 = (f32[128,256]{1,0:T(8,128)S(1)}, f32[128,256]{1,0:T(8,128)S(1)}, u32[]{:S(2)}, u32[]{:S(2)}) collective-permute-start(f32[128,256]{1,0:T(8,128)S(1)} %get-tuple-element.29.one.panel.refs_0_), channel_id=1, source_target_pairs={{0,2},{1,3},{2,4},{3,5},{4,6},{5,7},{6,0},{7,1},{8,10},{9,11},{10,... | collective-permute-start | bytes 393224 | tf_op jit(solution)/shard_map/ppermute | solution.py:349
  4.5 0.5 %first_slots.1.sent = f32[256,256]{1,0:T(8,128)S(1)} custom-call(f32[1024,256]{1,0:T(8,128)S(1)} %get-tuple-element.23.matrix, s32[2,256]{1,0:T(2,128)S(1)} %get-tuple-element.24.pivots), custom_call_target="tpu_custom_call" | custom-call | tf_op jit(solution)/shard_map/first_slots/pallas_call | solution.py:385
  5.0 1.6 %collective-permute-start = (f32[256,256]{1,0:T(8,128)S(1)}, f32[256,256]{1,0:T(8,128)S(1)}, u32[]{:S(2)}, u32[]{:S(2)}) collective-permute-start(f32[256,256]{1,0:T(8,128)S(1)} %first_slots.1.sent), channel_id=1, source_target_pairs={{0,8},{1,17},{2,10},{3,19},{4,12},{5,21},{6,14},{7,23},{8,0},{9,25... | collective-permute-start | bytes 786440 | tf_op jit(solution)/shard_map/ppermute | solution.py:408
  6.6 0.7 %prepare.1 = (f32[1024,256]{1,0:T(8,128)S(1)}, f32[256,256]{1,0:T(8,128)S(1)}, s32[256,256]{1,0:T(8,128)S(1)}) custom-call(f32[1024,256]{1,0:T(8,128)S(1)} %get-tuple-element.23.matrix, s32[2,256]{1,0:T(2,128)S(1)} %get-tuple-element.24.pivots), custom_call_target="tpu_custom_call" | custom-call | flops 1000000000 | tf_op jit(solution)/shard_map/prepare/pallas_call | solution.py:385
  7.3 2.3 %collective-permute-start.5 = (f32[128,256]{1,0:T(8,128)S(1)}, f32[128,256]{1,0:T(8,128)S(1)}, u32[]{:S(2)}, u32[]{:S(2)}) collective-permute-start(f32[128,256]{1,0:T(8,128)S(1)} %down_block.1), channel_id=1, source_target_pairs={{0,6},{1,7},{2,0},{3,1},{4,2},{5,3},{6,4},{7,5},{8,14},{9,15},{10,... | collective-permute-start | bytes 393224 | tf_op jit(solution)/shard_map/ppermute | solution.py:349
  9.6 0.5 %collective-permute-done.1.other.refs_1_ = f32[128,256]{1,0:T(8,128)S(1)} collective-permute-done((f32[128,256]{1,0:T(8,128)S(1)}, f32[128,256]{1,0:T(8,128)S(1)}, u32[]{:S(2)}, u32[]{:S(2)}) %collective-permute-start.1) | collective-permute-done | bytes 131104 | tf_op jit(solution)/shard_map/ppermute | solution.py:349
  10.2 0.3 holders.1
  10.5 1.0 %collective-permute-done.received.refs_0_ = f32[256,256]{1,0:T(8,128)S(1)} collective-permute-done((f32[256,256]{1,0:T(8,128)S(1)}, f32[256,256]{1,0:T(8,128)S(1)}, u32[]{:S(2)}, u32[]{:S(2)}) %collective-permute-start) | collective-permute-done | bytes 262176 | tf_op jit(solution)/shard_map/ppermute | solution.py:408
  11.5 0.2 collective-permute-done.2.refs_0_.refs_4_
  11.8 1.6 %collective-permute-start.3 = (f32[256,256]{1,0:T(8,128)S(1)}, f32[256,256]{1,0:T(8,128)S(1)}, u32[]{:S(2)}, u32[]{:S(2)}) collective-permute-start(f32[256,256]{1,0:T(8,128)S(1)} %merge.2.sent.before), channel_id=1, source_target_pairs={{0,16},{1,9},{2,18},{3,11},{4,20},{5,13},{6,22},{7,15},{8,24},{9,1... | collective-permute-start | bytes 786440 | tf_op jit(solution)/shard_map/ppermute | solution.py:408
  13.5 4.4 %collective-permute-done.4.refs_2_ = f32[128,256]{1,0:T(8,128)S(1)} collective-permute-done((f32[128,256]{1,0:T(8,128)S(1)}, f32[128,256]{1,0:T(8,128)S(1)}, u32[]{:S(2)}, u32[]{:S(2)}) %collective-permute-start.4) | collective-permute-done | bytes 131104 | tf_op jit(solution)/shard_map/ppermute | solution.py:349
  18.0 0.6 %collect.1 = (bf16[256,256]{1,0:T(8,128)(2,1)S(1)}, bf16[256,256]{1,0:T(8,128)(2,1)S(1)}) custom-call(s32[256,256]{1,0:T(8,128)S(1)} %get-tuple-element.28.before.places, f32[128,256]{1,0:T(8,128)S(1)} %get-tuple-element.29.one.panel.refs_0_, f32[128,256]{1,0:T(8,128)S(1)} %collective-permute-done.1.other.refs_1_, ...), custom_call_target="tpu_custom_call" | custom-call | flops 1500000000 | tf_op jit(solution)/shard_map/collect/pallas_call | solution.py:385
  18.6 0.7 %collective-permute-done.6.refs_4_.refs_5_ = f32[128,256]{1,0:T(8,128)S(1)} collective-permute-done((f32[128,256]{1,0:T(8,128)S(1)}, f32[128,256]{1,0:T(8,128)S(1)}, u32[]{:S(2)}, u32[]{:S(2)}) %collective-permute-start.6) | collective-permute-done | bytes 131104 | tf_op jit(solution)/shard_map/ppermute | solution.py:353
  19.2 0.7 %solve.1 = (f32[256,256]{1,0:T(8,128)S(1)}, f32[256,256]{1,0:T(8,128)S(1)}, f32[256,256]{1,0:T(8,128)S(1)}) custom-call(f32[1024,256]{1,0:T(8,128)S(1)} %get-tuple-element.23.matrix, s32[2,256]{1,0:T(2,128)S(1)} %get-tuple-element.24.pivots, f32[2,256,256]{2,1,0:T(8,128)S(1)} %copy-done, s32[256,256]{1,0:T(8,128)S(1)} %get-tuple-element.26.owner, ...), custom_call_target="tpu_custom_call" | custom-call | tf_op jit(solution)/shard_map/solve/pallas_call | solution.py:385
  19.9 1.6 %collective-permute-start.10 = (f32[256,256]{1,0:T(8,128)S(1)}, f32[256,256]{1,0:T(8,128)S(1)}, u32[]{:S(2)}, u32[]{:S(2)}) collective-permute-start(f32[256,256]{1,0:T(8,128)S(1)} %get-tuple-element.38.sent.before), channel_id=1, source_target_pairs={{0,8},{1,17},{2,10},{3,19},{4,12},{5,21},{6,14},{7,23},{8,0},{9,25... | collective-permute-start | bytes 786440 | tf_op jit(solution)/shard_map/ppermute | solution.py:408
  21.5 1.4 %collective-permute-start.12 = (f32[128,256]{1,0:T(8,128)S(1)}, f32[128,256]{1,0:T(8,128)S(1)}, u32[]{:S(2)}, u32[]{:S(2)}) collective-permute-start(f32[128,256]{1,0:T(8,128)S(1)} %far_block.1), channel_id=1, source_target_pairs={{0,4},{1,5},{2,6},{3,7},{4,0},{5,1},{6,2},{7,3},{8,12},{9,13},{10,... | collective-permute-start | bytes 393224 | tf_op jit(solution)/shard_map/ppermute | solution.py:349
  22.9 1.1 %update.1 = (f32[1024,256]{1,0:T(8,128)S(1)}, f32[256,256]{1,0:T(8,128)S(1)}) custom-call(f32[1024,256]{1,0:T(8,128)S(1)} %get-tuple-element.25.base, s32[2,256]{1,0:T(2,128)S(1)} %get-tuple-element.24.pivots, f32[256,256]{1,0:T(8,128)S(1)} %get-tuple-element.32.upper_in, f32[256,256]{1,0:T(8,128)S(1)} %get-tuple-element.33.displaced_in, ...), custom_call_target="tpu_custom_call" | custom-call | flops 5000000000 | tf_op jit(solution)/shard_map/update/pallas_call | solution.py:385
  24.1 2.3 %collective-permute-done.10.received.refs_0_ = f32[256,256]{1,0:T(8,128)S(1)} collective-permute-done((f32[256,256]{1,0:T(8,128)S(1)}, f32[256,256]{1,0:T(8,128)S(1)}, u32[]{:S(2)}, u32[]{:S(2)}) %collective-permute-start.10) | collective-permute-done | bytes 262176 | tf_op jit(solution)/shard_map/ppermute | solution.py:408
  26.5 1.6 %collective-permute-start.14 = (f32[256,256]{1,0:T(8,128)S(1)}, f32[256,256]{1,0:T(8,128)S(1)}, u32[]{:S(2)}, u32[]{:S(2)}) collective-permute-start(f32[256,256]{1,0:T(8,128)S(1)} %merge.3.before.sent), channel_id=1, source_target_pairs={{0,16},{1,9},{2,18},{3,11},{4,20},{5,13},{6,22},{7,15},{8,24},{9,1... | collective-permute-start | bytes 786440 | tf_op jit(solution)/shard_map/ppermute | solution.py:408
  28.2 3.8 %collective-permute-done.12.panel.far = f32[128,256]{1,0:T(8,128)S(1)} collective-permute-done((f32[128,256]{1,0:T(8,128)S(1)}, f32[128,256]{1,0:T(8,128)S(1)}, u32[]{:S(2)}, u32[]{:S(2)}) %collective-permute-start.12) | collective-permute-done | bytes 131104 | tf_op jit(solution)/shard_map/ppermute | solution.py:349
  32.2 0.2 halve.1
  32.4 1.0 %collective-permute-done.13.far_back = f32[128,256]{1,0:T(8,128)S(1)} collective-permute-done((f32[128,256]{1,0:T(8,128)S(1)}, f32[128,256]{1,0:T(8,128)S(1)}, u32[]{:S(2)}, u32[]{:S(2)}) %collective-permute-start.13) | collective-permute-done | bytes 131104 | tf_op jit(solution)/shard_map/ppermute | solution.py:353
  33.5 1.9 %finish.1 = f32[1024,256]{1,0:T(8,128)} custom-call(f32[1024,256]{1,0:T(8,128)S(1)} %get-tuple-element.34.base, s32[2,256]{1,0:T(2,128)S(1)} %get-tuple-element.24.pivots, f32[2,256,256]{2,1,0:T(8,128)S(1)} %copy-done, s32[256,256]{1,0:T(8,128)S(1)} %get-tuple-element.35.owner, f32[256,256]{1,0:T(8,128)S(1)} %get-tuple-element.36.refs_0_.top, ...), custom_call_target="tpu_custom_call" | custom-call | tf_op jit(solution)/shard_map/finish/pallas_call | solution.py:385
  (25 shorter events, 0.7 us)
Async XLA Ops:
  1.4 8.7 %collective-permute-start.1 = (f32[128,256]{1,0:T(8,128)S(1)}, f32[128,256]{1,0:T(8,128)S(1)}, u32[]{:S(2)}, u32[]{:S(2)}) collective-permute-start(f32[128,256]{1,0:T(8,128)S(1)} %get-tuple-element.29.one.panel.refs_0_), channel_id=1, source_target_pairs={{0,2},{1,3},{2,4},{3,5},{4,6},{5,7},{6,0},{7,1},{8,10},{9,11},{10,... | collective-permute-start | bytes 393224 | tf_op jit(solution)/shard_map/ppermute | solution.py:349
  5.0 6.4 %collective-permute-start = (f32[256,256]{1,0:T(8,128)S(1)}, f32[256,256]{1,0:T(8,128)S(1)}, u32[]{:S(2)}, u32[]{:S(2)}) collective-permute-start(f32[256,256]{1,0:T(8,128)S(1)} %first_slots.1.sent), channel_id=1, source_target_pairs={{0,8},{1,17},{2,10},{3,19},{4,12},{5,21},{6,14},{7,23},{8,0},{9,25... | collective-permute-start | bytes 786440 | tf_op jit(solution)/shard_map/ppermute | solution.py:408
  7.3 6.1 %collective-permute-start.5 = (f32[128,256]{1,0:T(8,128)S(1)}, f32[128,256]{1,0:T(8,128)S(1)}, u32[]{:S(2)}, u32[]{:S(2)}) collective-permute-start(f32[128,256]{1,0:T(8,128)S(1)} %down_block.1), channel_id=1, source_target_pairs={{0,6},{1,7},{2,0},{3,1},{4,2},{5,3},{6,4},{7,5},{8,14},{9,15},{10,... | collective-permute-start | bytes 393224 | tf_op jit(solution)/shard_map/ppermute | solution.py:349
  9.6 8.3 %collective-permute-start.8 = (f32[128,256]{1,0:T(8,128)S(1)}, f32[128,256]{1,0:T(8,128)S(1)}, u32[]{:S(2)}, u32[]{:S(2)}) collective-permute-start(f32[128,256]{1,0:T(8,128)S(1)} %get-tuple-element.37.own.panel.before), channel_id=1, source_target_pairs={{0,1},{1,0},{2,3},{3,2},{4,5},{5,4},{6,7},{7,6},{8,9},{9,8},{10,11... | collective-permute-start | bytes 393224 | tf_op jit(solution)/shard_map/ppermute | solution.py:353
  10.1 1.6 %collective-permute-start.2 = (f32[256,256]{1,0:T(8,128)S(1)}, f32[256,256]{1,0:T(8,128)S(1)}, u32[]{:S(2)}, u32[]{:S(2)}) collective-permute-start(f32[256,256]{1,0:T(8,128)S(1)} %stack.1), channel_id=1, source_target_pairs={{0,1},{1,0},{2,3},{3,2},{4,5},{5,4},{6,7},{7,6},{8,9},{9,8},{10,11... | collective-permute-start | bytes 786440 | tf_op jit(solution)/shard_map/ppermute | solution.py:353
  10.2 7.7 %collective-permute-start.4 = (f32[128,256]{1,0:T(8,128)S(1)}, f32[128,256]{1,0:T(8,128)S(1)}, u32[]{:S(2)}, u32[]{:S(2)}) collective-permute-start(f32[128,256]{1,0:T(8,128)S(1)} %collective-permute-done.1.other.refs_1_), channel_id=1, source_target_pairs={{0,2},{1,3},{2,4},{3,5},{4,6},{5,7},{6,0},{7,1},{8,10},{9,11},{10,... | collective-permute-start | bytes 393224 | tf_op jit(solution)/shard_map/ppermute | solution.py:349
  11.8 7.4 %collective-permute-start.3 = (f32[256,256]{1,0:T(8,128)S(1)}, f32[256,256]{1,0:T(8,128)S(1)}, u32[]{:S(2)}, u32[]{:S(2)}) collective-permute-start(f32[256,256]{1,0:T(8,128)S(1)} %merge.2.sent.before), channel_id=1, source_target_pairs={{0,16},{1,9},{2,18},{3,11},{4,20},{5,13},{6,22},{7,15},{8,24},{9,1... | collective-permute-start | bytes 786440 | tf_op jit(solution)/shard_map/ppermute | solution.py:408
  13.4 5.1 %collective-permute-start.7 = (f32[128,256]{1,0:T(8,128)S(1)}, f32[128,256]{1,0:T(8,128)S(1)}, u32[]{:S(2)}, u32[]{:S(2)}) collective-permute-start(f32[128,256]{1,0:T(8,128)S(1)} %collective-permute-done.5.refs_3_), channel_id=1, source_target_pairs={{0,1},{1,0},{2,3},{3,2},{4,5},{5,4},{6,7},{7,6},{8,9},{9,8},{10,11... | collective-permute-start | bytes 393224 | tf_op jit(solution)/shard_map/ppermute | solution.py:353
  17.9 1.3 %collective-permute-start.6 = (f32[128,256]{1,0:T(8,128)S(1)}, f32[128,256]{1,0:T(8,128)S(1)}, u32[]{:S(2)}, u32[]{:S(2)}) collective-permute-start(f32[128,256]{1,0:T(8,128)S(1)} %collective-permute-done.4.refs_2_), channel_id=1, source_target_pairs={{0,1},{1,0},{2,3},{3,2},{4,5},{5,4},{6,7},{7,6},{8,9},{9,8},{10,11... | collective-permute-start | bytes 393224 | tf_op jit(solution)/shard_map/ppermute | solution.py:353
  17.9 1.3 %copy-start = (f32[2,256,256]{2,1,0:T(8,128)S(1)}, f32[2,256,256]{2,1,0:T(8,128)}, u32[]{:S(2)}) copy-start(f32[2,256,256]{2,1,0:T(8,128)} %inverse.3) | copy-start | bytes 1572868
  17.9 10.2 %collective-permute-start.9 = (f32[256,256]{1,0:T(8,128)S(1)}, f32[256,256]{1,0:T(8,128)S(1)}, u32[]{:S(2)}, u32[]{:S(2)}) collective-permute-start(f32[256,256]{1,0:T(8,128)S(1)} %pack.1), channel_id=1, source_target_pairs={{0,2},{1,7},{2,4},{3,1},{4,6},{5,3},{6,0},{7,5},{8,10},{9,15},{10,... | collective-permute-start | bytes 786440 | tf_op jit(solution)/shard_map/ppermute | solution.py:371
  19.9 6.4 %collective-permute-start.10 = (f32[256,256]{1,0:T(8,128)S(1)}, f32[256,256]{1,0:T(8,128)S(1)}, u32[]{:S(2)}, u32[]{:S(2)}) collective-permute-start(f32[256,256]{1,0:T(8,128)S(1)} %get-tuple-element.38.sent.before), channel_id=1, source_target_pairs={{0,8},{1,17},{2,10},{3,19},{4,12},{5,21},{6,14},{7,23},{8,0},{9,25... | collective-permute-start | bytes 786440 | tf_op jit(solution)/shard_map/ppermute | solution.py:408
  21.5 10.5 %collective-permute-start.12 = (f32[128,256]{1,0:T(8,128)S(1)}, f32[128,256]{1,0:T(8,128)S(1)}, u32[]{:S(2)}, u32[]{:S(2)}) collective-permute-start(f32[128,256]{1,0:T(8,128)S(1)} %far_block.1), channel_id=1, source_target_pairs={{0,4},{1,5},{2,6},{3,7},{4,0},{5,1},{6,2},{7,3},{8,12},{9,13},{10,... | collective-permute-start | bytes 393224 | tf_op jit(solution)/shard_map/ppermute | solution.py:349
  26.5 7.0 %collective-permute-start.14 = (f32[256,256]{1,0:T(8,128)S(1)}, f32[256,256]{1,0:T(8,128)S(1)}, u32[]{:S(2)}, u32[]{:S(2)}) collective-permute-start(f32[256,256]{1,0:T(8,128)S(1)} %merge.3.before.sent), channel_id=1, source_target_pairs={{0,16},{1,9},{2,18},{3,11},{4,20},{5,13},{6,22},{7,15},{8,24},{9,1... | collective-permute-start | bytes 786440 | tf_op jit(solution)/shard_map/ppermute | solution.py:408
  28.1 4.1 %collective-permute-start.11 = (f32[256,256]{1,0:T(8,128)S(1)}, f32[256,256]{1,0:T(8,128)S(1)}, u32[]{:S(2)}, u32[]{:S(2)}) collective-permute-start(f32[256,256]{1,0:T(8,128)S(1)} %pair_piece.1), channel_id=1, source_target_pairs={{0,1},{1,0},{2,3},{3,2},{4,5},{5,4},{6,7},{7,6},{8,9},{9,8},{10,11... | collective-permute-start | bytes 786440 | tf_op jit(solution)/shard_map/ppermute | solution.py:353
  32.1 1.4 %collective-permute-start.13 = (f32[128,256]{1,0:T(8,128)S(1)}, f32[128,256]{1,0:T(8,128)S(1)}, u32[]{:S(2)}, u32[]{:S(2)}) collective-permute-start(f32[128,256]{1,0:T(8,128)S(1)} %far_piece.1), channel_id=1, source_target_pairs={{0,1},{1,0},{2,3},{3,2},{4,5},{5,4},{6,7},{7,6},{8,9},{9,8},{10,11... | collective-permute-start | bytes 393224 | tf_op jit(solution)/shard_map/ppermute | solution.py:353

commit v16 on v15

--- a/solution.py
+++ b/solution.py
@@ -38,12 +38,15 @@
     return high, low
 
 
-def dot(left, right):
-    return product(left[0], right[0]) + (product(left[0], right[1]) + product(left[1], right[0]))
+def dot(left, right, gather=None, moved=None):
+    lefts, rights = [left[0], left[0], left[1]], [right[0], right[1], right[0]]
+    if gather is not None:
+        lefts, rights = [gather, gather, *lefts], [*moved, *rights]
+    return product(jnp.concatenate(lefts, axis=1), jnp.concatenate(rights, axis=0))
 
 
 def pick(chosen, right):
-    return product(chosen, right[0]) + product(chosen, right[1])
+    return product(jnp.concatenate([chosen, chosen], axis=1), jnp.concatenate(right, axis=0))
 
 
 def one_hot(left, right):
@@ -272,7 +275,7 @@
     for start in range(0, rows_dev, width):
         part = slice(start, start + width)
         rows = iota((width, width), 0) + start
-        value = base[part, :] + (pick(one_hot(rows, offset), displaced) + dot((high[part, :], low[part, :]), upper))
+        value = base[part, :] + dot((high[part, :], low[part, :]), upper, one_hot(rows, offset), displaced)
         if start == step * width:
             value = jnp.where(lax.axis_index("prow") == 0, upper_in[...], value)
         if start == (step + 1) * width:
@@ -317,7 +320,7 @@
         else:
             factor = split(jnp.where(start + iota(panel.shape, 0) >= limit, -panel[...], F32(0)))
         gather = one_hot(iota((part, width), 0) + start, offset)
-        value = base[rows, :] + (pick(gather, displaced) + dot(factor, upper))
+        value = base[rows, :] + dot(factor, upper, gather, displaced)
         result[rows, :] = with_top(step, start, value, upper_ref)
         copies.append(pltpu.make_async_copy(result.at[rows, :], out.at[rows, :], sems.at[turn - 1]))
         copies[-1].start()

time: 35.5 us -> 35.5 us (level)
  transfers between devices with their start and end apart: 15 -> 15, of which waited for: 8 -> 8; matrix products, arithmetic and copies ran while one was open for 0% -> 0% of each run, Pallas kernels for 12% -> 13%
where the time goes in v16:
time: 35.5 us; the launch traced here: 35.4 us
  waiting for transfers between devices  13.8 us (39%)
  starting transfers between devices  13.7 us (39%)
  Pallas kernels  7.76 us (22%)
    ppermute x4, waiting for transfers between devices, shift(): lax.ppermute(block, 'pcol', [(i, (i + 2 * distance) % count) for i in ran...  8.71 us
    pallas_call x17, Pallas kernels, call(): pl.pallas_call(kernel, out_shape=outs, in_specs=specs or [VMEM] * len(ope...  7.76 us
    ppermute x4, starting transfers between devices, shift(): lax.ppermute(block, 'pcol', [(i, (i + 2 * distance) % count) for i in ran...  6.86 us
    ppermute x4, starting transfers between devices, exchange(): received.append(lax.ppermute(sent, ('prow', 'pcol'), pairs))  6.35 us
    ppermute x4, waiting for transfers between devices, exchange(): received.append(lax.ppermute(sent, ('prow', 'pcol'), pairs))  3.21 us
    ppermute x6, waiting for transfers between devices, across(): return lax.ppermute(block, 'pcol', [(i, i ^ 1) for i in range(count)])  1.89 us
  transfers between devices with their start and end apart: 15, of which 8 were waited for; matrix products, arithmetic and copies ran while one was open for 0% of the time, Pallas kernels for 13%

profile of v16, /device:TPU:0, one launch (start us, length us, event | category | flops | bytes accessed | tf_op | source)
XLA Modules:
  0.0 35.4 jit_solution(845664712166735936)
XLA Ops:
  0.0 1.4 %load.1 = (f32[1024,256]{1,0:T(8,128)S(1)}, s32[2,256]{1,0:T(2,128)S(1)}, f32[128,256]{1,0:T(8,128)S(1)}, f32[128,256]{1,0:T(8,128)S(1)}) custom-call(f32[1024,256]{1,0:T(8,128)} %matrix.1, s32[2,256]{1,0:T(2,128)} %pivots.1, f32[2,128,256]{2,1,0:T(8,128)} %panels.1), custom_call_target="tpu_custom_call" | custom-call | tf_op jit(solution)/shard_map/load/pallas_call | solution.py:388
  1.4 3.1 %collective-permute-start.1 = (f32[128,256]{1,0:T(8,128)S(1)}, f32[128,256]{1,0:T(8,128)S(1)}, u32[]{:S(2)}, u32[]{:S(2)}) collective-permute-start(f32[128,256]{1,0:T(8,128)S(1)} %get-tuple-element.29.one.panel.refs_0_), channel_id=1, source_target_pairs={{0,2},{1,3},{2,4},{3,5},{4,6},{5,7},{6,0},{7,1},{8,10},{9,11},{10,... | collective-permute-start | bytes 393224 | tf_op jit(solution)/shard_map/ppermute | solution.py:352
  4.5 0.6 %first_slots.1.sent = f32[256,256]{1,0:T(8,128)S(1)} custom-call(f32[1024,256]{1,0:T(8,128)S(1)} %get-tuple-element.23.matrix, s32[2,256]{1,0:T(2,128)S(1)} %get-tuple-element.24.pivots), custom_call_target="tpu_custom_call" | custom-call | tf_op jit(solution)/shard_map/first_slots/pallas_call | solution.py:388
  5.1 1.6 %collective-permute-start = (f32[256,256]{1,0:T(8,128)S(1)}, f32[256,256]{1,0:T(8,128)S(1)}, u32[]{:S(2)}, u32[]{:S(2)}) collective-permute-start(f32[256,256]{1,0:T(8,128)S(1)} %first_slots.1.sent), channel_id=1, source_target_pairs={{0,8},{1,17},{2,10},{3,19},{4,12},{5,21},{6,14},{7,23},{8,0},{9,25... | collective-permute-start | bytes 786440 | tf_op jit(solution)/shard_map/ppermute | solution.py:411
  6.6 0.7 %prepare.1 = (f32[1024,256]{1,0:T(8,128)S(1)}, f32[256,256]{1,0:T(8,128)S(1)}, s32[256,256]{1,0:T(8,128)S(1)}) custom-call(f32[1024,256]{1,0:T(8,128)S(1)} %get-tuple-element.23.matrix, s32[2,256]{1,0:T(2,128)S(1)} %get-tuple-element.24.pivots), custom_call_target="tpu_custom_call" | custom-call | flops 1000000000 | tf_op jit(solution)/shard_map/prepare/pallas_call | solution.py:388
  7.4 2.3 %collective-permute-start.5 = (f32[128,256]{1,0:T(8,128)S(1)}, f32[128,256]{1,0:T(8,128)S(1)}, u32[]{:S(2)}, u32[]{:S(2)}) collective-permute-start(f32[128,256]{1,0:T(8,128)S(1)} %down_block.1), channel_id=1, source_target_pairs={{0,6},{1,7},{2,0},{3,1},{4,2},{5,3},{6,4},{7,5},{8,14},{9,15},{10,... | collective-permute-start | bytes 393224 | tf_op jit(solution)/shard_map/ppermute | solution.py:352
  9.7 0.4 %collective-permute-done.1.other.refs_1_ = f32[128,256]{1,0:T(8,128)S(1)} collective-permute-done((f32[128,256]{1,0:T(8,128)S(1)}, f32[128,256]{1,0:T(8,128)S(1)}, u32[]{:S(2)}, u32[]{:S(2)}) %collective-permute-start.1) | collective-permute-done | bytes 131104 | tf_op jit(solution)/shard_map/ppermute | solution.py:352
  10.3 0.2 holders.1
  10.5 1.0 %collective-permute-done.received.refs_0_ = f32[256,256]{1,0:T(8,128)S(1)} collective-permute-done((f32[256,256]{1,0:T(8,128)S(1)}, f32[256,256]{1,0:T(8,128)S(1)}, u32[]{:S(2)}, u32[]{:S(2)}) %collective-permute-start) | collective-permute-done | bytes 262176 | tf_op jit(solution)/shard_map/ppermute | solution.py:411
  11.5 0.2 collective-permute-done.2.refs_0_.refs_4_
  11.8 1.6 %collective-permute-start.3 = (f32[256,256]{1,0:T(8,128)S(1)}, f32[256,256]{1,0:T(8,128)S(1)}, u32[]{:S(2)}, u32[]{:S(2)}) collective-permute-start(f32[256,256]{1,0:T(8,128)S(1)} %merge.2.sent.before), channel_id=1, source_target_pairs={{0,16},{1,9},{2,18},{3,11},{4,20},{5,13},{6,22},{7,15},{8,24},{9,1... | collective-permute-start | bytes 786440 | tf_op jit(solution)/shard_map/ppermute | solution.py:411
  13.4 4.4 %collective-permute-done.4.refs_2_ = f32[128,256]{1,0:T(8,128)S(1)} collective-permute-done((f32[128,256]{1,0:T(8,128)S(1)}, f32[128,256]{1,0:T(8,128)S(1)}, u32[]{:S(2)}, u32[]{:S(2)}) %collective-permute-start.4) | collective-permute-done | bytes 131104 | tf_op jit(solution)/shard_map/ppermute | solution.py:352
  18.0 0.6 %collect.1 = (bf16[256,256]{1,0:T(8,128)(2,1)S(1)}, bf16[256,256]{1,0:T(8,128)(2,1)S(1)}) custom-call(s32[256,256]{1,0:T(8,128)S(1)} %get-tuple-element.28.before.places, f32[128,256]{1,0:T(8,128)S(1)} %get-tuple-element.29.one.panel.refs_0_, f32[128,256]{1,0:T(8,128)S(1)} %collective-permute-done.1.other.refs_1_, ...), custom_call_target="tpu_custom_call" | custom-call | flops 1500000000 | tf_op jit(solution)/shard_map/collect/pallas_call | solution.py:388
  18.6 0.7 %collective-permute-done.6.refs_4_.refs_5_ = f32[128,256]{1,0:T(8,128)S(1)} collective-permute-done((f32[128,256]{1,0:T(8,128)S(1)}, f32[128,256]{1,0:T(8,128)S(1)}, u32[]{:S(2)}, u32[]{:S(2)}) %collective-permute-start.6) | collective-permute-done | bytes 131104 | tf_op jit(solution)/shard_map/ppermute | solution.py:356
  19.2 0.7 %solve.1 = (f32[256,256]{1,0:T(8,128)S(1)}, f32[256,256]{1,0:T(8,128)S(1)}, f32[256,256]{1,0:T(8,128)S(1)}) custom-call(f32[1024,256]{1,0:T(8,128)S(1)} %get-tuple-element.23.matrix, s32[2,256]{1,0:T(2,128)S(1)} %get-tuple-element.24.pivots, f32[2,256,256]{2,1,0:T(8,128)S(1)} %copy-done, s32[256,256]{1,0:T(8,128)S(1)} %get-tuple-element.26.owner, ...), custom_call_target="tpu_custom_call" | custom-call | tf_op jit(solution)/shard_map/solve/pallas_call | solution.py:388
  20.0 1.5 %collective-permute-start.10 = (f32[256,256]{1,0:T(8,128)S(1)}, f32[256,256]{1,0:T(8,128)S(1)}, u32[]{:S(2)}, u32[]{:S(2)}) collective-permute-start(f32[256,256]{1,0:T(8,128)S(1)} %get-tuple-element.38.sent.before), channel_id=1, source_target_pairs={{0,8},{1,17},{2,10},{3,19},{4,12},{5,21},{6,14},{7,23},{8,0},{9,25... | collective-permute-start | bytes 786440 | tf_op jit(solution)/shard_map/ppermute | solution.py:411
  21.5 1.5 %collective-permute-start.12 = (f32[128,256]{1,0:T(8,128)S(1)}, f32[128,256]{1,0:T(8,128)S(1)}, u32[]{:S(2)}, u32[]{:S(2)}) collective-permute-start(f32[128,256]{1,0:T(8,128)S(1)} %far_block.1), channel_id=1, source_target_pairs={{0,4},{1,5},{2,6},{3,7},{4,0},{5,1},{6,2},{7,3},{8,12},{9,13},{10,... | collective-permute-start | bytes 393224 | tf_op jit(solution)/shard_map/ppermute | solution.py:352
  23.0 1.2 %update.1 = (f32[1024,256]{1,0:T(8,128)S(1)}, f32[256,256]{1,0:T(8,128)S(1)}) custom-call(f32[1024,256]{1,0:T(8,128)S(1)} %get-tuple-element.25.base, s32[2,256]{1,0:T(2,128)S(1)} %get-tuple-element.24.pivots, f32[256,256]{1,0:T(8,128)S(1)} %get-tuple-element.32.upper_in, f32[256,256]{1,0:T(8,128)S(1)} %get-tuple-element.33.displaced_in, ...), custom_call_target="tpu_custom_call" | custom-call | flops 5000000000 | tf_op jit(solution)/shard_map/update/pallas_call | solution.py:388
  24.2 2.2 %collective-permute-done.10.received.refs_0_ = f32[256,256]{1,0:T(8,128)S(1)} collective-permute-done((f32[256,256]{1,0:T(8,128)S(1)}, f32[256,256]{1,0:T(8,128)S(1)}, u32[]{:S(2)}, u32[]{:S(2)}) %collective-permute-start.10) | collective-permute-done | bytes 262176 | tf_op jit(solution)/shard_map/ppermute | solution.py:411
  26.5 1.6 %collective-permute-start.14 = (f32[256,256]{1,0:T(8,128)S(1)}, f32[256,256]{1,0:T(8,128)S(1)}, u32[]{:S(2)}, u32[]{:S(2)}) collective-permute-start(f32[256,256]{1,0:T(8,128)S(1)} %merge.3.before.sent), channel_id=1, source_target_pairs={{0,16},{1,9},{2,18},{3,11},{4,20},{5,13},{6,22},{7,15},{8,24},{9,1... | collective-permute-start | bytes 786440 | tf_op jit(solution)/shard_map/ppermute | solution.py:411
  28.2 3.9 %collective-permute-done.12.panel.far = f32[128,256]{1,0:T(8,128)S(1)} collective-permute-done((f32[128,256]{1,0:T(8,128)S(1)}, f32[128,256]{1,0:T(8,128)S(1)}, u32[]{:S(2)}, u32[]{:S(2)}) %collective-permute-start.12) | collective-permute-done | bytes 131104 | tf_op jit(solution)/shard_map/ppermute | solution.py:352
  32.2 0.2 halve.1
  32.5 1.0 %collective-permute-done.13.far_back = f32[128,256]{1,0:T(8,128)S(1)} collective-permute-done((f32[128,256]{1,0:T(8,128)S(1)}, f32[128,256]{1,0:T(8,128)S(1)}, u32[]{:S(2)}, u32[]{:S(2)}) %collective-permute-start.13) | collective-permute-done | bytes 131104 | tf_op jit(solution)/shard_map/ppermute | solution.py:356
  33.5 1.9 %finish.1 = f32[1024,256]{1,0:T(8,128)} custom-call(f32[1024,256]{1,0:T(8,128)S(1)} %get-tuple-element.34.base, s32[2,256]{1,0:T(2,128)S(1)} %get-tuple-element.24.pivots, f32[2,256,256]{2,1,0:T(8,128)S(1)} %copy-done, s32[256,256]{1,0:T(8,128)S(1)} %get-tuple-element.35.owner, f32[256,256]{1,0:T(8,128)S(1)} %get-tuple-element.36.refs_0_.top, ...), custom_call_target="tpu_custom_call" | custom-call | tf_op jit(solution)/shard_map/finish/pallas_call | solution.py:388
  (25 shorter events, 0.7 us)
Async XLA Ops:
  1.4 8.7 %collective-permute-start.1 = (f32[128,256]{1,0:T(8,128)S(1)}, f32[128,256]{1,0:T(8,128)S(1)}, u32[]{:S(2)}, u32[]{:S(2)}) collective-permute-start(f32[128,256]{1,0:T(8,128)S(1)} %get-tuple-element.29.one.panel.refs_0_), channel_id=1, source_target_pairs={{0,2},{1,3},{2,4},{3,5},{4,6},{5,7},{6,0},{7,1},{8,10},{9,11},{10,... | collective-permute-start | bytes 393224 | tf_op jit(solution)/shard_map/ppermute | solution.py:352
  5.1 6.4 %collective-permute-start = (f32[256,256]{1,0:T(8,128)S(1)}, f32[256,256]{1,0:T(8,128)S(1)}, u32[]{:S(2)}, u32[]{:S(2)}) collective-permute-start(f32[256,256]{1,0:T(8,128)S(1)} %first_slots.1.sent), channel_id=1, source_target_pairs={{0,8},{1,17},{2,10},{3,19},{4,12},{5,21},{6,14},{7,23},{8,0},{9,25... | collective-permute-start | bytes 786440 | tf_op jit(solution)/shard_map/ppermute | solution.py:411
  7.4 6.1 %collective-permute-start.5 = (f32[128,256]{1,0:T(8,128)S(1)}, f32[128,256]{1,0:T(8,128)S(1)}, u32[]{:S(2)}, u32[]{:S(2)}) collective-permute-start(f32[128,256]{1,0:T(8,128)S(1)} %down_block.1), channel_id=1, source_target_pairs={{0,6},{1,7},{2,0},{3,1},{4,2},{5,3},{6,4},{7,5},{8,14},{9,15},{10,... | collective-permute-start | bytes 393224 | tf_op jit(solution)/shard_map/ppermute | solution.py:352
  9.7 8.2 %collective-permute-start.8 = (f32[128,256]{1,0:T(8,128)S(1)}, f32[128,256]{1,0:T(8,128)S(1)}, u32[]{:S(2)}, u32[]{:S(2)}) collective-permute-start(f32[128,256]{1,0:T(8,128)S(1)} %get-tuple-element.37.own.panel.before), channel_id=1, source_target_pairs={{0,1},{1,0},{2,3},{3,2},{4,5},{5,4},{6,7},{7,6},{8,9},{9,8},{10,11... | collective-permute-start | bytes 393224 | tf_op jit(solution)/shard_map/ppermute | solution.py:356
  10.1 1.6 %collective-permute-start.2 = (f32[256,256]{1,0:T(8,128)S(1)}, f32[256,256]{1,0:T(8,128)S(1)}, u32[]{:S(2)}, u32[]{:S(2)}) collective-permute-start(f32[256,256]{1,0:T(8,128)S(1)} %stack.1), channel_id=1, source_target_pairs={{0,1},{1,0},{2,3},{3,2},{4,5},{5,4},{6,7},{7,6},{8,9},{9,8},{10,11... | collective-permute-start | bytes 786440 | tf_op jit(solution)/shard_map/ppermute | solution.py:356
  10.3 7.6 %collective-permute-start.4 = (f32[128,256]{1,0:T(8,128)S(1)}, f32[128,256]{1,0:T(8,128)S(1)}, u32[]{:S(2)}, u32[]{:S(2)}) collective-permute-start(f32[128,256]{1,0:T(8,128)S(1)} %collective-permute-done.1.other.refs_1_), channel_id=1, source_target_pairs={{0,2},{1,3},{2,4},{3,5},{4,6},{5,7},{6,0},{7,1},{8,10},{9,11},{10,... | collective-permute-start | bytes 393224 | tf_op jit(solution)/shard_map/ppermute | solution.py:352
  11.8 7.4 %collective-permute-start.3 = (f32[256,256]{1,0:T(8,128)S(1)}, f32[256,256]{1,0:T(8,128)S(1)}, u32[]{:S(2)}, u32[]{:S(2)}) collective-permute-start(f32[256,256]{1,0:T(8,128)S(1)} %merge.2.sent.before), channel_id=1, source_target_pairs={{0,16},{1,9},{2,18},{3,11},{4,20},{5,13},{6,22},{7,15},{8,24},{9,1... | collective-permute-start | bytes 786440 | tf_op jit(solution)/shard_map/ppermute | solution.py:411
  13.4 5.1 %collective-permute-start.7 = (f32[128,256]{1,0:T(8,128)S(1)}, f32[128,256]{1,0:T(8,128)S(1)}, u32[]{:S(2)}, u32[]{:S(2)}) collective-permute-start(f32[128,256]{1,0:T(8,128)S(1)} %collective-permute-done.5.refs_3_), channel_id=1, source_target_pairs={{0,1},{1,0},{2,3},{3,2},{4,5},{5,4},{6,7},{7,6},{8,9},{9,8},{10,11... | collective-permute-start | bytes 393224 | tf_op jit(solution)/shard_map/ppermute | solution.py:356
  17.9 1.3 %collective-permute-start.6 = (f32[128,256]{1,0:T(8,128)S(1)}, f32[128,256]{1,0:T(8,128)S(1)}, u32[]{:S(2)}, u32[]{:S(2)}) collective-permute-start(f32[128,256]{1,0:T(8,128)S(1)} %collective-permute-done.4.refs_2_), channel_id=1, source_target_pairs={{0,1},{1,0},{2,3},{3,2},{4,5},{5,4},{6,7},{7,6},{8,9},{9,8},{10,11... | collective-permute-start | bytes 393224 | tf_op jit(solution)/shard_map/ppermute | solution.py:356
  17.9 1.3 %copy-start = (f32[2,256,256]{2,1,0:T(8,128)S(1)}, f32[2,256,256]{2,1,0:T(8,128)}, u32[]{:S(2)}) copy-start(f32[2,256,256]{2,1,0:T(8,128)} %inverse.3) | copy-start | bytes 1572868
  17.9 10.2 %collective-permute-start.9 = (f32[256,256]{1,0:T(8,128)S(1)}, f32[256,256]{1,0:T(8,128)S(1)}, u32[]{:S(2)}, u32[]{:S(2)}) collective-permute-start(f32[256,256]{1,0:T(8,128)S(1)} %pack.1), channel_id=1, source_target_pairs={{0,2},{1,7},{2,4},{3,1},{4,6},{5,3},{6,0},{7,5},{8,10},{9,15},{10,... | collective-permute-start | bytes 786440 | tf_op jit(solution)/shard_map/ppermute | solution.py:374
  20.0 6.4 %collective-permute-start.10 = (f32[256,256]{1,0:T(8,128)S(1)}, f32[256,256]{1,0:T(8,128)S(1)}, u32[]{:S(2)}, u32[]{:S(2)}) collective-permute-start(f32[256,256]{1,0:T(8,128)S(1)} %get-tuple-element.38.sent.before), channel_id=1, source_target_pairs={{0,8},{1,17},{2,10},{3,19},{4,12},{5,21},{6,14},{7,23},{8,0},{9,25... | collective-permute-start | bytes 786440 | tf_op jit(solution)/shard_map/ppermute | solution.py:411
  21.5 10.6 %collective-permute-start.12 = (f32[128,256]{1,0:T(8,128)S(1)}, f32[128,256]{1,0:T(8,128)S(1)}, u32[]{:S(2)}, u32[]{:S(2)}) collective-permute-start(f32[128,256]{1,0:T(8,128)S(1)} %far_block.1), channel_id=1, source_target_pairs={{0,4},{1,5},{2,6},{3,7},{4,0},{5,1},{6,2},{7,3},{8,12},{9,13},{10,... | collective-permute-start | bytes 393224 | tf_op jit(solution)/shard_map/ppermute | solution.py:352
  26.5 7.0 %collective-permute-start.14 = (f32[256,256]{1,0:T(8,128)S(1)}, f32[256,256]{1,0:T(8,128)S(1)}, u32[]{:S(2)}, u32[]{:S(2)}) collective-permute-start(f32[256,256]{1,0:T(8,128)S(1)} %merge.3.before.sent), channel_id=1, source_target_pairs={{0,16},{1,9},{2,18},{3,11},{4,20},{5,13},{6,22},{7,15},{8,24},{9,1... | collective-permute-start | bytes 786440 | tf_op jit(solution)/shard_map/ppermute | solution.py:411
  28.1 4.1 %collective-permute-start.11 = (f32[256,256]{1,0:T(8,128)S(1)}, f32[256,256]{1,0:T(8,128)S(1)}, u32[]{:S(2)}, u32[]{:S(2)}) collective-permute-start(f32[256,256]{1,0:T(8,128)S(1)} %pair_piece.1), channel_id=1, source_target_pairs={{0,1},{1,0},{2,3},{3,2},{4,5},{5,4},{6,7},{7,6},{8,9},{9,8},{10,11... | collective-permute-start | bytes 786440 | tf_op jit(solution)/shard_map/ppermute | solution.py:356
  32.1 1.4 %collective-permute-start.13 = (f32[128,256]{1,0:T(8,128)S(1)}, f32[128,256]{1,0:T(8,128)S(1)}, u32[]{:S(2)}, u32[]{:S(2)}) collective-permute-start(f32[128,256]{1,0:T(8,128)S(1)} %far_piece.1), channel_id=1, source_target_pairs={{0,1},{1,0},{2,3},{3,2},{4,5},{5,4},{6,7},{7,6},{8,9},{9,8},{10,11... | collective-permute-start | bytes 393224 | tf_op jit(solution)/shard_map/ppermute | solution.py:356

commit v17 on v16

--- a/solution.py
+++ b/solution.py
@@ -298,7 +298,7 @@
 
 def finish(bits, step, base, pivots, inverse, owner, top, high, low, far, far_back, sent, *refs):
     received, (out, panel, upper_ref, result, sems) = refs[:-5], refs[-5:]
-    rows_dev, chips = base.shape[0], sems.shape[0]
+    rows_dev, chips = base.shape[0], sems.shape[0] - 1
     part = rows_dev // chips
     picked = picked_rows(bits, sent, received, owner)
     width = picked.shape[0]
@@ -312,17 +312,19 @@
     panel[pl.ds(pl.multiple_of((1 - core) * rows, rows), rows), :] = far_back[...]
     limit = (step + 1) * width - lax.axis_index("prow") * rows_dev
     copies = []
-    for turn in range(1, chips + 1):
-        start = pl.multiple_of(lax.rem(opposite_chip(chips) + turn, chips) * part, part)
-        rows = pl.ds(start, part)
+    pieces = [(turn, 0, part) for turn in range(1, chips)] + [(chips, 0, part // 2), (chips, part // 2, part // 2)]
+    for turn, skip, size in pieces:
+        start = pl.multiple_of(lax.rem(opposite_chip(chips) + turn, chips) * part + skip, size)
+        rows = pl.ds(start, size)
         if turn < chips:
             factor = (high[rows, :], low[rows, :])
         else:
-            factor = split(jnp.where(start + iota(panel.shape, 0) >= limit, -panel[...], F32(0)))
-        gather = one_hot(iota((part, width), 0) + start, offset)
+            block = panel[skip : skip + size, :]
+            factor = split(jnp.where(start + iota(block.shape, 0) >= limit, -block, F32(0)))
+        gather = one_hot(iota((size, width), 0) + start, offset)
         value = base[rows, :] + dot(factor, upper, gather, displaced)
         result[rows, :] = with_top(step, start, value, upper_ref)
-        copies.append(pltpu.make_async_copy(result.at[rows, :], out.at[rows, :], sems.at[turn - 1]))
+        copies.append(pltpu.make_async_copy(result.at[rows, :], out.at[rows, :], sems.at[len(copies)]))
         copies[-1].start()
     for copy in copies:
         copy.wait()
@@ -475,7 +477,7 @@
             pltpu.VMEM((part, depth), F32),
             pltpu.VMEM((width, columns), F32),
             pltpu.VMEM((rows_dev, columns), F32),
-            pltpu.SemaphoreType.DMA((rows_dev // part,)),
+            pltpu.SemaphoreType.DMA((rows_dev // part + 1,)),
         ],
     )
 

time: 35.5 us -> 35.6 us (level)
  no operation moved by 1% of the time
where the time goes in v17:
time: 35.6 us; the launch traced here: 35.5 us
  waiting for transfers between devices  13.8 us (39%)
  starting transfers between devices  13.7 us (38%)
  Pallas kernels  7.85 us (22%)
    ppermute x4, waiting for transfers between devices, shift(): lax.ppermute(block, 'pcol', [(i, (i + 2 * distance) % count) for i in ran...  8.71 us
    pallas_call x17, Pallas kernels, call(): pl.pallas_call(kernel, out_shape=outs, in_specs=specs or [VMEM] * len(ope...  7.85 us
    ppermute x4, starting transfers between devices, shift(): lax.ppermute(block, 'pcol', [(i, (i + 2 * distance) % count) for i in ran...  6.86 us
    ppermute x4, starting transfers between devices, exchange(): received.append(lax.ppermute(sent, ('prow', 'pcol'), pairs))  6.35 us
    ppermute x4, waiting for transfers between devices, exchange(): received.append(lax.ppermute(sent, ('prow', 'pcol'), pairs))  3.21 us
    ppermute x6, waiting for transfers between devices, across(): return lax.ppermute(block, 'pcol', [(i, i ^ 1) for i in range(count)])  1.89 us
  transfers between devices with their start and end apart: 15, of which 8 were waited for; matrix products, arithmetic and copies ran while one was open for 0% of the time, Pallas kernels for 13%

profile of v17, /device:TPU:0, one launch (start us, length us, event | category | flops | bytes accessed | tf_op | source)
XLA Modules:
  0.0 35.5 jit_solution(9413645680591744487)
XLA Ops:
  0.0 1.4 %load.1 = (f32[1024,256]{1,0:T(8,128)S(1)}, s32[2,256]{1,0:T(2,128)S(1)}, f32[128,256]{1,0:T(8,128)S(1)}, f32[128,256]{1,0:T(8,128)S(1)}) custom-call(f32[1024,256]{1,0:T(8,128)} %matrix.1, s32[2,256]{1,0:T(2,128)} %pivots.1, f32[2,128,256]{2,1,0:T(8,128)} %panels.1), custom_call_target="tpu_custom_call" | custom-call | tf_op jit(solution)/shard_map/load/pallas_call | solution.py:390
  1.4 3.1 %collective-permute-start.1 = (f32[128,256]{1,0:T(8,128)S(1)}, f32[128,256]{1,0:T(8,128)S(1)}, u32[]{:S(2)}, u32[]{:S(2)}) collective-permute-start(f32[128,256]{1,0:T(8,128)S(1)} %get-tuple-element.29.one.panel.refs_0_), channel_id=1, source_target_pairs={{0,2},{1,3},{2,4},{3,5},{4,6},{5,7},{6,0},{7,1},{8,10},{9,11},{10,... | collective-permute-start | bytes 393224 | tf_op jit(solution)/shard_map/ppermute | solution.py:354
  4.5 0.6 %first_slots.1.sent = f32[256,256]{1,0:T(8,128)S(1)} custom-call(f32[1024,256]{1,0:T(8,128)S(1)} %get-tuple-element.23.matrix, s32[2,256]{1,0:T(2,128)S(1)} %get-tuple-element.24.pivots), custom_call_target="tpu_custom_call" | custom-call | tf_op jit(solution)/shard_map/first_slots/pallas_call | solution.py:390
  5.1 1.6 %collective-permute-start = (f32[256,256]{1,0:T(8,128)S(1)}, f32[256,256]{1,0:T(8,128)S(1)}, u32[]{:S(2)}, u32[]{:S(2)}) collective-permute-start(f32[256,256]{1,0:T(8,128)S(1)} %first_slots.1.sent), channel_id=1, source_target_pairs={{0,8},{1,17},{2,10},{3,19},{4,12},{5,21},{6,14},{7,23},{8,0},{9,25... | collective-permute-start | bytes 786440 | tf_op jit(solution)/shard_map/ppermute | solution.py:413
  6.6 0.7 %prepare.1 = (f32[1024,256]{1,0:T(8,128)S(1)}, f32[256,256]{1,0:T(8,128)S(1)}, s32[256,256]{1,0:T(8,128)S(1)}) custom-call(f32[1024,256]{1,0:T(8,128)S(1)} %get-tuple-element.23.matrix, s32[2,256]{1,0:T(2,128)S(1)} %get-tuple-element.24.pivots), custom_call_target="tpu_custom_call" | custom-call | flops 1000000000 | tf_op jit(solution)/shard_map/prepare/pallas_call | solution.py:390
  7.4 2.3 %collective-permute-start.5 = (f32[128,256]{1,0:T(8,128)S(1)}, f32[128,256]{1,0:T(8,128)S(1)}, u32[]{:S(2)}, u32[]{:S(2)}) collective-permute-start(f32[128,256]{1,0:T(8,128)S(1)} %down_block.1), channel_id=1, source_target_pairs={{0,6},{1,7},{2,0},{3,1},{4,2},{5,3},{6,4},{7,5},{8,14},{9,15},{10,... | collective-permute-start | bytes 393224 | tf_op jit(solution)/shard_map/ppermute | solution.py:354
  9.7 0.4 %collective-permute-done.1.other.refs_1_ = f32[128,256]{1,0:T(8,128)S(1)} collective-permute-done((f32[128,256]{1,0:T(8,128)S(1)}, f32[128,256]{1,0:T(8,128)S(1)}, u32[]{:S(2)}, u32[]{:S(2)}) %collective-permute-start.1) | collective-permute-done | bytes 131104 | tf_op jit(solution)/shard_map/ppermute | solution.py:354
  10.3 0.2 holders.1
  10.5 1.0 %collective-permute-done.received.refs_0_ = f32[256,256]{1,0:T(8,128)S(1)} collective-permute-done((f32[256,256]{1,0:T(8,128)S(1)}, f32[256,256]{1,0:T(8,128)S(1)}, u32[]{:S(2)}, u32[]{:S(2)}) %collective-permute-start) | collective-permute-done | bytes 262176 | tf_op jit(solution)/shard_map/ppermute | solution.py:413
  11.5 0.2 collective-permute-done.2.refs_0_.refs_4_
  11.8 1.6 %collective-permute-start.3 = (f32[256,256]{1,0:T(8,128)S(1)}, f32[256,256]{1,0:T(8,128)S(1)}, u32[]{:S(2)}, u32[]{:S(2)}) collective-permute-start(f32[256,256]{1,0:T(8,128)S(1)} %merge.2.sent.before), channel_id=1, source_target_pairs={{0,16},{1,9},{2,18},{3,11},{4,20},{5,13},{6,22},{7,15},{8,24},{9,1... | collective-permute-start | bytes 786440 | tf_op jit(solution)/shard_map/ppermute | solution.py:413
  13.4 4.4 %collective-permute-done.4.refs_2_ = f32[128,256]{1,0:T(8,128)S(1)} collective-permute-done((f32[128,256]{1,0:T(8,128)S(1)}, f32[128,256]{1,0:T(8,128)S(1)}, u32[]{:S(2)}, u32[]{:S(2)}) %collective-permute-start.4) | collective-permute-done | bytes 131104 | tf_op jit(solution)/shard_map/ppermute | solution.py:354
  18.0 0.6 %collect.1 = (bf16[256,256]{1,0:T(8,128)(2,1)S(1)}, bf16[256,256]{1,0:T(8,128)(2,1)S(1)}) custom-call(s32[256,256]{1,0:T(8,128)S(1)} %get-tuple-element.28.before.places, f32[128,256]{1,0:T(8,128)S(1)} %get-tuple-element.29.one.panel.refs_0_, f32[128,256]{1,0:T(8,128)S(1)} %collective-permute-done.1.other.refs_1_, ...), custom_call_target="tpu_custom_call" | custom-call | flops 1500000000 | tf_op jit(solution)/shard_map/collect/pallas_call | solution.py:390
  18.6 0.7 %collective-permute-done.6.refs_4_.refs_5_ = f32[128,256]{1,0:T(8,128)S(1)} collective-permute-done((f32[128,256]{1,0:T(8,128)S(1)}, f32[128,256]{1,0:T(8,128)S(1)}, u32[]{:S(2)}, u32[]{:S(2)}) %collective-permute-start.6) | collective-permute-done | bytes 131104 | tf_op jit(solution)/shard_map/ppermute | solution.py:358
  19.2 0.7 %solve.1 = (f32[256,256]{1,0:T(8,128)S(1)}, f32[256,256]{1,0:T(8,128)S(1)}, f32[256,256]{1,0:T(8,128)S(1)}) custom-call(f32[1024,256]{1,0:T(8,128)S(1)} %get-tuple-element.23.matrix, s32[2,256]{1,0:T(2,128)S(1)} %get-tuple-element.24.pivots, f32[2,256,256]{2,1,0:T(8,128)S(1)} %copy-done, s32[256,256]{1,0:T(8,128)S(1)} %get-tuple-element.26.owner, ...), custom_call_target="tpu_custom_call" | custom-call | tf_op jit(solution)/shard_map/solve/pallas_call | solution.py:390
  20.0 1.5 %collective-permute-start.10 = (f32[256,256]{1,0:T(8,128)S(1)}, f32[256,256]{1,0:T(8,128)S(1)}, u32[]{:S(2)}, u32[]{:S(2)}) collective-permute-start(f32[256,256]{1,0:T(8,128)S(1)} %get-tuple-element.38.sent.before), channel_id=1, source_target_pairs={{0,8},{1,17},{2,10},{3,19},{4,12},{5,21},{6,14},{7,23},{8,0},{9,25... | collective-permute-start | bytes 786440 | tf_op jit(solution)/shard_map/ppermute | solution.py:413
  21.5 1.5 %collective-permute-start.12 = (f32[128,256]{1,0:T(8,128)S(1)}, f32[128,256]{1,0:T(8,128)S(1)}, u32[]{:S(2)}, u32[]{:S(2)}) collective-permute-start(f32[128,256]{1,0:T(8,128)S(1)} %far_block.1), channel_id=1, source_target_pairs={{0,4},{1,5},{2,6},{3,7},{4,0},{5,1},{6,2},{7,3},{8,12},{9,13},{10,... | collective-permute-start | bytes 393224 | tf_op jit(solution)/shard_map/ppermute | solution.py:354
  23.0 1.2 %update.1 = (f32[1024,256]{1,0:T(8,128)S(1)}, f32[256,256]{1,0:T(8,128)S(1)}) custom-call(f32[1024,256]{1,0:T(8,128)S(1)} %get-tuple-element.25.base, s32[2,256]{1,0:T(2,128)S(1)} %get-tuple-element.24.pivots, f32[256,256]{1,0:T(8,128)S(1)} %get-tuple-element.32.upper_in, f32[256,256]{1,0:T(8,128)S(1)} %get-tuple-element.33.displaced_in, ...), custom_call_target="tpu_custom_call" | custom-call | flops 5000000000 | tf_op jit(solution)/shard_map/update/pallas_call | solution.py:390
  24.2 2.2 %collective-permute-done.10.received.refs_0_ = f32[256,256]{1,0:T(8,128)S(1)} collective-permute-done((f32[256,256]{1,0:T(8,128)S(1)}, f32[256,256]{1,0:T(8,128)S(1)}, u32[]{:S(2)}, u32[]{:S(2)}) %collective-permute-start.10) | collective-permute-done | bytes 262176 | tf_op jit(solution)/shard_map/ppermute | solution.py:413
  26.5 1.6 %collective-permute-start.14 = (f32[256,256]{1,0:T(8,128)S(1)}, f32[256,256]{1,0:T(8,128)S(1)}, u32[]{:S(2)}, u32[]{:S(2)}) collective-permute-start(f32[256,256]{1,0:T(8,128)S(1)} %merge.3.before.sent), channel_id=1, source_target_pairs={{0,16},{1,9},{2,18},{3,11},{4,20},{5,13},{6,22},{7,15},{8,24},{9,1... | collective-permute-start | bytes 786440 | tf_op jit(solution)/shard_map/ppermute | solution.py:413
  28.2 3.9 %collective-permute-done.12.panel.far = f32[128,256]{1,0:T(8,128)S(1)} collective-permute-done((f32[128,256]{1,0:T(8,128)S(1)}, f32[128,256]{1,0:T(8,128)S(1)}, u32[]{:S(2)}, u32[]{:S(2)}) %collective-permute-start.12) | collective-permute-done | bytes 131104 | tf_op jit(solution)/shard_map/ppermute | solution.py:354
  32.2 0.2 halve.1
  32.5 1.0 %collective-permute-done.13.far_back = f32[128,256]{1,0:T(8,128)S(1)} collective-permute-done((f32[128,256]{1,0:T(8,128)S(1)}, f32[128,256]{1,0:T(8,128)S(1)}, u32[]{:S(2)}, u32[]{:S(2)}) %collective-permute-start.13) | collective-permute-done | bytes 131104 | tf_op jit(solution)/shard_map/ppermute | solution.py:358
  33.5 2.0 %finish.1 = f32[1024,256]{1,0:T(8,128)} custom-call(f32[1024,256]{1,0:T(8,128)S(1)} %get-tuple-element.34.base, s32[2,256]{1,0:T(2,128)S(1)} %get-tuple-element.24.pivots, f32[2,256,256]{2,1,0:T(8,128)S(1)} %copy-done, s32[256,256]{1,0:T(8,128)S(1)} %get-tuple-element.35.owner, f32[256,256]{1,0:T(8,128)S(1)} %get-tuple-element.36.refs_0_.top, ...), custom_call_target="tpu_custom_call" | custom-call | tf_op jit(solution)/shard_map/finish/pallas_call | solution.py:390
  (25 shorter events, 0.7 us)
Async XLA Ops:
  1.4 8.7 %collective-permute-start.1 = (f32[128,256]{1,0:T(8,128)S(1)}, f32[128,256]{1,0:T(8,128)S(1)}, u32[]{:S(2)}, u32[]{:S(2)}) collective-permute-start(f32[128,256]{1,0:T(8,128)S(1)} %get-tuple-element.29.one.panel.refs_0_), channel_id=1, source_target_pairs={{0,2},{1,3},{2,4},{3,5},{4,6},{5,7},{6,0},{7,1},{8,10},{9,11},{10,... | collective-permute-start | bytes 393224 | tf_op jit(solution)/shard_map/ppermute | solution.py:354
  5.1 6.4 %collective-permute-start = (f32[256,256]{1,0:T(8,128)S(1)}, f32[256,256]{1,0:T(8,128)S(1)}, u32[]{:S(2)}, u32[]{:S(2)}) collective-permute-start(f32[256,256]{1,0:T(8,128)S(1)} %first_slots.1.sent), channel_id=1, source_target_pairs={{0,8},{1,17},{2,10},{3,19},{4,12},{5,21},{6,14},{7,23},{8,0},{9,25... | collective-permute-start | bytes 786440 | tf_op jit(solution)/shard_map/ppermute | solution.py:413
  7.4 6.1 %collective-permute-start.5 = (f32[128,256]{1,0:T(8,128)S(1)}, f32[128,256]{1,0:T(8,128)S(1)}, u32[]{:S(2)}, u32[]{:S(2)}) collective-permute-start(f32[128,256]{1,0:T(8,128)S(1)} %down_block.1), channel_id=1, source_target_pairs={{0,6},{1,7},{2,0},{3,1},{4,2},{5,3},{6,4},{7,5},{8,14},{9,15},{10,... | collective-permute-start | bytes 393224 | tf_op jit(solution)/shard_map/ppermute | solution.py:354
  9.7 8.2 %collective-permute-start.8 = (f32[128,256]{1,0:T(8,128)S(1)}, f32[128,256]{1,0:T(8,128)S(1)}, u32[]{:S(2)}, u32[]{:S(2)}) collective-permute-start(f32[128,256]{1,0:T(8,128)S(1)} %get-tuple-element.37.own.panel.before), channel_id=1, source_target_pairs={{0,1},{1,0},{2,3},{3,2},{4,5},{5,4},{6,7},{7,6},{8,9},{9,8},{10,11... | collective-permute-start | bytes 393224 | tf_op jit(solution)/shard_map/ppermute | solution.py:358
  10.1 1.6 %collective-permute-start.2 = (f32[256,256]{1,0:T(8,128)S(1)}, f32[256,256]{1,0:T(8,128)S(1)}, u32[]{:S(2)}, u32[]{:S(2)}) collective-permute-start(f32[256,256]{1,0:T(8,128)S(1)} %stack.1), channel_id=1, source_target_pairs={{0,1},{1,0},{2,3},{3,2},{4,5},{5,4},{6,7},{7,6},{8,9},{9,8},{10,11... | collective-permute-start | bytes 786440 | tf_op jit(solution)/shard_map/ppermute | solution.py:358
  10.3 7.6 %collective-permute-start.4 = (f32[128,256]{1,0:T(8,128)S(1)}, f32[128,256]{1,0:T(8,128)S(1)}, u32[]{:S(2)}, u32[]{:S(2)}) collective-permute-start(f32[128,256]{1,0:T(8,128)S(1)} %collective-permute-done.1.other.refs_1_), channel_id=1, source_target_pairs={{0,2},{1,3},{2,4},{3,5},{4,6},{5,7},{6,0},{7,1},{8,10},{9,11},{10,... | collective-permute-start | bytes 393224 | tf_op jit(solution)/shard_map/ppermute | solution.py:354
  11.8 7.4 %collective-permute-start.3 = (f32[256,256]{1,0:T(8,128)S(1)}, f32[256,256]{1,0:T(8,128)S(1)}, u32[]{:S(2)}, u32[]{:S(2)}) collective-permute-start(f32[256,256]{1,0:T(8,128)S(1)} %merge.2.sent.before), channel_id=1, source_target_pairs={{0,16},{1,9},{2,18},{3,11},{4,20},{5,13},{6,22},{7,15},{8,24},{9,1... | collective-permute-start | bytes 786440 | tf_op jit(solution)/shard_map/ppermute | solution.py:413
  13.4 5.1 %collective-permute-start.7 = (f32[128,256]{1,0:T(8,128)S(1)}, f32[128,256]{1,0:T(8,128)S(1)}, u32[]{:S(2)}, u32[]{:S(2)}) collective-permute-start(f32[128,256]{1,0:T(8,128)S(1)} %collective-permute-done.5.refs_3_), channel_id=1, source_target_pairs={{0,1},{1,0},{2,3},{3,2},{4,5},{5,4},{6,7},{7,6},{8,9},{9,8},{10,11... | collective-permute-start | bytes 393224 | tf_op jit(solution)/shard_map/ppermute | solution.py:358
  17.9 1.3 %collective-permute-start.6 = (f32[128,256]{1,0:T(8,128)S(1)}, f32[128,256]{1,0:T(8,128)S(1)}, u32[]{:S(2)}, u32[]{:S(2)}) collective-permute-start(f32[128,256]{1,0:T(8,128)S(1)} %collective-permute-done.4.refs_2_), channel_id=1, source_target_pairs={{0,1},{1,0},{2,3},{3,2},{4,5},{5,4},{6,7},{7,6},{8,9},{9,8},{10,11... | collective-permute-start | bytes 393224 | tf_op jit(solution)/shard_map/ppermute | solution.py:358
  17.9 1.3 %copy-start = (f32[2,256,256]{2,1,0:T(8,128)S(1)}, f32[2,256,256]{2,1,0:T(8,128)}, u32[]{:S(2)}) copy-start(f32[2,256,256]{2,1,0:T(8,128)} %inverse.3) | copy-start | bytes 1572868
  17.9 10.2 %collective-permute-start.9 = (f32[256,256]{1,0:T(8,128)S(1)}, f32[256,256]{1,0:T(8,128)S(1)}, u32[]{:S(2)}, u32[]{:S(2)}) collective-permute-start(f32[256,256]{1,0:T(8,128)S(1)} %pack.1), channel_id=1, source_target_pairs={{0,2},{1,7},{2,4},{3,1},{4,6},{5,3},{6,0},{7,5},{8,10},{9,15},{10,... | collective-permute-start | bytes 786440 | tf_op jit(solution)/shard_map/ppermute | solution.py:376
  20.0 6.4 %collective-permute-start.10 = (f32[256,256]{1,0:T(8,128)S(1)}, f32[256,256]{1,0:T(8,128)S(1)}, u32[]{:S(2)}, u32[]{:S(2)}) collective-permute-start(f32[256,256]{1,0:T(8,128)S(1)} %get-tuple-element.38.sent.before), channel_id=1, source_target_pairs={{0,8},{1,17},{2,10},{3,19},{4,12},{5,21},{6,14},{7,23},{8,0},{9,25... | collective-permute-start | bytes 786440 | tf_op jit(solution)/shard_map/ppermute | solution.py:413
  21.5 10.6 %collective-permute-start.12 = (f32[128,256]{1,0:T(8,128)S(1)}, f32[128,256]{1,0:T(8,128)S(1)}, u32[]{:S(2)}, u32[]{:S(2)}) collective-permute-start(f32[128,256]{1,0:T(8,128)S(1)} %far_block.1), channel_id=1, source_target_pairs={{0,4},{1,5},{2,6},{3,7},{4,0},{5,1},{6,2},{7,3},{8,12},{9,13},{10,... | collective-permute-start | bytes 393224 | tf_op jit(solution)/shard_map/ppermute | solution.py:354
  26.5 7.0 %collective-permute-start.14 = (f32[256,256]{1,0:T(8,128)S(1)}, f32[256,256]{1,0:T(8,128)S(1)}, u32[]{:S(2)}, u32[]{:S(2)}) collective-permute-start(f32[256,256]{1,0:T(8,128)S(1)} %merge.3.before.sent), channel_id=1, source_target_pairs={{0,16},{1,9},{2,18},{3,11},{4,20},{5,13},{6,22},{7,15},{8,24},{9,1... | collective-permute-start | bytes 786440 | tf_op jit(solution)/shard_map/ppermute | solution.py:413
  28.1 4.1 %collective-permute-start.11 = (f32[256,256]{1,0:T(8,128)S(1)}, f32[256,256]{1,0:T(8,128)S(1)}, u32[]{:S(2)}, u32[]{:S(2)}) collective-permute-start(f32[256,256]{1,0:T(8,128)S(1)} %pair_piece.1), channel_id=1, source_target_pairs={{0,1},{1,0},{2,3},{3,2},{4,5},{5,4},{6,7},{7,6},{8,9},{9,8},{10,11... | collective-permute-start | bytes 786440 | tf_op jit(solution)/shard_map/ppermute | solution.py:358
  32.1 1.4 %collective-permute-start.13 = (f32[128,256]{1,0:T(8,128)S(1)}, f32[128,256]{1,0:T(8,128)S(1)}, u32[]{:S(2)}, u32[]{:S(2)}) collective-permute-start(f32[128,256]{1,0:T(8,128)S(1)} %far_piece.1), channel_id=1, source_target_pairs={{0,1},{1,0},{2,3},{3,2},{4,5},{5,4},{6,7},{7,6},{8,9},{9,8},{10,11... | collective-permute-start | bytes 393224 | tf_op jit(solution)/shard_map/ppermute | solution.py:358

commit v18 on v17

--- a/solution.py
+++ b/solution.py
@@ -46,7 +46,7 @@
 
 
 def pick(chosen, right):
-    return product(jnp.concatenate([chosen, chosen], axis=1), jnp.concatenate(right, axis=0))
+    return product(chosen, right[0]) + product(chosen, right[1])
 
 
 def one_hot(left, right):

time: 35.6 us -> 35.6 us (level)
  transfers between devices with their start and end apart: 15 -> 15, of which waited for: 8 -> 8; matrix products, arithmetic and copies ran while one was open for 0% -> 0% of each run, Pallas kernels for 13% -> 12%
where the time goes in v18:
time: 35.6 us; the launch traced here: 35.5 us
  waiting for transfers between devices  13.9 us (39%)
  starting transfers between devices  13.6 us (38%)
  Pallas kernels  7.81 us (22%)
    ppermute x4, waiting for transfers between devices, shift(): lax.ppermute(block, 'pcol', [(i, (i + 2 * distance) % count) for i in ran...  8.74 us
    pallas_call x17, Pallas kernels, call(): pl.pallas_call(kernel, out_shape=outs, in_specs=specs or [VMEM] * len(ope...  7.81 us
    ppermute x4, starting transfers between devices, shift(): lax.ppermute(block, 'pcol', [(i, (i + 2 * distance) % count) for i in ran...  6.83 us
    ppermute x4, starting transfers between devices, exchange(): received.append(lax.ppermute(sent, ('prow', 'pcol'), pairs))  6.39 us
    ppermute x4, waiting for transfers between devices, exchange(): received.append(lax.ppermute(sent, ('prow', 'pcol'), pairs))  3.22 us
    ppermute x6, waiting for transfers between devices, across(): return lax.ppermute(block, 'pcol', [(i, i ^ 1) for i in range(count)])  1.94 us
  transfers between devices with their start and end apart: 15, of which 8 were waited for; matrix products, arithmetic and copies ran while one was open for 0% of the time, Pallas kernels for 12%

profile of v18, /device:TPU:0, one launch (start us, length us, event | category | flops | bytes accessed | tf_op | source)
XLA Modules:
  0.0 35.5 jit_solution(17990410486264776050)
XLA Ops:
  0.0 1.4 %load.1 = (f32[1024,256]{1,0:T(8,128)S(1)}, s32[2,256]{1,0:T(2,128)S(1)}, f32[128,256]{1,0:T(8,128)S(1)}, f32[128,256]{1,0:T(8,128)S(1)}) custom-call(f32[1024,256]{1,0:T(8,128)} %matrix.1, s32[2,256]{1,0:T(2,128)} %pivots.1, f32[2,128,256]{2,1,0:T(8,128)} %panels.1), custom_call_target="tpu_custom_call" | custom-call | tf_op jit(solution)/shard_map/load/pallas_call | solution.py:390
  1.4 3.1 %collective-permute-start.1 = (f32[128,256]{1,0:T(8,128)S(1)}, f32[128,256]{1,0:T(8,128)S(1)}, u32[]{:S(2)}, u32[]{:S(2)}) collective-permute-start(f32[128,256]{1,0:T(8,128)S(1)} %get-tuple-element.29.one.panel.refs_0_), channel_id=1, source_target_pairs={{0,2},{1,3},{2,4},{3,5},{4,6},{5,7},{6,0},{7,1},{8,10},{9,11},{10,... | collective-permute-start | bytes 393224 | tf_op jit(solution)/shard_map/ppermute | solution.py:354
  4.5 0.5 %first_slots.1.sent = f32[256,256]{1,0:T(8,128)S(1)} custom-call(f32[1024,256]{1,0:T(8,128)S(1)} %get-tuple-element.23.matrix, s32[2,256]{1,0:T(2,128)S(1)} %get-tuple-element.24.pivots), custom_call_target="tpu_custom_call" | custom-call | tf_op jit(solution)/shard_map/first_slots/pallas_call | solution.py:390
  5.0 1.6 %collective-permute-start = (f32[256,256]{1,0:T(8,128)S(1)}, f32[256,256]{1,0:T(8,128)S(1)}, u32[]{:S(2)}, u32[]{:S(2)}) collective-permute-start(f32[256,256]{1,0:T(8,128)S(1)} %first_slots.1.sent), channel_id=1, source_target_pairs={{0,8},{1,17},{2,10},{3,19},{4,12},{5,21},{6,14},{7,23},{8,0},{9,25... | collective-permute-start | bytes 786440 | tf_op jit(solution)/shard_map/ppermute | solution.py:413
  6.6 0.7 %prepare.1 = (f32[1024,256]{1,0:T(8,128)S(1)}, f32[256,256]{1,0:T(8,128)S(1)}, s32[256,256]{1,0:T(8,128)S(1)}) custom-call(f32[1024,256]{1,0:T(8,128)S(1)} %get-tuple-element.23.matrix, s32[2,256]{1,0:T(2,128)S(1)} %get-tuple-element.24.pivots), custom_call_target="tpu_custom_call" | custom-call | flops 1000000000 | tf_op jit(solution)/shard_map/prepare/pallas_call | solution.py:390
  7.3 2.3 %collective-permute-start.5 = (f32[128,256]{1,0:T(8,128)S(1)}, f32[128,256]{1,0:T(8,128)S(1)}, u32[]{:S(2)}, u32[]{:S(2)}) collective-permute-start(f32[128,256]{1,0:T(8,128)S(1)} %down_block.1), channel_id=1, source_target_pairs={{0,6},{1,7},{2,0},{3,1},{4,2},{5,3},{6,4},{7,5},{8,14},{9,15},{10,... | collective-permute-start | bytes 393224 | tf_op jit(solution)/shard_map/ppermute | solution.py:354
  9.6 0.5 %collective-permute-done.1.other.refs_1_ = f32[128,256]{1,0:T(8,128)S(1)} collective-permute-done((f32[128,256]{1,0:T(8,128)S(1)}, f32[128,256]{1,0:T(8,128)S(1)}, u32[]{:S(2)}, u32[]{:S(2)}) %collective-permute-start.1) | collective-permute-done | bytes 131104 | tf_op jit(solution)/shard_map/ppermute | solution.py:354
  10.2 0.3 holders.1
  10.5 1.0 %collective-permute-done.received.refs_0_ = f32[256,256]{1,0:T(8,128)S(1)} collective-permute-done((f32[256,256]{1,0:T(8,128)S(1)}, f32[256,256]{1,0:T(8,128)S(1)}, u32[]{:S(2)}, u32[]{:S(2)}) %collective-permute-start) | collective-permute-done | bytes 262176 | tf_op jit(solution)/shard_map/ppermute | solution.py:413
  11.5 0.2 collective-permute-done.2.refs_0_.refs_4_
  11.8 1.6 %collective-permute-start.3 = (f32[256,256]{1,0:T(8,128)S(1)}, f32[256,256]{1,0:T(8,128)S(1)}, u32[]{:S(2)}, u32[]{:S(2)}) collective-permute-start(f32[256,256]{1,0:T(8,128)S(1)} %merge.2.sent.before), channel_id=1, source_target_pairs={{0,16},{1,9},{2,18},{3,11},{4,20},{5,13},{6,22},{7,15},{8,24},{9,1... | collective-permute-start | bytes 786440 | tf_op jit(solution)/shard_map/ppermute | solution.py:413
  13.5 4.4 %collective-permute-done.4.refs_2_ = f32[128,256]{1,0:T(8,128)S(1)} collective-permute-done((f32[128,256]{1,0:T(8,128)S(1)}, f32[128,256]{1,0:T(8,128)S(1)}, u32[]{:S(2)}, u32[]{:S(2)}) %collective-permute-start.4) | collective-permute-done | bytes 131104 | tf_op jit(solution)/shard_map/ppermute | solution.py:354
  18.0 0.6 %collect.1 = (bf16[256,256]{1,0:T(8,128)(2,1)S(1)}, bf16[256,256]{1,0:T(8,128)(2,1)S(1)}) custom-call(s32[256,256]{1,0:T(8,128)S(1)} %get-tuple-element.28.before.places, f32[128,256]{1,0:T(8,128)S(1)} %get-tuple-element.29.one.panel.refs_0_, f32[128,256]{1,0:T(8,128)S(1)} %collective-permute-done.1.other.refs_1_, ...), custom_call_target="tpu_custom_call" | custom-call | flops 1500000000 | tf_op jit(solution)/shard_map/collect/pallas_call | solution.py:390
  18.6 0.7 %collective-permute-done.6.refs_4_.refs_5_ = f32[128,256]{1,0:T(8,128)S(1)} collective-permute-done((f32[128,256]{1,0:T(8,128)S(1)}, f32[128,256]{1,0:T(8,128)S(1)}, u32[]{:S(2)}, u32[]{:S(2)}) %collective-permute-start.6) | collective-permute-done | bytes 131104 | tf_op jit(solution)/shard_map/ppermute | solution.py:358
  19.2 0.7 %solve.1 = (f32[256,256]{1,0:T(8,128)S(1)}, f32[256,256]{1,0:T(8,128)S(1)}, f32[256,256]{1,0:T(8,128)S(1)}) custom-call(f32[1024,256]{1,0:T(8,128)S(1)} %get-tuple-element.23.matrix, s32[2,256]{1,0:T(2,128)S(1)} %get-tuple-element.24.pivots, f32[2,256,256]{2,1,0:T(8,128)S(1)} %copy-done, s32[256,256]{1,0:T(8,128)S(1)} %get-tuple-element.26.owner, ...), custom_call_target="tpu_custom_call" | custom-call | tf_op jit(solution)/shard_map/solve/pallas_call | solution.py:390
  19.9 1.6 %collective-permute-start.10 = (f32[256,256]{1,0:T(8,128)S(1)}, f32[256,256]{1,0:T(8,128)S(1)}, u32[]{:S(2)}, u32[]{:S(2)}) collective-permute-start(f32[256,256]{1,0:T(8,128)S(1)} %get-tuple-element.38.sent.before), channel_id=1, source_target_pairs={{0,8},{1,17},{2,10},{3,19},{4,12},{5,21},{6,14},{7,23},{8,0},{9,25... | collective-permute-start | bytes 786440 | tf_op jit(solution)/shard_map/ppermute | solution.py:413
  21.5 1.4 %collective-permute-start.12 = (f32[128,256]{1,0:T(8,128)S(1)}, f32[128,256]{1,0:T(8,128)S(1)}, u32[]{:S(2)}, u32[]{:S(2)}) collective-permute-start(f32[128,256]{1,0:T(8,128)S(1)} %far_block.1), channel_id=1, source_target_pairs={{0,4},{1,5},{2,6},{3,7},{4,0},{5,1},{6,2},{7,3},{8,12},{9,13},{10,... | collective-permute-start | bytes 393224 | tf_op jit(solution)/shard_map/ppermute | solution.py:354
  22.9 1.2 %update.1 = (f32[1024,256]{1,0:T(8,128)S(1)}, f32[256,256]{1,0:T(8,128)S(1)}) custom-call(f32[1024,256]{1,0:T(8,128)S(1)} %get-tuple-element.25.base, s32[2,256]{1,0:T(2,128)S(1)} %get-tuple-element.24.pivots, f32[256,256]{1,0:T(8,128)S(1)} %get-tuple-element.32.upper_in, f32[256,256]{1,0:T(8,128)S(1)} %get-tuple-element.33.displaced_in, ...), custom_call_target="tpu_custom_call" | custom-call | flops 5000000000 | tf_op jit(solution)/shard_map/update/pallas_call | solution.py:390
  24.1 2.3 %collective-permute-done.10.received.refs_0_ = f32[256,256]{1,0:T(8,128)S(1)} collective-permute-done((f32[256,256]{1,0:T(8,128)S(1)}, f32[256,256]{1,0:T(8,128)S(1)}, u32[]{:S(2)}, u32[]{:S(2)}) %collective-permute-start.10) | collective-permute-done | bytes 262176 | tf_op jit(solution)/shard_map/ppermute | solution.py:413
  26.5 1.6 %collective-permute-start.14 = (f32[256,256]{1,0:T(8,128)S(1)}, f32[256,256]{1,0:T(8,128)S(1)}, u32[]{:S(2)}, u32[]{:S(2)}) collective-permute-start(f32[256,256]{1,0:T(8,128)S(1)} %merge.3.before.sent), channel_id=1, source_target_pairs={{0,16},{1,9},{2,18},{3,11},{4,20},{5,13},{6,22},{7,15},{8,24},{9,1... | collective-permute-start | bytes 786440 | tf_op jit(solution)/shard_map/ppermute | solution.py:413
  28.2 3.8 %collective-permute-done.12.panel.far = f32[128,256]{1,0:T(8,128)S(1)} collective-permute-done((f32[128,256]{1,0:T(8,128)S(1)}, f32[128,256]{1,0:T(8,128)S(1)}, u32[]{:S(2)}, u32[]{:S(2)}) %collective-permute-start.12) | collective-permute-done | bytes 131104 | tf_op jit(solution)/shard_map/ppermute | solution.py:354
  32.2 0.2 halve.1
  32.4 1.0 %collective-permute-done.13.far_back = f32[128,256]{1,0:T(8,128)S(1)} collective-permute-done((f32[128,256]{1,0:T(8,128)S(1)}, f32[128,256]{1,0:T(8,128)S(1)}, u32[]{:S(2)}, u32[]{:S(2)}) %collective-permute-start.13) | collective-permute-done | bytes 131104 | tf_op jit(solution)/shard_map/ppermute | solution.py:358
  33.5 2.0 %finish.1 = f32[1024,256]{1,0:T(8,128)} custom-call(f32[1024,256]{1,0:T(8,128)S(1)} %get-tuple-element.34.base, s32[2,256]{1,0:T(2,128)S(1)} %get-tuple-element.24.pivots, f32[2,256,256]{2,1,0:T(8,128)S(1)} %copy-done, s32[256,256]{1,0:T(8,128)S(1)} %get-tuple-element.35.owner, f32[256,256]{1,0:T(8,128)S(1)} %get-tuple-element.36.refs_0_.top, ...), custom_call_target="tpu_custom_call" | custom-call | tf_op jit(solution)/shard_map/finish/pallas_call | solution.py:390
  (25 shorter events, 0.7 us)
Async XLA Ops:
  1.4 8.7 %collective-permute-start.1 = (f32[128,256]{1,0:T(8,128)S(1)}, f32[128,256]{1,0:T(8,128)S(1)}, u32[]{:S(2)}, u32[]{:S(2)}) collective-permute-start(f32[128,256]{1,0:T(8,128)S(1)} %get-tuple-element.29.one.panel.refs_0_), channel_id=1, source_target_pairs={{0,2},{1,3},{2,4},{3,5},{4,6},{5,7},{6,0},{7,1},{8,10},{9,11},{10,... | collective-permute-start | bytes 393224 | tf_op jit(solution)/shard_map/ppermute | solution.py:354
  5.0 6.4 %collective-permute-start = (f32[256,256]{1,0:T(8,128)S(1)}, f32[256,256]{1,0:T(8,128)S(1)}, u32[]{:S(2)}, u32[]{:S(2)}) collective-permute-start(f32[256,256]{1,0:T(8,128)S(1)} %first_slots.1.sent), channel_id=1, source_target_pairs={{0,8},{1,17},{2,10},{3,19},{4,12},{5,21},{6,14},{7,23},{8,0},{9,25... | collective-permute-start | bytes 786440 | tf_op jit(solution)/shard_map/ppermute | solution.py:413
  7.3 6.1 %collective-permute-start.5 = (f32[128,256]{1,0:T(8,128)S(1)}, f32[128,256]{1,0:T(8,128)S(1)}, u32[]{:S(2)}, u32[]{:S(2)}) collective-permute-start(f32[128,256]{1,0:T(8,128)S(1)} %down_block.1), channel_id=1, source_target_pairs={{0,6},{1,7},{2,0},{3,1},{4,2},{5,3},{6,4},{7,5},{8,14},{9,15},{10,... | collective-permute-start | bytes 393224 | tf_op jit(solution)/shard_map/ppermute | solution.py:354
  9.6 8.3 %collective-permute-start.8 = (f32[128,256]{1,0:T(8,128)S(1)}, f32[128,256]{1,0:T(8,128)S(1)}, u32[]{:S(2)}, u32[]{:S(2)}) collective-permute-start(f32[128,256]{1,0:T(8,128)S(1)} %get-tuple-element.37.own.panel.before), channel_id=1, source_target_pairs={{0,1},{1,0},{2,3},{3,2},{4,5},{5,4},{6,7},{7,6},{8,9},{9,8},{10,11... | collective-permute-start | bytes 393224 | tf_op jit(solution)/shard_map/ppermute | solution.py:358
  10.1 1.6 %collective-permute-start.2 = (f32[256,256]{1,0:T(8,128)S(1)}, f32[256,256]{1,0:T(8,128)S(1)}, u32[]{:S(2)}, u32[]{:S(2)}) collective-permute-start(f32[256,256]{1,0:T(8,128)S(1)} %stack.1), channel_id=1, source_target_pairs={{0,1},{1,0},{2,3},{3,2},{4,5},{5,4},{6,7},{7,6},{8,9},{9,8},{10,11... | collective-permute-start | bytes 786440 | tf_op jit(solution)/shard_map/ppermute | solution.py:358
  10.2 7.7 %collective-permute-start.4 = (f32[128,256]{1,0:T(8,128)S(1)}, f32[128,256]{1,0:T(8,128)S(1)}, u32[]{:S(2)}, u32[]{:S(2)}) collective-permute-start(f32[128,256]{1,0:T(8,128)S(1)} %collective-permute-done.1.other.refs_1_), channel_id=1, source_target_pairs={{0,2},{1,3},{2,4},{3,5},{4,6},{5,7},{6,0},{7,1},{8,10},{9,11},{10,... | collective-permute-start | bytes 393224 | tf_op jit(solution)/shard_map/ppermute | solution.py:354
  11.8 7.4 %collective-permute-start.3 = (f32[256,256]{1,0:T(8,128)S(1)}, f32[256,256]{1,0:T(8,128)S(1)}, u32[]{:S(2)}, u32[]{:S(2)}) collective-permute-start(f32[256,256]{1,0:T(8,128)S(1)} %merge.2.sent.before), channel_id=1, source_target_pairs={{0,16},{1,9},{2,18},{3,11},{4,20},{5,13},{6,22},{7,15},{8,24},{9,1... | collective-permute-start | bytes 786440 | tf_op jit(solution)/shard_map/ppermute | solution.py:413
  13.4 5.1 %collective-permute-start.7 = (f32[128,256]{1,0:T(8,128)S(1)}, f32[128,256]{1,0:T(8,128)S(1)}, u32[]{:S(2)}, u32[]{:S(2)}) collective-permute-start(f32[128,256]{1,0:T(8,128)S(1)} %collective-permute-done.5.refs_3_), channel_id=1, source_target_pairs={{0,1},{1,0},{2,3},{3,2},{4,5},{5,4},{6,7},{7,6},{8,9},{9,8},{10,11... | collective-permute-start | bytes 393224 | tf_op jit(solution)/shard_map/ppermute | solution.py:358
  17.9 1.3 %collective-permute-start.6 = (f32[128,256]{1,0:T(8,128)S(1)}, f32[128,256]{1,0:T(8,128)S(1)}, u32[]{:S(2)}, u32[]{:S(2)}) collective-permute-start(f32[128,256]{1,0:T(8,128)S(1)} %collective-permute-done.4.refs_2_), channel_id=1, source_target_pairs={{0,1},{1,0},{2,3},{3,2},{4,5},{5,4},{6,7},{7,6},{8,9},{9,8},{10,11... | collective-permute-start | bytes 393224 | tf_op jit(solution)/shard_map/ppermute | solution.py:358
  17.9 1.3 %copy-start = (f32[2,256,256]{2,1,0:T(8,128)S(1)}, f32[2,256,256]{2,1,0:T(8,128)}, u32[]{:S(2)}) copy-start(f32[2,256,256]{2,1,0:T(8,128)} %inverse.3) | copy-start | bytes 1572868
  17.9 10.2 %collective-permute-start.9 = (f32[256,256]{1,0:T(8,128)S(1)}, f32[256,256]{1,0:T(8,128)S(1)}, u32[]{:S(2)}, u32[]{:S(2)}) collective-permute-start(f32[256,256]{1,0:T(8,128)S(1)} %pack.1), channel_id=1, source_target_pairs={{0,2},{1,7},{2,4},{3,1},{4,6},{5,3},{6,0},{7,5},{8,10},{9,15},{10,... | collective-permute-start | bytes 786440 | tf_op jit(solution)/shard_map/ppermute | solution.py:376
  19.9 6.4 %collective-permute-start.10 = (f32[256,256]{1,0:T(8,128)S(1)}, f32[256,256]{1,0:T(8,128)S(1)}, u32[]{:S(2)}, u32[]{:S(2)}) collective-permute-start(f32[256,256]{1,0:T(8,128)S(1)} %get-tuple-element.38.sent.before), channel_id=1, source_target_pairs={{0,8},{1,17},{2,10},{3,19},{4,12},{5,21},{6,14},{7,23},{8,0},{9,25... | collective-permute-start | bytes 786440 | tf_op jit(solution)/shard_map/ppermute | solution.py:413
  21.5 10.5 %collective-permute-start.12 = (f32[128,256]{1,0:T(8,128)S(1)}, f32[128,256]{1,0:T(8,128)S(1)}, u32[]{:S(2)}, u32[]{:S(2)}) collective-permute-start(f32[128,256]{1,0:T(8,128)S(1)} %far_block.1), channel_id=1, source_target_pairs={{0,4},{1,5},{2,6},{3,7},{4,0},{5,1},{6,2},{7,3},{8,12},{9,13},{10,... | collective-permute-start | bytes 393224 | tf_op jit(solution)/shard_map/ppermute | solution.py:354
  26.5 7.0 %collective-permute-start.14 = (f32[256,256]{1,0:T(8,128)S(1)}, f32[256,256]{1,0:T(8,128)S(1)}, u32[]{:S(2)}, u32[]{:S(2)}) collective-permute-start(f32[256,256]{1,0:T(8,128)S(1)} %merge.3.before.sent), channel_id=1, source_target_pairs={{0,16},{1,9},{2,18},{3,11},{4,20},{5,13},{6,22},{7,15},{8,24},{9,1... | collective-permute-start | bytes 786440 | tf_op jit(solution)/shard_map/ppermute | solution.py:413
  28.1 4.1 %collective-permute-start.11 = (f32[256,256]{1,0:T(8,128)S(1)}, f32[256,256]{1,0:T(8,128)S(1)}, u32[]{:S(2)}, u32[]{:S(2)}) collective-permute-start(f32[256,256]{1,0:T(8,128)S(1)} %pair_piece.1), channel_id=1, source_target_pairs={{0,1},{1,0},{2,3},{3,2},{4,5},{5,4},{6,7},{7,6},{8,9},{9,8},{10,11... | collective-permute-start | bytes 786440 | tf_op jit(solution)/shard_map/ppermute | solution.py:358
  32.1 1.4 %collective-permute-start.13 = (f32[128,256]{1,0:T(8,128)S(1)}, f32[128,256]{1,0:T(8,128)S(1)}, u32[]{:S(2)}, u32[]{:S(2)}) collective-permute-start(f32[128,256]{1,0:T(8,128)S(1)} %far_piece.1), channel_id=1, source_target_pairs={{0,1},{1,0},{2,3},{3,2},{4,5},{5,4},{6,7},{7,6},{8,9},{9,8},{10,11... | collective-permute-start | bytes 393224 | tf_op jit(solution)/shard_map/ppermute | solution.py:358
